TPU v7x, 32 devices: a whole 2x2x4 slice. The times are simulated.
32 devices in a mesh: cfg: 2 (over x), wide: 4 (over z), narrow: 4 (over y, core).
Axes of the slice: x: 2, y: 2, z: 4, core: 2. Of those that a mesh axis runs over, the one named last changes fastest.
Arguments:
- hidden: bfloat16 [2, 512, 3072], P('cfg', 'wide', 'narrow'), may hold values from -120 to 120
- split_table: int32 [4], replicated, may hold values from 1 to 128, 256 in all
- modulation: float32 [8, 3072], P(None, 'narrow'), may hold values from -4 to 4
- expand_weight: bfloat16 [3072, 12288], P('narrow', 'wide'), may hold values from -0.109375 to 0.109375
- contract_weight: bfloat16 [12288, 3072], P('wide', 'narrow'), may hold values from -0.0546875 to 0.0546875
- output_weight: bfloat16 [3072, 64], P('narrow'), may hold values from -0.109375 to 0.109375
- latent: float32 [512, 64], P('wide'), may hold values from -6 to 6
- timestep: int32 [1], replicated, may hold values from 20 to 499
Outputs:
- layer_out: bfloat16 [2, 512, 3072], P('cfg', 'wide', 'narrow')
- clean_latent: float32 [512, 64], P('wide')
Inputs may be any that keep to these rules, and one draw needn't show every extreme that they name: `split_table`: the entries sum to 256, and the largest is exactly 128.
All inputs are finite; a program needn't handle non-finite values.
Results may differ from a plain program's by a relative error of at most 0.0056.
Values may be sent and summed in bfloat16 or wider, within the bound.
No kernel may reach another device: no remote copies, remote signals or barrier semaphores. Data moves between devices by JAX's collectives and lax.ppermute only.
A program may use at most 64 MiB of HBM per device.

v0:
```python
import jax
import jax.numpy as jnp
from jax import lax
from jax.sharding import PartitionSpec as P

D = 3072
TEXT = 226


norm_eps = 1e-05
guidance = 6.0


def alpha_table():
    steps_index = jnp.arange(1000, dtype=jnp.int32)
    start_root = 0.00085**0.5
    end_root = 0.012**0.5
    roots = start_root + (end_root - start_root) * steps_index.astype(jnp.float32) / 999.0
    return (steps_index, jnp.cumprod(1.0 - roots * roots))


def feature_norm(values, shifts, scaling):
    totals, squares = lax.psum(
        (jnp.sum(values, -1, keepdims=True), jnp.sum(values * values, -1, keepdims=True)), "narrow"
    )
    average = totals / D
    variance = squares / D - average * average
    return (values - average) * lax.rsqrt(variance + norm_eps) * (1.0 + scaling) + shifts


def on_device(
    hidden, split_table, modulation, expand_weight, contract_weight, output_weight, latent, timestep
):
    capacity = hidden.shape[1]
    wide_index = lax.axis_index("wide")
    table_index = jnp.arange(split_table.shape[0], dtype=jnp.int32)
    offset = jnp.sum(jnp.where(table_index < wide_index, split_table, 0))
    own_count = jnp.sum(jnp.where(table_index == wide_index, split_table, 0))
    slot_index = jnp.arange(capacity, dtype=jnp.int32)
    position = offset + slot_index
    slot_live = slot_index < own_count
    is_text = slot_live & (position < TEXT)
    is_video = slot_live & (position >= TEXT)
    text_column = is_text[:, None]
    shifts = jnp.where(text_column, modulation[3], modulation[0])
    scaling = jnp.where(text_column, modulation[4], modulation[1])
    gating = jnp.where(text_column, modulation[5], modulation[2])
    values = hidden[0].astype(jnp.float32)
    normed = feature_norm(values, shifts, scaling).astype(jnp.bfloat16)
    hidden_part = jnp.dot(
        lax.all_gather(normed, "wide", axis=0, tiled=True),
        expand_weight,
        preferred_element_type=jnp.float32,
    )
    hidden_pre = lax.psum(hidden_part, "narrow")
    activated = jax.nn.gelu(hidden_pre, approximate=True).astype(jnp.bfloat16)
    ff_result = lax.psum_scatter(
        jnp.dot(activated, contract_weight, preferred_element_type=jnp.float32),
        "wide",
        scatter_dimension=0,
        tiled=True,
    )
    layer_out = jnp.where(slot_live[:, None], values + gating * ff_result, 0.0).astype(jnp.bfloat16)
    final_in = layer_out.astype(jnp.float32)
    final_normed = feature_norm(final_in, modulation[6], modulation[7]).astype(jnp.bfloat16)
    velocity_part = jnp.dot(final_normed, output_weight, preferred_element_type=jnp.float32)
    copy_weight = jnp.where(lax.axis_index("cfg") == 0, guidance, 1.0 - guidance)
    guided = lax.psum(velocity_part * copy_weight, ("cfg", "narrow"))
    steps_index, alpha_bar = alpha_table()
    alpha_now = jnp.sum(jnp.where(steps_index == timestep[0], alpha_bar, 0.0))
    clean_latent = jnp.where(
        is_video[:, None], jnp.sqrt(alpha_now) * latent - jnp.sqrt(1.0 - alpha_now) * guided, 0.0
    )
    return (layer_out[None], clean_latent)


def solution(mesh):
    return jax.shard_map(
        on_device,
        mesh=mesh,
        in_specs=(
            P("cfg", "wide", "narrow"),
            P(),
            P(None, "narrow"),
            P("narrow", "wide"),
            P("wide", "narrow"),
            P("narrow", None),
            P("wide", None),
            P(),
        ),
        out_specs=(P("cfg", "wide", "narrow"), P("wide", None)),
        check_vma=False,
    )
```

profile of v0, /device:TPU:0, one launch (start us, length us, event | category | flops | bytes accessed | tf_op | source)
XLA Modules:
  0.0 251.0 jit_solution(221754160541477280)
XLA Ops:
  7.2 1.0 convert_reduce_fusion.1
  8.3 1.1 fusion.17
  9.3 1.1 add_reduce_fusion
  10.4 1.3 fusion.30
  11.7 1.3 compare_and_fusion.1
  13.0 8.4 %all-reduce.2 = (f32[128,1]{0,1:T(1,128)S(1)}, f32[128,1]{0,1:T(1,128)S(1)}) all-reduce(f32[128,1]{0,1:T(1,128)S(1)} %bitcast.48, f32[128,1]{0,1:T(1,128)S(1)} %bitcast.47), channel_id=1, replica_groups=mesh['cfg'=2,'wide'=4,'narrow'=4] {'narrow'}, use_global_device_ids=true, to_apply=%region_5.6 | all-reduce | flops 256 | bytes 2048 | tf_op jit(solution)/shard_map/psum | solution.py:23
  21.4 1.1 fusion.16
  22.5 19.6 %all_gather.3 = bf16[512,768]{1,0:T(8,128)(2,1)S(1)} all-gather(bf16[128,768]{1,0:T(8,128)(2,1)S(1)} %fusion.16), channel_id=1, replica_groups=mesh['cfg'=2,'wide'=4,'narrow'=4] {'wide'}, dimensions={0}, use_global_device_ids=true | all-gather | bytes 983040 | tf_op jit(solution)/shard_map/all_gather | solution.py:51
  42.2 6.9 %fusion.37 = f32[512,3072]{1,0:T(8,128)} fusion(bf16[512,768]{1,0:T(8,128)(2,1)S(1)} %all_gather.3, bf16[768,3072]{1,0:T(8,128)(2,1)} %param.11), kind=kOutput, calls=%fused_computation.66 | convolution fusion | flops 2415919104 | bytes 11796480 | tf_op jit(solution)/shard_map/dot_general | solution.py:50
  49.1 118.4 %all-reduce.5.cloned.1.call-done = f32[512,3072]{1,0:T(8,128)} async-done(((f32[512,3072]{1,0:T(8,128)}), f32[512,3072]{1,0:T(8,128)}) %all-reduce.5.cloned.1.call-update) | async-done | bytes 6291472 | tf_op jit(solution)/shard_map/psum | solution.py:55
  167.5 9.0 %fusion.8 = f32[512,768]{1,0:T(8,128)} fusion(bf16[3072,768]{1,0:T(8,128)(2,1)} %param.12, f32[512,3072]{1,0:T(8,128)} %all-reduce.5.cloned.1.call-done), kind=kOutput, calls=%fused_computation.9 | convolution fusion | flops 2430074880 | bytes 12582912 | tf_op jit(solution)/shard_map/dot_general | solution.py:58
  176.6 0.3 reduce-window.9
  176.9 0.1 slice.40
  177.6 0.1 slice_reduce_fusion
  177.7 0.1 multiply_bitcast_fusion
  177.8 0.6 select_reduce_fusion
  179.8 0.7 iota_compare_fusion.1
  180.4 1.3 compare_and_fusion
  181.7 30.5 %reduce-scatter.2.cloned.1.call-done = f32[128,768]{1,0:T(8,128)} async-done(((f32[512,768]{1,0:T(8,128)}), f32[128,768]{1,0:T(8,128)}) %reduce-scatter.2.cloned.1.call-update) | async-done | bytes 393232 | tf_op jit(solution)/shard_map/reduce_scatter | solution.py:57
  212.2 1.3 convert_reduce_fusion
  213.5 6.4 %all-reduce.1 = (f32[128,1]{0,1:T(1,128)S(1)}, f32[128,1]{0,1:T(1,128)S(1)}) all-reduce(f32[128,1]{0,1:T(1,128)S(1)} %bitcast.50, f32[128,1]{0,1:T(1,128)S(1)} %bitcast.49), channel_id=1, replica_groups=mesh['cfg'=2,'wide'=4,'narrow'=4] {'narrow'}, use_global_device_ids=true, to_apply=%region_14.15 | all-reduce | flops 256 | bytes 2048 | tf_op jit(solution)/shard_map/psum | solution.py:23
  219.9 0.3 convolution_multiply_fusion
  220.2 23.3 %psum.47 = f32[128,64]{0,1:T(8,128)S(1)} all-reduce(f32[128,64]{0,1:T(8,128)S(1)} %convolution_multiply_fusion), channel_id=1, replica_groups=mesh['cfg'=2,'wide'=4,'narrow'=4] {'cfg','narrow'}, use_global_device_ids=true, to_apply=%region_15.16 | all-reduce | flops 8192 | bytes 65536 | tf_op jit(solution)/shard_map/psum | solution.py:68
  243.5 0.6 subtract_select_fusion
  (17 shorter events, 0.2 us)
Async XLA Ops:
  7.2 212.8 %copy-start = (bf16[768,64]{0,1:T(8,128)(2,1)S(1)}, bf16[768,64]{0,1:T(8,128)(2,1)}, u32[]{:S(2)}) copy-start(bf16[768,64]{0,1:T(8,128)(2,1)} %param.13) | copy-start | bytes 294916
  7.2 160.3 %all-reduce.5.cloned.1.call-start = ((), (), s32[]{:S(2)}) async-start(), calls=%async_computation.1 | async-start | bytes 12582912 | tf_op jit(solution)/shard_map/psum | solution.py:55
  49.1 163.1 %copy-start.1 = (bf16[1,128,768]{2,1,0:T(8,128)(2,1)S(1)}, bf16[1,128,768]{2,1,0:T(8,128)(2,1)}, u32[]{:S(2)}) copy-start(bf16[1,128,768]{2,1,0:T(8,128)(2,1)} %param.8) | copy-start | bytes 589828
  49.1 194.4 %copy-start.3 = (f32[128,64]{0,1:T(8,128)S(1)}, f32[128,64]{0,1:T(8,128)}, u32[]{:S(2)}) copy-start(f32[128,64]{0,1:T(8,128)} %param.14) | copy-start | bytes 98308
  49.1 163.1 %reduce-scatter.2.cloned.1.call-start = ((), (), s32[]{:S(2)}) async-start(), calls=%async_computation.2 | async-start | bytes 1966080 | tf_op jit(solution)/shard_map/reduce_scatter | solution.py:57
  213.5 30.7 %copy-start.2 = (bf16[128,768]{1,0:T(8,128)(2,1)}, bf16[128,768]{1,0:T(8,128)(2,1)S(1)}, u32[]{:S(2)}) copy-start(bf16[128,768]{1,0:T(8,128)(2,1)S(1)} %get-tuple-element.18) | copy-start | bytes 589828
Sparse Core Ops, SparseCore 0:
  49.2 118.2 all-reduce.4
  176.7 35.4 reduce-scatter.1
where the time goes:
time: 251 us
  waiting for transfers between devices  149 us (59%)
  blocking collectives  57.7 us (23%)
  matrix products  16.2 us (6%)
  between operations  16.1 us (6%)
  other arithmetic  11.8 us (5%)
    psum x1, waiting for transfers between devices, on_device(): hidden_pre = lax.psum(hidden_part, 'narrow')  118 us
    reduce_scatter x1, waiting for transfers between devices, on_device(): lax.psum_scatter(jnp.dot(activated, contract_weight, preferred_element_ty...  30.5 us
    psum x1, blocking collectives, on_device(): guided = lax.psum(velocity_part * copy_weight, ('cfg', 'narrow'))  23.3 us
    all_gather x1, blocking collectives, on_device(): lax.all_gather(normed, 'wide', axis=0, tiled=True)  19.6 us
    psum x2, blocking collectives, feature_norm(): lax.psum((jnp.sum(values, -1, keepdims=True), jnp.sum(values * values, -1...  14.8 us
    dot_general x1, matrix products, on_device(): jnp.dot(activated, contract_weight, preferred_element_type=jnp.float32)  9.02 us
    dot_general x1, matrix products, on_device(): jnp.dot(lax.all_gather(normed, 'wide', axis=0, tiled=True), expand_weight...  6.88 us
  transfers between devices with their start and end apart: 2, of which 2 were waited for; matrix products, arithmetic and copies ran while one was open for 1% of the time, Pallas kernels for 0%

commit v1 on v0

--- a/solution.py
+++ b/solution.py
@@ -28,7 +28,7 @@
     return (values - average) * lax.rsqrt(variance + norm_eps) * (1.0 + scaling) + shifts
 
 
-def on_device(
+def any_slice(
     hidden, split_table, modulation, expand_weight, contract_weight, output_weight, latent, timestep
 ):
     capacity = hidden.shape[1]
@@ -74,9 +74,159 @@
     return (layer_out[None], clean_latent)
 
 
+def swap(array, axis, distance, size):
+    return lax.ppermute(array, axis, [(i, i ^ distance) for i in range(size)])
+
+
+def core_swap(array):
+    return swap(array, "narrow", 1, 4)
+
+
+def y_swap(array):
+    return swap(array, "narrow", 2, 4)
+
+
+def pick(table, index):
+    return jnp.sum(jnp.where(jnp.arange(4, dtype=jnp.int32) == index, table, 0))
+
+
+def four_blocks(
+    hidden, split_table, modulation, expand_weight, contract_weight, output_weight, latent, timestep
+):
+    capacity = hidden.shape[1]
+    half = capacity // 2
+    block = lax.axis_index("wide")
+    first_core = lax.axis_index("narrow") % 2 == 0
+    units = expand_weight.shape[1] // 2
+
+    counts = split_table
+    order = jnp.arange(4, dtype=jnp.int32)
+    earlier = order[None, :] < order[:, None]
+    largest = jnp.min(jnp.where(counts == capacity, order, 4))
+    other_counts = jnp.where(order == largest, 0, counts)
+    other_before = jnp.sum(jnp.where(earlier, other_counts[None, :], 0), 1)
+    first_counts = jnp.where(
+        order == largest, half, jnp.clip(half - other_before, 0, counts)
+    )
+    offsets = jnp.sum(jnp.where(earlier, counts[None, :], 0), 1)
+    own_first = pick(first_counts, block)
+    own_count = pick(counts, block)
+    offset = pick(offsets, block)
+
+    slot_index = jnp.arange(capacity, dtype=jnp.int32)
+    position = offset + slot_index
+    slot_live = slot_index < own_count
+    is_text = slot_live & (position < TEXT)
+    is_video = slot_live & (position >= TEXT)
+    text_column = is_text[:, None]
+    shifts = jnp.where(text_column, modulation[3], modulation[0])
+    scaling = jnp.where(text_column, modulation[4], modulation[1])
+    gating = jnp.where(text_column, modulation[5], modulation[2])
+
+    piece_row = jnp.arange(half, dtype=jnp.int32)
+    rows_a, rows_b = [], []
+    base_a, base_b = 0, 0
+    for s in range(4):
+        of_first, of_count = pick(first_counts, block ^ s), pick(counts, block ^ s)
+        rows_a.append(jnp.where(piece_row < of_first, base_a + piece_row, -1))
+        slot = jnp.where(piece_row >= of_first, piece_row, piece_row + half)
+        rows_b.append(jnp.where(slot < of_count, base_b + slot - of_first, -1))
+        base_a, base_b = base_a + of_first, base_b + of_count - of_first
+    chunk_row = jnp.arange(capacity, dtype=jnp.int32)
+    place_a = (chunk_row[:, None] == jnp.concatenate(rows_a)[None, :]).astype(jnp.bfloat16)
+    place_b = (chunk_row[:, None] == jnp.concatenate(rows_b)[None, :]).astype(jnp.bfloat16)
+
+    values = hidden[0].astype(jnp.float32)
+    sums = jnp.concatenate(
+        [jnp.sum(values, -1)[None], jnp.sum(values * values, -1)[None]], 0
+    )
+    sums = sums + core_swap(sums)
+    sums = sums + y_swap(sums)
+    average = (sums[0] / D)[:, None]
+    variance = (sums[1] / D)[:, None] - average * average
+    normed = (values - average) * lax.rsqrt(variance + norm_eps) * (1.0 + scaling) + shifts
+    normed = jnp.where(slot_live[:, None], normed, 0.0).astype(jnp.bfloat16)
+    piece_a = normed[:half]
+    piece_b = jnp.where((piece_row < own_first)[:, None], normed[half:], normed[:half])
+
+    def feed_forward(piece, place):
+        pieces = [piece] + [swap(piece, "wide", s, 4) for s in (1, 2, 3)]
+        tokens = jnp.dot(
+            place, jnp.concatenate(pieces, 0), preferred_element_type=jnp.float32
+        ).astype(jnp.bfloat16)
+        part = jnp.dot(tokens, expand_weight, preferred_element_type=jnp.float32)
+        kept = jnp.where(first_core, part[:, :units], part[:, units:])
+        sent = jnp.where(first_core, part[:, units:], part[:, :units]).astype(jnp.bfloat16)
+        kept = kept + core_swap(sent).astype(jnp.float32)
+        hidden_pre = kept + y_swap(kept.astype(jnp.bfloat16)).astype(jnp.float32)
+        activated = jax.nn.gelu(hidden_pre, approximate=True).astype(jnp.bfloat16)
+        other = core_swap(activated)
+        whole = jnp.concatenate(
+            [jnp.where(first_core, activated, other), jnp.where(first_core, other, activated)], 1
+        )
+        part_out = jnp.dot(whole, contract_weight, preferred_element_type=jnp.float32).astype(
+            jnp.bfloat16
+        )
+        spread = lax.dot_general(
+            place, part_out, (((0,), (0,)), ((), ())), preferred_element_type=jnp.float32
+        ).astype(jnp.bfloat16)
+        total = spread[:half].astype(jnp.float32)
+        for s in (1, 2, 3):
+            total = total + swap(spread[s * half : (s + 1) * half], "wide", s, 4).astype(jnp.float32)
+        return total
+
+    out_a = feed_forward(piece_a, place_a)
+    out_b = feed_forward(piece_b, place_b)
+    ff_result = jnp.concatenate(
+        [jnp.where((piece_row < own_first)[:, None], out_a, out_b), out_b], 0
+    )
+    layer_out = jnp.where(slot_live[:, None], values + gating * ff_result, 0.0).astype(jnp.bfloat16)
+
+    final_in = layer_out.astype(jnp.float32)
+    features = final_in.shape[1]
+    total = jnp.sum(final_in, -1, keepdims=True)
+    square = jnp.sum(final_in * final_in, -1, keepdims=True)
+    centre = total / features
+    scale = 1.0 + modulation[7]
+    weight = output_weight.astype(jnp.float32)
+    column_scale = jnp.sum(scale[:, None] * weight, 0, keepdims=True)
+    column_shift = jnp.sum(modulation[6][:, None] * weight, 0, keepdims=True)
+    product = jnp.dot(
+        ((final_in - centre) * scale).astype(jnp.bfloat16),
+        output_weight,
+        preferred_element_type=jnp.float32,
+    )
+    product = product + centre * column_scale
+    width = product.shape[1]
+    lanes = jnp.arange(width, dtype=jnp.int32)[None, :]
+    side = jnp.where(lanes == 0, total, jnp.where(lanes == 1, square, 0.0))
+    ends = jnp.concatenate([column_scale, column_shift], 1)
+    bundle = jnp.concatenate(
+        [jnp.concatenate([product, side], 1), jnp.broadcast_to(ends, (8, 2 * width))], 0
+    )
+    bundle = bundle + core_swap(bundle)
+    bundle = bundle + y_swap(bundle)
+    average = bundle[:capacity, width : width + 1] / D
+    variance = bundle[:capacity, width + 1 : width + 2] / D - average * average
+    velocity = (bundle[:capacity, :width] - average * bundle[capacity : capacity + 1, :width]) * lax.rsqrt(
+        variance + norm_eps
+    ) + bundle[capacity : capacity + 1, width:]
+    copy_weight = jnp.where(lax.axis_index("cfg") == 0, guidance, 1.0 - guidance)
+    velocity = velocity * copy_weight
+    guided = velocity + swap(velocity, "cfg", 1, 2)
+
+    steps_index, alpha_bar = alpha_table()
+    alpha_now = jnp.sum(jnp.where(steps_index == timestep[0], alpha_bar, 0.0))
+    clean_latent = jnp.where(
+        is_video[:, None], jnp.sqrt(alpha_now) * latent - jnp.sqrt(1.0 - alpha_now) * guided, 0.0
+    )
+    return (layer_out[None], clean_latent)
+
+
 def solution(mesh):
+    by_swaps = (mesh.shape["wide"], mesh.shape["narrow"], mesh.shape["cfg"]) == (4, 4, 2)
     return jax.shard_map(
-        on_device,
+        four_blocks if by_swaps else any_slice,
         mesh=mesh,
         in_specs=(
             P("cfg", "wide", "narrow"),

time: 251 us -> 121 us (0.48)
  waiting for transfers between devices: 149 us -> 37.9 us
  blocking collectives: 57.7 us -> 0 us
  starting transfers between devices: 0.08 us -> 28.6 us
  other arithmetic: 11.8 us -> 29.9 us
  between operations: 16.1 us -> 8.78 us
    psum x1 -> x0, waiting for transfers between devices: 118 us -> none  [on_device(): hidden_pre = lax.psum(hidden_part, 'narrow')]
    psum x3 -> x0, blocking collectives: 38.1 us -> none  [the longest x1 23.3 us: on_device(): guided = lax.psum(velocity_part * copy_weight, ('cfg', 'narrow'))]
    ppermute x0 -> x23, waiting for transfers between devices: none -> 37.9 us  [swap(): return lax.ppermute(array, axis, [(i, i ^ distance) for i in range(size)])]
    reduce_scatter x1 -> x0, waiting for transfers between devices: 30.5 us -> none  [on_device(): lax.psum_scatter(jnp.dot(activated, contract_weight, preferred_element_ty...]
    ppermute x0 -> x23, starting transfers between devices: none -> 28.6 us  [swap(): return lax.ppermute(array, axis, [(i, i ^ distance) for i in range(size)])]
    all_gather x1 -> x0, blocking collectives: 19.6 us -> none  [on_device(): lax.all_gather(normed, 'wide', axis=0, tiled=True)]
    select_n x1 -> x12, other arithmetic: 0.62 us -> 10.4 us  [the longest x2 5 us: four_blocks(): rows_b.append(jnp.where(slot < of_count, base_b + slot - of_first, -1))]
    reduce_sum x5 -> x10, other arithmetic: 5.26 us -> 9.51 us  [the longest x3 4.06 us: pick(): return jnp.sum(jnp.where(jnp.arange(4, dtype=jnp.int32) == index, table, 0))]
  transfers between devices with their start and end apart: 2 -> 23, of which waited for: 2 -> 11; matrix products, arithmetic and copies ran while one was open for 1% -> 32% of each run, Pallas kernels for 0% -> 0%
where the time goes in v1:
time: 121 us; the launch traced here: 120 us
  waiting for transfers between devices  37.9 us (31%)
  other arithmetic  29.9 us (25%)
  starting transfers between devices  28.6 us (24%)
  matrix products  13.8 us (11%)
  between operations  8.78 us (7%)
    ppermute x23, waiting for transfers between devices, swap(): return lax.ppermute(array, axis, [(i, i ^ distance) for i in range(size)])  37.9 us
    ppermute x23, starting transfers between devices, swap(): return lax.ppermute(array, axis, [(i, i ^ distance) for i in range(size)])  28.6 us
    dot_general x2, matrix products, feed_forward(): lax.dot_general(place, part_out, (((0,), (0,)), ((), ())), preferred_elem...  6.81 us
    dot_general x2, matrix products, feed_forward(): part = jnp.dot(tokens, expand_weight, preferred_element_type=jnp.float32)  6.76 us
    select_n x2, other arithmetic, four_blocks(): rows_b.append(jnp.where(slot < of_count, base_b + slot - of_first, -1))  5 us
    reduce_sum x3, other arithmetic, pick(): return jnp.sum(jnp.where(jnp.arange(4, dtype=jnp.int32) == index, table, 0))  4.06 us
    select_n x3, other arithmetic, four_blocks(): rows_a.append(jnp.where(piece_row < of_first, base_a + piece_row, -1))  3.05 us
  transfers between devices with their start and end apart: 23, of which 11 were waited for; matrix products, arithmetic and copies ran while one was open for 32% of the time, Pallas kernels for 0%

profile of v1, /device:TPU:0, one launch (start us, length us, event | category | flops | bytes accessed | tf_op | source)
XLA Modules:
  0.0 120.1 jit_solution(3041409571934601990)
XLA Ops:
  6.8 2.0 %fusion.94 = (s32[]{:T(128)}, s32[]{:T(128)}, s32[]{:T(128)}, s32[]{:T(128)}) fusion(s32[]{:T(128)S(6)} %xor.14, s32[]{:T(128)S(6)} %xor.13, s32[]{:T(128)S(6)} %xor.12, s32[]{:T(128)S(6)} %axis_index.33, s32[4]{0:T(128)} %param.9, s32[4]{0:T(128)S(1)} %select_reduce_fusion.1, s32[]{:T(128)} %get-tuple-element.22), kind=kLoop, calls=%fused_computation.151 | loop fusion | flops 64 | bytes 68 | tf_op jit(solution)/shard_map/reduce_sum | solution.py:90
  11.2 2.4 %compare_select_fusion.4 = (s32[64]{0:T(128)S(1)}, s32[64]{0:T(128)S(1)}) fusion(s32[]{:T(128)S(6)} %sub.75, s32[]{:T(128)} %get-tuple-element.21, s32[]{:T(128)} %get-tuple-element.18, s32[]{:T(128)} %get-tuple-element.23, s32[]{:T(128)} %get-tuple-element.19), kind=kLoop, calls=%fused_computation.127 | loop fusion | flops 768 | bytes 532 | tf_op jit(solution)/shard_map/jit(_where)/select_n | solution.py:133
  21.5 1.8 %compare_select_fusion.8 = (s32[64]{0:T(128)S(1)}, s32[64]{0:T(128)S(1)}) fusion(s32[]{:T(128)S(6)} %add.197, s32[]{:T(128)} %get-tuple-element.16, s32[]{:T(128)} %get-tuple-element.19, s32[]{:T(128)} %get-tuple-element.18), kind=kLoop, calls=%fused_computation.131 | loop fusion | flops 384 | bytes 528 | tf_op jit(solution)/shard_map/jit(_where)/select_n | solution.py:131
  23.4 2.6 %compare_select_fusion = (s32[64]{0:T(128)S(1)}, s32[64]{0:T(128)S(1)}) fusion(s32[]{:T(128)S(6)} %sub.79, s32[]{:T(128)} %get-tuple-element.20, s32[]{:T(128)} %get-tuple-element.16, s32[]{:T(128)S(6)} %sub.77, s32[]{:T(128)} %get-tuple-element.24, s32[]{:T(128)} %get-tuple-element.17), kind=kLoop, calls=%fused_computation.123 | loop fusion | flops 832 | bytes 536 | tf_op jit(solution)/shard_map/jit(_where)/select_n | solution.py:133
  26.0 1.6 %fusion.74 = (f32[64]{0:T(128)}, f32[64]{0:T(128)}) fusion(bf16[768,64]{0,1:T(8,128)(2,1)} %param.13, f32[768]{0:T(1024)S(1)} %get-tuple-element.8, f32[768]{0:T(1024)S(1)} %get-tuple-element.15), kind=kLoop, calls=%fused_computation.81 | loop fusion | flops 245632 | bytes 104960 | tf_op jit(solution)/shard_map/reduce_sum | solution.py:192
  28.4 2.6 %collective-permute-start.1 = (f32[2,128]{1,0:T(2,128)S(1)}, f32[2,128]{1,0:T(2,128)S(1)}, u32[]{:S(2)}, u32[]{:S(2)}) collective-permute-start(f32[2,128]{1,0:T(2,128)S(1)} %fusion.109), channel_id=1, source_target_pairs={{0,2},{1,3},{2,0},{3,1},{4,6},{5,7},{6,4},{7,5},{8,10},{9,11},{10,... | collective-permute-start | bytes 3080 | tf_op jit(solution)/shard_map/ppermute | solution.py:78
  33.9 2.1 %collective-permute-start.11 = (bf16[64,768]{1,0:T(8,128)(2,1)S(1)}, bf16[64,768]{1,0:T(8,128)(2,1)S(1)}, u32[]{:S(2)}, u32[]{:S(2)}) collective-permute-start(bf16[64,768]{1,0:T(8,128)(2,1)S(1)} %get-tuple-element.38), channel_id=1, source_target_pairs={{0,4},{4,0},{8,12},{12,8},{1,5},{5,1},{9,13},{13,9},{2,6},{6,2},{1... | collective-permute-start | bytes 294920 | tf_op jit(solution)/shard_map/ppermute | solution.py:78
  36.0 2.6 %collective-permute-start.12 = (bf16[64,768]{1,0:T(8,128)(2,1)S(1)}, bf16[64,768]{1,0:T(8,128)(2,1)S(1)}, u32[]{:S(2)}, u32[]{:S(2)}) collective-permute-start(bf16[64,768]{1,0:T(8,128)(2,1)S(1)} %get-tuple-element.38), channel_id=1, source_target_pairs={{0,8},{4,12},{8,0},{12,4},{1,9},{5,13},{9,1},{13,5},{2,10},{6,14},... | collective-permute-start | bytes 294920 | tf_op jit(solution)/shard_map/ppermute | solution.py:78
  40.1 3.5 %collective-permute-start.3 = (bf16[64,768]{1,0:T(8,128)(2,1)S(1)}, bf16[64,768]{1,0:T(8,128)(2,1)S(1)}, u32[]{:S(2)}, u32[]{:S(2)}) collective-permute-start(bf16[64,768]{1,0:T(8,128)(2,1)S(1)} %get-tuple-element.39), channel_id=1, source_target_pairs={{0,8},{4,12},{8,0},{12,4},{1,9},{5,13},{9,1},{13,5},{2,10},{6,14},... | collective-permute-start | bytes 294920 | tf_op jit(solution)/shard_map/ppermute | solution.py:78
  43.6 2.9 %collective-permute-done.12 = bf16[64,768]{1,0:T(8,128)(2,1)S(1)} collective-permute-done((bf16[64,768]{1,0:T(8,128)(2,1)S(1)}, bf16[64,768]{1,0:T(8,128)(2,1)S(1)}, u32[]{:S(2)}, u32[]{:S(2)}) %collective-permute-start.12) | collective-permute-done | bytes 98336 | tf_op jit(solution)/shard_map/ppermute | solution.py:78
  46.6 3.3 %fusion.1 = f32[128,3072]{1,0:T(8,128)S(1)} fusion(bf16[768,3072]{1,0:T(8,128)(2,1)} %param.11, bf16[64,768]{1,0:T(8,128)(2,1)S(1)} %collective-permute-done.13, bf16[64,768]{1,0:T(8,128)(2,1)S(1)} %collective-permute-done.12, bf16[64,768]{1,0:T(8,128)(2,1)S(1)} %collective-permute-done.11, bf16[64,768]{1,0:T(8,128)(2,1)S(1)} %get-tuple-element.38, ...), kind=kOutput, calls=%fused_computation.9 | convolution fusion | flops 656015360 | bytes 6685696 | tf_op jit(solution)/shard_map/dot_general | solution.py:157
  50.6 3.8 %collective-permute-done.3 = bf16[64,768]{1,0:T(8,128)(2,1)S(1)} collective-permute-done((bf16[64,768]{1,0:T(8,128)(2,1)S(1)}, bf16[64,768]{1,0:T(8,128)(2,1)S(1)}, u32[]{:S(2)}, u32[]{:S(2)}) %collective-permute-start.3) | collective-permute-done | bytes 98336 | tf_op jit(solution)/shard_map/ppermute | solution.py:78
  55.1 3.5 %fusion = f32[128,3072]{1,0:T(8,128)S(1)} fusion(bf16[768,3072]{1,0:T(8,128)(2,1)} %param.11, bf16[64,768]{1,0:T(8,128)(2,1)} %collective-permute-done.4, bf16[64,768]{1,0:T(8,128)(2,1)} %copy-done.3, bf16[64,768]{1,0:T(8,128)(2,1)} %collective-permute-done.2, bf16[64,768]{1,0:T(8,128)(2,1)} %copy-done.1, s32[256]{0:T(256)} %pad_add_fusion), kind=kOutput, calls=%fused_computation.8 | convolution fusion | flops 656015360 | bytes 6685696 | tf_op jit(solution)/shard_map/dot_general | solution.py:157
  62.1 8.8 %collective-permute-done.15 = bf16[128,1536]{1,0:T(8,128)(2,1)S(1)} collective-permute-done((bf16[128,1536]{1,0:T(8,128)(2,1)S(1)}, bf16[128,1536]{1,0:T(8,128)(2,1)S(1)}, u32[]{:S(2)}, u32[]{:S(2)}) %collective-permute-start.15) | collective-permute-done | bytes 393248 | tf_op jit(solution)/shard_map/ppermute | solution.py:78
  71.3 7.6 %collective-permute-done.6 = bf16[128,1536]{1,0:T(8,128)(2,1)S(1)} collective-permute-done((bf16[128,1536]{1,0:T(8,128)(2,1)S(1)}, bf16[128,1536]{1,0:T(8,128)(2,1)S(1)}, u32[]{:S(2)}, u32[]{:S(2)}) %collective-permute-start.6) | collective-permute-done | bytes 393248 | tf_op jit(solution)/shard_map/ppermute | solution.py:78
  79.4 3.4 %convolution_convert_fusion = bf16[256,768]{1,0:T(8,128)(2,1)S(1)} fusion(bf16[3072,768]{1,0:T(8,128)(2,1)} %param.12, bf16[128,1536]{1,0:T(8,128)(2,1)S(1)} %get-tuple-element.29, bf16[128,1536]{1,0:T(8,128)(2,1)S(1)} %get-tuple-element.28, s32[256]{0:T(256)} %copy-done.5), kind=kOutput, calls=%fused_computation | convolution fusion | flops 656211968 | bytes 5899264 | tf_op jit(solution)/shard_map/dot_general | solution.py:170
  82.9 2.7 %collective-permute-start.17 = (bf16[64,768]{1,0:T(8,128)(2,1)S(1)}, bf16[64,768]{1,0:T(8,128)(2,1)S(1)}, u32[]{:S(2)}, u32[]{:S(2)}) collective-permute-start(bf16[64,768]{1,0:T(8,128)(2,1)S(1)} %get-tuple-element.32), channel_id=1, source_target_pairs={{0,4},{4,0},{8,12},{12,8},{1,5},{5,1},{9,13},{13,9},{2,6},{6,2},{1... | collective-permute-start | bytes 294920 | tf_op jit(solution)/shard_map/ppermute | solution.py:78
  88.5 3.4 %convolution_convert_fusion.1 = bf16[256,768]{1,0:T(8,128)(2,1)S(1)} fusion(bf16[3072,768]{1,0:T(8,128)(2,1)} %param.12, bf16[128,1536]{1,0:T(8,128)(2,1)S(1)} %get-tuple-element.31, bf16[128,1536]{1,0:T(8,128)(2,1)S(1)} %get-tuple-element.30, s32[256]{0:T(256)S(1)} %copy-done.6), kind=kOutput, calls=%fused_computation.1 | convolution fusion | flops 656211968 | bytes 5899264 | tf_op jit(solution)/shard_map/dot_general | solution.py:170
  92.0 2.5 %collective-permute-start.10 = (bf16[64,768]{1,0:T(8,128)(2,1)S(1)}, bf16[64,768]{1,0:T(8,128)(2,1)S(1)}, u32[]{:S(2)}, u32[]{:S(2)}) collective-permute-start(bf16[64,768]{1,0:T(8,128)(2,1)S(1)} %get-tuple-element.36), channel_id=1, source_target_pairs={{0,12},{4,8},{8,4},{12,0},{1,13},{5,9},{9,5},{13,1},{2,14},{6,10},... | collective-permute-start | bytes 294920 | tf_op jit(solution)/shard_map/ppermute | solution.py:78
  94.6 1.8 %collective-permute-start.9 = (bf16[64,768]{1,0:T(8,128)(2,1)S(1)}, bf16[64,768]{1,0:T(8,128)(2,1)S(1)}, u32[]{:S(2)}, u32[]{:S(2)}) collective-permute-start(bf16[64,768]{1,0:T(8,128)(2,1)S(1)} %get-tuple-element.37), channel_id=1, source_target_pairs={{0,8},{4,12},{8,0},{12,4},{1,9},{5,13},{9,1},{13,5},{2,10},{6,14},... | collective-permute-start | bytes 294920 | tf_op jit(solution)/shard_map/ppermute | solution.py:78
  96.5 3.0 %collective-permute-done.10 = bf16[64,768]{1,0:T(8,128)(2,1)S(1)} collective-permute-done((bf16[64,768]{1,0:T(8,128)(2,1)S(1)}, bf16[64,768]{1,0:T(8,128)(2,1)S(1)}, u32[]{:S(2)}, u32[]{:S(2)}) %collective-permute-start.10) | collective-permute-done | bytes 98336 | tf_op jit(solution)/shard_map/ppermute | solution.py:78
  100.7 5.5 %collective-permute-done.9 = bf16[64,768]{1,0:T(8,128)(2,1)S(1)} collective-permute-done((bf16[64,768]{1,0:T(8,128)(2,1)S(1)}, bf16[64,768]{1,0:T(8,128)(2,1)S(1)}, u32[]{:S(2)}, u32[]{:S(2)}) %collective-permute-start.9) | collective-permute-done | bytes 98336 | tf_op jit(solution)/shard_map/ppermute | solution.py:78
  112.0 3.2 %collective-permute-done.21 = f32[136,128]{0,1:T(8,128)S(1)} collective-permute-done((f32[136,128]{0,1:T(8,128)S(1)}, f32[136,128]{0,1:T(8,128)S(1)}, u32[]{:S(2)}, u32[]{:S(2)}) %collective-permute-start.21) | collective-permute-done | bytes 69664 | tf_op jit(solution)/shard_map/ppermute | solution.py:78
  117.8 1.6 %collective-permute-done.22 = f32[128,64]{0,1:T(8,128)S(1)} collective-permute-done((f32[128,64]{0,1:T(8,128)S(1)}, f32[128,64]{0,1:T(8,128)S(1)}, u32[]{:S(2)}, u32[]{:S(2)}) %collective-permute-start.22) | collective-permute-done | bytes 32800 | tf_op jit(solution)/shard_map/ppermute | solution.py:78
  (121 shorter events, 33.2 us)
Async XLA Ops:
  2.7 25.6 %collective-permute-start = (f32[2,128]{1,0:T(2,128)S(1)}, f32[2,128]{1,0:T(2,128)S(1)}, u32[]{:S(2)}, u32[]{:S(2)}) collective-permute-start(f32[2,128]{1,0:T(2,128)S(1)} %pad_maximum_fusion.1), channel_id=1, source_target_pairs={{0,1},{1,0},{2,3},{3,2},{4,5},{5,4},{6,7},{7,6},{8,9},{9,8},{10,11... | collective-permute-start | bytes 3080 | tf_op jit(solution)/shard_map/ppermute | solution.py:78
  17.8 36.6 %copy-start.7 = (pred[128]{0:T(512)(128)(4,1)}, pred[128]{0:T(512)(128)(4,1)S(1)}, u32[]{:S(2)}) copy-start(pred[128]{0:T(512)(128)(4,1)S(1)} %get-tuple-element.46) | copy-start | bytes 388
  28.4 4.1 %collective-permute-start.1 = (f32[2,128]{1,0:T(2,128)S(1)}, f32[2,128]{1,0:T(2,128)S(1)}, u32[]{:S(2)}, u32[]{:S(2)}) collective-permute-start(f32[2,128]{1,0:T(2,128)S(1)} %fusion.109), channel_id=1, source_target_pairs={{0,2},{1,3},{2,0},{3,1},{4,6},{5,7},{6,4},{7,5},{8,10},{9,11},{10,... | collective-permute-start | bytes 3080 | tf_op jit(solution)/shard_map/ppermute | solution.py:78
  33.9 9.8 %collective-permute-start.11 = (bf16[64,768]{1,0:T(8,128)(2,1)S(1)}, bf16[64,768]{1,0:T(8,128)(2,1)S(1)}, u32[]{:S(2)}, u32[]{:S(2)}) collective-permute-start(bf16[64,768]{1,0:T(8,128)(2,1)S(1)} %get-tuple-element.38), channel_id=1, source_target_pairs={{0,4},{4,0},{8,12},{12,8},{1,5},{5,1},{9,13},{13,9},{2,6},{6,2},{1... | collective-permute-start | bytes 294920 | tf_op jit(solution)/shard_map/ppermute | solution.py:78
  36.0 10.5 %collective-permute-start.12 = (bf16[64,768]{1,0:T(8,128)(2,1)S(1)}, bf16[64,768]{1,0:T(8,128)(2,1)S(1)}, u32[]{:S(2)}, u32[]{:S(2)}) collective-permute-start(bf16[64,768]{1,0:T(8,128)(2,1)S(1)} %get-tuple-element.38), channel_id=1, source_target_pairs={{0,8},{4,12},{8,0},{12,4},{1,9},{5,13},{9,1},{13,5},{2,10},{6,14},... | collective-permute-start | bytes 294920 | tf_op jit(solution)/shard_map/ppermute | solution.py:78
  38.6 8.0 %collective-permute-start.13 = (bf16[64,768]{1,0:T(8,128)(2,1)S(1)}, bf16[64,768]{1,0:T(8,128)(2,1)S(1)}, u32[]{:S(2)}, u32[]{:S(2)}) collective-permute-start(bf16[64,768]{1,0:T(8,128)(2,1)S(1)} %get-tuple-element.38), channel_id=1, source_target_pairs={{0,12},{4,8},{8,4},{12,0},{1,13},{5,9},{9,5},{13,1},{2,14},{6,10},... | collective-permute-start | bytes 294920 | tf_op jit(solution)/shard_map/ppermute | solution.py:78
  39.2 11.4 %collective-permute-start.2 = (bf16[64,768]{1,0:T(8,128)(2,1)S(1)}, bf16[64,768]{1,0:T(8,128)(2,1)}, u32[]{:S(2)}, u32[]{:S(2)}) collective-permute-start(bf16[64,768]{1,0:T(8,128)(2,1)S(1)} %get-tuple-element.39), channel_id=1, source_target_pairs={{0,4},{4,0},{8,12},{12,8},{1,5},{5,1},{9,13},{13,9},{2,6},{6,2},{1... | collective-permute-start | bytes 294920 | tf_op jit(solution)/shard_map/ppermute | solution.py:78
  40.1 14.3 %collective-permute-start.3 = (bf16[64,768]{1,0:T(8,128)(2,1)S(1)}, bf16[64,768]{1,0:T(8,128)(2,1)S(1)}, u32[]{:S(2)}, u32[]{:S(2)}) collective-permute-start(bf16[64,768]{1,0:T(8,128)(2,1)S(1)} %get-tuple-element.39), channel_id=1, source_target_pairs={{0,8},{4,12},{8,0},{12,4},{1,9},{5,13},{9,1},{13,5},{2,10},{6,14},... | collective-permute-start | bytes 294920 | tf_op jit(solution)/shard_map/ppermute | solution.py:78
  43.6 11.5 %collective-permute-start.4 = (bf16[64,768]{1,0:T(8,128)(2,1)S(1)}, bf16[64,768]{1,0:T(8,128)(2,1)}, u32[]{:S(2)}, u32[]{:S(2)}) collective-permute-start(bf16[64,768]{1,0:T(8,128)(2,1)S(1)} %get-tuple-element.39), channel_id=1, source_target_pairs={{0,12},{4,8},{8,4},{12,0},{1,13},{5,9},{9,5},{13,1},{2,14},{6,10},... | collective-permute-start | bytes 294920 | tf_op jit(solution)/shard_map/ppermute | solution.py:78
  50.6 8.1 %collective-permute-start.14 = (bf16[128,1536]{1,0:T(8,128)(2,1)}, bf16[128,1536]{1,0:T(8,128)(2,1)S(1)}, u32[]{:S(2)}, u32[]{:S(2)}) collective-permute-start(bf16[128,1536]{1,0:T(8,128)(2,1)} %select_convert_fusion), channel_id=1, source_target_pairs={{0,1},{1,0},{2,3},{3,2},{4,5},{5,4},{6,7},{7,6},{8,9},{9,8},{10,11... | collective-permute-start | bytes 1179656 | tf_op jit(solution)/shard_map/ppermute | solution.py:78
  58.7 1.8 %collective-permute-start.5 = (bf16[128,1536]{1,0:T(8,128)(2,1)S(1)}, bf16[128,1536]{1,0:T(8,128)(2,1)S(1)}, u32[]{:S(2)}, u32[]{:S(2)}) collective-permute-start(bf16[128,1536]{1,0:T(8,128)(2,1)S(1)} %select_convert_fusion.1), channel_id=1, source_target_pairs={{0,1},{1,0},{2,3},{3,2},{4,5},{5,4},{6,7},{7,6},{8,9},{9,8},{10,11... | collective-permute-start | bytes 1179656 | tf_op jit(solution)/shard_map/ppermute | solution.py:78
  58.9 12.0 %collective-permute-start.15 = (bf16[128,1536]{1,0:T(8,128)(2,1)S(1)}, bf16[128,1536]{1,0:T(8,128)(2,1)S(1)}, u32[]{:S(2)}, u32[]{:S(2)}) collective-permute-start(bf16[128,1536]{1,0:T(8,128)(2,1)S(1)} %fusion.89), channel_id=1, source_target_pairs={{0,2},{1,3},{2,0},{3,1},{4,6},{5,7},{6,4},{7,5},{8,10},{9,11},{10,... | collective-permute-start | bytes 1179656 | tf_op jit(solution)/shard_map/ppermute | solution.py:78
  60.6 18.3 %collective-permute-start.6 = (bf16[128,1536]{1,0:T(8,128)(2,1)S(1)}, bf16[128,1536]{1,0:T(8,128)(2,1)S(1)}, u32[]{:S(2)}, u32[]{:S(2)}) collective-permute-start(bf16[128,1536]{1,0:T(8,128)(2,1)S(1)} %fusion.88), channel_id=1, source_target_pairs={{0,2},{1,3},{2,0},{3,1},{4,6},{5,7},{6,4},{7,5},{8,10},{9,11},{10,... | collective-permute-start | bytes 1179656 | tf_op jit(solution)/shard_map/ppermute | solution.py:78
  71.3 8.1 %collective-permute-start.16 = (bf16[128,1536]{1,0:T(8,128)(2,1)S(1)}, bf16[128,1536]{1,0:T(8,128)(2,1)S(1)}, u32[]{:S(2)}, u32[]{:S(2)}) collective-permute-start(bf16[128,1536]{1,0:T(8,128)(2,1)S(1)} %fusion.17), channel_id=1, source_target_pairs={{0,1},{1,0},{2,3},{3,2},{4,5},{5,4},{6,7},{7,6},{8,9},{9,8},{10,11... | collective-permute-start | bytes 1179656 | tf_op jit(solution)/shard_map/ppermute | solution.py:78
  79.3 9.1 %collective-permute-start.7 = (bf16[128,1536]{1,0:T(8,128)(2,1)S(1)}, bf16[128,1536]{1,0:T(8,128)(2,1)S(1)}, u32[]{:S(2)}, u32[]{:S(2)}) collective-permute-start(bf16[128,1536]{1,0:T(8,128)(2,1)S(1)} %fusion.9), channel_id=1, source_target_pairs={{0,1},{1,0},{2,3},{3,2},{4,5},{5,4},{6,7},{7,6},{8,9},{9,8},{10,11... | collective-permute-start | bytes 1179656 | tf_op jit(solution)/shard_map/ppermute | solution.py:78
  82.9 11.7 %collective-permute-start.17 = (bf16[64,768]{1,0:T(8,128)(2,1)S(1)}, bf16[64,768]{1,0:T(8,128)(2,1)S(1)}, u32[]{:S(2)}, u32[]{:S(2)}) collective-permute-start(bf16[64,768]{1,0:T(8,128)(2,1)S(1)} %get-tuple-element.32), channel_id=1, source_target_pairs={{0,4},{4,0},{8,12},{12,8},{1,5},{5,1},{9,13},{13,9},{2,6},{6,2},{1... | collective-permute-start | bytes 294920 | tf_op jit(solution)/shard_map/ppermute | solution.py:78
  85.7 10.8 %collective-permute-start.18 = (bf16[64,768]{1,0:T(8,128)(2,1)S(1)}, bf16[64,768]{1,0:T(8,128)(2,1)S(1)}, u32[]{:S(2)}, u32[]{:S(2)}) collective-permute-start(bf16[64,768]{1,0:T(8,128)(2,1)S(1)} %get-tuple-element.34), channel_id=1, source_target_pairs={{0,8},{4,12},{8,0},{12,4},{1,9},{5,13},{9,1},{13,5},{2,10},{6,14},... | collective-permute-start | bytes 294920 | tf_op jit(solution)/shard_map/ppermute | solution.py:78
  87.0 9.5 %collective-permute-start.19 = (bf16[64,768]{1,0:T(8,128)(2,1)S(1)}, bf16[64,768]{1,0:T(8,128)(2,1)S(1)}, u32[]{:S(2)}, u32[]{:S(2)}) collective-permute-start(bf16[64,768]{1,0:T(8,128)(2,1)S(1)} %get-tuple-element.33), channel_id=1, source_target_pairs={{0,12},{4,8},{8,4},{12,0},{1,13},{5,9},{9,5},{13,1},{2,14},{6,10},... | collective-permute-start | bytes 294920 | tf_op jit(solution)/shard_map/ppermute | solution.py:78
  92.0 7.5 %collective-permute-start.10 = (bf16[64,768]{1,0:T(8,128)(2,1)S(1)}, bf16[64,768]{1,0:T(8,128)(2,1)S(1)}, u32[]{:S(2)}, u32[]{:S(2)}) collective-permute-start(bf16[64,768]{1,0:T(8,128)(2,1)S(1)} %get-tuple-element.36), channel_id=1, source_target_pairs={{0,12},{4,8},{8,4},{12,0},{1,13},{5,9},{9,5},{13,1},{2,14},{6,10},... | collective-permute-start | bytes 294920 | tf_op jit(solution)/shard_map/ppermute | solution.py:78
  94.5 6.2 %collective-permute-start.8 = (bf16[64,768]{1,0:T(8,128)(2,1)S(1)}, bf16[64,768]{1,0:T(8,128)(2,1)S(1)}, u32[]{:S(2)}, u32[]{:S(2)}) collective-permute-start(bf16[64,768]{1,0:T(8,128)(2,1)S(1)} %get-tuple-element.35), channel_id=1, source_target_pairs={{0,4},{4,0},{8,12},{12,8},{1,5},{5,1},{9,13},{13,9},{2,6},{6,2},{1... | collective-permute-start | bytes 294920 | tf_op jit(solution)/shard_map/ppermute | solution.py:78
  94.6 11.6 %collective-permute-start.9 = (bf16[64,768]{1,0:T(8,128)(2,1)S(1)}, bf16[64,768]{1,0:T(8,128)(2,1)S(1)}, u32[]{:S(2)}, u32[]{:S(2)}) collective-permute-start(bf16[64,768]{1,0:T(8,128)(2,1)S(1)} %get-tuple-element.37), channel_id=1, source_target_pairs={{0,8},{4,12},{8,0},{12,4},{1,9},{5,13},{9,1},{13,5},{2,10},{6,14},... | collective-permute-start | bytes 294920 | tf_op jit(solution)/shard_map/ppermute | solution.py:78
  107.1 2.1 %collective-permute-start.20 = (f32[136,128]{0,1:T(8,128)S(1)}, f32[136,128]{0,1:T(8,128)S(1)}, u32[]{:S(2)}, u32[]{:S(2)}) collective-permute-start(f32[136,128]{0,1:T(8,128)S(1)} %pad_maximum_fusion), channel_id=1, source_target_pairs={{0,1},{1,0},{2,3},{3,2},{4,5},{5,4},{6,7},{7,6},{8,9},{9,8},{10,11... | collective-permute-start | bytes 208904 | tf_op jit(solution)/shard_map/ppermute | solution.py:78
  109.2 6.0 %collective-permute-start.21 = (f32[136,128]{0,1:T(8,128)S(1)}, f32[136,128]{0,1:T(8,128)S(1)}, u32[]{:S(2)}, u32[]{:S(2)}) collective-permute-start(f32[136,128]{0,1:T(8,128)S(1)} %fusion.110), channel_id=1, source_target_pairs={{0,2},{1,3},{2,0},{3,1},{4,6},{5,7},{6,4},{7,5},{8,10},{9,11},{10,... | collective-permute-start | bytes 208904 | tf_op jit(solution)/shard_map/ppermute | solution.py:78
  115.4 4.0 %collective-permute-start.22 = (f32[128,64]{0,1:T(8,128)S(1)}, f32[128,64]{0,1:T(8,128)S(1)}, u32[]{:S(2)}, u32[]{:S(2)}) collective-permute-start(f32[128,64]{0,1:T(8,128)S(1)} %fusion.87), channel_id=1, source_target_pairs={{0,16},{16,0},{1,17},{17,1},{2,18},{18,2},{3,19},{19,3},{4,20},{20... | collective-permute-start | bytes 98312 | tf_op jit(solution)/shard_map/ppermute | solution.py:78
  (16 other events, 331.8 us)

commit v2 on v0

--- a/solution.py
+++ b/solution.py
@@ -1,6 +1,11 @@
+import functools
+
 import jax
 import jax.numpy as jnp
+import numpy as np
 from jax import lax
+from jax.experimental import pallas as pl
+from jax.experimental.pallas import tpu as pltpu
 from jax.sharding import PartitionSpec as P
 
 D = 3072
@@ -28,7 +33,7 @@
     return (values - average) * lax.rsqrt(variance + norm_eps) * (1.0 + scaling) + shifts
 
 
-def on_device(
+def any_slice(
     hidden, split_table, modulation, expand_weight, contract_weight, output_weight, latent, timestep
 ):
     capacity = hidden.shape[1]
@@ -74,9 +79,469 @@
     return (layer_out[None], clean_latent)
 
 
+QUOTAS = (0, 64, 128)
+CAP = 128
+CHUNKS = len(QUOTAS) - 1
+F32, BF16 = jnp.float32, jnp.bfloat16
+
+
+def size_of(k):
+    return QUOTAS[k + 1] - QUOTAS[k]
+
+
+def swap(array, axis, distance, size):
+    return lax.ppermute(array, axis, [(i, i ^ distance) for i in range(size)])
+
+
+def z_swaps(array):
+    return [swap(array, "wide", s, 4) for s in (1, 2, 3)]
+
+
+def choose(values, index):
+    out = values[0]
+    for i in range(1, 4):
+        out = jnp.where(index == i, values[i], out)
+    return out
+
+
+def layout(table):
+    counts = [table[b] for b in range(4)]
+    largest = jnp.int32(3)
+    for b in (2, 1, 0):
+        largest = jnp.where(counts[b] == CAP, b, largest)
+    starts, others, ranks, offsets = [], [], [], []
+    rank, offset = jnp.int32(0), jnp.int32(0)
+    for b in range(4):
+        other = jnp.where(largest == b, 0, 1)
+        ranks.append(rank * other)
+        others.append(other)
+        offsets.append(offset)
+        rank = rank + other * counts[b]
+        offset = offset + counts[b]
+    block = lax.axis_index("wide")
+    of = lambda values: [choose(values, jnp.bitwise_xor(block, s)) for s in range(4)]
+    return of(ranks), of(counts), of(others), of(offsets)[0], choose(offsets, largest)
+
+
+def text_rows(k, largest_offset):
+    size = size_of(k)
+    row = lax.broadcasted_iota(jnp.int32, (2 * size, 1), 0)
+    rank = jnp.where(row < size, row, row - size) + QUOTAS[k]
+    position = jnp.where(
+        row < size, rank + largest_offset, jnp.where(rank < largest_offset, rank, rank + CAP)
+    )
+    return position < TEXT
+
+
+def sums_kernel(mod, out_weight, w, own_out, other_out, ends_out, buffer, sems):
+    core = lax.axis_index("narrow") % 2
+    units = buffer.shape[1] // 2
+    copies = []
+    for t in range(2):
+        copies.append(
+            pltpu.make_async_copy(
+                w.at[:, pl.ds(t * units, units)], buffer.at[:, pl.ds(t * units, units)], sems.at[t]
+            )
+        )
+        copies[-1].start()
+    row = lax.broadcasted_iota(jnp.int32, (8, 1), 0)
+    rows = jnp.where(row == 0, 1.0 + mod[1:2, :], jnp.zeros((8, 1), F32))
+    rows = jnp.where(row == 1, 1.0 + mod[4:5, :], rows)
+    rows = jnp.where(row == 2, mod[0:1, :], rows)
+    rows = jnp.where(row == 3, mod[3:4, :], rows)
+    high = rows.astype(BF16)
+    low = (rows - high.astype(F32)).astype(BF16)
+    both = jnp.concatenate([high, low], 0)
+    ends = jnp.where(row == 0, 1.0 + mod[7:8, :], mod[6:7, :])
+    high = ends.astype(BF16)
+    low = (ends - high.astype(F32)).astype(BF16)
+    ends = jnp.dot(jnp.concatenate([high, low], 0), out_weight[...], preferred_element_type=F32)
+    ends = ends[:8] + ends[8:]
+    ends_out[...] = jnp.concatenate(
+        [jnp.broadcast_to(ends[0:1], ends.shape), jnp.broadcast_to(ends[1:2], ends.shape)], 1
+    )
+    for t in range(2):
+        copies[t].wait()
+        part = jnp.dot(both, buffer[:, t * units : (t + 1) * units], preferred_element_type=F32)
+        part = part[:8] + part[8:]
+
+        @pl.when(core == t)
+        def _():
+            own_out[...] = part
+
+        @pl.when(core != t)
+        def _():
+            other_out[...] = part
+
+
+def fetch(w, start, buffer, sems, tiles, axis):
+    width = buffer.shape[axis] // tiles
+    copies = []
+    for t in range(tiles):
+        source = pl.ds(pl.multiple_of(start + t * width, 128), width)
+        place = pl.ds(t * width, width)
+        if axis == 1:
+            copy = pltpu.make_async_copy(w.at[:, source], buffer.at[:, place], sems.at[t])
+        else:
+            copy = pltpu.make_async_copy(w.at[source, :], buffer.at[place, :], sems.at[t])
+        copy.start()
+        copies.append(copy)
+    return copies, width
+
+
+def expand_sent_kernel(k, table, mod, *refs):
+    pieces = refs[: 4 * (k + 1)]
+    w, z_out, sent_out, side_out, buffer, sems = refs[4 * (k + 1) :]
+    core = lax.axis_index("narrow") % 2
+    units = buffer.shape[1]
+    tiles = sems.shape[0]
+    copies, width = fetch(w, (1 - core) * units, buffer, sems, tiles, 1)
+
+    size = size_of(k)
+    ranks, counts, others, _, largest_offset = layout(table)
+    places = []
+    for p in range(k + 1):
+        piece = size_of(p)
+        lane = lax.broadcasted_iota(jnp.int32, (1, 4 * piece), 1)
+        which, slot = lane // piece, lane % piece + QUOTAS[p]
+        rank = slot + choose(ranks, which) - QUOTAS[k]
+        live = (rank >= 0) & (rank < size) & (slot < choose(counts, which))
+        row = jnp.where(live, rank + choose(others, which) * size, -1)
+        at = lax.broadcasted_iota(jnp.int32, (2 * size, 4 * piece), 0)
+        places.append(jnp.where(at == row, 1.0, 0.0).astype(BF16))
+    place = jnp.concatenate(places, 1)
+    tokens = jnp.concatenate([piece[...] for piece in pieces], 0)
+    x = jnp.dot(place, tokens, preferred_element_type=F32)
+
+    centre = (jnp.sum(x, -1, keepdims=True) / x.shape[1]).astype(BF16).astype(F32)
+    x = x - centre
+    total = jnp.sum(x, -1, keepdims=True)
+    square = jnp.sum(x * x, -1, keepdims=True)
+    text = text_rows(k, largest_offset)
+    z = (x * (1.0 + jnp.where(text, mod[4:5, :], mod[1:2, :]))).astype(BF16)
+    z_out[...] = z
+    total_high = total.astype(BF16).astype(F32)
+    square_high = square.astype(BF16).astype(F32)
+    lane = lax.broadcasted_iota(jnp.int32, (2 * size, 128), 1) - 8 * core
+    side = jnp.where((lane == 0) | (lane == 1), centre, 0.0)
+    side = jnp.where(lane == 4, total_high, side)
+    side = jnp.where(lane == 5, total - total_high, side)
+    side = jnp.where(lane == 6, square_high, side)
+    side = jnp.where(lane == 7, square - square_high, side).astype(BF16)
+    side_out[...] = side
+    sent_out[:, units:] = side
+    for t in range(tiles):
+        copies[t].wait()
+        sent_out[:, t * width : (t + 1) * width] = jnp.dot(
+            z, buffer[:, t * width : (t + 1) * width], preferred_element_type=F32
+        ).astype(BF16)
+
+
+def expand_kept_kernel(z, w, kept_out, buffer, sems):
+    core = lax.axis_index("narrow") % 2
+    units = buffer.shape[1]
+    tiles = sems.shape[0]
+    copies, width = fetch(w, core * units, buffer, sems, tiles, 1)
+    for t in range(tiles):
+        copies[t].wait()
+        kept_out[:, t * width : (t + 1) * width] = jnp.dot(
+            z[...], buffer[:, t * width : (t + 1) * width], preferred_element_type=F32
+        )
+
+
+def merge_kernel(kept, side, came, total_out, sent_out):
+    units = kept.shape[1]
+    total = kept[...] + came[:, :units].astype(F32)
+    total_out[...] = total
+    sent_out[:, :units] = total.astype(BF16)
+    sent_out[:, units:] = (side[...].astype(F32) + came[:, units:].astype(F32)).astype(BF16)
+
+
+def activate_kernel(k, features, table, total, sent, came, sums_own, sums_other, act_out):
+    units = total.shape[1]
+    size = size_of(k)
+    text = text_rows(k, layout(table)[4])
+    sides = [sent[:, units:].astype(F32), came[:, units:].astype(F32)]
+    lane = lax.broadcasted_iota(jnp.int32, (2 * size, 128), 1)
+    field = lane % 8
+    used = lane < 16
+    summed = sides[0] + sides[1]
+    add = lambda values, mask: jnp.sum(jnp.where(mask, values, 0.0), -1, keepdims=True)
+    centres = add(summed, used & (field == 0))
+    totals = add(summed, used & ((field == 4) | (field == 5)))
+    average = (centres * features + totals) / D
+    spread = add(summed, used & ((field == 6) | (field == 7)))
+    factors = []
+    for side in sides:
+        apart = side - average
+        for core in range(2):
+            own = (lane // 8) == core
+            off = add(apart, own & (field == 0))
+            spread = spread + off * (
+                2.0 * add(side, own & ((field == 4) | (field == 5))) + features * off
+            )
+        factors.append(apart)
+    variance = spread / D
+    scale = lax.rsqrt(variance + norm_eps)
+    of_text = jnp.where(text, 1, 0)
+    mine = used & ((field % 2) == of_text)
+    pre = total[...] + came[:, :units].astype(F32)
+    extra = jnp.zeros_like(pre)
+    for factor, sums in zip(factors, (sums_own, sums_other)):
+        factor = jnp.where(
+            mine & (field < 2), factor * scale, jnp.where(mine & (field < 4), 1.0, 0.0)
+        )
+        extra = extra + jnp.dot(
+            factor[:, :16], sums[...], precision=lax.Precision.HIGHEST, preferred_element_type=F32
+        )
+    act_out[...] = jax.nn.gelu(pre * scale + extra, approximate=True).astype(BF16)
+
+
+def contract_own_kernel(act, w, out, buffer, sems):
+    core = lax.axis_index("narrow") % 2
+    tiles = sems.shape[0]
+    copies, width = fetch(w, core * buffer.shape[0], buffer, sems, tiles, 0)
+    total = None
+    for t in range(tiles):
+        copies[t].wait()
+        part = jnp.dot(
+            act[:, t * width : (t + 1) * width],
+            buffer[t * width : (t + 1) * width, :],
+            preferred_element_type=F32,
+        )
+        total = part if total is None else total + part
+    out[...] = total
+
+
+def contract_other_kernel(k, table, act, so_far, w, *refs):
+    outs, buffer, sems = refs[:4], refs[4], refs[5]
+    core = lax.axis_index("narrow") % 2
+    tiles = sems.shape[0]
+    copies, width = fetch(w, (1 - core) * buffer.shape[0], buffer, sems, tiles, 0)
+    size = size_of(k)
+    ranks, counts, others, _, _ = layout(table)
+    places = []
+    for s in range(4):
+        first = jnp.maximum(QUOTAS[k] - ranks[s], 0)
+        last = jnp.minimum(counts[s], QUOTAS[k + 1] - ranks[s])
+        index = lax.broadcasted_iota(jnp.int32, (size, 1), 0)
+        slot = first + jnp.bitwise_and(index - first, size - 1)
+        row = jnp.where(slot < last, slot + ranks[s] - QUOTAS[k] + others[s] * size, -1)
+        at = lax.broadcasted_iota(jnp.int32, (size, 2 * size), 1)
+        places.append(jnp.where(at == row, 1.0, 0.0).astype(BF16))
+    total = so_far[...]
+    for t in range(tiles):
+        copies[t].wait()
+        total = total + jnp.dot(
+            act[:, t * width : (t + 1) * width],
+            buffer[t * width : (t + 1) * width, :],
+            preferred_element_type=F32,
+        )
+    spread = jnp.dot(
+        jnp.concatenate(places, 0), total.astype(BF16), preferred_element_type=F32
+    ).astype(BF16)
+    for s in range(4):
+        outs[s][...] = spread[s * size : (s + 1) * size]
+
+
+def finish_kernel(table, hidden, mod, out_weight, ends, *refs):
+    pieces, (layer_out, bundle_out) = refs[: 4 * CHUNKS], refs[4 * CHUNKS :]
+    ranks, counts, _, offset, _ = layout(table)
+    slot = lax.broadcasted_iota(jnp.int32, (CAP, 1), 0)
+    live = slot < counts[0]
+    text = slot + offset < TEXT
+    rank = slot + ranks[0]
+    result = jnp.zeros(hidden.shape, F32)
+    for k in range(CHUNKS):
+        total = pieces[4 * k][...].astype(F32)
+        for s in (1, 2, 3):
+            total = total + pieces[4 * k + s][...].astype(F32)
+        total = jnp.concatenate([total] * (CAP // size_of(k)), 0)
+        result = jnp.where((rank >= QUOTAS[k]) & (rank < QUOTAS[k + 1]), total, result)
+    gate = jnp.where(text, mod[5:6, :], mod[2:3, :])
+    layer = jnp.where(live, hidden[...].astype(F32) + gate * result, 0.0).astype(BF16)
+    layer_out[...] = layer
+    x = layer.astype(F32)
+    total = jnp.sum(x, -1, keepdims=True)
+    square = jnp.sum(x * x, -1, keepdims=True)
+    centre = total / x.shape[1]
+    product = jnp.dot(
+        ((x - centre) * (1.0 + mod[7:8, :])).astype(BF16),
+        out_weight[...],
+        preferred_element_type=F32,
+    )
+    width = product.shape[1]
+    bundle_out[:CAP, :width] = product + centre * ends[0:1, :width]
+    lane = lax.broadcasted_iota(jnp.int32, (CAP, width), 1)
+    bundle_out[:CAP, width:] = jnp.where(lane == 0, total, jnp.where(lane == 1, square, 0.0))
+    bundle_out[CAP:, :] = ends[...]
+
+
+def velocity_kernel(first, second, third, fourth, out):
+    bundle = (first[...] + second[...]) + (third[...] + fourth[...])
+    width = bundle.shape[1] // 2
+    average = bundle[:CAP, width : width + 1] / D
+    variance = bundle[:CAP, width + 1 : width + 2] / D - average * average
+    velocity = (bundle[:CAP, :width] - average * bundle[CAP : CAP + 1, :width]) * lax.rsqrt(
+        variance + norm_eps
+    ) + bundle[CAP : CAP + 1, width:]
+    out[...] = velocity * jnp.where(lax.axis_index("cfg") == 0, guidance, 1.0 - guidance)
+
+
+def latent_kernel(table, timestep, alphas, latent, mine, other, out):
+    _, counts, _, offset, _ = layout(table)
+    slot = lax.broadcasted_iota(jnp.int32, (CAP, 1), 0)
+    video = (slot < counts[0]) & (slot + offset >= TEXT)
+    index = lax.broadcasted_iota(jnp.int32, (8, 128), 0) * 128 + lax.broadcasted_iota(
+        jnp.int32, (8, 128), 1
+    )
+    alpha = jnp.sum(
+        jnp.sum(jnp.where(index == timestep[0], alphas[...], 0.0), 0, keepdims=True),
+        1,
+        keepdims=True,
+    )
+    clean = jnp.sqrt(alpha) * latent[...] - jnp.sqrt(1.0 - alpha) * (mine[...] + other[...])
+    out[...] = jnp.where(video, clean, 0.0)
+
+
+def alpha_constant():
+    ends = np.sqrt(np.float64(0.00085)), np.sqrt(np.float64(0.012))
+    betas = np.linspace(ends[0], ends[1], 1000, dtype=np.float64) ** 2
+    return np.pad(np.cumprod(1.0 - betas), (0, 24)).astype(np.float32).reshape(8, 128)
+
+
+def call(kernel, outs, args, spaces, scratch=(), flops=0, moved=0):
+    kinds = {"v": pltpu.VMEM, "s": pltpu.SMEM, "a": pl.ANY}
+    return pl.pallas_call(
+        kernel,
+        out_shape=[jax.ShapeDtypeStruct(shape, dtype) for shape, dtype in outs],
+        in_specs=[pl.BlockSpec(memory_space=kinds[letter]) for letter in spaces],
+        out_specs=[pl.BlockSpec(memory_space=pltpu.VMEM) for _ in outs],
+        scratch_shapes=list(scratch),
+        compiler_params=pltpu.CompilerParams(vmem_limit_bytes=24 * 2**20),
+        cost_estimate=pl.CostEstimate(flops=flops, bytes_accessed=moved, transcendentals=0),
+    )(*args)
+
+
+def four_blocks(
+    hidden, split_table, modulation, expand_weight, contract_weight, output_weight, latent, timestep
+):
+    hidden = hidden[0]
+    features = hidden.shape[1]
+    units = expand_weight.shape[1] // 2
+    width = output_weight.shape[1]
+    first_core = lax.axis_index("narrow") % 2 == 0
+
+    arrived = []
+    for k in range(CHUNKS):
+        piece = hidden[QUOTAS[k] : QUOTAS[k + 1]]
+        arrived.append([piece] + z_swaps(piece))
+
+    sums_mine, sums_sent, ends = call(
+        sums_kernel,
+        [((8, units), F32), ((8, units), F32), ((8, 2 * width), F32)],
+        [modulation, output_weight, expand_weight],
+        "vva",
+        [pltpu.VMEM(expand_weight.shape, BF16), pltpu.SemaphoreType.DMA((2,))],
+        2 * 16 * features * 2 * units,
+        2 * features * 2 * units,
+    )
+    sums_came = swap(sums_sent, "narrow", 1, 4)
+    sums_chip = jnp.where(
+        first_core,
+        jnp.concatenate([sums_mine, sums_came], 0),
+        jnp.concatenate([sums_came, sums_mine], 0),
+    )
+    sums_other = swap(sums_chip, "narrow", 2, 4)
+
+    tiles = 3
+    half_flops = lambda k: 2 * 2 * size_of(k) * features * units
+    half_bytes = 2 * features * units
+    expand_scratch = [pltpu.VMEM((features, units), BF16), pltpu.SemaphoreType.DMA((tiles,))]
+    contract_scratch = [pltpu.VMEM((units, features), BF16), pltpu.SemaphoreType.DMA((tiles,))]
+    returned = []
+    for k in range(CHUNKS):
+        rows = 2 * size_of(k)
+        pieces = [piece for phase in arrived[: k + 1] for piece in phase]
+        z, sent, side = call(
+            functools.partial(expand_sent_kernel, k),
+            [((rows, features), BF16), ((rows, units + 128), BF16), ((rows, 128), BF16)],
+            [split_table, modulation, *pieces, expand_weight],
+            "sv" + "v" * len(pieces) + "a",
+            expand_scratch,
+            half_flops(k),
+            half_bytes,
+        )
+        came = swap(sent, "narrow", 1, 4)
+        (kept,) = call(
+            expand_kept_kernel,
+            [((rows, units), F32)],
+            [z, expand_weight],
+            "va",
+            expand_scratch,
+            half_flops(k),
+            half_bytes,
+        )
+        total, sent = call(
+            merge_kernel,
+            [((rows, units), F32), ((rows, units + 128), BF16)],
+            [kept, side, came],
+            "vvv",
+        )
+        came = swap(sent, "narrow", 2, 4)
+        (act,) = call(
+            functools.partial(activate_kernel, k, features),
+            [((rows, units), BF16)],
+            [split_table, total, sent, came, sums_chip, sums_other],
+            "svvvvv",
+        )
+        act_came = swap(act, "narrow", 1, 4)
+        (out,) = call(
+            contract_own_kernel,
+            [((rows, features), F32)],
+            [act, contract_weight],
+            "va",
+            contract_scratch,
+            half_flops(k),
+            half_bytes,
+        )
+        pieces = call(
+            functools.partial(contract_other_kernel, k),
+            [((size_of(k), features), BF16)] * 4,
+            [split_table, act_came, out, contract_weight],
+            "svva",
+            contract_scratch,
+            half_flops(k),
+            half_bytes,
+        )
+        returned.append(pieces[0])
+        returned.extend(swap(pieces[s], "wide", s, 4) for s in (1, 2, 3))
+
+    layer_out, bundle = call(
+        finish_kernel,
+        [((CAP, features), BF16), ((CAP + 8, 2 * width), F32)],
+        [split_table, hidden, modulation, output_weight, ends, *returned],
+        "svvvv" + "v" * len(returned),
+    )
+    (velocity,) = call(
+        velocity_kernel,
+        [((CAP, width), F32)],
+        [bundle] + [swap(bundle, "narrow", n, 4) for n in (1, 2, 3)],
+        "vvvv",
+    )
+    (clean_latent,) = call(
+        latent_kernel,
+        [((CAP, width), F32)],
+        [split_table, timestep, alpha_constant(), latent, velocity, swap(velocity, "cfg", 1, 2)],
+        "ssvvvv",
+    )
+    return (layer_out[None], clean_latent)
+
+
 def solution(mesh):
+    by_swaps = (mesh.shape["wide"], mesh.shape["narrow"], mesh.shape["cfg"]) == (4, 4, 2)
     return jax.shard_map(
-        on_device,
+        four_blocks if by_swaps else any_slice,
         mesh=mesh,
         in_specs=(
             P("cfg", "wide", "narrow"),

time: 251 us -> 108 us (0.43)
  waiting for transfers between devices: 149 us -> 37.8 us
  blocking collectives: 57.7 us -> 0 us
  starting transfers between devices: 0.08 us -> 28.2 us
  Pallas kernels: 0 us -> 21.4 us
  local copies, waits for them, and re-layouts: 0.22 us -> 17.4 us
  matrix products: 16.2 us -> 0 us
  between operations: 16.1 us -> 1.58 us
  other arithmetic: 11.8 us -> 0.89 us
    psum x1 -> x0, waiting for transfers between devices: 118 us -> none  [on_device(): hidden_pre = lax.psum(hidden_part, 'narrow')]
    psum x3 -> x0, blocking collectives: 38.1 us -> none  [the longest x1 23.3 us: on_device(): guided = lax.psum(velocity_part * copy_weight, ('cfg', 'narrow'))]
    ppermute x0 -> x24, waiting for transfers between devices: none -> 37.8 us  [swap(): return lax.ppermute(array, axis, [(i, i ^ distance) for i in range(size)])]
    reduce_scatter x1 -> x0, waiting for transfers between devices: 30.5 us -> none  [on_device(): lax.psum_scatter(jnp.dot(activated, contract_weight, preferred_element_ty...]
    ppermute x0 -> x24, starting transfers between devices: none -> 28.2 us  [swap(): return lax.ppermute(array, axis, [(i, i ^ distance) for i in range(size)])]
    pallas_call x0 -> x16, Pallas kernels: none -> 21.4 us  [call(): pl.pallas_call(kernel, out_shape=[jax.ShapeDtypeStruct(shape, dtype) for...]
    all_gather x1 -> x0, blocking collectives: 19.6 us -> none  [on_device(): lax.all_gather(normed, 'wide', axis=0, tiled=True)]
    unnamed x8 -> x39, local copies, waits for them, and re-layouts: 0.03 us -> 16.4 us
  transfers between devices with their start and end apart: 2 -> 24, of which waited for: 2 -> 9; matrix products, arithmetic and copies ran while one was open for 1% -> 1% of each run, Pallas kernels for 0% -> 16%
where the time goes in v2:
time: 108 us; the launch traced here: 107 us
  waiting for transfers between devices  37.8 us (35%)
  starting transfers between devices  28.2 us (26%)
  Pallas kernels  21.4 us (20%)
  local copies, waits for them, and re-layouts  17.4 us (16%)
  between operations  1.58 us (1%)
    ppermute x24, waiting for transfers between devices, swap(): return lax.ppermute(array, axis, [(i, i ^ distance) for i in range(size)])  37.8 us
    ppermute x24, starting transfers between devices, swap(): return lax.ppermute(array, axis, [(i, i ^ distance) for i in range(size)])  28.2 us
    pallas_call x16, Pallas kernels, call(): pl.pallas_call(kernel, out_shape=[jax.ShapeDtypeStruct(shape, dtype) for...  21.4 us
    unnamed x39, local copies, waits for them, and re-layouts  16.4 us
  transfers between devices with their start and end apart: 24, of which 9 were waited for; matrix products, arithmetic and copies ran while one was open for 1% of the time, Pallas kernels for 16%

profile of v2, /device:TPU:0, one launch (start us, length us, event | category | flops | bytes accessed | tf_op | source)
XLA Modules:
  0.0 107.3 jit_solution(4956572571051602206)
XLA Ops:
  1.6 3.1 %collective-permute-start = (bf16[64,768]{1,0:T(8,128)(2,1)S(1)}, bf16[64,768]{1,0:T(8,128)(2,1)S(1)}, u32[]{:S(2)}, u32[]{:S(2)}) collective-permute-start(bf16[64,768]{1,0:T(8,128)(2,1)S(1)} %get-tuple-element.51.refs_0_), channel_id=1, source_target_pairs={{0,4},{4,0},{8,12},{12,8},{1,5},{5,1},{9,13},{13,9},{2,6},{6,2},{1... | collective-permute-start | bytes 294920 | tf_op jit(solution)/shard_map/ppermute | solution.py:93
  4.7 2.6 %collective-permute-start.1 = (bf16[64,768]{1,0:T(8,128)(2,1)S(1)}, bf16[64,768]{1,0:T(8,128)(2,1)S(1)}, u32[]{:S(2)}, u32[]{:S(2)}) collective-permute-start(bf16[64,768]{1,0:T(8,128)(2,1)S(1)} %get-tuple-element.51.refs_0_), channel_id=1, source_target_pairs={{0,8},{4,12},{8,0},{12,4},{1,9},{5,13},{9,1},{13,5},{2,10},{6,14},... | collective-permute-start | bytes 294920 | tf_op jit(solution)/shard_map/ppermute | solution.py:93
  8.2 3.5 %collective-permute-start.12 = (bf16[64,768]{1,0:T(8,128)(2,1)S(1)}, bf16[64,768]{1,0:T(8,128)(2,1)S(1)}, u32[]{:S(2)}, u32[]{:S(2)}) collective-permute-start(bf16[64,768]{1,0:T(8,128)(2,1)S(1)} %get-tuple-element.50.refs_4_), channel_id=1, source_target_pairs={{0,8},{4,12},{8,0},{12,4},{1,9},{5,13},{9,1},{13,5},{2,10},{6,14},... | collective-permute-start | bytes 294920 | tf_op jit(solution)/shard_map/ppermute | solution.py:93
  12.3 3.0 %collective-permute-done.1.refs_2_ = bf16[64,768]{1,0:T(8,128)(2,1)S(1)} collective-permute-done((bf16[64,768]{1,0:T(8,128)(2,1)S(1)}, bf16[64,768]{1,0:T(8,128)(2,1)S(1)}, u32[]{:S(2)}, u32[]{:S(2)}) %collective-permute-start.1) | collective-permute-done | bytes 98336 | tf_op jit(solution)/shard_map/ppermute | solution.py:93
  15.3 8.2 %collective-permute-done.12.refs_6_ = bf16[64,768]{1,0:T(8,128)(2,1)S(1)} collective-permute-done((bf16[64,768]{1,0:T(8,128)(2,1)S(1)}, bf16[64,768]{1,0:T(8,128)(2,1)S(1)}, u32[]{:S(2)}, u32[]{:S(2)}) %collective-permute-start.12) | collective-permute-done | bytes 98336 | tf_op jit(solution)/shard_map/ppermute | solution.py:93
  23.5 2.3 %copy-done = bf16[768,3072]{1,0:T(8,128)(2,1)S(1)} copy-done((bf16[768,3072]{1,0:T(8,128)(2,1)S(1)}, bf16[768,3072]{1,0:T(8,128)(2,1)}, u32[]{:S(2)}) %copy-start) | copy-done | bytes 4718616
  27.3 2.2 %shard_map.111 = (bf16[128,768]{1,0:T(8,128)(2,1)S(1)}, bf16[128,1664]{1,0:T(8,128)(2,1)S(1)}, bf16[128,128]{1,0:T(8,128)(2,1)S(1)}) custom-call(s32[4]{0:T(128)S(1)} %copy-done.13, f32[8,768]{1,0:T(8,128)S(1)} %copy-done.9, bf16[64,768]{1,0:T(8,128)(2,1)S(1)} %get-tuple-element.51.refs_0_, bf16[64,768]{1,0:T(8,128)(2,1)S(1)} %collective-permute-done.refs_1_, ...), custom_call_target="tpu_custom_call" | custom-call | flops 301989888 | bytes 2359296 | tf_op jit(solution)/shard_map/pallas_call | solution.py:415
  29.6 2.2 %shard_map.105 = (bf16[128,768]{1,0:T(8,128)(2,1)S(1)}, bf16[128,1664]{1,0:T(8,128)(2,1)S(1)}, bf16[128,128]{1,0:T(8,128)(2,1)S(1)}) custom-call(s32[4]{0:T(128)S(1)} %copy-done.13, f32[8,768]{1,0:T(8,128)S(1)} %copy-done.9, bf16[64,768]{1,0:T(8,128)(2,1)S(1)} %get-tuple-element.51.refs_0_, bf16[64,768]{1,0:T(8,128)(2,1)S(1)} %collective-permute-done.refs_1_, ...), custom_call_target="tpu_custom_call" | custom-call | flops 301989888 | bytes 2359296 | tf_op jit(solution)/shard_map/pallas_call | solution.py:415
  35.5 2.3 %copy-done.2 = bf16[768,3072]{1,0:T(8,128)(2,1)S(1)} copy-done((bf16[768,3072]{1,0:T(8,128)(2,1)S(1)}, bf16[768,3072]{1,0:T(8,128)(2,1)}, u32[]{:S(2)}) %copy-start.2) | copy-done | bytes 4718616
  37.8 2.4 %shard_map.104 = (f32[8,1536]{1,0:T(8,128)S(1)}, f32[8,1536]{1,0:T(8,128)}, f32[8,128]{1,0:T(8,128)S(1)}) custom-call(f32[8,768]{1,0:T(8,128)S(1)} %copy-done.10, bf16[768,64]{1,0:T(8,128)(2,1)S(1)} %copy.12.out_weight, bf16[768,3072]{1,0:T(8,128)(2,1)S(1)} %copy-done.2), custom_call_target="tpu_custom_call" | custom-call | flops 75497472 | bytes 4718592 | tf_op jit(solution)/shard_map/pallas_call | solution.py:415
  44.7 12.0 %collective-permute-done.6.sums_other = f32[16,1536]{1,0:T(8,128)S(1)} collective-permute-done((f32[16,1536]{1,0:T(8,128)S(1)}, f32[16,1536]{1,0:T(8,128)S(1)}, u32[]{:S(2)}, u32[]{:S(2)}) %collective-permute-start.6) | collective-permute-done | bytes 98336 | tf_op jit(solution)/shard_map/ppermute | solution.py:93
  56.8 2.3 %shard_map.114.act = bf16[128,1536]{1,0:T(8,128)(2,1)S(1)} custom-call(s32[4]{0:T(128)S(1)} %copy-done.14, f32[128,1536]{1,0:T(8,128)S(1)} %get-tuple-element.40.total, bf16[128,1664]{1,0:T(8,128)(2,1)S(1)} %get-tuple-element.41.sent, bf16[128,1664]{1,0:T(8,128)(2,1)S(1)} %collective-permute-done.15.came, f32[16,1536]{1,0:T(8,128)S(1)} %maximum_select_fusion.sums_own, ...), custom_call_target="tpu_custom_call" | custom-call | tf_op jit(solution)/shard_map/pallas_call | solution.py:415
  59.1 2.2 %shard_map.108.act = bf16[128,1536]{1,0:T(8,128)(2,1)S(1)} custom-call(s32[4]{0:T(128)S(1)} %copy-done.14, f32[128,1536]{1,0:T(8,128)S(1)} %get-tuple-element.29.total, bf16[128,1664]{1,0:T(8,128)(2,1)S(1)} %get-tuple-element.30.sent, bf16[128,1664]{1,0:T(8,128)(2,1)S(1)} %collective-permute-done.4.came, f32[16,1536]{1,0:T(8,128)S(1)} %maximum_select_fusion.sums_own, ...), custom_call_target="tpu_custom_call" | custom-call | tf_op jit(solution)/shard_map/pallas_call | solution.py:415
  61.9 2.3 %copy-done.4 = bf16[3072,768]{1,0:T(8,128)(2,1)S(1)} copy-done((bf16[3072,768]{1,0:T(8,128)(2,1)S(1)}, bf16[3072,768]{1,0:T(8,128)(2,1)}, u32[]{:S(2)}) %copy-start.4) | copy-done | bytes 4718616
  65.2 2.3 %copy-done.5 = bf16[3072,768]{1,0:T(8,128)(2,1)S(1)} copy-done((bf16[3072,768]{1,0:T(8,128)(2,1)S(1)}, bf16[3072,768]{1,0:T(8,128)(2,1)}, u32[]{:S(2)}) %copy-start.5) | copy-done | bytes 4718616
  70.9 2.3 %copy-done.6 = bf16[3072,768]{1,0:T(8,128)(2,1)S(1)} copy-done((bf16[3072,768]{1,0:T(8,128)(2,1)S(1)}, bf16[3072,768]{1,0:T(8,128)(2,1)}, u32[]{:S(2)}) %copy-start.6) | copy-done | bytes 4718616
  77.0 2.3 %copy-done.7 = bf16[3072,768]{1,0:T(8,128)(2,1)S(1)} copy-done((bf16[3072,768]{1,0:T(8,128)(2,1)S(1)}, bf16[3072,768]{1,0:T(8,128)(2,1)}, u32[]{:S(2)}) %copy-start.7) | copy-done | bytes 4718616
  79.3 1.7 %shard_map.110 = (bf16[64,768]{1,0:T(8,128)(2,1)S(1)}, bf16[64,768]{1,0:T(8,128)(2,1)S(1)}, bf16[64,768]{1,0:T(8,128)(2,1)S(1)}, bf16[64,768]{1,0:T(8,128)(2,1)S(1)}) custom-call(s32[4]{0:T(128)S(1)} %copy-done.14, bf16[128,1536]{1,0:T(8,128)(2,1)S(1)} %collective-permute-done.7.act, f32[128,768]{1,0:T(8,128)S(1)} %shard_map.109.so_far, ...), custom_call_target="tpu_custom_call" | custom-call | flops 301989888 | bytes 2359296 | tf_op jit(solution)/shard_map/pallas_call | solution.py:415
  81.1 2.5 %collective-permute-start.10 = (bf16[64,768]{1,0:T(8,128)(2,1)S(1)}, bf16[64,768]{1,0:T(8,128)(2,1)S(1)}, u32[]{:S(2)}, u32[]{:S(2)}) collective-permute-start(bf16[64,768]{1,0:T(8,128)(2,1)S(1)} %get-tuple-element.36), channel_id=1, source_target_pairs={{0,12},{4,8},{8,4},{12,0},{1,13},{5,9},{9,5},{13,1},{2,14},{6,10},... | collective-permute-start | bytes 294920 | tf_op jit(solution)/shard_map/ppermute | solution.py:93
  83.6 1.9 %collective-permute-start.9 = (bf16[64,768]{1,0:T(8,128)(2,1)S(1)}, bf16[64,768]{1,0:T(8,128)(2,1)S(1)}, u32[]{:S(2)}, u32[]{:S(2)}) collective-permute-start(bf16[64,768]{1,0:T(8,128)(2,1)S(1)} %get-tuple-element.35), channel_id=1, source_target_pairs={{0,8},{4,12},{8,0},{12,4},{1,9},{5,13},{9,1},{13,5},{2,10},{6,14},... | collective-permute-start | bytes 294920 | tf_op jit(solution)/shard_map/ppermute | solution.py:93
  85.5 3.2 %collective-permute-done.10.refs_3_ = bf16[64,768]{1,0:T(8,128)(2,1)S(1)} collective-permute-done((bf16[64,768]{1,0:T(8,128)(2,1)S(1)}, bf16[64,768]{1,0:T(8,128)(2,1)S(1)}, u32[]{:S(2)}, u32[]{:S(2)}) %collective-permute-start.10) | collective-permute-done | bytes 98336 | tf_op jit(solution)/shard_map/ppermute | solution.py:93
  89.1 5.1 %collective-permute-done.9.refs_2_ = bf16[64,768]{1,0:T(8,128)(2,1)S(1)} collective-permute-done((bf16[64,768]{1,0:T(8,128)(2,1)S(1)}, bf16[64,768]{1,0:T(8,128)(2,1)S(1)}, u32[]{:S(2)}, u32[]{:S(2)}) %collective-permute-start.9) | collective-permute-done | bytes 98336 | tf_op jit(solution)/shard_map/ppermute | solution.py:93
  97.5 2.8 %collective-permute-done.21.third = f32[136,128]{1,0:T(8,128)S(1)} collective-permute-done((f32[136,128]{1,0:T(8,128)S(1)}, f32[136,128]{1,0:T(8,128)S(1)}, u32[]{:S(2)}, u32[]{:S(2)}) %collective-permute-start.21) | collective-permute-done | bytes 69664 | tf_op jit(solution)/shard_map/ppermute | solution.py:93
  103.9 2.0 %collective-permute-done.23.other = f32[128,64]{1,0:T(8,128)S(1)} collective-permute-done((f32[128,64]{1,0:T(8,128)S(1)}, f32[128,64]{1,0:T(8,128)S(1)}, u32[]{:S(2)}, u32[]{:S(2)}) %collective-permute-start.23) | collective-permute-done | bytes 32800 | tf_op jit(solution)/shard_map/ppermute | solution.py:93
  (81 shorter events, 28.6 us)
Async XLA Ops:
  1.6 10.1 %collective-permute-start = (bf16[64,768]{1,0:T(8,128)(2,1)S(1)}, bf16[64,768]{1,0:T(8,128)(2,1)S(1)}, u32[]{:S(2)}, u32[]{:S(2)}) collective-permute-start(bf16[64,768]{1,0:T(8,128)(2,1)S(1)} %get-tuple-element.51.refs_0_), channel_id=1, source_target_pairs={{0,4},{4,0},{8,12},{12,8},{1,5},{5,1},{9,13},{13,9},{2,6},{6,2},{1... | collective-permute-start | bytes 294920 | tf_op jit(solution)/shard_map/ppermute | solution.py:93
  4.7 10.7 %collective-permute-start.1 = (bf16[64,768]{1,0:T(8,128)(2,1)S(1)}, bf16[64,768]{1,0:T(8,128)(2,1)S(1)}, u32[]{:S(2)}, u32[]{:S(2)}) collective-permute-start(bf16[64,768]{1,0:T(8,128)(2,1)S(1)} %get-tuple-element.51.refs_0_), channel_id=1, source_target_pairs={{0,8},{4,12},{8,0},{12,4},{1,9},{5,13},{9,1},{13,5},{2,10},{6,14},... | collective-permute-start | bytes 294920 | tf_op jit(solution)/shard_map/ppermute | solution.py:93
  7.3 8.1 %collective-permute-start.2 = (bf16[64,768]{1,0:T(8,128)(2,1)S(1)}, bf16[64,768]{1,0:T(8,128)(2,1)S(1)}, u32[]{:S(2)}, u32[]{:S(2)}) collective-permute-start(bf16[64,768]{1,0:T(8,128)(2,1)S(1)} %get-tuple-element.51.refs_0_), channel_id=1, source_target_pairs={{0,12},{4,8},{8,4},{12,0},{1,13},{5,9},{9,5},{13,1},{2,14},{6,10},... | collective-permute-start | bytes 294920 | tf_op jit(solution)/shard_map/ppermute | solution.py:93
  7.3 8.1 %collective-permute-start.11 = (bf16[64,768]{1,0:T(8,128)(2,1)S(1)}, bf16[64,768]{1,0:T(8,128)(2,1)S(1)}, u32[]{:S(2)}, u32[]{:S(2)}) collective-permute-start(bf16[64,768]{1,0:T(8,128)(2,1)S(1)} %get-tuple-element.50.refs_4_), channel_id=1, source_target_pairs={{0,4},{4,0},{8,12},{12,8},{1,5},{5,1},{9,13},{13,9},{2,6},{6,2},{1... | collective-permute-start | bytes 294920 | tf_op jit(solution)/shard_map/ppermute | solution.py:93
  8.2 15.4 %collective-permute-start.12 = (bf16[64,768]{1,0:T(8,128)(2,1)S(1)}, bf16[64,768]{1,0:T(8,128)(2,1)S(1)}, u32[]{:S(2)}, u32[]{:S(2)}) collective-permute-start(bf16[64,768]{1,0:T(8,128)(2,1)S(1)} %get-tuple-element.50.refs_4_), channel_id=1, source_target_pairs={{0,8},{4,12},{8,0},{12,4},{1,9},{5,13},{9,1},{13,5},{2,10},{6,14},... | collective-permute-start | bytes 294920 | tf_op jit(solution)/shard_map/ppermute | solution.py:93
  11.7 11.9 %collective-permute-start.13 = (bf16[64,768]{1,0:T(8,128)(2,1)S(1)}, bf16[64,768]{1,0:T(8,128)(2,1)S(1)}, u32[]{:S(2)}, u32[]{:S(2)}) collective-permute-start(bf16[64,768]{1,0:T(8,128)(2,1)S(1)} %get-tuple-element.50.refs_4_), channel_id=1, source_target_pairs={{0,12},{4,8},{8,4},{12,0},{1,13},{5,9},{9,5},{13,1},{2,14},{6,10},... | collective-permute-start | bytes 294920 | tf_op jit(solution)/shard_map/ppermute | solution.py:93
  29.5 4.1 %collective-permute-start.14 = (bf16[128,1664]{1,0:T(8,128)(2,1)S(1)}, bf16[128,1664]{1,0:T(8,128)(2,1)S(1)}, u32[]{:S(2)}, u32[]{:S(2)}) collective-permute-start(bf16[128,1664]{1,0:T(8,128)(2,1)S(1)} %get-tuple-element.39), channel_id=1, source_target_pairs={{0,1},{1,0},{2,3},{3,2},{4,5},{5,4},{6,7},{7,6},{8,9},{9,8},{10,11... | collective-permute-start | bytes 1277960 | tf_op jit(solution)/shard_map/ppermute | solution.py:93
  31.8 9.7 %collective-permute-start.3 = (bf16[128,1664]{1,0:T(8,128)(2,1)S(1)}, bf16[128,1664]{1,0:T(8,128)(2,1)S(1)}, u32[]{:S(2)}, u32[]{:S(2)}) collective-permute-start(bf16[128,1664]{1,0:T(8,128)(2,1)S(1)} %get-tuple-element.28), channel_id=1, source_target_pairs={{0,1},{1,0},{2,3},{3,2},{4,5},{5,4},{6,7},{7,6},{8,9},{9,8},{10,11... | collective-permute-start | bytes 1277960 | tf_op jit(solution)/shard_map/ppermute | solution.py:93
  33.7 23.1 %collective-permute-start.15 = (bf16[128,1664]{1,0:T(8,128)(2,1)S(1)}, bf16[128,1664]{1,0:T(8,128)(2,1)S(1)}, u32[]{:S(2)}, u32[]{:S(2)}) collective-permute-start(bf16[128,1664]{1,0:T(8,128)(2,1)S(1)} %get-tuple-element.41.sent), channel_id=1, source_target_pairs={{0,2},{1,3},{2,0},{3,1},{4,6},{5,7},{6,4},{7,5},{8,10},{9,11},{10,... | collective-permute-start | bytes 1277960 | tf_op jit(solution)/shard_map/ppermute | solution.py:93
  40.3 2.0 %collective-permute-start.5 = (f32[8,1536]{1,0:T(8,128)}, f32[8,1536]{1,0:T(8,128)}, u32[]{:S(2)}, u32[]{:S(2)}) collective-permute-start(f32[8,1536]{1,0:T(8,128)} %get-tuple-element.32), channel_id=1, source_target_pairs={{0,1},{1,0},{2,3},{3,2},{4,5},{5,4},{6,7},{7,6},{8,9},{9,8},{10,11... | collective-permute-start | bytes 147464 | tf_op jit(solution)/shard_map/ppermute | solution.py:93
  41.7 17.4 %collective-permute-start.4 = (bf16[128,1664]{1,0:T(8,128)(2,1)S(1)}, bf16[128,1664]{1,0:T(8,128)(2,1)S(1)}, u32[]{:S(2)}, u32[]{:S(2)}) collective-permute-start(bf16[128,1664]{1,0:T(8,128)(2,1)S(1)} %get-tuple-element.30.sent), channel_id=1, source_target_pairs={{0,2},{1,3},{2,0},{3,1},{4,6},{5,7},{6,4},{7,5},{8,10},{9,11},{10,... | collective-permute-start | bytes 1277960 | tf_op jit(solution)/shard_map/ppermute | solution.py:93
  43.1 13.6 %collective-permute-start.6 = (f32[16,1536]{1,0:T(8,128)S(1)}, f32[16,1536]{1,0:T(8,128)S(1)}, u32[]{:S(2)}, u32[]{:S(2)}) collective-permute-start(f32[16,1536]{1,0:T(8,128)S(1)} %maximum_select_fusion.sums_own), channel_id=1, source_target_pairs={{0,2},{1,3},{2,0},{3,1},{4,6},{5,7},{6,4},{7,5},{8,10},{9,11},{10,... | collective-permute-start | bytes 294920 | tf_op jit(solution)/shard_map/ppermute | solution.py:93
  59.0 6.1 %collective-permute-start.16 = (bf16[128,1536]{1,0:T(8,128)(2,1)S(1)}, bf16[128,1536]{1,0:T(8,128)(2,1)S(1)}, u32[]{:S(2)}, u32[]{:S(2)}) collective-permute-start(bf16[128,1536]{1,0:T(8,128)(2,1)S(1)} %shard_map.114.act), channel_id=1, source_target_pairs={{0,1},{1,0},{2,3},{3,2},{4,5},{5,4},{6,7},{7,6},{8,9},{9,8},{10,11... | collective-permute-start | bytes 1179656 | tf_op jit(solution)/shard_map/ppermute | solution.py:93
  61.4 15.6 %collective-permute-start.7 = (bf16[128,1536]{1,0:T(8,128)(2,1)S(1)}, bf16[128,1536]{1,0:T(8,128)(2,1)S(1)}, u32[]{:S(2)}, u32[]{:S(2)}) collective-permute-start(bf16[128,1536]{1,0:T(8,128)(2,1)S(1)} %shard_map.108.act), channel_id=1, source_target_pairs={{0,1},{1,0},{2,3},{3,2},{4,5},{5,4},{6,7},{7,6},{8,9},{9,8},{10,11... | collective-permute-start | bytes 1179656 | tf_op jit(solution)/shard_map/ppermute | solution.py:93
  69.2 14.3 %collective-permute-start.17 = (bf16[64,768]{1,0:T(8,128)(2,1)S(1)}, bf16[64,768]{1,0:T(8,128)(2,1)S(1)}, u32[]{:S(2)}, u32[]{:S(2)}) collective-permute-start(bf16[64,768]{1,0:T(8,128)(2,1)S(1)} %get-tuple-element.43), channel_id=1, source_target_pairs={{0,4},{4,0},{8,12},{12,8},{1,5},{5,1},{9,13},{13,9},{2,6},{6,2},{1... | collective-permute-start | bytes 294920 | tf_op jit(solution)/shard_map/ppermute | solution.py:93
  74.1 11.4 %collective-permute-start.18 = (bf16[64,768]{1,0:T(8,128)(2,1)S(1)}, bf16[64,768]{1,0:T(8,128)(2,1)S(1)}, u32[]{:S(2)}, u32[]{:S(2)}) collective-permute-start(bf16[64,768]{1,0:T(8,128)(2,1)S(1)} %get-tuple-element.44), channel_id=1, source_target_pairs={{0,8},{4,12},{8,0},{12,4},{1,9},{5,13},{9,1},{13,5},{2,10},{6,14},... | collective-permute-start | bytes 294920 | tf_op jit(solution)/shard_map/ppermute | solution.py:93
  75.6 9.9 %collective-permute-start.19 = (bf16[64,768]{1,0:T(8,128)(2,1)S(1)}, bf16[64,768]{1,0:T(8,128)(2,1)S(1)}, u32[]{:S(2)}, u32[]{:S(2)}) collective-permute-start(bf16[64,768]{1,0:T(8,128)(2,1)S(1)} %get-tuple-element.45), channel_id=1, source_target_pairs={{0,12},{4,8},{8,4},{12,0},{1,13},{5,9},{9,5},{13,1},{2,14},{6,10},... | collective-permute-start | bytes 294920 | tf_op jit(solution)/shard_map/ppermute | solution.py:93
  81.1 7.7 %collective-permute-start.10 = (bf16[64,768]{1,0:T(8,128)(2,1)S(1)}, bf16[64,768]{1,0:T(8,128)(2,1)S(1)}, u32[]{:S(2)}, u32[]{:S(2)}) collective-permute-start(bf16[64,768]{1,0:T(8,128)(2,1)S(1)} %get-tuple-element.36), channel_id=1, source_target_pairs={{0,12},{4,8},{8,4},{12,0},{1,13},{5,9},{9,5},{13,1},{2,14},{6,10},... | collective-permute-start | bytes 294920 | tf_op jit(solution)/shard_map/ppermute | solution.py:93
  83.6 5.5 %collective-permute-start.8 = (bf16[64,768]{1,0:T(8,128)(2,1)S(1)}, bf16[64,768]{1,0:T(8,128)(2,1)S(1)}, u32[]{:S(2)}, u32[]{:S(2)}) collective-permute-start(bf16[64,768]{1,0:T(8,128)(2,1)S(1)} %get-tuple-element.34), channel_id=1, source_target_pairs={{0,4},{4,0},{8,12},{12,8},{1,5},{5,1},{9,13},{13,9},{2,6},{6,2},{1... | collective-permute-start | bytes 294920 | tf_op jit(solution)/shard_map/ppermute | solution.py:93
  83.6 10.5 %collective-permute-start.9 = (bf16[64,768]{1,0:T(8,128)(2,1)S(1)}, bf16[64,768]{1,0:T(8,128)(2,1)S(1)}, u32[]{:S(2)}, u32[]{:S(2)}) collective-permute-start(bf16[64,768]{1,0:T(8,128)(2,1)S(1)} %get-tuple-element.35), channel_id=1, source_target_pairs={{0,8},{4,12},{8,0},{12,4},{1,9},{5,13},{9,1},{13,5},{2,10},{6,14},... | collective-permute-start | bytes 294920 | tf_op jit(solution)/shard_map/ppermute | solution.py:93
  95.6 1.9 %collective-permute-start.20 = (f32[136,128]{1,0:T(8,128)S(1)}, f32[136,128]{1,0:T(8,128)S(1)}, u32[]{:S(2)}, u32[]{:S(2)}) collective-permute-start(f32[136,128]{1,0:T(8,128)S(1)} %get-tuple-element.47.first), channel_id=1, source_target_pairs={{0,1},{1,0},{2,3},{3,2},{4,5},{5,4},{6,7},{7,6},{8,9},{9,8},{10,11... | collective-permute-start | bytes 208904 | tf_op jit(solution)/shard_map/ppermute | solution.py:93
  95.6 4.7 %collective-permute-start.21 = (f32[136,128]{1,0:T(8,128)S(1)}, f32[136,128]{1,0:T(8,128)S(1)}, u32[]{:S(2)}, u32[]{:S(2)}) collective-permute-start(f32[136,128]{1,0:T(8,128)S(1)} %get-tuple-element.47.first), channel_id=1, source_target_pairs={{0,2},{1,3},{2,0},{3,1},{4,6},{5,7},{6,4},{7,5},{8,10},{9,11},{10,... | collective-permute-start | bytes 208904 | tf_op jit(solution)/shard_map/ppermute | solution.py:93
  97.1 4.2 %collective-permute-start.22 = (f32[136,128]{1,0:T(8,128)S(1)}, f32[136,128]{1,0:T(8,128)S(1)}, u32[]{:S(2)}, u32[]{:S(2)}) collective-permute-start(f32[136,128]{1,0:T(8,128)S(1)} %get-tuple-element.47.first), channel_id=1, source_target_pairs={{0,3},{1,2},{2,1},{3,0},{4,7},{5,6},{6,5},{7,4},{8,11},{9,10},{10,... | collective-permute-start | bytes 208904 | tf_op jit(solution)/shard_map/ppermute | solution.py:93
  101.6 4.3 %collective-permute-start.23 = (f32[128,64]{1,0:T(8,128)S(1)}, f32[128,64]{1,0:T(8,128)S(1)}, u32[]{:S(2)}, u32[]{:S(2)}) collective-permute-start(f32[128,64]{1,0:T(8,128)S(1)} %shard_map.118.mine), channel_id=1, source_target_pairs={{0,16},{16,0},{1,17},{17,1},{2,18},{18,2},{3,19},{19,3},{4,20},{20... | collective-permute-start | bytes 98312 | tf_op jit(solution)/shard_map/ppermute | solution.py:93
  (18 other events, 135.8 us)

commit v3 on v2

--- a/solution.py
+++ b/solution.py
@@ -83,6 +83,16 @@
 CAP = 128
 CHUNKS = len(QUOTAS) - 1
 F32, BF16 = jnp.float32, jnp.bfloat16
+TILE = 512
+WEIGHTS = {
+    "prepare": 1,
+    "expand_sent": 10**10,
+    "expand_kept": 10**10,
+    "merge": 1,
+    "activate": 1,
+    "contract_own": 10**10,
+    "contract_other": 1,
+}
 
 
 def size_of(k):
@@ -133,69 +143,89 @@
     return position < TEXT
 
 
-def sums_kernel(mod, out_weight, w, own_out, other_out, ends_out, buffer, sems):
+def high_low(values):
+    high = values.astype(BF16)
+    return high, (values - high.astype(F32)).astype(BF16)
+
+
+def load(source, place, sems):
+    parts = sems.shape[0]
+    height = source.shape[0] // parts
+    copies = []
+    for t in range(parts):
+        rows = pl.ds(t * height, height)
+        copies.append(pltpu.make_async_copy(source.at[rows, :], place.at[rows, :], sems.at[t]))
+        copies[-1].start()
+    return copies
+
+
+def hold_kernel(source, place, sems):
+    for copy in load(source, place, sems):
+        copy.wait()
+
+
+def prepare_kernel(hidden, mod, out_weight, w, *refs):
+    later, (held, own_out, other_out, sems) = refs[: CHUNKS - 1], refs[CHUNKS - 1 :]
     core = lax.axis_index("narrow") % 2
-    units = buffer.shape[1] // 2
-    copies = []
-    for t in range(2):
-        copies.append(
-            pltpu.make_async_copy(
-                w.at[:, pl.ds(t * units, units)], buffer.at[:, pl.ds(t * units, units)], sems.at[t]
-            )
-        )
-        copies[-1].start()
+    units = own_out.shape[1]
+    copies = load(w, held, sems)
+    for k in range(1, CHUNKS):
+        later[k - 1][...] = hidden[QUOTAS[k] : QUOTAS[k + 1], :]
     row = lax.broadcasted_iota(jnp.int32, (8, 1), 0)
     rows = jnp.where(row == 0, 1.0 + mod[1:2, :], jnp.zeros((8, 1), F32))
     rows = jnp.where(row == 1, 1.0 + mod[4:5, :], rows)
     rows = jnp.where(row == 2, mod[0:1, :], rows)
     rows = jnp.where(row == 3, mod[3:4, :], rows)
-    high = rows.astype(BF16)
-    low = (rows - high.astype(F32)).astype(BF16)
-    both = jnp.concatenate([high, low], 0)
-    ends = jnp.where(row == 0, 1.0 + mod[7:8, :], mod[6:7, :])
-    high = ends.astype(BF16)
-    low = (ends - high.astype(F32)).astype(BF16)
-    ends = jnp.dot(jnp.concatenate([high, low], 0), out_weight[...], preferred_element_type=F32)
+    both = jnp.concatenate(high_low(rows), 0)
+    rows = jnp.where(row == 4, 1.0 + mod[7:8, :], jnp.zeros((8, 1), F32))
+    rows = jnp.where(row == 5, mod[6:7, :], rows)
+    ends = lax.dot_general(
+        jnp.concatenate(high_low(rows), 0),
+        out_weight[...],
+        (((1,), (1,)), ((), ())),
+        preferred_element_type=F32,
+    )
     ends = ends[:8] + ends[8:]
-    ends_out[...] = jnp.concatenate(
-        [jnp.broadcast_to(ends[0:1], ends.shape), jnp.broadcast_to(ends[1:2], ends.shape)], 1
-    )
+    ends = jnp.concatenate([ends, jnp.zeros((8, 128 - ends.shape[1]), F32)], 1)
+    for copy in copies:
+        copy.wait()
     for t in range(2):
-        copies[t].wait()
-        part = jnp.dot(both, buffer[:, t * units : (t + 1) * units], preferred_element_type=F32)
+        part = jnp.dot(both, held[:, t * units : (t + 1) * units], preferred_element_type=F32)
         part = part[:8] + part[8:]
 
         @pl.when(core == t)
         def _():
             own_out[...] = part
+            own_out[:, :128] = part[:, :128] + ends
 
         @pl.when(core != t)
         def _():
             other_out[...] = part
-
-
-def fetch(w, start, buffer, sems, tiles, axis):
-    width = buffer.shape[axis] // tiles
-    copies = []
-    for t in range(tiles):
-        source = pl.ds(pl.multiple_of(start + t * width, 128), width)
-        place = pl.ds(t * width, width)
-        if axis == 1:
-            copy = pltpu.make_async_copy(w.at[:, source], buffer.at[:, place], sems.at[t])
-        else:
-            copy = pltpu.make_async_copy(w.at[source, :], buffer.at[place, :], sems.at[t])
-        copy.start()
-        copies.append(copy)
-    return copies, width
+            other_out[:, :128] = part[:, :128] + ends
+
+
+def chip_kernel(mine, came, out):
+    first = lax.axis_index("narrow") % 2 == 0
+    out[:8, :] = jnp.where(first, mine[...], came[...])
+    out[8:, :] = jnp.where(first, came[...], mine[...])
+
+
+def factors_kernel(mine, chip, other, out, ends_out):
+    rows = []
+    for sums in (chip, other):
+        high, low = high_low(sums[...])
+        rows += [high, low, high]
+    out[...] = jnp.concatenate(rows + [jnp.zeros((32, chip.shape[1]), BF16)], 0)
+    total = (chip[:8, :128] + chip[8:, :128]) + (other[:8, :128] + other[8:, :128])
+    ends_out[...] = jnp.concatenate([total, mine[:, :128], jnp.zeros((112, 128), F32)], 0).T
 
 
 def expand_sent_kernel(k, table, mod, *refs):
     pieces = refs[: 4 * (k + 1)]
-    w, z_out, sent_out, side_out, buffer, sems = refs[4 * (k + 1) :]
+    w = refs[4 * (k + 1)]
+    z_out, sent_out, side_out = refs[-3:]
     core = lax.axis_index("narrow") % 2
-    units = buffer.shape[1]
-    tiles = sems.shape[0]
-    copies, width = fetch(w, (1 - core) * units, buffer, sems, tiles, 1)
+    units = w.shape[1] // 2
 
     size = size_of(k)
     ranks, counts, others, _, largest_offset = layout(table)
@@ -230,26 +260,21 @@
     side = jnp.where(lane == 7, square - square_high, side).astype(BF16)
     side_out[...] = side
     sent_out[:, units:] = side
-    for t in range(tiles):
-        copies[t].wait()
-        sent_out[:, t * width : (t + 1) * width] = jnp.dot(
-            z, buffer[:, t * width : (t + 1) * width], preferred_element_type=F32
-        ).astype(BF16)
-
-
-def expand_kept_kernel(z, w, kept_out, buffer, sems):
+    for t in range(0, units, TILE):
+        columns = pl.ds(pl.multiple_of((1 - core) * units + t, 128), TILE)
+        sent_out[:, t : t + TILE] = jnp.dot(z, w[:, columns], preferred_element_type=F32).astype(BF16)
+
+
+def expand_kept_kernel(z, w, kept_out):
     core = lax.axis_index("narrow") % 2
-    units = buffer.shape[1]
-    tiles = sems.shape[0]
-    copies, width = fetch(w, core * units, buffer, sems, tiles, 1)
-    for t in range(tiles):
-        copies[t].wait()
-        kept_out[:, t * width : (t + 1) * width] = jnp.dot(
-            z[...], buffer[:, t * width : (t + 1) * width], preferred_element_type=F32
-        )
-
-
-def merge_kernel(kept, side, came, total_out, sent_out):
+    units = w.shape[1] // 2
+    for t in range(0, units, TILE):
+        columns = pl.ds(pl.multiple_of(core * units + t, 128), TILE)
+        kept_out[:, t : t + TILE] = jnp.dot(z[...], w[:, columns], preferred_element_type=F32)
+
+
+def merge_kernel(kept, side, came, *refs):
+    total_out, sent_out = refs[-2:]
     units = kept.shape[1]
     total = kept[...] + came[:, :units].astype(F32)
     total_out[...] = total
@@ -257,7 +282,8 @@
     sent_out[:, units:] = (side[...].astype(F32) + came[:, units:].astype(F32)).astype(BF16)
 
 
-def activate_kernel(k, features, table, total, sent, came, sums_own, sums_other, act_out):
+def activate_kernel(k, features, table, total, sent, came, factors, *refs):
+    act_out = refs[-1]
     units = total.shape[1]
     size = size_of(k)
     text = text_rows(k, layout(table)[4])
@@ -271,7 +297,7 @@
     totals = add(summed, used & ((field == 4) | (field == 5)))
     average = (centres * features + totals) / D
     spread = add(summed, used & ((field == 6) | (field == 7)))
-    factors = []
+    aparts = []
     for side in sides:
         apart = side - average
         for core in range(2):
@@ -280,44 +306,40 @@
             spread = spread + off * (
                 2.0 * add(side, own & ((field == 4) | (field == 5))) + features * off
             )
-        factors.append(apart)
+        aparts.append(apart)
     variance = spread / D
     scale = lax.rsqrt(variance + norm_eps)
     of_text = jnp.where(text, 1, 0)
     mine = used & ((field % 2) == of_text)
-    pre = total[...] + came[:, :units].astype(F32)
-    extra = jnp.zeros_like(pre)
-    for factor, sums in zip(factors, (sums_own, sums_other)):
+    packed, shift = None, 0
+    for apart in aparts:
         factor = jnp.where(
-            mine & (field < 2), factor * scale, jnp.where(mine & (field < 4), 1.0, 0.0)
-        )
-        extra = extra + jnp.dot(
-            factor[:, :16], sums[...], precision=lax.Precision.HIGHEST, preferred_element_type=F32
-        )
-    act_out[...] = jax.nn.gelu(pre * scale + extra, approximate=True).astype(BF16)
-
-
-def contract_own_kernel(act, w, out, buffer, sems):
+            mine & (field < 2), apart * scale, jnp.where(mine & (field < 4), 1.0, 0.0)
+        )
+        high = factor.astype(BF16).astype(F32)
+        for part in (high, high, factor - high):
+            part = pltpu.roll(part, shift, 1) if shift else part
+            packed = part if packed is None else packed + part
+            shift += 16
+    packed = packed.astype(BF16)
+    for t in range(0, units, TILE):
+        columns = slice(t, t + TILE)
+        pre = total[:, columns] + came[:, columns].astype(F32)
+        extra = jnp.dot(packed, factors[:, columns], preferred_element_type=F32)
+        act_out[:, columns] = jax.nn.gelu(pre * scale + extra, approximate=True).astype(BF16)
+
+
+def contract_own_kernel(act, w, out):
     core = lax.axis_index("narrow") % 2
-    tiles = sems.shape[0]
-    copies, width = fetch(w, core * buffer.shape[0], buffer, sems, tiles, 0)
-    total = None
-    for t in range(tiles):
-        copies[t].wait()
-        part = jnp.dot(
-            act[:, t * width : (t + 1) * width],
-            buffer[t * width : (t + 1) * width, :],
-            preferred_element_type=F32,
-        )
-        total = part if total is None else total + part
-    out[...] = total
-
-
-def contract_other_kernel(k, table, act, so_far, w, *refs):
-    outs, buffer, sems = refs[:4], refs[4], refs[5]
+    units = w.shape[0] // 2
+    rows = pl.ds(pl.multiple_of(core * units, 128), units)
+    out[...] = jnp.dot(act[...], w[rows, :], preferred_element_type=F32)
+
+
+def contract_other_kernel(k, table, act, so_far, w, *outs):
     core = lax.axis_index("narrow") % 2
-    tiles = sems.shape[0]
-    copies, width = fetch(w, (1 - core) * buffer.shape[0], buffer, sems, tiles, 0)
+    units = w.shape[0] // 2
+    rows = pl.ds(pl.multiple_of((1 - core) * units, 128), units)
     size = size_of(k)
     ranks, counts, others, _, _ = layout(table)
     places = []
@@ -329,14 +351,7 @@
         row = jnp.where(slot < last, slot + ranks[s] - QUOTAS[k] + others[s] * size, -1)
         at = lax.broadcasted_iota(jnp.int32, (size, 2 * size), 1)
         places.append(jnp.where(at == row, 1.0, 0.0).astype(BF16))
-    total = so_far[...]
-    for t in range(tiles):
-        copies[t].wait()
-        total = total + jnp.dot(
-            act[:, t * width : (t + 1) * width],
-            buffer[t * width : (t + 1) * width, :],
-            preferred_element_type=F32,
-        )
+    total = so_far[...] + jnp.dot(act[...], w[rows, :], preferred_element_type=F32)
     spread = jnp.dot(
         jnp.concatenate(places, 0), total.astype(BF16), preferred_element_type=F32
     ).astype(BF16)
@@ -362,35 +377,34 @@
     layer = jnp.where(live, hidden[...].astype(F32) + gate * result, 0.0).astype(BF16)
     layer_out[...] = layer
     x = layer.astype(F32)
-    total = jnp.sum(x, -1, keepdims=True)
-    square = jnp.sum(x * x, -1, keepdims=True)
-    centre = total / x.shape[1]
-    product = jnp.dot(
-        ((x - centre) * (1.0 + mod[7:8, :])).astype(BF16),
-        out_weight[...],
-        preferred_element_type=F32,
-    )
-    width = product.shape[1]
-    bundle_out[:CAP, :width] = product + centre * ends[0:1, :width]
-    lane = lax.broadcasted_iota(jnp.int32, (CAP, width), 1)
-    bundle_out[:CAP, width:] = jnp.where(lane == 0, total, jnp.where(lane == 1, square, 0.0))
-    bundle_out[CAP:, :] = ends[...]
-
-
-def velocity_kernel(first, second, third, fourth, out):
-    bundle = (first[...] + second[...]) + (third[...] + fourth[...])
-    width = bundle.shape[1] // 2
-    average = bundle[:CAP, width : width + 1] / D
-    variance = bundle[:CAP, width + 1 : width + 2] / D - average * average
-    velocity = (bundle[:CAP, :width] - average * bundle[CAP : CAP + 1, :width]) * lax.rsqrt(
+    centre = jnp.sum(x, -1, keepdims=True) / x.shape[1]
+    ones = jnp.ones((8, x.shape[1]), BF16)
+    across = lambda left, right: lax.dot_general(
+        left, right, (((1,), (1,)), ((), ())), preferred_element_type=F32
+    )
+    high, low = high_low(x * x)
+    total, square = across(ones, layer), across(ones, high) + across(ones, low)
+    width = out_weight.shape[0]
+    product = across(out_weight[...], ((x - centre) * (1.0 + mod[7:8, :])).astype(BF16))
+    bundle_out[:width, :] = product + total[0:1] / x.shape[1] * ends[:width, 12:13]
+    row = lax.broadcasted_iota(jnp.int32, (8, CAP), 0)
+    bundle_out[width:, :] = jnp.where(row == 0, total, square)
+
+
+def velocity_kernel(ends, first, second, third, fourth, out):
+    total = (first[...] + second[...]) + (third[...] + fourth[...])
+    width = out.shape[0]
+    average = total[width : width + 1] / D
+    variance = total[width + 1 : width + 2] / D - average * average
+    velocity = (total[:width] - average * ends[:width, 4:5]) * lax.rsqrt(
         variance + norm_eps
-    ) + bundle[CAP : CAP + 1, width:]
+    ) + ends[:width, 5:6]
     out[...] = velocity * jnp.where(lax.axis_index("cfg") == 0, guidance, 1.0 - guidance)
 
 
 def latent_kernel(table, timestep, alphas, latent, mine, other, out):
     _, counts, _, offset, _ = layout(table)
-    slot = lax.broadcasted_iota(jnp.int32, (CAP, 1), 0)
+    slot = lax.broadcasted_iota(jnp.int32, (1, CAP), 1)
     video = (slot < counts[0]) & (slot + offset >= TEXT)
     index = lax.broadcasted_iota(jnp.int32, (8, 128), 0) * 128 + lax.broadcasted_iota(
         jnp.int32, (8, 128), 1
@@ -410,7 +424,7 @@
     return np.pad(np.cumprod(1.0 - betas), (0, 24)).astype(np.float32).reshape(8, 128)
 
 
-def call(kernel, outs, args, spaces, scratch=(), flops=0, moved=0):
+def call(kernel, outs, args, spaces, scratch=(), weight=0):
     kinds = {"v": pltpu.VMEM, "s": pltpu.SMEM, "a": pl.ANY}
     return pl.pallas_call(
         kernel,
@@ -419,7 +433,7 @@
         out_specs=[pl.BlockSpec(memory_space=pltpu.VMEM) for _ in outs],
         scratch_shapes=list(scratch),
         compiler_params=pltpu.CompilerParams(vmem_limit_bytes=24 * 2**20),
-        cost_estimate=pl.CostEstimate(flops=flops, bytes_accessed=moved, transcendentals=0),
+        cost_estimate=pl.CostEstimate(flops=weight, bytes_accessed=1, transcendentals=0),
     )(*args)
 
 
@@ -430,112 +444,128 @@
     features = hidden.shape[1]
     units = expand_weight.shape[1] // 2
     width = output_weight.shape[1]
-    first_core = lax.axis_index("narrow") % 2 == 0
-
-    arrived = []
-    for k in range(CHUNKS):
-        piece = hidden[QUOTAS[k] : QUOTAS[k + 1]]
+    out_weight = output_weight.T
+
+    piece = hidden[: QUOTAS[1]]
+    arrived = [[piece] + z_swaps(piece)]
+
+    in_place = lambda weight: pltpu.with_memory_space_constraint(weight, pltpu.HBM)
+    *later, held_in, sums_mine, sums_sent = call(
+        prepare_kernel,
+        [((size_of(k), features), BF16) for k in range(1, CHUNKS)]
+        + [(expand_weight.shape, BF16)]
+        + [((8, units), F32)] * 2,
+        [hidden, modulation, out_weight, in_place(expand_weight)],
+        "vvva",
+        [pltpu.SemaphoreType.DMA((4,))],
+        WEIGHTS["prepare"],
+    )
+    (held_out,) = call(
+        hold_kernel,
+        [(contract_weight.shape, BF16)],
+        [in_place(contract_weight)],
+        "a",
+        [pltpu.SemaphoreType.DMA((4,))],
+        WEIGHTS["prepare"],
+    )
+    for piece in later:
         arrived.append([piece] + z_swaps(piece))
-
-    sums_mine, sums_sent, ends = call(
-        sums_kernel,
-        [((8, units), F32), ((8, units), F32), ((8, 2 * width), F32)],
-        [modulation, output_weight, expand_weight],
-        "vva",
-        [pltpu.VMEM(expand_weight.shape, BF16), pltpu.SemaphoreType.DMA((2,))],
-        2 * 16 * features * 2 * units,
-        2 * features * 2 * units,
-    )
-    sums_came = swap(sums_sent, "narrow", 1, 4)
-    sums_chip = jnp.where(
-        first_core,
-        jnp.concatenate([sums_mine, sums_came], 0),
-        jnp.concatenate([sums_came, sums_mine], 0),
-    )
-    sums_other = swap(sums_chip, "narrow", 2, 4)
-
-    tiles = 3
-    half_flops = lambda k: 2 * 2 * size_of(k) * features * units
-    half_bytes = 2 * features * units
-    expand_scratch = [pltpu.VMEM((features, units), BF16), pltpu.SemaphoreType.DMA((tiles,))]
-    contract_scratch = [pltpu.VMEM((units, features), BF16), pltpu.SemaphoreType.DMA((tiles,))]
-    returned = []
+    (sums_chip,) = call(
+        chip_kernel, [((16, units), F32)], [sums_mine, swap(sums_sent, "narrow", 1, 4)], "vv"
+    )
+    factors, ends = call(
+        factors_kernel,
+        [((128, units), BF16), ((128, 128), F32)],
+        [sums_mine, sums_chip, swap(sums_chip, "narrow", 2, 4)],
+        "vvv",
+    )
+
+    returned, merged = [], []
+    before, merge_before = [], [factors]
     for k in range(CHUNKS):
         rows = 2 * size_of(k)
         pieces = [piece for phase in arrived[: k + 1] for piece in phase]
         z, sent, side = call(
             functools.partial(expand_sent_kernel, k),
             [((rows, features), BF16), ((rows, units + 128), BF16), ((rows, 128), BF16)],
-            [split_table, modulation, *pieces, expand_weight],
-            "sv" + "v" * len(pieces) + "a",
-            expand_scratch,
-            half_flops(k),
-            half_bytes,
+            [split_table, modulation, *pieces, held_in, *before],
+            "sv" + "v" * len(pieces) + "v" + "a" * len(before),
+            (),
+            WEIGHTS["expand_sent"],
         )
         came = swap(sent, "narrow", 1, 4)
         (kept,) = call(
             expand_kept_kernel,
             [((rows, units), F32)],
-            [z, expand_weight],
-            "va",
-            expand_scratch,
-            half_flops(k),
-            half_bytes,
+            [z, held_in],
+            "vv",
+            (),
+            WEIGHTS["expand_kept"],
         )
         total, sent = call(
             merge_kernel,
             [((rows, units), F32), ((rows, units + 128), BF16)],
-            [kept, side, came],
-            "vvv",
-        )
-        came = swap(sent, "narrow", 2, 4)
+            [kept, side, came, *merge_before],
+            "vvv" + "a" * len(merge_before),
+            (),
+            WEIGHTS["merge"],
+        )
+        before, merge_before = [sent, held_out], []
+        merged.append((total, sent, swap(sent, "narrow", 2, 4)))
+    before = []
+    for k in range(CHUNKS):
+        rows = 2 * size_of(k)
+        total, sent, came = merged[k]
+        if k + 1 < CHUNKS:
+            before = before + [merged[k + 1][1]]
         (act,) = call(
             functools.partial(activate_kernel, k, features),
             [((rows, units), BF16)],
-            [split_table, total, sent, came, sums_chip, sums_other],
-            "svvvvv",
+            [split_table, total, sent, came, factors, *before],
+            "svvvv" + "a" * len(before),
+            (),
+            WEIGHTS["activate"],
         )
         act_came = swap(act, "narrow", 1, 4)
         (out,) = call(
             contract_own_kernel,
             [((rows, features), F32)],
-            [act, contract_weight],
-            "va",
-            contract_scratch,
-            half_flops(k),
-            half_bytes,
+            [act, held_out],
+            "vv",
+            (),
+            WEIGHTS["contract_own"],
         )
         pieces = call(
             functools.partial(contract_other_kernel, k),
             [((size_of(k), features), BF16)] * 4,
-            [split_table, act_came, out, contract_weight],
-            "svva",
-            contract_scratch,
-            half_flops(k),
-            half_bytes,
-        )
+            [split_table, act_came, out, held_out],
+            "svvv",
+            (),
+            WEIGHTS["contract_other"],
+        )
+        before = [pieces[0]]
         returned.append(pieces[0])
         returned.extend(swap(pieces[s], "wide", s, 4) for s in (1, 2, 3))
 
     layer_out, bundle = call(
         finish_kernel,
-        [((CAP, features), BF16), ((CAP + 8, 2 * width), F32)],
-        [split_table, hidden, modulation, output_weight, ends, *returned],
+        [((CAP, features), BF16), ((width + 8, CAP), F32)],
+        [split_table, hidden, modulation, out_weight, ends, *returned],
         "svvvv" + "v" * len(returned),
     )
     (velocity,) = call(
         velocity_kernel,
-        [((CAP, width), F32)],
-        [bundle] + [swap(bundle, "narrow", n, 4) for n in (1, 2, 3)],
-        "vvvv",
+        [((width, CAP), F32)],
+        [ends, bundle] + [swap(bundle, "narrow", n, 4) for n in (1, 2, 3)],
+        "vvvvv",
     )
     (clean_latent,) = call(
         latent_kernel,
-        [((CAP, width), F32)],
-        [split_table, timestep, alpha_constant(), latent, velocity, swap(velocity, "cfg", 1, 2)],
+        [((width, CAP), F32)],
+        [split_table, timestep, alpha_constant(), latent.T, velocity, swap(velocity, "cfg", 1, 2)],
         "ssvvvv",
     )
-    return (layer_out[None], clean_latent)
+    return (layer_out[None], clean_latent.T)
 
 
 def solution(mesh):

time: 108 us -> 75.5 us (0.70)
  waiting for transfers between devices: 37.8 us -> 23.3 us
  local copies, waits for them, and re-layouts: 17.4 us -> 3.5 us
  Pallas kernels: 21.4 us -> 18.9 us
    ppermute x24, waiting for transfers between devices: 37.8 us -> 23.3 us  [swap(): return lax.ppermute(array, axis, [(i, i ^ distance) for i in range(size)])]
    unnamed x39 -> x18, local copies, waits for them, and re-layouts: 16.4 us -> 2.59 us
    pallas_call x16 -> x19, Pallas kernels: 21.4 us -> 18.9 us  [call(): pl.pallas_call(kernel, out_shape=[jax.ShapeDtypeStruct(shape, dtype) for...]
  transfers between devices with their start and end apart: 24 -> 24, of which waited for: 9 -> 12; matrix products, arithmetic and copies ran while one was open for 1% -> 0% of each run, Pallas kernels for 16% -> 21%
where the time goes in v3:
time: 75.5 us; the launch traced here: 75.2 us
  starting transfers between devices  28 us (37%)
  waiting for transfers between devices  23.3 us (31%)
  Pallas kernels  18.9 us (25%)
  local copies, waits for them, and re-layouts  3.5 us (5%)
  between operations  1.52 us (2%)
    ppermute x24, starting transfers between devices, swap(): return lax.ppermute(array, axis, [(i, i ^ distance) for i in range(size)])  28 us
    ppermute x24, waiting for transfers between devices, swap(): return lax.ppermute(array, axis, [(i, i ^ distance) for i in range(size)])  23.3 us
    pallas_call x19, Pallas kernels, call(): pl.pallas_call(kernel, out_shape=[jax.ShapeDtypeStruct(shape, dtype) for...  18.9 us
    unnamed x18, local copies, waits for them, and re-layouts  2.59 us
  transfers between devices with their start and end apart: 24, of which 12 were waited for; matrix products, arithmetic and copies ran while one was open for 0% of the time, Pallas kernels for 21%

profile of v3, /device:TPU:0, one launch (start us, length us, event | category | flops | bytes accessed | tf_op | source)
XLA Modules:
  0.0 75.2 jit_solution(8666412964005975148)
XLA Ops:
  1.5 3.0 %collective-permute-start.2 = (bf16[64,768]{1,0:T(8,128)(2,1)S(1)}, bf16[64,768]{1,0:T(8,128)(2,1)S(1)}, u32[]{:S(2)}, u32[]{:S(2)}) collective-permute-start(bf16[64,768]{1,0:T(8,128)(2,1)S(1)} %slice_bitcast_fusion.refs_0_), channel_id=1, source_target_pairs={{0,4},{4,0},{8,12},{12,8},{1,5},{5,1},{9,13},{13,9},{2,6},{6,2},{1... | collective-permute-start | bytes 294920 | tf_op jit(solution)/shard_map/ppermute | solution.py:103
  4.6 2.6 %collective-permute-start.3 = (bf16[64,768]{1,0:T(8,128)(2,1)S(1)}, bf16[64,768]{1,0:T(8,128)(2,1)S(1)}, u32[]{:S(2)}, u32[]{:S(2)}) collective-permute-start(bf16[64,768]{1,0:T(8,128)(2,1)S(1)} %slice_bitcast_fusion.refs_0_), channel_id=1, source_target_pairs={{0,8},{4,12},{8,0},{12,4},{1,9},{5,13},{9,1},{13,5},{2,10},{6,14},... | collective-permute-start | bytes 294920 | tf_op jit(solution)/shard_map/ppermute | solution.py:103
  9.7 3.2 %shard_map.104 = (bf16[64,768]{1,0:T(8,128)(2,1)S(1)}, bf16[768,3072]{1,0:T(8,128)(2,1)S(1)}, f32[8,1536]{1,0:T(8,128)S(1)}, f32[8,1536]{1,0:T(8,128)S(1)}) custom-call(bf16[128,768]{1,0:T(8,128)(2,1)S(1)} %bitcast.7, f32[8,768]{1,0:T(8,128)S(1)} %copy-done.4, bf16[64,768]{1,0:T(8,128)(2,1)S(1)} %bitcast.9, bf16[768,3072]{1,0:T(8,128)(2,1)} %w.1), custom_call_target="tpu_custom_call" | custom-call | flops 1 | bytes 1 | tf_op jit(solution)/shard_map/pallas_call | solution.py:429
  14.0 2.4 %shard_map.110.refs_10_.w = bf16[3072,768]{1,0:T(8,128)(2,1)S(1)} custom-call(bf16[3072,768]{1,0:T(8,128)(2,1)} %source.1), custom_call_target="tpu_custom_call" | custom-call | flops 1 | bytes 1 | tf_op jit(solution)/shard_map/pallas_call | solution.py:429
  16.4 3.6 %collective-permute-start.8 = (bf16[64,768]{1,0:T(8,128)(2,1)S(1)}, bf16[64,768]{1,0:T(8,128)(2,1)S(1)}, u32[]{:S(2)}, u32[]{:S(2)}) collective-permute-start(bf16[64,768]{1,0:T(8,128)(2,1)S(1)} %get-tuple-element.38.refs_4_), channel_id=1, source_target_pairs={{0,8},{4,12},{8,0},{12,4},{1,9},{5,13},{9,1},{13,5},{2,10},{6,14},... | collective-permute-start | bytes 294920 | tf_op jit(solution)/shard_map/ppermute | solution.py:103
  20.1 1.7 %collective-permute-start.1 = (f32[16,1536]{1,0:T(8,128)S(1)}, f32[16,1536]{1,0:T(8,128)S(1)}, u32[]{:S(2)}, u32[]{:S(2)}) collective-permute-start(f32[16,1536]{1,0:T(8,128)S(1)} %shard_map.105.chip), channel_id=1, source_target_pairs={{0,2},{1,3},{2,0},{3,1},{4,6},{5,7},{6,4},{7,5},{8,10},{9,11},{10,... | collective-permute-start | bytes 294920 | tf_op jit(solution)/shard_map/ppermute | solution.py:103
  21.8 1.4 %shard_map.107 = (bf16[128,768]{1,0:T(8,128)(2,1)S(1)}, bf16[128,1664]{1,0:T(8,128)(2,1)S(1)}, bf16[128,128]{1,0:T(8,128)(2,1)S(1)}) custom-call(s32[4]{0:T(128)S(1)} %copy-done.7, f32[8,768]{1,0:T(8,128)S(1)} %copy-done.5, bf16[64,768]{1,0:T(8,128)(2,1)S(1)} %slice_bitcast_fusion.refs_0_, bf16[64,768]{1,0:T(8,128)(2,1)S(1)} %collective-permute-done.2.refs_1_, ...), custom_call_target="tpu_custom_call" | custom-call | flops 10000000000 | bytes 1 | tf_op jit(solution)/shard_map/pallas_call | solution.py:429
  25.1 1.6 %collective-permute-start.6 = (bf16[128,1664]{1,0:T(8,128)(2,1)S(1)}, bf16[128,1664]{1,0:T(8,128)(2,1)S(1)}, u32[]{:S(2)}, u32[]{:S(2)}) collective-permute-start(bf16[128,1664]{1,0:T(8,128)(2,1)S(1)} %get-tuple-element.37.refs_9_.sent), channel_id=1, source_target_pairs={{0,2},{1,3},{2,0},{3,1},{4,6},{5,7},{6,4},{7,5},{8,10},{9,11},{10,... | collective-permute-start | bytes 1277960 | tf_op jit(solution)/shard_map/ppermute | solution.py:103
  27.0 1.4 %shard_map.111 = (bf16[128,768]{1,0:T(8,128)(2,1)S(1)}, bf16[128,1664]{1,0:T(8,128)(2,1)S(1)}, bf16[128,128]{1,0:T(8,128)(2,1)S(1)}) custom-call(s32[4]{0:T(128)S(1)} %copy-done.7, f32[8,768]{1,0:T(8,128)S(1)} %copy-done.5, bf16[64,768]{1,0:T(8,128)(2,1)S(1)} %slice_bitcast_fusion.refs_0_, bf16[64,768]{1,0:T(8,128)(2,1)S(1)} %collective-permute-done.2.refs_1_, ...), custom_call_target="tpu_custom_call" | custom-call | flops 10000000000 | bytes 1 | tf_op jit(solution)/shard_map/pallas_call | solution.py:429
  30.4 1.8 %collective-permute-start.15 = (bf16[128,1664]{1,0:T(8,128)(2,1)S(1)}, bf16[128,1664]{1,0:T(8,128)(2,1)S(1)}, u32[]{:S(2)}, u32[]{:S(2)}) collective-permute-start(bf16[128,1664]{1,0:T(8,128)(2,1)S(1)} %get-tuple-element.42.refs_0_.sent), channel_id=1, source_target_pairs={{0,2},{1,3},{2,0},{3,1},{4,6},{5,7},{6,4},{7,5},{8,10},{9,11},{10,... | collective-permute-start | bytes 1277960 | tf_op jit(solution)/shard_map/ppermute | solution.py:103
  32.2 5.7 %collective-permute-done.6.came = bf16[128,1664]{1,0:T(8,128)(2,1)S(1)} collective-permute-done((bf16[128,1664]{1,0:T(8,128)(2,1)S(1)}, bf16[128,1664]{1,0:T(8,128)(2,1)S(1)}, u32[]{:S(2)}, u32[]{:S(2)}) %collective-permute-start.6) | collective-permute-done | bytes 426016 | tf_op jit(solution)/shard_map/ppermute | solution.py:103
  37.9 1.3 %shard_map.114.act = bf16[128,1536]{1,0:T(8,128)(2,1)S(1)} custom-call(s32[4]{0:T(128)S(1)} %copy-done.7, f32[128,1536]{1,0:T(8,128)S(1)} %get-tuple-element.36.total, bf16[128,1664]{1,0:T(8,128)(2,1)S(1)} %get-tuple-element.37.refs_9_.sent, bf16[128,1664]{1,0:T(8,128)(2,1)S(1)} %collective-permute-done.6.came, ...), custom_call_target="tpu_custom_call" | custom-call | flops 1 | bytes 1 | tf_op jit(solution)/shard_map/pallas_call | solution.py:429
  40.9 1.3 %shard_map.116 = (bf16[64,768]{1,0:T(8,128)(2,1)S(1)}, bf16[64,768]{1,0:T(8,128)(2,1)S(1)}, bf16[64,768]{1,0:T(8,128)(2,1)S(1)}, bf16[64,768]{1,0:T(8,128)(2,1)S(1)}) custom-call(s32[4]{0:T(128)S(1)} %copy-done.7, bf16[128,1536]{1,0:T(8,128)(2,1)S(1)} %collective-permute-done.11.act, f32[128,768]{1,0:T(8,128)S(1)} %shard_map.115.so_far, ...), custom_call_target="tpu_custom_call" | custom-call | flops 1 | bytes 1 | tf_op jit(solution)/shard_map/pallas_call | solution.py:429
  42.7 3.8 %collective-permute-start.13 = (bf16[64,768]{1,0:T(8,128)(2,1)S(1)}, bf16[64,768]{1,0:T(8,128)(2,1)S(1)}, u32[]{:S(2)}, u32[]{:S(2)}) collective-permute-start(bf16[64,768]{1,0:T(8,128)(2,1)S(1)} %get-tuple-element.45), channel_id=1, source_target_pairs={{0,8},{4,12},{8,0},{12,4},{1,9},{5,13},{9,1},{13,5},{2,10},{6,14},... | collective-permute-start | bytes 294920 | tf_op jit(solution)/shard_map/ppermute | solution.py:103
  46.7 1.3 %shard_map.117.act = bf16[128,1536]{1,0:T(8,128)(2,1)S(1)} custom-call(s32[4]{0:T(128)S(1)} %copy-done.7, f32[128,1536]{1,0:T(8,128)S(1)} %get-tuple-element.47.total, bf16[128,1664]{1,0:T(8,128)(2,1)S(1)} %get-tuple-element.42.refs_0_.sent, bf16[128,1664]{1,0:T(8,128)(2,1)S(1)} %collective-permute-done.15.came, ...), custom_call_target="tpu_custom_call" | custom-call | flops 1 | bytes 1 | tf_op jit(solution)/shard_map/pallas_call | solution.py:429
  49.8 1.3 %shard_map.119 = (bf16[64,768]{1,0:T(8,128)(2,1)S(1)}, bf16[64,768]{1,0:T(8,128)(2,1)S(1)}, bf16[64,768]{1,0:T(8,128)(2,1)S(1)}, bf16[64,768]{1,0:T(8,128)(2,1)S(1)}) custom-call(s32[4]{0:T(128)S(1)} %copy-done.7, bf16[128,1536]{1,0:T(8,128)(2,1)S(1)} %collective-permute-done.16.act, f32[128,768]{1,0:T(8,128)S(1)} %shard_map.118.so_far, ...), custom_call_target="tpu_custom_call" | custom-call | flops 1 | bytes 1 | tf_op jit(solution)/shard_map/pallas_call | solution.py:429
  51.6 3.8 %collective-permute-start.18 = (bf16[64,768]{1,0:T(8,128)(2,1)S(1)}, bf16[64,768]{1,0:T(8,128)(2,1)S(1)}, u32[]{:S(2)}, u32[]{:S(2)}) collective-permute-start(bf16[64,768]{1,0:T(8,128)(2,1)S(1)} %get-tuple-element.50), channel_id=1, source_target_pairs={{0,8},{4,12},{8,0},{12,4},{1,9},{5,13},{9,1},{13,5},{2,10},{6,14},... | collective-permute-start | bytes 294920 | tf_op jit(solution)/shard_map/ppermute | solution.py:103
  55.6 2.0 %collective-permute-done.17.refs_5_ = bf16[64,768]{1,0:T(8,128)(2,1)S(1)} collective-permute-done((bf16[64,768]{1,0:T(8,128)(2,1)S(1)}, bf16[64,768]{1,0:T(8,128)(2,1)S(1)}, u32[]{:S(2)}, u32[]{:S(2)}) %collective-permute-start.17) | collective-permute-done | bytes 98336 | tf_op jit(solution)/shard_map/ppermute | solution.py:103
  57.6 5.7 %collective-permute-done.18.refs_6_ = bf16[64,768]{1,0:T(8,128)(2,1)S(1)} collective-permute-done((bf16[64,768]{1,0:T(8,128)(2,1)S(1)}, bf16[64,768]{1,0:T(8,128)(2,1)S(1)}, u32[]{:S(2)}, u32[]{:S(2)}) %collective-permute-start.18) | collective-permute-done | bytes 98336 | tf_op jit(solution)/shard_map/ppermute | solution.py:103
  63.3 1.5 %shard_map.120 = (bf16[128,768]{1,0:T(8,128)(2,1)}, f32[72,128]{1,0:T(8,128)S(1)}) custom-call(s32[4]{0:T(128)S(1)} %copy-done.7, bf16[128,768]{1,0:T(8,128)(2,1)S(1)} %bitcast.8, f32[8,768]{1,0:T(8,128)S(1)} %copy-done.5, bf16[64,768]{1,0:T(8,128)(2,1)S(1)} %bitcast.10, f32[128,128]{1,0:T(8,128)S(1)} %get-tuple-element.30.ends, ...), custom_call_target="tpu_custom_call" | custom-call | bytes 1 | tf_op jit(solution)/shard_map/pallas_call | solution.py:429
  64.8 1.6 %collective-permute-start.21 = (f32[72,128]{1,0:T(8,128)S(1)}, f32[72,128]{1,0:T(8,128)S(1)}, u32[]{:S(2)}, u32[]{:S(2)}) collective-permute-start(f32[72,128]{1,0:T(8,128)S(1)} %get-tuple-element.53.first), channel_id=1, source_target_pairs={{0,2},{1,3},{2,0},{3,1},{4,6},{5,7},{6,4},{7,5},{8,10},{9,11},{10,... | collective-permute-start | bytes 110600 | tf_op jit(solution)/shard_map/ppermute | solution.py:103
  66.7 2.1 %collective-permute-done.21.third = f32[72,128]{1,0:T(8,128)S(1)} collective-permute-done((f32[72,128]{1,0:T(8,128)S(1)}, f32[72,128]{1,0:T(8,128)S(1)}, u32[]{:S(2)}, u32[]{:S(2)}) %collective-permute-start.21) | collective-permute-done | bytes 36896 | tf_op jit(solution)/shard_map/ppermute | solution.py:103
  69.9 1.6 %collective-permute-start.23 = (f32[64,128]{1,0:T(8,128)S(1)}, f32[64,128]{1,0:T(8,128)S(1)}, u32[]{:S(2)}, u32[]{:S(2)}) collective-permute-start(f32[64,128]{1,0:T(8,128)S(1)} %shard_map.121.mine), channel_id=1, source_target_pairs={{0,16},{16,0},{1,17},{17,1},{2,18},{18,2},{3,19},{19,3},{4,20},{20... | collective-permute-start | bytes 98312 | tf_op jit(solution)/shard_map/ppermute | solution.py:103
  72.1 1.8 %collective-permute-done.23.other = f32[64,128]{1,0:T(8,128)S(1)} collective-permute-done((f32[64,128]{1,0:T(8,128)S(1)}, f32[64,128]{1,0:T(8,128)S(1)}, u32[]{:S(2)}, u32[]{:S(2)}) %collective-permute-start.23) | collective-permute-done | bytes 32800 | tf_op jit(solution)/shard_map/ppermute | solution.py:103
  (62 shorter events, 16.3 us)
Async XLA Ops:
  1.5 18.4 %collective-permute-start.2 = (bf16[64,768]{1,0:T(8,128)(2,1)S(1)}, bf16[64,768]{1,0:T(8,128)(2,1)S(1)}, u32[]{:S(2)}, u32[]{:S(2)}) collective-permute-start(bf16[64,768]{1,0:T(8,128)(2,1)S(1)} %slice_bitcast_fusion.refs_0_), channel_id=1, source_target_pairs={{0,4},{4,0},{8,12},{12,8},{1,5},{5,1},{9,13},{13,9},{2,6},{6,2},{1... | collective-permute-start | bytes 294920 | tf_op jit(solution)/shard_map/ppermute | solution.py:103
  4.6 15.5 %collective-permute-start.3 = (bf16[64,768]{1,0:T(8,128)(2,1)S(1)}, bf16[64,768]{1,0:T(8,128)(2,1)S(1)}, u32[]{:S(2)}, u32[]{:S(2)}) collective-permute-start(bf16[64,768]{1,0:T(8,128)(2,1)S(1)} %slice_bitcast_fusion.refs_0_), channel_id=1, source_target_pairs={{0,8},{4,12},{8,0},{12,4},{1,9},{5,13},{9,1},{13,5},{2,10},{6,14},... | collective-permute-start | bytes 294920 | tf_op jit(solution)/shard_map/ppermute | solution.py:103
  7.1 14.6 %collective-permute-start.4 = (bf16[64,768]{1,0:T(8,128)(2,1)S(1)}, bf16[64,768]{1,0:T(8,128)(2,1)S(1)}, u32[]{:S(2)}, u32[]{:S(2)}) collective-permute-start(bf16[64,768]{1,0:T(8,128)(2,1)S(1)} %slice_bitcast_fusion.refs_0_), channel_id=1, source_target_pairs={{0,12},{4,8},{8,4},{12,0},{1,13},{5,9},{9,5},{13,1},{2,14},{6,10},... | collective-permute-start | bytes 294920 | tf_op jit(solution)/shard_map/ppermute | solution.py:103
  12.9 3.4 %collective-permute-start = (f32[8,1536]{1,0:T(8,128)S(1)}, f32[8,1536]{1,0:T(8,128)S(1)}, u32[]{:S(2)}, u32[]{:S(2)}) collective-permute-start(f32[8,1536]{1,0:T(8,128)S(1)} %get-tuple-element.29), channel_id=1, source_target_pairs={{0,1},{1,0},{2,3},{3,2},{4,5},{5,4},{6,7},{7,6},{8,9},{9,8},{10,11... | collective-permute-start | bytes 147464 | tf_op jit(solution)/shard_map/ppermute | solution.py:103
  13.1 13.7 %collective-permute-start.7 = (bf16[64,768]{1,0:T(8,128)(2,1)S(1)}, bf16[64,768]{1,0:T(8,128)(2,1)S(1)}, u32[]{:S(2)}, u32[]{:S(2)}) collective-permute-start(bf16[64,768]{1,0:T(8,128)(2,1)S(1)} %get-tuple-element.38.refs_4_), channel_id=1, source_target_pairs={{0,4},{4,0},{8,12},{12,8},{1,5},{5,1},{9,13},{13,9},{2,6},{6,2},{1... | collective-permute-start | bytes 294920 | tf_op jit(solution)/shard_map/ppermute | solution.py:103
  16.4 10.6 %collective-permute-start.8 = (bf16[64,768]{1,0:T(8,128)(2,1)S(1)}, bf16[64,768]{1,0:T(8,128)(2,1)S(1)}, u32[]{:S(2)}, u32[]{:S(2)}) collective-permute-start(bf16[64,768]{1,0:T(8,128)(2,1)S(1)} %get-tuple-element.38.refs_4_), channel_id=1, source_target_pairs={{0,8},{4,12},{8,0},{12,4},{1,9},{5,13},{9,1},{13,5},{2,10},{6,14},... | collective-permute-start | bytes 294920 | tf_op jit(solution)/shard_map/ppermute | solution.py:103
  20.0 7.1 %collective-permute-start.9 = (bf16[64,768]{1,0:T(8,128)(2,1)S(1)}, bf16[64,768]{1,0:T(8,128)(2,1)S(1)}, u32[]{:S(2)}, u32[]{:S(2)}) collective-permute-start(bf16[64,768]{1,0:T(8,128)(2,1)S(1)} %get-tuple-element.38.refs_4_), channel_id=1, source_target_pairs={{0,12},{4,8},{8,4},{12,0},{1,13},{5,9},{9,5},{13,1},{2,14},{6,10},... | collective-permute-start | bytes 294920 | tf_op jit(solution)/shard_map/ppermute | solution.py:103
  20.1 4.7 %collective-permute-start.1 = (f32[16,1536]{1,0:T(8,128)S(1)}, f32[16,1536]{1,0:T(8,128)S(1)}, u32[]{:S(2)}, u32[]{:S(2)}) collective-permute-start(f32[16,1536]{1,0:T(8,128)S(1)} %shard_map.105.chip), channel_id=1, source_target_pairs={{0,2},{1,3},{2,0},{3,1},{4,6},{5,7},{6,4},{7,5},{8,10},{9,11},{10,... | collective-permute-start | bytes 294920 | tf_op jit(solution)/shard_map/ppermute | solution.py:103
  23.2 1.8 %collective-permute-start.5 = (bf16[128,1664]{1,0:T(8,128)(2,1)S(1)}, bf16[128,1664]{1,0:T(8,128)(2,1)S(1)}, u32[]{:S(2)}, u32[]{:S(2)}) collective-permute-start(bf16[128,1664]{1,0:T(8,128)(2,1)S(1)} %get-tuple-element.34), channel_id=1, source_target_pairs={{0,1},{1,0},{2,3},{3,2},{4,5},{5,4},{6,7},{7,6},{8,9},{9,8},{10,11... | collective-permute-start | bytes 1277960 | tf_op jit(solution)/shard_map/ppermute | solution.py:103
  25.1 12.7 %collective-permute-start.6 = (bf16[128,1664]{1,0:T(8,128)(2,1)S(1)}, bf16[128,1664]{1,0:T(8,128)(2,1)S(1)}, u32[]{:S(2)}, u32[]{:S(2)}) collective-permute-start(bf16[128,1664]{1,0:T(8,128)(2,1)S(1)} %get-tuple-element.37.refs_9_.sent), channel_id=1, source_target_pairs={{0,2},{1,3},{2,0},{3,1},{4,6},{5,7},{6,4},{7,5},{8,10},{9,11},{10,... | collective-permute-start | bytes 1277960 | tf_op jit(solution)/shard_map/ppermute | solution.py:103
  28.4 1.8 %collective-permute-start.10 = (bf16[128,1664]{1,0:T(8,128)(2,1)S(1)}, bf16[128,1664]{1,0:T(8,128)(2,1)S(1)}, u32[]{:S(2)}, u32[]{:S(2)}) collective-permute-start(bf16[128,1664]{1,0:T(8,128)(2,1)S(1)} %get-tuple-element.41), channel_id=1, source_target_pairs={{0,1},{1,0},{2,3},{3,2},{4,5},{5,4},{6,7},{7,6},{8,9},{9,8},{10,11... | collective-permute-start | bytes 1277960 | tf_op jit(solution)/shard_map/ppermute | solution.py:103
  30.4 16.3 %collective-permute-start.15 = (bf16[128,1664]{1,0:T(8,128)(2,1)S(1)}, bf16[128,1664]{1,0:T(8,128)(2,1)S(1)}, u32[]{:S(2)}, u32[]{:S(2)}) collective-permute-start(bf16[128,1664]{1,0:T(8,128)(2,1)S(1)} %get-tuple-element.42.refs_0_.sent), channel_id=1, source_target_pairs={{0,2},{1,3},{2,0},{3,1},{4,6},{5,7},{6,4},{7,5},{8,10},{9,11},{10,... | collective-permute-start | bytes 1277960 | tf_op jit(solution)/shard_map/ppermute | solution.py:103
  39.2 1.8 %collective-permute-start.11 = (bf16[128,1536]{1,0:T(8,128)(2,1)S(1)}, bf16[128,1536]{1,0:T(8,128)(2,1)S(1)}, u32[]{:S(2)}, u32[]{:S(2)}) collective-permute-start(bf16[128,1536]{1,0:T(8,128)(2,1)S(1)} %shard_map.114.act), channel_id=1, source_target_pairs={{0,1},{1,0},{2,3},{3,2},{4,5},{5,4},{6,7},{7,6},{8,9},{9,8},{10,11... | collective-permute-start | bytes 1179656 | tf_op jit(solution)/shard_map/ppermute | solution.py:103
  42.3 13.1 %collective-permute-start.12 = (bf16[64,768]{1,0:T(8,128)(2,1)S(1)}, bf16[64,768]{1,0:T(8,128)(2,1)S(1)}, u32[]{:S(2)}, u32[]{:S(2)}) collective-permute-start(bf16[64,768]{1,0:T(8,128)(2,1)S(1)} %get-tuple-element.44), channel_id=1, source_target_pairs={{0,4},{4,0},{8,12},{12,8},{1,5},{5,1},{9,13},{13,9},{2,6},{6,2},{1... | collective-permute-start | bytes 294920 | tf_op jit(solution)/shard_map/ppermute | solution.py:103
  42.7 12.9 %collective-permute-start.13 = (bf16[64,768]{1,0:T(8,128)(2,1)S(1)}, bf16[64,768]{1,0:T(8,128)(2,1)S(1)}, u32[]{:S(2)}, u32[]{:S(2)}) collective-permute-start(bf16[64,768]{1,0:T(8,128)(2,1)S(1)} %get-tuple-element.45), channel_id=1, source_target_pairs={{0,8},{4,12},{8,0},{12,4},{1,9},{5,13},{9,1},{13,5},{2,10},{6,14},... | collective-permute-start | bytes 294920 | tf_op jit(solution)/shard_map/ppermute | solution.py:103
  46.5 9.1 %collective-permute-start.14 = (bf16[64,768]{1,0:T(8,128)(2,1)S(1)}, bf16[64,768]{1,0:T(8,128)(2,1)S(1)}, u32[]{:S(2)}, u32[]{:S(2)}) collective-permute-start(bf16[64,768]{1,0:T(8,128)(2,1)S(1)} %get-tuple-element.46), channel_id=1, source_target_pairs={{0,12},{4,8},{8,4},{12,0},{1,13},{5,9},{9,5},{13,1},{2,14},{6,10},... | collective-permute-start | bytes 294920 | tf_op jit(solution)/shard_map/ppermute | solution.py:103
  48.0 1.8 %collective-permute-start.16 = (bf16[128,1536]{1,0:T(8,128)(2,1)S(1)}, bf16[128,1536]{1,0:T(8,128)(2,1)S(1)}, u32[]{:S(2)}, u32[]{:S(2)}) collective-permute-start(bf16[128,1536]{1,0:T(8,128)(2,1)S(1)} %shard_map.117.act), channel_id=1, source_target_pairs={{0,1},{1,0},{2,3},{3,2},{4,5},{5,4},{6,7},{7,6},{8,9},{9,8},{10,11... | collective-permute-start | bytes 1179656 | tf_op jit(solution)/shard_map/ppermute | solution.py:103
  51.2 6.4 %collective-permute-start.17 = (bf16[64,768]{1,0:T(8,128)(2,1)S(1)}, bf16[64,768]{1,0:T(8,128)(2,1)S(1)}, u32[]{:S(2)}, u32[]{:S(2)}) collective-permute-start(bf16[64,768]{1,0:T(8,128)(2,1)S(1)} %get-tuple-element.49), channel_id=1, source_target_pairs={{0,4},{4,0},{8,12},{12,8},{1,5},{5,1},{9,13},{13,9},{2,6},{6,2},{1... | collective-permute-start | bytes 294920 | tf_op jit(solution)/shard_map/ppermute | solution.py:103
  51.6 11.7 %collective-permute-start.18 = (bf16[64,768]{1,0:T(8,128)(2,1)S(1)}, bf16[64,768]{1,0:T(8,128)(2,1)S(1)}, u32[]{:S(2)}, u32[]{:S(2)}) collective-permute-start(bf16[64,768]{1,0:T(8,128)(2,1)S(1)} %get-tuple-element.50), channel_id=1, source_target_pairs={{0,8},{4,12},{8,0},{12,4},{1,9},{5,13},{9,1},{13,5},{2,10},{6,14},... | collective-permute-start | bytes 294920 | tf_op jit(solution)/shard_map/ppermute | solution.py:103
  55.4 7.9 %collective-permute-start.19 = (bf16[64,768]{1,0:T(8,128)(2,1)S(1)}, bf16[64,768]{1,0:T(8,128)(2,1)S(1)}, u32[]{:S(2)}, u32[]{:S(2)}) collective-permute-start(bf16[64,768]{1,0:T(8,128)(2,1)S(1)} %get-tuple-element.51), channel_id=1, source_target_pairs={{0,12},{4,8},{8,4},{12,0},{1,13},{5,9},{9,5},{13,1},{2,14},{6,10},... | collective-permute-start | bytes 294920 | tf_op jit(solution)/shard_map/ppermute | solution.py:103
  64.8 1.9 %collective-permute-start.20 = (f32[72,128]{1,0:T(8,128)S(1)}, f32[72,128]{1,0:T(8,128)S(1)}, u32[]{:S(2)}, u32[]{:S(2)}) collective-permute-start(f32[72,128]{1,0:T(8,128)S(1)} %get-tuple-element.53.first), channel_id=1, source_target_pairs={{0,1},{1,0},{2,3},{3,2},{4,5},{5,4},{6,7},{7,6},{8,9},{9,8},{10,11... | collective-permute-start | bytes 110600 | tf_op jit(solution)/shard_map/ppermute | solution.py:103
  64.8 4.0 %collective-permute-start.21 = (f32[72,128]{1,0:T(8,128)S(1)}, f32[72,128]{1,0:T(8,128)S(1)}, u32[]{:S(2)}, u32[]{:S(2)}) collective-permute-start(f32[72,128]{1,0:T(8,128)S(1)} %get-tuple-element.53.first), channel_id=1, source_target_pairs={{0,2},{1,3},{2,0},{3,1},{4,6},{5,7},{6,4},{7,5},{8,10},{9,11},{10,... | collective-permute-start | bytes 110600 | tf_op jit(solution)/shard_map/ppermute | solution.py:103
  66.5 3.4 %collective-permute-start.22 = (f32[72,128]{1,0:T(8,128)S(1)}, f32[72,128]{1,0:T(8,128)S(1)}, u32[]{:S(2)}, u32[]{:S(2)}) collective-permute-start(f32[72,128]{1,0:T(8,128)S(1)} %get-tuple-element.53.first), channel_id=1, source_target_pairs={{0,3},{1,2},{2,1},{3,0},{4,7},{5,6},{6,5},{7,4},{8,11},{9,10},{10,... | collective-permute-start | bytes 110600 | tf_op jit(solution)/shard_map/ppermute | solution.py:103
  69.9 4.0 %collective-permute-start.23 = (f32[64,128]{1,0:T(8,128)S(1)}, f32[64,128]{1,0:T(8,128)S(1)}, u32[]{:S(2)}, u32[]{:S(2)}) collective-permute-start(f32[64,128]{1,0:T(8,128)S(1)} %shard_map.121.mine), channel_id=1, source_target_pairs={{0,16},{16,0},{1,17},{17,1},{2,18},{18,2},{3,19},{19,3},{4,20},{20... | collective-permute-start | bytes 98312 | tf_op jit(solution)/shard_map/ppermute | solution.py:103
  (9 other events, 100.0 us)

commit v4 on v0

--- a/solution.py
+++ b/solution.py
@@ -1,6 +1,11 @@
+import functools
+
 import jax
 import jax.numpy as jnp
+import numpy as np
 from jax import lax
+from jax.experimental import pallas as pl
+from jax.experimental.pallas import tpu as pltpu
 from jax.sharding import PartitionSpec as P
 
 D = 3072
@@ -28,7 +33,7 @@
     return (values - average) * lax.rsqrt(variance + norm_eps) * (1.0 + scaling) + shifts
 
 
-def on_device(
+def any_slice(
     hidden, split_table, modulation, expand_weight, contract_weight, output_weight, latent, timestep
 ):
     capacity = hidden.shape[1]
@@ -74,9 +79,537 @@
     return (layer_out[None], clean_latent)
 
 
+QUOTAS = (0, 64, 128)
+CAP = 128
+CHUNKS = len(QUOTAS) - 1
+F32, BF16 = jnp.float32, jnp.bfloat16
+TILE = 512
+LONG = 10**10
+
+
+def size_of(k):
+    return QUOTAS[k + 1] - QUOTAS[k]
+
+
+def swap(array, axis, distance, size):
+    return lax.ppermute(array, axis, [(i, i ^ distance) for i in range(size)])
+
+
+def z_swaps(array):
+    return [swap(array, "wide", s, 4) for s in (1, 2, 3)]
+
+
+def choose(values, index):
+    out = values[0]
+    for i in range(1, 4):
+        out = jnp.where(index == i, values[i], out)
+    return out
+
+
+def layout(table):
+    counts = [table[b] for b in range(4)]
+    largest = jnp.int32(3)
+    for b in (2, 1, 0):
+        largest = jnp.where(counts[b] == CAP, b, largest)
+    starts, others, ranks, offsets = [], [], [], []
+    rank, offset = jnp.int32(0), jnp.int32(0)
+    for b in range(4):
+        other = jnp.where(largest == b, 0, 1)
+        ranks.append(rank * other)
+        others.append(other)
+        offsets.append(offset)
+        rank = rank + other * counts[b]
+        offset = offset + counts[b]
+    block = lax.axis_index("wide")
+    of = lambda values: [choose(values, jnp.bitwise_xor(block, s)) for s in range(4)]
+    return of(ranks), of(counts), of(others), of(offsets)[0], choose(offsets, largest)
+
+
+def high_low(values):
+    high = values.astype(BF16)
+    return high, (values - high.astype(F32)).astype(BF16)
+
+
+def load(source, place, sems):
+    parts = sems.shape[0]
+    height = source.shape[0] // parts
+    copies = []
+    for t in range(parts):
+        rows = pl.ds(t * height, height)
+        copies.append(pltpu.make_async_copy(source.at[rows, :], place.at[rows, :], sems.at[t]))
+        copies[-1].start()
+    return copies
+
+
+def hold_kernel(source, _, place, sems):
+    for copy in load(source, place, sems):
+        copy.wait()
+
+
+def text_rows(k, largest_offset):
+    size = size_of(k)
+    row = lax.broadcasted_iota(jnp.int32, (2 * size, 1), 0)
+    rank = jnp.where(row < size, row, row - size) + QUOTAS[k]
+    position = jnp.where(
+        row < size, rank + largest_offset, jnp.where(rank < largest_offset, rank, rank + CAP)
+    )
+    return position < TEXT
+
+
+def gather_matrix(k, ranks, counts, others):
+    size = size_of(k)
+    places = []
+    for p in range(k + 1):
+        piece = size_of(p)
+        lane = lax.broadcasted_iota(jnp.int32, (1, 4 * piece), 1)
+        which, slot = lane // piece, lane % piece + QUOTAS[p]
+        rank = slot + choose(ranks, which) - QUOTAS[k]
+        live = (rank >= 0) & (rank < size) & (slot < choose(counts, which))
+        row = jnp.where(live, rank + choose(others, which) * size, -1)
+        at = lax.broadcasted_iota(jnp.int32, (2 * size, 4 * piece), 0)
+        places.append(jnp.where(at == row, 1.0, 0.0).astype(BF16))
+    return jnp.concatenate(places, 1)
+
+
+def spread_matrix(k, ranks, counts, others):
+    size = size_of(k)
+    places = []
+    for s in range(4):
+        first = jnp.maximum(QUOTAS[k] - ranks[s], 0)
+        last = jnp.minimum(counts[s], QUOTAS[k + 1] - ranks[s])
+        index = lax.broadcasted_iota(jnp.int32, (size, 1), 0)
+        slot = first + jnp.bitwise_and(index - first, size - 1)
+        row = jnp.where(slot < last, slot + ranks[s] - QUOTAS[k] + others[s] * size, -1)
+        at = lax.broadcasted_iota(jnp.int32, (size, 2 * size), 1)
+        places.append(jnp.where(at == row, 1.0, 0.0).astype(BF16))
+    return jnp.concatenate(places, 0)
+
+
+def prepare_kernel(table, hidden, mod_in, out_weight, w, *refs):
+    later, refs = refs[: CHUNKS - 1], refs[CHUNKS - 1 :]
+    gathers, refs = refs[:CHUNKS], refs[CHUNKS:]
+    spreads, refs = refs[:CHUNKS], refs[CHUNKS:]
+    texts, refs = refs[:CHUNKS], refs[CHUNKS:]
+    held, tokens, mod, weight, mine_out, sent_out, slots_out, video_out, sems, small = refs
+    core = lax.axis_index("narrow") % 2
+    units = w.shape[1] // 2
+    copies = [
+        pltpu.make_async_copy(source, place, small.at[i])
+        for i, (source, place) in enumerate(((mod_in, mod), (out_weight, weight), (hidden, tokens)))
+    ]
+    for copy in copies:
+        copy.start()
+    big = load(w, held, sems)
+
+    ranks, counts, others, offset, largest_offset = layout(table)
+    for k in range(CHUNKS):
+        gathers[k][...] = gather_matrix(k, ranks, counts, others)
+        spreads[k][...] = spread_matrix(k, ranks, counts, others)
+        text = jnp.where(text_rows(k, largest_offset), 1.0, 0.0)
+        texts[k][...] = jnp.broadcast_to(text, texts[k].shape)
+    slot = lax.broadcasted_iota(jnp.int32, (CAP, 128), 0)
+    lane = lax.broadcasted_iota(jnp.int32, (CAP, 128), 1)
+    rank = slot + ranks[0]
+    flag = lambda condition: jnp.where(condition, 1.0, 0.0)
+    kind = jnp.where(lane == 0, flag(slot < counts[0]), flag(slot + offset < TEXT))
+    for k in range(CHUNKS):
+        kind = jnp.where(
+            lane == 2 + k, flag((rank >= QUOTAS[k]) & (rank < QUOTAS[k + 1])), kind
+        )
+    slots_out[...] = kind
+    slot = lax.broadcasted_iota(jnp.int32, (8, CAP), 1)
+    video_out[...] = jnp.where((slot < counts[0]) & (slot + offset >= TEXT), 1.0, 0.0)
+
+    for copy in copies:
+        copy.wait()
+    for k in range(1, CHUNKS):
+        later[k - 1][...] = tokens[QUOTAS[k] : QUOTAS[k + 1], :]
+    row = lax.broadcasted_iota(jnp.int32, (8, 1), 0)
+    rows = jnp.where(row == 0, 1.0 + mod[1:2, :], jnp.zeros((8, 1), F32))
+    rows = jnp.where(row == 1, 1.0 + mod[4:5, :], rows)
+    rows = jnp.where(row == 2, mod[0:1, :], rows)
+    rows = jnp.where(row == 3, mod[3:4, :], rows)
+    both = jnp.concatenate(high_low(rows), 0)
+    rows = jnp.where(row == 0, 1.0 + mod[7:8, :], jnp.zeros((8, 1), F32))
+    rows = jnp.where(row == 1, mod[6:7, :], rows)
+    ends = lax.dot_general(
+        jnp.concatenate(high_low(rows), 0),
+        weight[...],
+        (((1,), (1,)), ((), ())),
+        preferred_element_type=F32,
+    )
+    ends = ends[:8] + ends[8:]
+    ends = jnp.concatenate([ends, jnp.zeros((8, 128 - ends.shape[1]), F32)], 1)
+
+    def rows_of(part):
+        part = jnp.where(core == 0, part, pltpu.roll(part, 4, 0))
+        high, low = high_low(part)
+        return jnp.concatenate([high.astype(F32), low.astype(F32)], 0).astype(BF16)
+
+    ends = rows_of(ends)
+    mine_out[:, units:] = ends
+    sent_out[:, units:] = ends
+    for copy in big:
+        copy.wait()
+    for t in range(2):
+        part = jnp.dot(both, held[:, t * units : (t + 1) * units], preferred_element_type=F32)
+        part = rows_of(part[:8] + part[8:])
+
+        @pl.when(core == t)
+        def _():
+            mine_out[:, :units] = part
+
+        @pl.when(core != t)
+        def _():
+            sent_out[:, :units] = part
+
+
+def expand_sent_kernel(k, text, mod, place, *refs):
+    pieces, (w, sums) = refs[: 4 * (k + 1)], refs[4 * (k + 1) : 4 * (k + 1) + 2]
+    z_out, sent_out, side_out = refs[-3:]
+    core = lax.axis_index("narrow") % 2
+    units = w.shape[1] // 2
+    rows = z_out.shape[0]
+    tokens = jnp.concatenate([piece[...] for piece in pieces], 0)
+    x = jnp.dot(place[...], tokens, preferred_element_type=F32)
+    centre = (jnp.sum(x, -1, keepdims=True) / x.shape[1]).astype(BF16).astype(F32)
+    x = x - centre
+    z = (x * (1.0 + jnp.where(text[:, :1] > 0.5, mod[4:5, :], mod[1:2, :]))).astype(BF16)
+    z_out[...] = z
+    for t in range(0, units, TILE):
+        columns = pl.ds(pl.multiple_of((1 - core) * units + t, 128), TILE)
+        sent_out[:rows, t : t + TILE] = jnp.dot(
+            z, w[:, columns], preferred_element_type=F32
+        ).astype(BF16)
+    total = jnp.sum(x, -1, keepdims=True)
+    square = jnp.sum(x * x, -1, keepdims=True)
+    total_high = total.astype(BF16).astype(F32)
+    square_high = square.astype(BF16).astype(F32)
+    lane = lax.broadcasted_iota(jnp.int32, (rows, 128), 1) - 4 * core
+    side = jnp.where((lane == 0) | (lane == 1), centre, 0.0)
+    side = jnp.where(lane == 16, total_high, side)
+    side = jnp.where(lane == 17, total - total_high, side)
+    side = jnp.where(lane == 18, square_high, side)
+    side = jnp.where(lane == 19, square - square_high, side).astype(BF16)
+    side_out[...] = side
+    sent_out[:rows, units:] = side
+    if k == 0:
+        sent_out[rows:, :] = sums[...]
+
+
+def expand_kept_kernel(z, w, kept_out):
+    core = lax.axis_index("narrow") % 2
+    units = w.shape[1] // 2
+    for t in range(0, units, TILE):
+        columns = pl.ds(pl.multiple_of(core * units + t, 128), TILE)
+        kept_out[:, t : t + TILE] = jnp.dot(z[...], w[:, columns], preferred_element_type=F32)
+
+
+def merge_kernel(k, kept, side, came, sums, total_out, sent_out):
+    rows, units = kept.shape
+    total = kept[...] + came[:rows, :units].astype(F32)
+    total_out[...] = total
+    sent_out[:rows, :units] = total.astype(BF16)
+    sent_out[:rows, units:] = (side[...].astype(F32) + came[:rows, units:].astype(F32)).astype(BF16)
+    if k == 0:
+        sent_out[rows:, :] = (sums[...].astype(F32) + came[rows:, :].astype(F32)).astype(BF16)
+
+
+def activate_kernel(features, text, total, sent, came, first_sent, first_came, *refs):
+    act_out = refs[-1]
+    rows, units = total.shape
+    sides = [sent[:rows, units:].astype(F32), came[:rows, units:].astype(F32)]
+    lane = lax.broadcasted_iota(jnp.int32, (rows, 128), 1)
+    field = lane % 4
+    summed = sides[0] + sides[1]
+    add = lambda values, mask: jnp.sum(jnp.where(mask, values, 0.0), -1, keepdims=True)
+    centres, measures = lane < 8, (lane >= 16) & (lane < 24)
+    average = (
+        add(summed, centres & (field == 0)) * features + add(summed, measures & (field < 2))
+    ) / D
+    spread = add(summed, measures & (field >= 2))
+    aparts = []
+    for side in sides:
+        apart = jnp.where(centres, side - average, 0.0)
+        for core in range(2):
+            off = add(apart, lane == 4 * core)
+            own = lane // 4 == 4 + core
+            spread = spread + off * (2.0 * add(side, own & (field < 2)) + features * off)
+        aparts.append(apart)
+    scale = lax.rsqrt(spread / D + norm_eps)
+    of_text = jnp.where(text[...] > 0.5, 1, 0)
+    mine = centres & (lane % 2 == of_text)
+    packed, shift = None, 0
+    for apart in aparts:
+        factor = jnp.where(mine, jnp.where(field < 2, apart * scale, 1.0), 0.0)
+        high = factor.astype(BF16).astype(F32)
+        for part in (high, high, factor - high, factor - high):
+            part = pltpu.roll(part, shift, 1) if shift else part
+            packed = part if packed is None else packed + part
+            shift += 8
+    packed = packed[:, :64].astype(BF16)
+    own, other = first_sent[-16:, :units], first_came[-16:, :units]
+    factors = jnp.concatenate([own, own, other, other], 0)
+    for t in range(0, units, TILE):
+        columns = slice(t, t + TILE)
+        pre = total[:, columns] + came[:rows, columns].astype(F32)
+        extra = jnp.dot(packed, factors[:, columns], preferred_element_type=F32)
+        act_out[:, columns] = jax.nn.gelu(pre * scale + extra, approximate=True).astype(BF16)
+
+
+def contract_own_kernel(k, act, w, mine, first_sent, first_came, out, *ends_out):
+    core = lax.axis_index("narrow") % 2
+    units = w.shape[0] // 2
+    rows = pl.ds(pl.multiple_of(core * units, 128), units)
+    out[...] = jnp.dot(act[...], w[rows, :], preferred_element_type=F32)
+    if k == 0:
+        total = first_sent[-16:, units:].astype(F32) + first_came[-16:, units:].astype(F32)
+        total = total[:8] + total[8:]
+        total = total + pltpu.roll(total, 4, 0)
+        own = mine[:, units:].astype(F32)
+        own = own[:8] + own[8:]
+        own = own + pltpu.roll(own, 4, 0)
+        ends_out[0][...] = jnp.concatenate([total, own, jnp.zeros((112, 128), F32)], 0).T
+
+
+def contract_other_kernel(k, place, act, so_far, w, *outs):
+    core = lax.axis_index("narrow") % 2
+    units = w.shape[0] // 2
+    rows = pl.ds(pl.multiple_of((1 - core) * units, 128), units)
+    total = so_far[...] + jnp.dot(act[...], w[rows, :], preferred_element_type=F32)
+    spread = jnp.dot(place[...], total.astype(BF16), preferred_element_type=F32).astype(BF16)
+    size = size_of(k)
+    for s in range(4):
+        outs[s][...] = spread[s * size : (s + 1) * size]
+
+
+def finish_kernel(slots, hidden, mod, out_weight, ends, *refs):
+    pieces, (layer_out, bundle_out) = refs[: 4 * CHUNKS], refs[4 * CHUNKS :]
+    result = jnp.zeros(hidden.shape, F32)
+    for k in range(CHUNKS):
+        total = pieces[4 * k][...].astype(F32)
+        for s in (1, 2, 3):
+            total = total + pieces[4 * k + s][...].astype(F32)
+        total = jnp.concatenate([total] * (CAP // size_of(k)), 0)
+        result = jnp.where(slots[:, 2 + k : 3 + k] > 0.5, total, result)
+    gate = jnp.where(slots[:, 1:2] > 0.5, mod[5:6, :], mod[2:3, :])
+    layer = hidden[...].astype(F32) + gate * result
+    layer = jnp.where(slots[:, 0:1] > 0.5, layer, 0.0).astype(BF16)
+    layer_out[...] = layer
+    x = layer.astype(F32)
+    centre = jnp.sum(x, -1, keepdims=True) / x.shape[1]
+    ones = jnp.ones((8, x.shape[1]), BF16)
+    across = lambda left, right: lax.dot_general(
+        left, right, (((1,), (1,)), ((), ())), preferred_element_type=F32
+    )
+    high, low = high_low(x * x)
+    total, square = across(ones, layer), across(ones, high) + across(ones, low)
+    width = out_weight.shape[0]
+    product = across(out_weight[...], ((x - centre) * (1.0 + mod[7:8, :])).astype(BF16))
+    bundle_out[:width, :] = product + total[0:1] / x.shape[1] * ends[:width, 8:9]
+    row = lax.broadcasted_iota(jnp.int32, (8, CAP), 0)
+    bundle_out[width:, :] = jnp.where(row == 0, total, square)
+
+
+def write_kernel(layer, out):
+    out[...] = layer[...]
+
+
+def velocity_kernel(ends, first, second, third, fourth, out):
+    total = (first[...] + second[...]) + (third[...] + fourth[...])
+    width = out.shape[0]
+    average = total[width : width + 1] / D
+    variance = total[width + 1 : width + 2] / D - average * average
+    velocity = (total[:width] - average * ends[:width, 0:1]) * lax.rsqrt(
+        variance + norm_eps
+    ) + ends[:width, 1:2]
+    out[...] = velocity * jnp.where(lax.axis_index("cfg") == 0, guidance, 1.0 - guidance)
+
+
+def noise_kernel(timestep, alphas, video, latent, base_out, factor_out):
+    index = lax.broadcasted_iota(jnp.int32, (8, 128), 0) * 128 + lax.broadcasted_iota(
+        jnp.int32, (8, 128), 1
+    )
+    alpha = jnp.sum(
+        jnp.sum(jnp.where(index == timestep[0], alphas[...], 0.0), 0, keepdims=True),
+        1,
+        keepdims=True,
+    )
+    base_out[...] = jnp.where(video[0:1] > 0.5, jnp.sqrt(alpha) * latent[...], 0.0)
+    factor_out[...] = jnp.where(video[...] > 0.5, jnp.sqrt(1.0 - alpha), 0.0)
+
+
+def latent_kernel(base, factor, mine, other, out):
+    guided = jnp.where(factor[0:1] > 0.0, mine[...] + other[...], 0.0)
+    out[...] = base[...] - factor[0:1] * guided
+
+
+def alpha_constant():
+    ends = np.sqrt(np.float64(0.00085)), np.sqrt(np.float64(0.012))
+    betas = np.linspace(ends[0], ends[1], 1000, dtype=np.float64) ** 2
+    return np.pad(np.cumprod(1.0 - betas), (0, 24)).astype(np.float32).reshape(8, 128)
+
+
+def call(kernel, outs, args, spaces, scratch=(), weight=1):
+    kinds = {"v": pltpu.VMEM, "s": pltpu.SMEM, "a": pl.ANY}
+    return pl.pallas_call(
+        kernel,
+        out_shape=[jax.ShapeDtypeStruct(shape, dtype) for shape, dtype in outs],
+        in_specs=[pl.BlockSpec(memory_space=kinds[letter]) for letter in spaces],
+        out_specs=[pl.BlockSpec(memory_space=pltpu.VMEM) for _ in outs],
+        scratch_shapes=list(scratch),
+        compiler_params=pltpu.CompilerParams(vmem_limit_bytes=24 * 2**20),
+        cost_estimate=pl.CostEstimate(flops=weight, bytes_accessed=1, transcendentals=0),
+    )(*args)
+
+
+def four_blocks(
+    hidden, split_table, modulation, expand_weight, contract_weight, output_weight, latent, timestep
+):
+    hidden = hidden[0]
+    features = hidden.shape[1]
+    units = expand_weight.shape[1] // 2
+    width = output_weight.shape[1]
+    payload = units + 128
+
+    piece = hidden[: QUOTAS[1]]
+    arrived = [[piece] + z_swaps(piece)]
+
+    in_place = lambda array: pltpu.with_memory_space_constraint(array, pltpu.HBM)
+    chunks = range(CHUNKS)
+    made = call(
+        prepare_kernel,
+        [((size_of(k), features), BF16) for k in chunks[1:]]
+        + [((2 * size_of(k), 4 * QUOTAS[k + 1]), BF16) for k in chunks]
+        + [((4 * size_of(k), 2 * size_of(k)), BF16) for k in chunks]
+        + [((2 * size_of(k), 128), F32) for k in chunks]
+        + [
+            (expand_weight.shape, BF16),
+            (hidden.shape, BF16),
+            (modulation.shape, F32),
+            ((width, features), BF16),
+            ((16, payload), BF16),
+            ((16, payload), BF16),
+            ((CAP, 128), F32),
+            ((8, CAP), F32),
+        ],
+        [
+            split_table,
+            in_place(hidden),
+            in_place(modulation),
+            in_place(output_weight.T),
+            in_place(expand_weight),
+        ],
+        "saaaa",
+        [pltpu.SemaphoreType.DMA((4,)), pltpu.SemaphoreType.DMA((3,))],
+    )
+    later, made = made[: CHUNKS - 1], made[CHUNKS - 1 :]
+    gathers, made = made[:CHUNKS], made[CHUNKS:]
+    spreads, made = made[:CHUNKS], made[CHUNKS:]
+    texts, made = made[:CHUNKS], made[CHUNKS:]
+    held_in, tokens, mod, out_weight, sums_mine, sums_sent, slots, video = made
+    for piece in later:
+        arrived.append([piece] + z_swaps(piece))
+
+    merged = []
+    before = []
+    for k in chunks:
+        rows = 2 * size_of(k)
+        sent_rows = rows + (16 if k == 0 else 0)
+        pieces = [piece for phase in arrived[: k + 1] for piece in phase]
+        z, sent, side = call(
+            functools.partial(expand_sent_kernel, k),
+            [((rows, features), BF16), ((sent_rows, payload), BF16), ((rows, 128), BF16)],
+            [texts[k], mod, gathers[k], *pieces, held_in, sums_sent, *before],
+            "vvv" + "v" * len(pieces) + "vv" + "a" * len(before),
+            weight=LONG,
+        )
+        came = swap(sent, "narrow", 1, 4)
+        (kept,) = call(
+            expand_kept_kernel, [((rows, units), F32)], [z, held_in], "vv", weight=LONG
+        )
+        total, sent = call(
+            functools.partial(merge_kernel, k),
+            [((rows, units), F32), ((sent_rows, payload), BF16)],
+            [kept, side, came, sums_mine],
+            "vvvv",
+        )
+        before = [sent]
+        merged.append((total, sent, swap(sent, "narrow", 2, 4)))
+
+    (held_out,) = call(
+        hold_kernel,
+        [(contract_weight.shape, BF16)],
+        [in_place(contract_weight), merged[-1][1]],
+        "aa",
+        [pltpu.SemaphoreType.DMA((4,))],
+    )
+    returned = []
+    before = [held_out]
+    first = merged[0][1:]
+    for k in chunks:
+        rows = 2 * size_of(k)
+        total, sent, came = merged[k]
+        if k + 1 < CHUNKS:
+            before = before + [merged[k + 1][1]]
+        (act,) = call(
+            functools.partial(activate_kernel, features),
+            [((rows, units), BF16)],
+            [texts[k], total, sent, came, *first, *before],
+            "vvvvvv" + "a" * len(before),
+        )
+        act_came = swap(act, "narrow", 1, 4)
+        out, *ends_made = call(
+            functools.partial(contract_own_kernel, k),
+            [((rows, features), F32)] + ([((128, 128), F32)] if k == 0 else []),
+            [act, held_out, sums_mine, *first],
+            "vvvvv",
+            weight=LONG,
+        )
+        ends = ends_made[0] if k == 0 else ends
+        pieces = call(
+            functools.partial(contract_other_kernel, k),
+            [((size_of(k), features), BF16)] * 4,
+            [spreads[k], act_came, out, held_out],
+            "vvvv",
+        )
+        before = [pieces[0]]
+        returned.append(pieces[0])
+        returned.extend(swap(pieces[s], "wide", s, 4) for s in (1, 2, 3))
+
+    layer, bundle = call(
+        finish_kernel,
+        [((CAP, features), BF16), ((width + 8, CAP), F32)],
+        [slots, tokens, mod, out_weight, ends, *returned],
+        "v" * (5 + len(returned)),
+    )
+    (layer_out,) = call(write_kernel, [((CAP, features), BF16)], [layer], "v", weight=LONG)
+    (velocity,) = call(
+        velocity_kernel,
+        [((width, CAP), F32)],
+        [ends, bundle] + [swap(bundle, "narrow", n, 4) for n in (1, 2, 3)],
+        "vvvvv",
+    )
+    base, factor = call(
+        noise_kernel,
+        [((width, CAP), F32), ((8, CAP), F32)],
+        [timestep, alpha_constant(), video, latent.T],
+        "svvv",
+        weight=LONG,
+    )
+    (clean_latent,) = call(
+        latent_kernel,
+        [((width, CAP), F32)],
+        [base, factor, velocity, swap(velocity, "cfg", 1, 2)],
+        "vvvv",
+    )
+    return (layer_out[None], clean_latent.T)
+
+
 def solution(mesh):
+    by_swaps = (mesh.shape["wide"], mesh.shape["narrow"], mesh.shape["cfg"]) == (4, 4, 2)
     return jax.shard_map(
-        on_device,
+        four_blocks if by_swaps else any_slice,
         mesh=mesh,
         in_specs=(
             P("cfg", "wide", "narrow"),

time: 251 us -> 73.5 us (0.29)
  waiting for transfers between devices: 149 us -> 28.6 us
  blocking collectives: 57.7 us -> 0 us
  starting transfers between devices: 0.08 us -> 26.2 us
  matrix products: 16.2 us -> 0 us
  Pallas kernels: 0 us -> 15.5 us
  between operations: 16.1 us -> 1.48 us
  other arithmetic: 11.8 us -> 0 us
    psum x1 -> x0, waiting for transfers between devices: 118 us -> none  [on_device(): hidden_pre = lax.psum(hidden_part, 'narrow')]
    psum x3 -> x0, blocking collectives: 38.1 us -> none  [the longest x1 23.3 us: on_device(): guided = lax.psum(velocity_part * copy_weight, ('cfg', 'narrow'))]
    reduce_scatter x1 -> x0, waiting for transfers between devices: 30.5 us -> none  [on_device(): lax.psum_scatter(jnp.dot(activated, contract_weight, preferred_element_ty...]
    ppermute x0 -> x22, waiting for transfers between devices: none -> 28.6 us  [swap(): return lax.ppermute(array, axis, [(i, i ^ distance) for i in range(size)])]
    ppermute x0 -> x22, starting transfers between devices: none -> 26.2 us  [swap(): return lax.ppermute(array, axis, [(i, i ^ distance) for i in range(size)])]
    all_gather x1 -> x0, blocking collectives: 19.6 us -> none  [on_device(): lax.all_gather(normed, 'wide', axis=0, tiled=True)]
    dot_general x3 -> x0, matrix products: 16.2 us -> none  [the longest x1 9.02 us: on_device(): jnp.dot(activated, contract_weight, preferred_element_type=jnp.float32)]
    pallas_call x0 -> x19, Pallas kernels: none -> 15.5 us  [call(): pl.pallas_call(kernel, out_shape=[jax.ShapeDtypeStruct(shape, dtype) for...]
  transfers between devices with their start and end apart: 2 -> 22, of which waited for: 2 -> 12; matrix products, arithmetic and copies ran while one was open for 1% -> 0% of each run, Pallas kernels for 0% -> 18%
where the time goes in v4:
time: 73.5 us; the launch traced here: 73.3 us
  waiting for transfers between devices  28.6 us (39%)
  starting transfers between devices  26.2 us (36%)
  Pallas kernels  15.5 us (21%)
  local copies, waits for them, and re-layouts  1.57 us (2%)
  between operations  1.48 us (2%)
    ppermute x22, waiting for transfers between devices, swap(): return lax.ppermute(array, axis, [(i, i ^ distance) for i in range(size)])  28.6 us
    ppermute x22, starting transfers between devices, swap(): return lax.ppermute(array, axis, [(i, i ^ distance) for i in range(size)])  26.2 us
    pallas_call x19, Pallas kernels, call(): pl.pallas_call(kernel, out_shape=[jax.ShapeDtypeStruct(shape, dtype) for...  15.5 us
  transfers between devices with their start and end apart: 22, of which 12 were waited for; matrix products, arithmetic and copies ran while one was open for 0% of the time, Pallas kernels for 18%

profile of v4, /device:TPU:0, one launch (start us, length us, event | category | flops | bytes accessed | tf_op | source)
XLA Modules:
  0.0 73.3 jit_solution(14385809825335258343)
XLA Ops:
  0.6 0.9 %slice_bitcast_fusion.refs_0_ = bf16[64,768]{1,0:T(8,128)(2,1)S(1)} fusion(bf16[1,128,768]{2,1,0:T(8,128)(2,1)} %param.9), kind=kLoop, calls=%fused_computation | loop fusion | bytes 196608 | tf_op jit(solution)/shard_map/slice | solution.py:475
  1.5 3.0 %collective-permute-start = (bf16[64,768]{1,0:T(8,128)(2,1)S(1)}, bf16[64,768]{1,0:T(8,128)(2,1)S(1)}, u32[]{:S(2)}, u32[]{:S(2)}) collective-permute-start(bf16[64,768]{1,0:T(8,128)(2,1)S(1)} %slice_bitcast_fusion.refs_0_), channel_id=1, source_target_pairs={{0,4},{4,0},{8,12},{12,8},{1,5},{5,1},{9,13},{13,9},{2,6},{6,2},{1... | collective-permute-start | bytes 294920 | tf_op jit(solution)/shard_map/ppermute | solution.py:95
  4.6 2.6 %collective-permute-start.1 = (bf16[64,768]{1,0:T(8,128)(2,1)S(1)}, bf16[64,768]{1,0:T(8,128)(2,1)S(1)}, u32[]{:S(2)}, u32[]{:S(2)}) collective-permute-start(bf16[64,768]{1,0:T(8,128)(2,1)S(1)} %slice_bitcast_fusion.refs_0_), channel_id=1, source_target_pairs={{0,8},{4,12},{8,0},{12,4},{1,9},{5,13},{9,1},{13,5},{2,10},{6,14},... | collective-permute-start | bytes 294920 | tf_op jit(solution)/shard_map/ppermute | solution.py:95
  7.8 4.0 %shard_map.104 = (bf16[64,768]{1,0:T(8,128)(2,1)S(1)}, bf16[128,256]{1,0:T(8,128)(2,1)S(1)}, bf16[128,512]{1,0:T(8,128)(2,1)S(1)}, bf16[256,128]{1,0:T(8,128)(2,...) custom-call(s32[4]{0:T(128)S(1)} %copy-done, ...), custom_call_target="tpu_custom_call" | custom-call | flops 1 | bytes 1 | tf_op jit(solution)/shard_map/pallas_call | solution.py:455
  11.8 1.0 %collective-permute-start.5 = (bf16[64,768]{1,0:T(8,128)(2,1)S(1)}, bf16[64,768]{1,0:T(8,128)(2,1)S(1)}, u32[]{:S(2)}, u32[]{:S(2)}) collective-permute-start(bf16[64,768]{1,0:T(8,128)(2,1)S(1)} %get-tuple-element.57.refs_4_), channel_id=1, source_target_pairs={{0,4},{4,0},{8,12},{12,8},{1,5},{5,1},{9,13},{13,9},{2,6},{6,2},{1... | collective-permute-start | bytes 294920 | tf_op jit(solution)/shard_map/ppermute | solution.py:95
  12.8 3.5 %collective-permute-start.6 = (bf16[64,768]{1,0:T(8,128)(2,1)S(1)}, bf16[64,768]{1,0:T(8,128)(2,1)S(1)}, u32[]{:S(2)}, u32[]{:S(2)}) collective-permute-start(bf16[64,768]{1,0:T(8,128)(2,1)S(1)} %get-tuple-element.57.refs_4_), channel_id=1, source_target_pairs={{0,8},{4,12},{8,0},{12,4},{1,9},{5,13},{9,1},{13,5},{2,10},{6,14},... | collective-permute-start | bytes 294920 | tf_op jit(solution)/shard_map/ppermute | solution.py:95
  17.7 1.3 %collective-permute-done.3.came = bf16[144,1664]{1,0:T(8,128)(2,1)S(1)} collective-permute-done((bf16[144,1664]{1,0:T(8,128)(2,1)S(1)}, bf16[144,1664]{1,0:T(8,128)(2,1)S(1)}, u32[]{:S(2)}, u32[]{:S(2)}) %collective-permute-start.3) | collective-permute-done | bytes 479264 | tf_op jit(solution)/shard_map/ppermute | solution.py:95
  19.2 1.8 %collective-permute-start.4 = (bf16[144,1664]{1,0:T(8,128)(2,1)S(1)}, bf16[144,1664]{1,0:T(8,128)(2,1)S(1)}, u32[]{:S(2)}, u32[]{:S(2)}) collective-permute-start(bf16[144,1664]{1,0:T(8,128)(2,1)S(1)} %get-tuple-element.54.refs_10_.sent.first_sent), channel_id=1, source_target_pairs={{0,2},{1,3},{2,0},{3,1},{4,6},{5,7},{6,4},{7,5},{8,10},{9,11},{10,... | collective-permute-start | bytes 1437704 | tf_op jit(solution)/shard_map/ppermute | solution.py:95
  21.0 2.3 %collective-permute-done.6.refs_6_ = bf16[64,768]{1,0:T(8,128)(2,1)S(1)} collective-permute-done((bf16[64,768]{1,0:T(8,128)(2,1)S(1)}, bf16[64,768]{1,0:T(8,128)(2,1)S(1)}, u32[]{:S(2)}, u32[]{:S(2)}) %collective-permute-start.6) | collective-permute-done | bytes 98336 | tf_op jit(solution)/shard_map/ppermute | solution.py:95
  24.7 1.2 %collective-permute-done.8.came = bf16[128,1664]{1,0:T(8,128)(2,1)S(1)} collective-permute-done((bf16[128,1664]{1,0:T(8,128)(2,1)S(1)}, bf16[128,1664]{1,0:T(8,128)(2,1)S(1)}, u32[]{:S(2)}, u32[]{:S(2)}) %collective-permute-start.8) | collective-permute-done | bytes 426016 | tf_op jit(solution)/shard_map/ppermute | solution.py:95
  26.1 1.6 %collective-permute-start.13 = (bf16[128,1664]{1,0:T(8,128)(2,1)S(1)}, bf16[128,1664]{1,0:T(8,128)(2,1)S(1)}, u32[]{:S(2)}, u32[]{:S(2)}) collective-permute-start(bf16[128,1664]{1,0:T(8,128)(2,1)S(1)} %get-tuple-element.61._.refs_1_.sent), channel_id=1, source_target_pairs={{0,2},{1,3},{2,0},{3,1},{4,6},{5,7},{6,4},{7,5},{8,10},{9,11},{10,... | collective-permute-start | bytes 1277960 | tf_op jit(solution)/shard_map/ppermute | solution.py:95
  27.7 2.4 %shard_map.111.refs_0_.w = bf16[3072,768]{1,0:T(8,128)(2,1)S(1)} custom-call(bf16[3072,768]{1,0:T(8,128)(2,1)} %source.1, bf16[128,1664]{1,0:T(8,128)(2,1)S(1)} %get-tuple-element.61._.refs_1_.sent), custom_call_target="tpu_custom_call" | custom-call | flops 1 | bytes 1 | tf_op jit(solution)/shard_map/pallas_call | solution.py:455
  30.0 3.0 %collective-permute-done.4.came.first_came = bf16[144,1664]{1,0:T(8,128)(2,1)S(1)} collective-permute-done((bf16[144,1664]{1,0:T(8,128)(2,1)S(1)}, bf16[144,1664]{1,0:T(8,128)(2,1)S(1)}, u32[]{:S(2)}, u32[]{:S(2)}) %collective-permute-start.4) | collective-permute-done | bytes 479264 | tf_op jit(solution)/shard_map/ppermute | solution.py:95
  34.4 1.2 %collective-permute-done.9.act = bf16[128,1536]{1,0:T(8,128)(2,1)S(1)} collective-permute-done((bf16[128,1536]{1,0:T(8,128)(2,1)S(1)}, bf16[128,1536]{1,0:T(8,128)(2,1)S(1)}, u32[]{:S(2)}, u32[]{:S(2)}) %collective-permute-start.9) | collective-permute-done | bytes 393248 | tf_op jit(solution)/shard_map/ppermute | solution.py:95
  36.4 5.0 %collective-permute-done.13.came = bf16[128,1664]{1,0:T(8,128)(2,1)S(1)} collective-permute-done((bf16[128,1664]{1,0:T(8,128)(2,1)S(1)}, bf16[128,1664]{1,0:T(8,128)(2,1)S(1)}, u32[]{:S(2)}, u32[]{:S(2)}) %collective-permute-start.13) | collective-permute-done | bytes 426016 | tf_op jit(solution)/shard_map/ppermute | solution.py:95
  42.9 3.8 %collective-permute-start.11 = (bf16[64,768]{1,0:T(8,128)(2,1)S(1)}, bf16[64,768]{1,0:T(8,128)(2,1)S(1)}, u32[]{:S(2)}, u32[]{:S(2)}) collective-permute-start(bf16[64,768]{1,0:T(8,128)(2,1)S(1)} %get-tuple-element.67), channel_id=1, source_target_pairs={{0,8},{4,12},{8,0},{12,4},{1,9},{5,13},{9,1},{13,5},{2,10},{6,14},... | collective-permute-start | bytes 294920 | tf_op jit(solution)/shard_map/ppermute | solution.py:95
  48.6 3.8 %collective-permute-start.16 = (bf16[64,768]{1,0:T(8,128)(2,1)S(1)}, bf16[64,768]{1,0:T(8,128)(2,1)S(1)}, u32[]{:S(2)}, u32[]{:S(2)}) collective-permute-start(bf16[64,768]{1,0:T(8,128)(2,1)S(1)} %get-tuple-element.73), channel_id=1, source_target_pairs={{0,8},{4,12},{8,0},{12,4},{1,9},{5,13},{9,1},{13,5},{2,10},{6,14},... | collective-permute-start | bytes 294920 | tf_op jit(solution)/shard_map/ppermute | solution.py:95
  53.2 1.3 %collective-permute-done.11.refs_2_ = bf16[64,768]{1,0:T(8,128)(2,1)S(1)} collective-permute-done((bf16[64,768]{1,0:T(8,128)(2,1)S(1)}, bf16[64,768]{1,0:T(8,128)(2,1)S(1)}, u32[]{:S(2)}, u32[]{:S(2)}) %collective-permute-start.11) | collective-permute-done | bytes 98336 | tf_op jit(solution)/shard_map/ppermute | solution.py:95
  55.1 7.8 %collective-permute-done.16.refs_6_ = bf16[64,768]{1,0:T(8,128)(2,1)S(1)} collective-permute-done((bf16[64,768]{1,0:T(8,128)(2,1)S(1)}, bf16[64,768]{1,0:T(8,128)(2,1)S(1)}, u32[]{:S(2)}, u32[]{:S(2)}) %collective-permute-start.16) | collective-permute-done | bytes 98336 | tf_op jit(solution)/shard_map/ppermute | solution.py:95
  63.6 1.6 %collective-permute-start.19 = (f32[72,128]{1,0:T(8,128)S(1)}, f32[72,128]{1,0:T(8,128)S(1)}, u32[]{:S(2)}, u32[]{:S(2)}) collective-permute-start(f32[72,128]{1,0:T(8,128)S(1)} %get-tuple-element.79.first), channel_id=1, source_target_pairs={{0,2},{1,3},{2,0},{3,1},{4,6},{5,7},{6,4},{7,5},{8,10},{9,11},{10,... | collective-permute-start | bytes 110600 | tf_op jit(solution)/shard_map/ppermute | solution.py:95
  65.6 2.0 %collective-permute-done.19.third = f32[72,128]{1,0:T(8,128)S(1)} collective-permute-done((f32[72,128]{1,0:T(8,128)S(1)}, f32[72,128]{1,0:T(8,128)S(1)}, u32[]{:S(2)}, u32[]{:S(2)}) %collective-permute-start.19) | collective-permute-done | bytes 36896 | tf_op jit(solution)/shard_map/ppermute | solution.py:95
  67.6 1.0 %collective-permute-done.20.fourth = f32[72,128]{1,0:T(8,128)S(1)} collective-permute-done((f32[72,128]{1,0:T(8,128)S(1)}, f32[72,128]{1,0:T(8,128)S(1)}, u32[]{:S(2)}, u32[]{:S(2)}) %collective-permute-start.20) | collective-permute-done | bytes 36896 | tf_op jit(solution)/shard_map/ppermute | solution.py:95
  68.7 1.6 %collective-permute-start.21 = (f32[64,128]{1,0:T(8,128)S(1)}, f32[64,128]{1,0:T(8,128)S(1)}, u32[]{:S(2)}, u32[]{:S(2)}) collective-permute-start(f32[64,128]{1,0:T(8,128)S(1)} %shard_map.121.mine), channel_id=1, source_target_pairs={{0,16},{16,0},{1,17},{17,1},{2,18},{18,2},{3,19},{19,3},{4,20},{20... | collective-permute-start | bytes 98312 | tf_op jit(solution)/shard_map/ppermute | solution.py:95
  70.9 1.7 %collective-permute-done.21.other = f32[64,128]{1,0:T(8,128)S(1)} collective-permute-done((f32[64,128]{1,0:T(8,128)S(1)}, f32[64,128]{1,0:T(8,128)S(1)}, u32[]{:S(2)}, u32[]{:S(2)}) %collective-permute-start.21) | collective-permute-done | bytes 32800 | tf_op jit(solution)/shard_map/ppermute | solution.py:95
  (46 shorter events, 12.3 us)
Async XLA Ops:
  1.5 14.8 %collective-permute-start = (bf16[64,768]{1,0:T(8,128)(2,1)S(1)}, bf16[64,768]{1,0:T(8,128)(2,1)S(1)}, u32[]{:S(2)}, u32[]{:S(2)}) collective-permute-start(bf16[64,768]{1,0:T(8,128)(2,1)S(1)} %slice_bitcast_fusion.refs_0_), channel_id=1, source_target_pairs={{0,4},{4,0},{8,12},{12,8},{1,5},{5,1},{9,13},{13,9},{2,6},{6,2},{1... | collective-permute-start | bytes 294920 | tf_op jit(solution)/shard_map/ppermute | solution.py:95
  4.6 11.7 %collective-permute-start.1 = (bf16[64,768]{1,0:T(8,128)(2,1)S(1)}, bf16[64,768]{1,0:T(8,128)(2,1)S(1)}, u32[]{:S(2)}, u32[]{:S(2)}) collective-permute-start(bf16[64,768]{1,0:T(8,128)(2,1)S(1)} %slice_bitcast_fusion.refs_0_), channel_id=1, source_target_pairs={{0,8},{4,12},{8,0},{12,4},{1,9},{5,13},{9,1},{13,5},{2,10},{6,14},... | collective-permute-start | bytes 294920 | tf_op jit(solution)/shard_map/ppermute | solution.py:95
  7.1 9.2 %collective-permute-start.2 = (bf16[64,768]{1,0:T(8,128)(2,1)S(1)}, bf16[64,768]{1,0:T(8,128)(2,1)S(1)}, u32[]{:S(2)}, u32[]{:S(2)}) collective-permute-start(bf16[64,768]{1,0:T(8,128)(2,1)S(1)} %slice_bitcast_fusion.refs_0_), channel_id=1, source_target_pairs={{0,12},{4,8},{8,4},{12,0},{1,13},{5,9},{9,5},{13,1},{2,14},{6,10},... | collective-permute-start | bytes 294920 | tf_op jit(solution)/shard_map/ppermute | solution.py:95
  11.8 9.2 %collective-permute-start.5 = (bf16[64,768]{1,0:T(8,128)(2,1)S(1)}, bf16[64,768]{1,0:T(8,128)(2,1)S(1)}, u32[]{:S(2)}, u32[]{:S(2)}) collective-permute-start(bf16[64,768]{1,0:T(8,128)(2,1)S(1)} %get-tuple-element.57.refs_4_), channel_id=1, source_target_pairs={{0,4},{4,0},{8,12},{12,8},{1,5},{5,1},{9,13},{13,9},{2,6},{6,2},{1... | collective-permute-start | bytes 294920 | tf_op jit(solution)/shard_map/ppermute | solution.py:95
  12.8 10.5 %collective-permute-start.6 = (bf16[64,768]{1,0:T(8,128)(2,1)S(1)}, bf16[64,768]{1,0:T(8,128)(2,1)S(1)}, u32[]{:S(2)}, u32[]{:S(2)}) collective-permute-start(bf16[64,768]{1,0:T(8,128)(2,1)S(1)} %get-tuple-element.57.refs_4_), channel_id=1, source_target_pairs={{0,8},{4,12},{8,0},{12,4},{1,9},{5,13},{9,1},{13,5},{2,10},{6,14},... | collective-permute-start | bytes 294920 | tf_op jit(solution)/shard_map/ppermute | solution.py:95
  16.3 7.0 %collective-permute-start.7 = (bf16[64,768]{1,0:T(8,128)(2,1)S(1)}, bf16[64,768]{1,0:T(8,128)(2,1)S(1)}, u32[]{:S(2)}, u32[]{:S(2)}) collective-permute-start(bf16[64,768]{1,0:T(8,128)(2,1)S(1)} %get-tuple-element.57.refs_4_), channel_id=1, source_target_pairs={{0,12},{4,8},{8,4},{12,0},{1,13},{5,9},{9,5},{13,1},{2,14},{6,10},... | collective-permute-start | bytes 294920 | tf_op jit(solution)/shard_map/ppermute | solution.py:95
  17.1 1.9 %collective-permute-start.3 = (bf16[144,1664]{1,0:T(8,128)(2,1)S(1)}, bf16[144,1664]{1,0:T(8,128)(2,1)S(1)}, u32[]{:S(2)}, u32[]{:S(2)}) collective-permute-start(bf16[144,1664]{1,0:T(8,128)(2,1)S(1)} %get-tuple-element.51), channel_id=1, source_target_pairs={{0,1},{1,0},{2,3},{3,2},{4,5},{5,4},{6,7},{7,6},{8,9},{9,8},{10,11... | collective-permute-start | bytes 1437704 | tf_op jit(solution)/shard_map/ppermute | solution.py:95
  19.2 13.9 %collective-permute-start.4 = (bf16[144,1664]{1,0:T(8,128)(2,1)S(1)}, bf16[144,1664]{1,0:T(8,128)(2,1)S(1)}, u32[]{:S(2)}, u32[]{:S(2)}) collective-permute-start(bf16[144,1664]{1,0:T(8,128)(2,1)S(1)} %get-tuple-element.54.refs_10_.sent.first_sent), channel_id=1, source_target_pairs={{0,2},{1,3},{2,0},{3,1},{4,6},{5,7},{6,4},{7,5},{8,10},{9,11},{10,... | collective-permute-start | bytes 1437704 | tf_op jit(solution)/shard_map/ppermute | solution.py:95
  24.1 1.8 %collective-permute-start.8 = (bf16[128,1664]{1,0:T(8,128)(2,1)S(1)}, bf16[128,1664]{1,0:T(8,128)(2,1)S(1)}, u32[]{:S(2)}, u32[]{:S(2)}) collective-permute-start(bf16[128,1664]{1,0:T(8,128)(2,1)S(1)} %get-tuple-element.60), channel_id=1, source_target_pairs={{0,1},{1,0},{2,3},{3,2},{4,5},{5,4},{6,7},{7,6},{8,9},{9,8},{10,11... | collective-permute-start | bytes 1277960 | tf_op jit(solution)/shard_map/ppermute | solution.py:95
  26.1 15.3 %collective-permute-start.13 = (bf16[128,1664]{1,0:T(8,128)(2,1)S(1)}, bf16[128,1664]{1,0:T(8,128)(2,1)S(1)}, u32[]{:S(2)}, u32[]{:S(2)}) collective-permute-start(bf16[128,1664]{1,0:T(8,128)(2,1)S(1)} %get-tuple-element.61._.refs_1_.sent), channel_id=1, source_target_pairs={{0,2},{1,3},{2,0},{3,1},{4,6},{5,7},{6,4},{7,5},{8,10},{9,11},{10,... | collective-permute-start | bytes 1277960 | tf_op jit(solution)/shard_map/ppermute | solution.py:95
  33.8 1.8 %collective-permute-start.9 = (bf16[128,1536]{1,0:T(8,128)(2,1)S(1)}, bf16[128,1536]{1,0:T(8,128)(2,1)S(1)}, u32[]{:S(2)}, u32[]{:S(2)}) collective-permute-start(bf16[128,1536]{1,0:T(8,128)(2,1)S(1)} %shard_map.112.act), channel_id=1, source_target_pairs={{0,1},{1,0},{2,3},{3,2},{4,5},{5,4},{6,7},{7,6},{8,9},{9,8},{10,11... | collective-permute-start | bytes 1179656 | tf_op jit(solution)/shard_map/ppermute | solution.py:95
  42.2 5.0 %collective-permute-start.14 = (bf16[128,1536]{1,0:T(8,128)(2,1)S(1)}, bf16[128,1536]{1,0:T(8,128)(2,1)S(1)}, u32[]{:S(2)}, u32[]{:S(2)}) collective-permute-start(bf16[128,1536]{1,0:T(8,128)(2,1)S(1)} %shard_map.115.act), channel_id=1, source_target_pairs={{0,1},{1,0},{2,3},{3,2},{4,5},{5,4},{6,7},{7,6},{8,9},{9,8},{10,11... | collective-permute-start | bytes 1179656 | tf_op jit(solution)/shard_map/ppermute | solution.py:95
  42.2 10.2 %collective-permute-start.10 = (bf16[64,768]{1,0:T(8,128)(2,1)S(1)}, bf16[64,768]{1,0:T(8,128)(2,1)S(1)}, u32[]{:S(2)}, u32[]{:S(2)}) collective-permute-start(bf16[64,768]{1,0:T(8,128)(2,1)S(1)} %get-tuple-element.66), channel_id=1, source_target_pairs={{0,4},{4,0},{8,12},{12,8},{1,5},{5,1},{9,13},{13,9},{2,6},{6,2},{1... | collective-permute-start | bytes 294920 | tf_op jit(solution)/shard_map/ppermute | solution.py:95
  42.9 11.6 %collective-permute-start.11 = (bf16[64,768]{1,0:T(8,128)(2,1)S(1)}, bf16[64,768]{1,0:T(8,128)(2,1)S(1)}, u32[]{:S(2)}, u32[]{:S(2)}) collective-permute-start(bf16[64,768]{1,0:T(8,128)(2,1)S(1)} %get-tuple-element.67), channel_id=1, source_target_pairs={{0,8},{4,12},{8,0},{12,4},{1,9},{5,13},{9,1},{13,5},{2,10},{6,14},... | collective-permute-start | bytes 294920 | tf_op jit(solution)/shard_map/ppermute | solution.py:95
  46.7 7.8 %collective-permute-start.12 = (bf16[64,768]{1,0:T(8,128)(2,1)S(1)}, bf16[64,768]{1,0:T(8,128)(2,1)S(1)}, u32[]{:S(2)}, u32[]{:S(2)}) collective-permute-start(bf16[64,768]{1,0:T(8,128)(2,1)S(1)} %get-tuple-element.68), channel_id=1, source_target_pairs={{0,12},{4,8},{8,4},{12,0},{1,13},{5,9},{9,5},{13,1},{2,14},{6,10},... | collective-permute-start | bytes 294920 | tf_op jit(solution)/shard_map/ppermute | solution.py:95
  47.2 18.3 %copy-start.1 = (f32[128,64]{0,1:T(8,128)S(1)}, f32[128,64]{0,1:T(8,128)}, u32[]{:S(2)}) copy-start(f32[128,64]{0,1:T(8,128)} %param.15) | copy-start | bytes 98308
  47.2 18.3 %copy-start.2 = (f32[8,128]{1,0:T(8,128)S(1)}, f32[8,128]{1,0:T(8,128)}, u32[]{:S(2)}) copy-start(f32[8,128]{1,0:T(8,128)} %constant.2.clone.alphas) | copy-start | bytes 12292
  48.0 7.1 %collective-permute-start.15 = (bf16[64,768]{1,0:T(8,128)(2,1)S(1)}, bf16[64,768]{1,0:T(8,128)(2,1)S(1)}, u32[]{:S(2)}, u32[]{:S(2)}) collective-permute-start(bf16[64,768]{1,0:T(8,128)(2,1)S(1)} %get-tuple-element.72), channel_id=1, source_target_pairs={{0,4},{4,0},{8,12},{12,8},{1,5},{5,1},{9,13},{13,9},{2,6},{6,2},{1... | collective-permute-start | bytes 294920 | tf_op jit(solution)/shard_map/ppermute | solution.py:95
  48.6 14.3 %collective-permute-start.16 = (bf16[64,768]{1,0:T(8,128)(2,1)S(1)}, bf16[64,768]{1,0:T(8,128)(2,1)S(1)}, u32[]{:S(2)}, u32[]{:S(2)}) collective-permute-start(bf16[64,768]{1,0:T(8,128)(2,1)S(1)} %get-tuple-element.73), channel_id=1, source_target_pairs={{0,8},{4,12},{8,0},{12,4},{1,9},{5,13},{9,1},{13,5},{2,10},{6,14},... | collective-permute-start | bytes 294920 | tf_op jit(solution)/shard_map/ppermute | solution.py:95
  52.5 10.5 %collective-permute-start.17 = (bf16[64,768]{1,0:T(8,128)(2,1)S(1)}, bf16[64,768]{1,0:T(8,128)(2,1)S(1)}, u32[]{:S(2)}, u32[]{:S(2)}) collective-permute-start(bf16[64,768]{1,0:T(8,128)(2,1)S(1)} %get-tuple-element.74), channel_id=1, source_target_pairs={{0,12},{4,8},{8,4},{12,0},{1,13},{5,9},{9,5},{13,1},{2,14},{6,10},... | collective-permute-start | bytes 294920 | tf_op jit(solution)/shard_map/ppermute | solution.py:95
  63.5 2.0 %collective-permute-start.18 = (f32[72,128]{1,0:T(8,128)S(1)}, f32[72,128]{1,0:T(8,128)S(1)}, u32[]{:S(2)}, u32[]{:S(2)}) collective-permute-start(f32[72,128]{1,0:T(8,128)S(1)} %get-tuple-element.79.first), channel_id=1, source_target_pairs={{0,1},{1,0},{2,3},{3,2},{4,5},{5,4},{6,7},{7,6},{8,9},{9,8},{10,11... | collective-permute-start | bytes 110600 | tf_op jit(solution)/shard_map/ppermute | solution.py:95
  63.6 4.0 %collective-permute-start.19 = (f32[72,128]{1,0:T(8,128)S(1)}, f32[72,128]{1,0:T(8,128)S(1)}, u32[]{:S(2)}, u32[]{:S(2)}) collective-permute-start(f32[72,128]{1,0:T(8,128)S(1)} %get-tuple-element.79.first), channel_id=1, source_target_pairs={{0,2},{1,3},{2,0},{3,1},{4,6},{5,7},{6,4},{7,5},{8,10},{9,11},{10,... | collective-permute-start | bytes 110600 | tf_op jit(solution)/shard_map/ppermute | solution.py:95
  65.2 3.4 %collective-permute-start.20 = (f32[72,128]{1,0:T(8,128)S(1)}, f32[72,128]{1,0:T(8,128)S(1)}, u32[]{:S(2)}, u32[]{:S(2)}) collective-permute-start(f32[72,128]{1,0:T(8,128)S(1)} %get-tuple-element.79.first), channel_id=1, source_target_pairs={{0,3},{1,2},{2,1},{3,0},{4,7},{5,6},{6,5},{7,4},{8,11},{9,10},{10,... | collective-permute-start | bytes 110600 | tf_op jit(solution)/shard_map/ppermute | solution.py:95
  68.7 4.0 %collective-permute-start.21 = (f32[64,128]{1,0:T(8,128)S(1)}, f32[64,128]{1,0:T(8,128)S(1)}, u32[]{:S(2)}, u32[]{:S(2)}) collective-permute-start(f32[64,128]{1,0:T(8,128)S(1)} %shard_map.121.mine), channel_id=1, source_target_pairs={{0,16},{16,0},{1,17},{17,1},{2,18},{18,2},{3,19},{19,3},{4,20},{20... | collective-permute-start | bytes 98312 | tf_op jit(solution)/shard_map/ppermute | solution.py:95
  (1 other events, 0.7 us)

commit v5 on v4

--- a/solution.py
+++ b/solution.py
@@ -141,6 +141,27 @@
     return copies
 
 
+def load_half(source, half, place, sems):
+    width = place.shape[1]
+    copies = []
+    for t in range(0, width, TILE):
+        columns = pl.ds(pl.multiple_of(half * width + t, 128), TILE)
+        copies.append(
+            pltpu.make_async_copy(
+                source.at[:, columns], place.at[:, pl.ds(t, TILE)], sems.at[len(copies)]
+            )
+        )
+        copies[-1].start()
+    return copies
+
+
+def rows_of(parts, core):
+    total = parts[:8] + parts[8:]
+    total = jnp.where(core == 0, total, pltpu.roll(total, 4, 0))
+    high, low = high_low(total)
+    return jnp.concatenate([high.astype(F32), low.astype(F32)], 0).astype(BF16)
+
+
 def hold_kernel(source, _, place, sems):
     for copy in load(source, place, sems):
         copy.wait()
@@ -185,22 +206,29 @@
     return jnp.concatenate(places, 0)
 
 
-def prepare_kernel(table, hidden, mod_in, out_weight, w, *refs):
+def take_kernel(source, out, sem):
+    copy = pltpu.make_async_copy(source.at[pl.ds(0, out.shape[0]), :], out, sem)
+    copy.start()
+    copy.wait()
+
+
+def prepare_kernel(table_in, hidden, mod_in, out_weight, w, *refs):
     later, refs = refs[: CHUNKS - 1], refs[CHUNKS - 1 :]
     gathers, refs = refs[:CHUNKS], refs[CHUNKS:]
     spreads, refs = refs[:CHUNKS], refs[CHUNKS:]
     texts, refs = refs[:CHUNKS], refs[CHUNKS:]
-    held, tokens, mod, weight, mine_out, sent_out, slots_out, video_out, sems, small = refs
+    held, tokens, mod, weight, rows_out, ends_out, slots_out, video_out, table, sems, small = refs
     core = lax.axis_index("narrow") % 2
-    units = w.shape[1] // 2
+    sources = (table_in, mod_in, out_weight, hidden)
     copies = [
         pltpu.make_async_copy(source, place, small.at[i])
-        for i, (source, place) in enumerate(((mod_in, mod), (out_weight, weight), (hidden, tokens)))
+        for i, (source, place) in enumerate(zip(sources, (table, mod, weight, tokens)))
     ]
     for copy in copies:
         copy.start()
-    big = load(w, held, sems)
-
+    big = load_half(w, 1 - core, held, sems)
+
+    copies[0].wait()
     ranks, counts, others, offset, largest_offset = layout(table)
     for k in range(CHUNKS):
         gathers[k][...] = gather_matrix(k, ranks, counts, others)
@@ -220,67 +248,50 @@
     slot = lax.broadcasted_iota(jnp.int32, (8, CAP), 1)
     video_out[...] = jnp.where((slot < counts[0]) & (slot + offset >= TEXT), 1.0, 0.0)
 
-    for copy in copies:
-        copy.wait()
-    for k in range(1, CHUNKS):
-        later[k - 1][...] = tokens[QUOTAS[k] : QUOTAS[k + 1], :]
+    copies[1].wait()
     row = lax.broadcasted_iota(jnp.int32, (8, 1), 0)
     rows = jnp.where(row == 0, 1.0 + mod[1:2, :], jnp.zeros((8, 1), F32))
     rows = jnp.where(row == 1, 1.0 + mod[4:5, :], rows)
     rows = jnp.where(row == 2, mod[0:1, :], rows)
     rows = jnp.where(row == 3, mod[3:4, :], rows)
-    both = jnp.concatenate(high_low(rows), 0)
+    rows_out[...] = jnp.concatenate(high_low(rows), 0)
     rows = jnp.where(row == 0, 1.0 + mod[7:8, :], jnp.zeros((8, 1), F32))
     rows = jnp.where(row == 1, mod[6:7, :], rows)
+    copies[2].wait()
     ends = lax.dot_general(
         jnp.concatenate(high_low(rows), 0),
         weight[...],
         (((1,), (1,)), ((), ())),
         preferred_element_type=F32,
     )
-    ends = ends[:8] + ends[8:]
-    ends = jnp.concatenate([ends, jnp.zeros((8, 128 - ends.shape[1]), F32)], 1)
-
-    def rows_of(part):
-        part = jnp.where(core == 0, part, pltpu.roll(part, 4, 0))
-        high, low = high_low(part)
-        return jnp.concatenate([high.astype(F32), low.astype(F32)], 0).astype(BF16)
-
-    ends = rows_of(ends)
-    mine_out[:, units:] = ends
-    sent_out[:, units:] = ends
+    ends = rows_of(ends, core)
+    ends_out[...] = jnp.concatenate([ends, jnp.zeros((16, 128 - ends.shape[1]), BF16)], 1)
+    copies[3].wait()
+    for k in range(1, CHUNKS):
+        later[k - 1][...] = tokens[QUOTAS[k] : QUOTAS[k + 1], :]
     for copy in big:
         copy.wait()
-    for t in range(2):
-        part = jnp.dot(both, held[:, t * units : (t + 1) * units], preferred_element_type=F32)
-        part = rows_of(part[:8] + part[8:])
-
-        @pl.when(core == t)
-        def _():
-            mine_out[:, :units] = part
-
-        @pl.when(core != t)
-        def _():
-            sent_out[:, :units] = part
 
 
 def expand_sent_kernel(k, text, mod, place, *refs):
-    pieces, (w, sums) = refs[: 4 * (k + 1)], refs[4 * (k + 1) : 4 * (k + 1) + 2]
+    pieces, (w, sums, ends) = refs[: 4 * (k + 1)], refs[4 * (k + 1) : 4 * (k + 1) + 3]
     z_out, sent_out, side_out = refs[-3:]
     core = lax.axis_index("narrow") % 2
-    units = w.shape[1] // 2
-    rows = z_out.shape[0]
+    units = w.shape[1]
+    rows = side_out.shape[0]
     tokens = jnp.concatenate([piece[...] for piece in pieces], 0)
     x = jnp.dot(place[...], tokens, preferred_element_type=F32)
     centre = (jnp.sum(x, -1, keepdims=True) / x.shape[1]).astype(BF16).astype(F32)
     x = x - centre
     z = (x * (1.0 + jnp.where(text[:, :1] > 0.5, mod[4:5, :], mod[1:2, :]))).astype(BF16)
+    if k == 0:
+        z = jnp.concatenate([z, sums[...]], 0)
     z_out[...] = z
     for t in range(0, units, TILE):
-        columns = pl.ds(pl.multiple_of((1 - core) * units + t, 128), TILE)
-        sent_out[:rows, t : t + TILE] = jnp.dot(
-            z, w[:, columns], preferred_element_type=F32
-        ).astype(BF16)
+        product = jnp.dot(z, w[:, t : t + TILE], preferred_element_type=F32)
+        sent_out[:rows, t : t + TILE] = product[:rows].astype(BF16)
+        if k == 0:
+            sent_out[rows:, t : t + TILE] = rows_of(product[rows:], core)
     total = jnp.sum(x, -1, keepdims=True)
     square = jnp.sum(x * x, -1, keepdims=True)
     total_high = total.astype(BF16).astype(F32)
@@ -294,25 +305,35 @@
     side_out[...] = side
     sent_out[:rows, units:] = side
     if k == 0:
-        sent_out[rows:, :] = sums[...]
-
-
-def expand_kept_kernel(z, w, kept_out):
+        sent_out[rows:, units:] = ends[...]
+
+
+def first_kept_kernel(z, w, kept_out, sums_out, held, sems):
     core = lax.axis_index("narrow") % 2
-    units = w.shape[1] // 2
-    for t in range(0, units, TILE):
-        columns = pl.ds(pl.multiple_of(core * units + t, 128), TILE)
-        kept_out[:, t : t + TILE] = jnp.dot(z[...], w[:, columns], preferred_element_type=F32)
-
-
-def merge_kernel(k, kept, side, came, sums, total_out, sent_out):
+    rows = kept_out.shape[0]
+    for t, copy in enumerate(load_half(w, core, held, sems)):
+        copy.wait()
+        columns = slice(t * TILE, (t + 1) * TILE)
+        product = jnp.dot(z[...], held[:, columns], preferred_element_type=F32)
+        kept_out[:, columns] = product[:rows]
+        sums_out[:, columns] = rows_of(product[rows:], core)
+
+
+def kept_kernel(z, w, kept_out):
+    for t in range(0, w.shape[1], TILE):
+        kept_out[:, t : t + TILE] = jnp.dot(z[...], w[:, t : t + TILE], preferred_element_type=F32)
+
+
+def merge_kernel(k, kept, side, came, sums, ends, total_out, sent_out):
     rows, units = kept.shape
+    add = lambda left, right: (left[...].astype(F32) + right.astype(F32)).astype(BF16)
     total = kept[...] + came[:rows, :units].astype(F32)
     total_out[...] = total
     sent_out[:rows, :units] = total.astype(BF16)
-    sent_out[:rows, units:] = (side[...].astype(F32) + came[:rows, units:].astype(F32)).astype(BF16)
+    sent_out[:rows, units:] = add(side, came[:rows, units:])
     if k == 0:
-        sent_out[rows:, :] = (sums[...].astype(F32) + came[rows:, :].astype(F32)).astype(BF16)
+        sent_out[rows:, :units] = add(sums, came[rows:, :units])
+        sent_out[rows:, units:] = add(ends, came[rows:, units:])
 
 
 def activate_kernel(features, text, total, sent, came, first_sent, first_came, *refs):
@@ -366,7 +387,7 @@
         total = first_sent[-16:, units:].astype(F32) + first_came[-16:, units:].astype(F32)
         total = total[:8] + total[8:]
         total = total + pltpu.roll(total, 4, 0)
-        own = mine[:, units:].astype(F32)
+        own = mine[...].astype(F32)
         own = own[:8] + own[8:]
         own = own + pltpu.roll(own, 4, 0)
         ends_out[0][...] = jnp.concatenate([total, own, jnp.zeros((112, 128), F32)], 0).T
@@ -415,15 +436,8 @@
     out[...] = layer[...]
 
 
-def velocity_kernel(ends, first, second, third, fourth, out):
-    total = (first[...] + second[...]) + (third[...] + fourth[...])
-    width = out.shape[0]
-    average = total[width : width + 1] / D
-    variance = total[width + 1 : width + 2] / D - average * average
-    velocity = (total[:width] - average * ends[:width, 0:1]) * lax.rsqrt(
-        variance + norm_eps
-    ) + ends[:width, 1:2]
-    out[...] = velocity * jnp.where(lax.axis_index("cfg") == 0, guidance, 1.0 - guidance)
+def add_kernel(left, right, out):
+    out[...] = left[...] + right[...]
 
 
 def noise_kernel(timestep, alphas, video, latent, base_out, factor_out):
@@ -439,8 +453,22 @@
     factor_out[...] = jnp.where(video[...] > 0.5, jnp.sqrt(1.0 - alpha), 0.0)
 
 
-def latent_kernel(base, factor, mine, other, out):
-    guided = jnp.where(factor[0:1] > 0.0, mine[...] + other[...], 0.0)
+def latent_kernel(base, factor, ends, mine, mine_y, other, other_y, out):
+    width = out.shape[0]
+
+    def velocity(total):
+        average = total[width : width + 1] / D
+        variance = total[width + 1 : width + 2] / D - average * average
+        return (total[:width] - average * ends[:width, 0:1]) * lax.rsqrt(
+            variance + norm_eps
+        ) + ends[:width, 1:2]
+
+    first = lax.axis_index("cfg") == 0
+    guided = velocity(mine[...] + mine_y[...]) * jnp.where(first, guidance, 1.0 - guidance)
+    guided = guided + velocity(other[...] + other_y[...]) * jnp.where(
+        first, 1.0 - guidance, guidance
+    )
+    guided = jnp.where(factor[0:1] > 0.0, guided, 0.0)
     out[...] = base[...] - factor[0:1] * guided
 
 
@@ -472,10 +500,17 @@
     width = output_weight.shape[1]
     payload = units + 128
 
-    piece = hidden[: QUOTAS[1]]
+    in_place = lambda array: pltpu.with_memory_space_constraint(array, pltpu.HBM)
+    (piece,) = call(
+        take_kernel,
+        [((QUOTAS[1], features), BF16)],
+        [in_place(hidden)],
+        "a",
+        [pltpu.SemaphoreType.DMA(())],
+    )
     arrived = [[piece] + z_swaps(piece)]
 
-    in_place = lambda array: pltpu.with_memory_space_constraint(array, pltpu.HBM)
+    tiles = units // TILE
     chunks = range(CHUNKS)
     made = call(
         prepare_kernel,
@@ -484,30 +519,34 @@
         + [((4 * size_of(k), 2 * size_of(k)), BF16) for k in chunks]
         + [((2 * size_of(k), 128), F32) for k in chunks]
         + [
-            (expand_weight.shape, BF16),
+            ((features, units), BF16),
             (hidden.shape, BF16),
             (modulation.shape, F32),
             ((width, features), BF16),
-            ((16, payload), BF16),
-            ((16, payload), BF16),
+            ((16, features), BF16),
+            ((16, 128), BF16),
             ((CAP, 128), F32),
             ((8, CAP), F32),
         ],
         [
-            split_table,
+            in_place(split_table),
             in_place(hidden),
             in_place(modulation),
             in_place(output_weight.T),
             in_place(expand_weight),
         ],
-        "saaaa",
-        [pltpu.SemaphoreType.DMA((4,)), pltpu.SemaphoreType.DMA((3,))],
+        "aaaaa",
+        [
+            pltpu.SMEM(split_table.shape, jnp.int32),
+            pltpu.SemaphoreType.DMA((tiles,)),
+            pltpu.SemaphoreType.DMA((4,)),
+        ],
     )
     later, made = made[: CHUNKS - 1], made[CHUNKS - 1 :]
     gathers, made = made[:CHUNKS], made[CHUNKS:]
     spreads, made = made[:CHUNKS], made[CHUNKS:]
     texts, made = made[:CHUNKS], made[CHUNKS:]
-    held_in, tokens, mod, out_weight, sums_mine, sums_sent, slots, video = made
+    held_sent, tokens, mod, out_weight, rows_in, ends_mine, slots, video = made
     for piece in later:
         arrived.append([piece] + z_swaps(piece))
 
@@ -519,20 +558,28 @@
         pieces = [piece for phase in arrived[: k + 1] for piece in phase]
         z, sent, side = call(
             functools.partial(expand_sent_kernel, k),
-            [((rows, features), BF16), ((sent_rows, payload), BF16), ((rows, 128), BF16)],
-            [texts[k], mod, gathers[k], *pieces, held_in, sums_sent, *before],
-            "vvv" + "v" * len(pieces) + "vv" + "a" * len(before),
+            [((sent_rows, features), BF16), ((sent_rows, payload), BF16), ((rows, 128), BF16)],
+            [texts[k], mod, gathers[k], *pieces, held_sent, rows_in, ends_mine, *before],
+            "vvv" + "v" * len(pieces) + "vvv" + "a" * len(before),
             weight=LONG,
         )
         came = swap(sent, "narrow", 1, 4)
-        (kept,) = call(
-            expand_kept_kernel, [((rows, units), F32)], [z, held_in], "vv", weight=LONG
-        )
+        if k == 0:
+            kept, sums, held_kept = call(
+                first_kept_kernel,
+                [((rows, units), F32), ((16, units), BF16), ((features, units), BF16)],
+                [z, in_place(expand_weight)],
+                "va",
+                [pltpu.SemaphoreType.DMA((tiles,))],
+                weight=LONG,
+            )
+        else:
+            (kept,) = call(kept_kernel, [((rows, units), F32)], [z, held_kept], "vv", weight=LONG)
         total, sent = call(
             functools.partial(merge_kernel, k),
             [((rows, units), F32), ((sent_rows, payload), BF16)],
-            [kept, side, came, sums_mine],
-            "vvvv",
+            [kept, side, came, sums, ends_mine],
+            "vvvvv",
         )
         before = [sent]
         merged.append((total, sent, swap(sent, "narrow", 2, 4)))
@@ -562,7 +609,7 @@
         out, *ends_made = call(
             functools.partial(contract_own_kernel, k),
             [((rows, features), F32)] + ([((128, 128), F32)] if k == 0 else []),
-            [act, held_out, sums_mine, *first],
+            [act, held_out, ends_mine, *first],
             "vvvvv",
             weight=LONG,
         )
@@ -573,7 +620,7 @@
             [spreads[k], act_came, out, held_out],
             "vvvv",
         )
-        before = [pieces[0]]
+        before = pieces
         returned.append(pieces[0])
         returned.extend(swap(pieces[s], "wide", s, 4) for s in (1, 2, 3))
 
@@ -584,11 +631,8 @@
         "v" * (5 + len(returned)),
     )
     (layer_out,) = call(write_kernel, [((CAP, features), BF16)], [layer], "v", weight=LONG)
-    (velocity,) = call(
-        velocity_kernel,
-        [((width, CAP), F32)],
-        [ends, bundle] + [swap(bundle, "narrow", n, 4) for n in (1, 2, 3)],
-        "vvvvv",
+    (bundle,) = call(
+        add_kernel, [((width + 8, CAP), F32)], [bundle, swap(bundle, "narrow", 1, 4)], "vv"
     )
     base, factor = call(
         noise_kernel,
@@ -600,8 +644,8 @@
     (clean_latent,) = call(
         latent_kernel,
         [((width, CAP), F32)],
-        [base, factor, velocity, swap(velocity, "cfg", 1, 2)],
-        "vvvv",
+        [base, factor, ends, bundle] + [swap(bundle, ("cfg", "narrow"), n, 8) for n in (2, 4, 6)],
+        "vvvvvvv",
     )
     return (layer_out[None], clean_latent.T)
 

time: 73.5 us -> 72.4 us (0.985)
  starting transfers between devices: 26.2 us -> 31.9 us
  waiting for transfers between devices: 28.6 us -> 23 us
  local copies, waits for them, and re-layouts: 1.57 us -> 0.01 us
    ppermute x22, starting transfers between devices: 26.2 us -> 31.9 us  [swap(): return lax.ppermute(array, axis, [(i, i ^ distance) for i in range(size)])]
    ppermute x22, waiting for transfers between devices: 28.6 us -> 23 us  [swap(): return lax.ppermute(array, axis, [(i, i ^ distance) for i in range(size)])]
    slice x1 -> x0, local copies, waits for them, and re-layouts: 0.9 us -> none  [four_blocks(): piece = hidden[:QUOTAS[1]]]
    pallas_call x19 -> x20, Pallas kernels: 15.5 us -> 15.8 us  [call(): pl.pallas_call(kernel, out_shape=[jax.ShapeDtypeStruct(shape, dtype) for...]
  transfers between devices with their start and end apart: 22 -> 22, of which waited for: 12 -> 11; matrix products, arithmetic and copies ran while one was open for 0% -> 0% of each run, Pallas kernels for 18% -> 19%
where the time goes in v5:
time: 72.4 us; the launch traced here: 72.2 us
  starting transfers between devices  31.9 us (44%)
  waiting for transfers between devices  23 us (32%)
  Pallas kernels  15.8 us (22%)
  between operations  1.51 us (2%)
    ppermute x22, starting transfers between devices, swap(): return lax.ppermute(array, axis, [(i, i ^ distance) for i in range(size)])  31.9 us
    ppermute x22, waiting for transfers between devices, swap(): return lax.ppermute(array, axis, [(i, i ^ distance) for i in range(size)])  23 us
    pallas_call x20, Pallas kernels, call(): pl.pallas_call(kernel, out_shape=[jax.ShapeDtypeStruct(shape, dtype) for...  15.8 us
  transfers between devices with their start and end apart: 22, of which 11 were waited for; matrix products, arithmetic and copies ran while one was open for 0% of the time, Pallas kernels for 19%

profile of v5, /device:TPU:0, one launch (start us, length us, event | category | flops | bytes accessed | tf_op | source)
XLA Modules:
  0.0 72.2 jit_solution(18383828588446479892)
XLA Ops:
  1.5 3.1 %collective-permute-start = (bf16[64,768]{1,0:T(8,128)(2,1)S(1)}, bf16[64,768]{1,0:T(8,128)(2,1)S(1)}, u32[]{:S(2)}, u32[]{:S(2)}) collective-permute-start(bf16[64,768]{1,0:T(8,128)(2,1)S(1)} %shard_map.105.refs_0_), channel_id=1, source_target_pairs={{0,4},{4,0},{8,12},{12,8},{1,5},{5,1},{9,13},{13,9},{2,6},{6,2},{1... | collective-permute-start | bytes 294920 | tf_op jit(solution)/shard_map/ppermute | solution.py:95
  4.6 2.6 %collective-permute-start.1 = (bf16[64,768]{1,0:T(8,128)(2,1)S(1)}, bf16[64,768]{1,0:T(8,128)(2,1)S(1)}, u32[]{:S(2)}, u32[]{:S(2)}) collective-permute-start(bf16[64,768]{1,0:T(8,128)(2,1)S(1)} %shard_map.105.refs_0_), channel_id=1, source_target_pairs={{0,8},{4,12},{8,0},{12,4},{1,9},{5,13},{9,1},{13,5},{2,10},{6,14},... | collective-permute-start | bytes 294920 | tf_op jit(solution)/shard_map/ppermute | solution.py:95
  7.2 1.9 %shard_map.104 = (bf16[64,768]{1,0:T(8,128)(2,1)S(1)}, bf16[128,256]{1,0:T(8,128)(2,1)S(1)}, bf16[128,512]{1,0:T(8,128)(2,1)S(1)}, bf16[256,128]{1,0:T(8,128)(2,...) custom-call(s32[4]{0:T(128)} %table_in.1, ...), custom_call_target="tpu_custom_call" | custom-call | flops 1 | bytes 1 | tf_op jit(solution)/shard_map/pallas_call | solution.py:483
  10.1 3.5 %collective-permute-start.6 = (bf16[64,768]{1,0:T(8,128)(2,1)S(1)}, bf16[64,768]{1,0:T(8,128)(2,1)S(1)}, u32[]{:S(2)}, u32[]{:S(2)}) collective-permute-start(bf16[64,768]{1,0:T(8,128)(2,1)S(1)} %get-tuple-element.62.refs_4_), channel_id=1, source_target_pairs={{0,8},{4,12},{8,0},{12,4},{1,9},{5,13},{9,1},{13,5},{2,10},{6,14},... | collective-permute-start | bytes 294920 | tf_op jit(solution)/shard_map/ppermute | solution.py:95
  13.6 1.7 %collective-permute-done.1.refs_2_ = bf16[64,768]{1,0:T(8,128)(2,1)S(1)} collective-permute-done((bf16[64,768]{1,0:T(8,128)(2,1)S(1)}, bf16[64,768]{1,0:T(8,128)(2,1)S(1)}, u32[]{:S(2)}, u32[]{:S(2)}) %collective-permute-start.1) | collective-permute-done | bytes 98336 | tf_op jit(solution)/shard_map/ppermute | solution.py:95
  16.2 2.1 %shard_map.107 = (f32[128,1536]{1,0:T(8,128)S(1)}, bf16[16,1536]{1,0:T(8,128)(2,1)S(1)}, bf16[768,1536]{1,0:T(8,128)(2,1)S(1)}) custom-call(bf16[144,768]{1,0:T(8,128)(2,1)S(1)} %get-tuple-element.53.z, bf16[768,3072]{1,0:T(8,128)(2,1)} %w.3), custom_call_target="tpu_custom_call" | custom-call | flops 10000000000 | bytes 1 | tf_op jit(solution)/shard_map/pallas_call | solution.py:483
  18.4 1.6 %collective-permute-start.4 = (bf16[144,1664]{1,0:T(8,128)(2,1)S(1)}, bf16[144,1664]{1,0:T(8,128)(2,1)S(1)}, u32[]{:S(2)}, u32[]{:S(2)}) collective-permute-start(bf16[144,1664]{1,0:T(8,128)(2,1)S(1)} %get-tuple-element.59.refs_11_.sent.first_sent), channel_id=1, source_target_pairs={{0,2},{1,3},{2,0},{3,1},{4,6},{5,7},{6,4},{7,5},{8,10},{9,11},{10,... | collective-permute-start | bytes 1437704 | tf_op jit(solution)/shard_map/ppermute | solution.py:95
  20.0 3.4 %collective-permute-done.6.refs_6_ = bf16[64,768]{1,0:T(8,128)(2,1)S(1)} collective-permute-done((bf16[64,768]{1,0:T(8,128)(2,1)S(1)}, bf16[64,768]{1,0:T(8,128)(2,1)S(1)}, u32[]{:S(2)}, u32[]{:S(2)}) %collective-permute-start.6) | collective-permute-done | bytes 98336 | tf_op jit(solution)/shard_map/ppermute | solution.py:95
  24.9 1.3 %collective-permute-done.8.came = bf16[128,1664]{1,0:T(8,128)(2,1)S(1)} collective-permute-done((bf16[128,1664]{1,0:T(8,128)(2,1)S(1)}, bf16[128,1664]{1,0:T(8,128)(2,1)S(1)}, u32[]{:S(2)}, u32[]{:S(2)}) %collective-permute-start.8) | collective-permute-done | bytes 426016 | tf_op jit(solution)/shard_map/ppermute | solution.py:95
  26.3 1.6 %collective-permute-start.13 = (bf16[128,1664]{1,0:T(8,128)(2,1)S(1)}, bf16[128,1664]{1,0:T(8,128)(2,1)S(1)}, u32[]{:S(2)}, u32[]{:S(2)}) collective-permute-start(bf16[128,1664]{1,0:T(8,128)(2,1)S(1)} %get-tuple-element.67._.refs_1_.sent), channel_id=1, source_target_pairs={{0,2},{1,3},{2,0},{3,1},{4,6},{5,7},{6,4},{7,5},{8,10},{9,11},{10,... | collective-permute-start | bytes 1277960 | tf_op jit(solution)/shard_map/ppermute | solution.py:95
  27.9 2.4 %shard_map.112.refs_0_.w = bf16[3072,768]{1,0:T(8,128)(2,1)S(1)} custom-call(bf16[3072,768]{1,0:T(8,128)(2,1)} %source.1, bf16[128,1664]{1,0:T(8,128)(2,1)S(1)} %get-tuple-element.67._.refs_1_.sent), custom_call_target="tpu_custom_call" | custom-call | flops 1 | bytes 1 | tf_op jit(solution)/shard_map/pallas_call | solution.py:483
  30.3 2.0 %collective-permute-done.4.came.first_came = bf16[144,1664]{1,0:T(8,128)(2,1)S(1)} collective-permute-done((bf16[144,1664]{1,0:T(8,128)(2,1)S(1)}, bf16[144,1664]{1,0:T(8,128)(2,1)S(1)}, u32[]{:S(2)}, u32[]{:S(2)}) %collective-permute-start.4) | collective-permute-done | bytes 479264 | tf_op jit(solution)/shard_map/ppermute | solution.py:95
  33.6 1.2 %collective-permute-done.9.act = bf16[128,1536]{1,0:T(8,128)(2,1)S(1)} collective-permute-done((bf16[128,1536]{1,0:T(8,128)(2,1)S(1)}, bf16[128,1536]{1,0:T(8,128)(2,1)S(1)}, u32[]{:S(2)}, u32[]{:S(2)}) %collective-permute-start.9) | collective-permute-done | bytes 393248 | tf_op jit(solution)/shard_map/ppermute | solution.py:95
  35.6 6.8 %collective-permute-start.10 = (bf16[64,768]{1,0:T(8,128)(2,1)S(1)}, bf16[64,768]{1,0:T(8,128)(2,1)S(1)}, u32[]{:S(2)}, u32[]{:S(2)}) collective-permute-start(bf16[64,768]{1,0:T(8,128)(2,1)S(1)} %get-tuple-element.72.refs_1_), channel_id=1, source_target_pairs={{0,4},{4,0},{8,12},{12,8},{1,5},{5,1},{9,13},{13,9},{2,6},{6,2},{1... | collective-permute-start | bytes 294920 | tf_op jit(solution)/shard_map/ppermute | solution.py:95
  43.5 1.4 %collective-permute-start.12 = (bf16[64,768]{1,0:T(8,128)(2,1)S(1)}, bf16[64,768]{1,0:T(8,128)(2,1)S(1)}, u32[]{:S(2)}, u32[]{:S(2)}) collective-permute-start(bf16[64,768]{1,0:T(8,128)(2,1)S(1)} %get-tuple-element.74.refs_3_), channel_id=1, source_target_pairs={{0,12},{4,8},{8,4},{12,0},{1,13},{5,9},{9,5},{13,1},{2,14},{6,10},... | collective-permute-start | bytes 294920 | tf_op jit(solution)/shard_map/ppermute | solution.py:95
  46.2 1.2 %collective-permute-done.14.act = bf16[128,1536]{1,0:T(8,128)(2,1)S(1)} collective-permute-done((bf16[128,1536]{1,0:T(8,128)(2,1)S(1)}, bf16[128,1536]{1,0:T(8,128)(2,1)S(1)}, u32[]{:S(2)}, u32[]{:S(2)}) %collective-permute-start.14) | collective-permute-done | bytes 393248 | tf_op jit(solution)/shard_map/ppermute | solution.py:95
  48.2 2.9 %collective-permute-start.15 = (bf16[64,768]{1,0:T(8,128)(2,1)S(1)}, bf16[64,768]{1,0:T(8,128)(2,1)S(1)}, u32[]{:S(2)}, u32[]{:S(2)}) collective-permute-start(bf16[64,768]{1,0:T(8,128)(2,1)S(1)} %get-tuple-element.78), channel_id=1, source_target_pairs={{0,4},{4,0},{8,12},{12,8},{1,5},{5,1},{9,13},{13,9},{2,6},{6,2},{1... | collective-permute-start | bytes 294920 | tf_op jit(solution)/shard_map/ppermute | solution.py:95
  52.2 1.4 %collective-permute-start.17 = (bf16[64,768]{1,0:T(8,128)(2,1)S(1)}, bf16[64,768]{1,0:T(8,128)(2,1)S(1)}, u32[]{:S(2)}, u32[]{:S(2)}) collective-permute-start(bf16[64,768]{1,0:T(8,128)(2,1)S(1)} %get-tuple-element.80), channel_id=1, source_target_pairs={{0,12},{4,8},{8,4},{12,0},{1,13},{5,9},{9,5},{13,1},{2,14},{6,10},... | collective-permute-start | bytes 294920 | tf_op jit(solution)/shard_map/ppermute | solution.py:95
  54.3 1.6 %collective-permute-done.15.refs_5_ = bf16[64,768]{1,0:T(8,128)(2,1)S(1)} collective-permute-done((bf16[64,768]{1,0:T(8,128)(2,1)S(1)}, bf16[64,768]{1,0:T(8,128)(2,1)S(1)}, u32[]{:S(2)}, u32[]{:S(2)}) %collective-permute-start.15) | collective-permute-done | bytes 98336 | tf_op jit(solution)/shard_map/ppermute | solution.py:95
  55.9 5.9 %collective-permute-done.16.refs_6_ = bf16[64,768]{1,0:T(8,128)(2,1)S(1)} collective-permute-done((bf16[64,768]{1,0:T(8,128)(2,1)S(1)}, bf16[64,768]{1,0:T(8,128)(2,1)S(1)}, u32[]{:S(2)}, u32[]{:S(2)}) %collective-permute-start.16) | collective-permute-done | bytes 98336 | tf_op jit(solution)/shard_map/ppermute | solution.py:95
  63.6 1.5 %collective-permute-start.19 = (f32[72,128]{1,0:T(8,128)S(1)}, f32[72,128]{1,0:T(8,128)S(1)}, u32[]{:S(2)}, u32[]{:S(2)}) collective-permute-start(f32[72,128]{1,0:T(8,128)S(1)} %shard_map.122.mine), channel_id=1, source_target_pairs={{0,2},{1,3},{2,0},{3,1},{16,18},{17,19},{18,16},{19,17},{4,6},{5,7... | collective-permute-start | bytes 110600 | tf_op jit(solution)/shard_map/ppermute | solution.py:95
  65.2 1.5 %collective-permute-start.20 = (f32[72,128]{1,0:T(8,128)S(1)}, f32[72,128]{1,0:T(8,128)S(1)}, u32[]{:S(2)}, u32[]{:S(2)}) collective-permute-start(f32[72,128]{1,0:T(8,128)S(1)} %shard_map.122.mine), channel_id=1, source_target_pairs={{0,16},{1,17},{2,18},{3,19},{16,0},{17,1},{18,2},{19,3},{4,20},{5,... | collective-permute-start | bytes 110600 | tf_op jit(solution)/shard_map/ppermute | solution.py:95
  67.8 1.7 %collective-permute-done.20.other = f32[72,128]{1,0:T(8,128)S(1)} collective-permute-done((f32[72,128]{1,0:T(8,128)S(1)}, f32[72,128]{1,0:T(8,128)S(1)}, u32[]{:S(2)}, u32[]{:S(2)}) %collective-permute-start.20) | collective-permute-done | bytes 36896 | tf_op jit(solution)/shard_map/ppermute | solution.py:95
  69.5 2.0 %collective-permute-done.21.other_y = f32[72,128]{1,0:T(8,128)S(1)} collective-permute-done((f32[72,128]{1,0:T(8,128)S(1)}, f32[72,128]{1,0:T(8,128)S(1)}, u32[]{:S(2)}, u32[]{:S(2)}) %collective-permute-start.21) | collective-permute-done | bytes 36896 | tf_op jit(solution)/shard_map/ppermute | solution.py:95
  (44 shorter events, 14.6 us)
Async XLA Ops:
  1.5 12.1 %collective-permute-start = (bf16[64,768]{1,0:T(8,128)(2,1)S(1)}, bf16[64,768]{1,0:T(8,128)(2,1)S(1)}, u32[]{:S(2)}, u32[]{:S(2)}) collective-permute-start(bf16[64,768]{1,0:T(8,128)(2,1)S(1)} %shard_map.105.refs_0_), channel_id=1, source_target_pairs={{0,4},{4,0},{8,12},{12,8},{1,5},{5,1},{9,13},{13,9},{2,6},{6,2},{1... | collective-permute-start | bytes 294920 | tf_op jit(solution)/shard_map/ppermute | solution.py:95
  4.6 10.7 %collective-permute-start.1 = (bf16[64,768]{1,0:T(8,128)(2,1)S(1)}, bf16[64,768]{1,0:T(8,128)(2,1)S(1)}, u32[]{:S(2)}, u32[]{:S(2)}) collective-permute-start(bf16[64,768]{1,0:T(8,128)(2,1)S(1)} %shard_map.105.refs_0_), channel_id=1, source_target_pairs={{0,8},{4,12},{8,0},{12,4},{1,9},{5,13},{9,1},{13,5},{2,10},{6,14},... | collective-permute-start | bytes 294920 | tf_op jit(solution)/shard_map/ppermute | solution.py:95
  7.2 8.1 %collective-permute-start.2 = (bf16[64,768]{1,0:T(8,128)(2,1)S(1)}, bf16[64,768]{1,0:T(8,128)(2,1)S(1)}, u32[]{:S(2)}, u32[]{:S(2)}) collective-permute-start(bf16[64,768]{1,0:T(8,128)(2,1)S(1)} %shard_map.105.refs_0_), channel_id=1, source_target_pairs={{0,12},{4,8},{8,4},{12,0},{1,13},{5,9},{9,5},{13,1},{2,14},{6,10},... | collective-permute-start | bytes 294920 | tf_op jit(solution)/shard_map/ppermute | solution.py:95
  9.2 10.9 %collective-permute-start.5 = (bf16[64,768]{1,0:T(8,128)(2,1)S(1)}, bf16[64,768]{1,0:T(8,128)(2,1)S(1)}, u32[]{:S(2)}, u32[]{:S(2)}) collective-permute-start(bf16[64,768]{1,0:T(8,128)(2,1)S(1)} %get-tuple-element.62.refs_4_), channel_id=1, source_target_pairs={{0,4},{4,0},{8,12},{12,8},{1,5},{5,1},{9,13},{13,9},{2,6},{6,2},{1... | collective-permute-start | bytes 294920 | tf_op jit(solution)/shard_map/ppermute | solution.py:95
  10.1 13.4 %collective-permute-start.6 = (bf16[64,768]{1,0:T(8,128)(2,1)S(1)}, bf16[64,768]{1,0:T(8,128)(2,1)S(1)}, u32[]{:S(2)}, u32[]{:S(2)}) collective-permute-start(bf16[64,768]{1,0:T(8,128)(2,1)S(1)} %get-tuple-element.62.refs_4_), channel_id=1, source_target_pairs={{0,8},{4,12},{8,0},{12,4},{1,9},{5,13},{9,1},{13,5},{2,10},{6,14},... | collective-permute-start | bytes 294920 | tf_op jit(solution)/shard_map/ppermute | solution.py:95
  13.6 9.9 %collective-permute-start.7 = (bf16[64,768]{1,0:T(8,128)(2,1)S(1)}, bf16[64,768]{1,0:T(8,128)(2,1)S(1)}, u32[]{:S(2)}, u32[]{:S(2)}) collective-permute-start(bf16[64,768]{1,0:T(8,128)(2,1)S(1)} %get-tuple-element.62.refs_4_), channel_id=1, source_target_pairs={{0,12},{4,8},{8,4},{12,0},{1,13},{5,9},{9,5},{13,1},{2,14},{6,10},... | collective-permute-start | bytes 294920 | tf_op jit(solution)/shard_map/ppermute | solution.py:95
  16.2 2.1 %collective-permute-start.3 = (bf16[144,1664]{1,0:T(8,128)(2,1)S(1)}, bf16[144,1664]{1,0:T(8,128)(2,1)S(1)}, u32[]{:S(2)}, u32[]{:S(2)}) collective-permute-start(bf16[144,1664]{1,0:T(8,128)(2,1)S(1)} %get-tuple-element.56), channel_id=1, source_target_pairs={{0,1},{1,0},{2,3},{3,2},{4,5},{5,4},{6,7},{7,6},{8,9},{9,8},{10,11... | collective-permute-start | bytes 1437704 | tf_op jit(solution)/shard_map/ppermute | solution.py:95
  18.4 13.8 %collective-permute-start.4 = (bf16[144,1664]{1,0:T(8,128)(2,1)S(1)}, bf16[144,1664]{1,0:T(8,128)(2,1)S(1)}, u32[]{:S(2)}, u32[]{:S(2)}) collective-permute-start(bf16[144,1664]{1,0:T(8,128)(2,1)S(1)} %get-tuple-element.59.refs_11_.sent.first_sent), channel_id=1, source_target_pairs={{0,2},{1,3},{2,0},{3,1},{4,6},{5,7},{6,4},{7,5},{8,10},{9,11},{10,... | collective-permute-start | bytes 1437704 | tf_op jit(solution)/shard_map/ppermute | solution.py:95
  24.3 1.8 %collective-permute-start.8 = (bf16[128,1664]{1,0:T(8,128)(2,1)S(1)}, bf16[128,1664]{1,0:T(8,128)(2,1)S(1)}, u32[]{:S(2)}, u32[]{:S(2)}) collective-permute-start(bf16[128,1664]{1,0:T(8,128)(2,1)S(1)} %get-tuple-element.66), channel_id=1, source_target_pairs={{0,1},{1,0},{2,3},{3,2},{4,5},{5,4},{6,7},{7,6},{8,9},{9,8},{10,11... | collective-permute-start | bytes 1277960 | tf_op jit(solution)/shard_map/ppermute | solution.py:95
  26.3 18.6 %collective-permute-start.13 = (bf16[128,1664]{1,0:T(8,128)(2,1)S(1)}, bf16[128,1664]{1,0:T(8,128)(2,1)S(1)}, u32[]{:S(2)}, u32[]{:S(2)}) collective-permute-start(bf16[128,1664]{1,0:T(8,128)(2,1)S(1)} %get-tuple-element.67._.refs_1_.sent), channel_id=1, source_target_pairs={{0,2},{1,3},{2,0},{3,1},{4,6},{5,7},{6,4},{7,5},{8,10},{9,11},{10,... | collective-permute-start | bytes 1277960 | tf_op jit(solution)/shard_map/ppermute | solution.py:95
  33.0 1.8 %collective-permute-start.9 = (bf16[128,1536]{1,0:T(8,128)(2,1)S(1)}, bf16[128,1536]{1,0:T(8,128)(2,1)S(1)}, u32[]{:S(2)}, u32[]{:S(2)}) collective-permute-start(bf16[128,1536]{1,0:T(8,128)(2,1)S(1)} %shard_map.113.act), channel_id=1, source_target_pairs={{0,1},{1,0},{2,3},{3,2},{4,5},{5,4},{6,7},{7,6},{8,9},{9,8},{10,11... | collective-permute-start | bytes 1179656 | tf_op jit(solution)/shard_map/ppermute | solution.py:95
  35.6 16.7 %collective-permute-start.10 = (bf16[64,768]{1,0:T(8,128)(2,1)S(1)}, bf16[64,768]{1,0:T(8,128)(2,1)S(1)}, u32[]{:S(2)}, u32[]{:S(2)}) collective-permute-start(bf16[64,768]{1,0:T(8,128)(2,1)S(1)} %get-tuple-element.72.refs_1_), channel_id=1, source_target_pairs={{0,4},{4,0},{8,12},{12,8},{1,5},{5,1},{9,13},{13,9},{2,6},{6,2},{1... | collective-permute-start | bytes 294920 | tf_op jit(solution)/shard_map/ppermute | solution.py:95
  42.4 11.9 %collective-permute-start.11 = (bf16[64,768]{1,0:T(8,128)(2,1)S(1)}, bf16[64,768]{1,0:T(8,128)(2,1)S(1)}, u32[]{:S(2)}, u32[]{:S(2)}) collective-permute-start(bf16[64,768]{1,0:T(8,128)(2,1)S(1)} %get-tuple-element.73.refs_2_), channel_id=1, source_target_pairs={{0,8},{4,12},{8,0},{12,4},{1,9},{5,13},{9,1},{13,5},{2,10},{6,14},... | collective-permute-start | bytes 294920 | tf_op jit(solution)/shard_map/ppermute | solution.py:95
  43.5 10.8 %collective-permute-start.12 = (bf16[64,768]{1,0:T(8,128)(2,1)S(1)}, bf16[64,768]{1,0:T(8,128)(2,1)S(1)}, u32[]{:S(2)}, u32[]{:S(2)}) collective-permute-start(bf16[64,768]{1,0:T(8,128)(2,1)S(1)} %get-tuple-element.74.refs_3_), channel_id=1, source_target_pairs={{0,12},{4,8},{8,4},{12,0},{1,13},{5,9},{9,5},{13,1},{2,14},{6,10},... | collective-permute-start | bytes 294920 | tf_op jit(solution)/shard_map/ppermute | solution.py:95
  45.6 1.8 %collective-permute-start.14 = (bf16[128,1536]{1,0:T(8,128)(2,1)S(1)}, bf16[128,1536]{1,0:T(8,128)(2,1)S(1)}, u32[]{:S(2)}, u32[]{:S(2)}) collective-permute-start(bf16[128,1536]{1,0:T(8,128)(2,1)S(1)} %shard_map.116.act), channel_id=1, source_target_pairs={{0,1},{1,0},{2,3},{3,2},{4,5},{5,4},{6,7},{7,6},{8,9},{9,8},{10,11... | collective-permute-start | bytes 1179656 | tf_op jit(solution)/shard_map/ppermute | solution.py:95
  46.2 16.2 %copy-start = (f32[128,64]{0,1:T(8,128)S(1)}, f32[128,64]{0,1:T(8,128)}, u32[]{:S(2)}) copy-start(f32[128,64]{0,1:T(8,128)} %param.15) | copy-start | bytes 98308
  46.2 16.2 %copy-start.1 = (f32[8,128]{1,0:T(8,128)S(1)}, f32[8,128]{1,0:T(8,128)}, u32[]{:S(2)}) copy-start(f32[8,128]{1,0:T(8,128)} %constant.2.clone.alphas) | copy-start | bytes 12292
  48.2 7.7 %collective-permute-start.15 = (bf16[64,768]{1,0:T(8,128)(2,1)S(1)}, bf16[64,768]{1,0:T(8,128)(2,1)S(1)}, u32[]{:S(2)}, u32[]{:S(2)}) collective-permute-start(bf16[64,768]{1,0:T(8,128)(2,1)S(1)} %get-tuple-element.78), channel_id=1, source_target_pairs={{0,4},{4,0},{8,12},{12,8},{1,5},{5,1},{9,13},{13,9},{2,6},{6,2},{1... | collective-permute-start | bytes 294920 | tf_op jit(solution)/shard_map/ppermute | solution.py:95
  51.1 10.7 %collective-permute-start.16 = (bf16[64,768]{1,0:T(8,128)(2,1)S(1)}, bf16[64,768]{1,0:T(8,128)(2,1)S(1)}, u32[]{:S(2)}, u32[]{:S(2)}) collective-permute-start(bf16[64,768]{1,0:T(8,128)(2,1)S(1)} %get-tuple-element.79), channel_id=1, source_target_pairs={{0,8},{4,12},{8,0},{12,4},{1,9},{5,13},{9,1},{13,5},{2,10},{6,14},... | collective-permute-start | bytes 294920 | tf_op jit(solution)/shard_map/ppermute | solution.py:95
  52.2 9.5 %collective-permute-start.17 = (bf16[64,768]{1,0:T(8,128)(2,1)S(1)}, bf16[64,768]{1,0:T(8,128)(2,1)S(1)}, u32[]{:S(2)}, u32[]{:S(2)}) collective-permute-start(bf16[64,768]{1,0:T(8,128)(2,1)S(1)} %get-tuple-element.80), channel_id=1, source_target_pairs={{0,12},{4,8},{8,4},{12,0},{1,13},{5,9},{9,5},{13,1},{2,14},{6,10},... | collective-permute-start | bytes 294920 | tf_op jit(solution)/shard_map/ppermute | solution.py:95
  62.4 1.3 %collective-permute-start.18 = (f32[72,128]{1,0:T(8,128)S(1)}, f32[72,128]{1,0:T(8,128)S(1)}, u32[]{:S(2)}, u32[]{:S(2)}) collective-permute-start(f32[72,128]{1,0:T(8,128)S(1)} %get-tuple-element.85.left), channel_id=1, source_target_pairs={{0,1},{1,0},{2,3},{3,2},{4,5},{5,4},{6,7},{7,6},{8,9},{9,8},{10,11... | collective-permute-start | bytes 110600 | tf_op jit(solution)/shard_map/ppermute | solution.py:95
  63.6 4.2 %collective-permute-start.19 = (f32[72,128]{1,0:T(8,128)S(1)}, f32[72,128]{1,0:T(8,128)S(1)}, u32[]{:S(2)}, u32[]{:S(2)}) collective-permute-start(f32[72,128]{1,0:T(8,128)S(1)} %shard_map.122.mine), channel_id=1, source_target_pairs={{0,2},{1,3},{2,0},{3,1},{16,18},{17,19},{18,16},{19,17},{4,6},{5,7... | collective-permute-start | bytes 110600 | tf_op jit(solution)/shard_map/ppermute | solution.py:95
  65.2 4.3 %collective-permute-start.20 = (f32[72,128]{1,0:T(8,128)S(1)}, f32[72,128]{1,0:T(8,128)S(1)}, u32[]{:S(2)}, u32[]{:S(2)}) collective-permute-start(f32[72,128]{1,0:T(8,128)S(1)} %shard_map.122.mine), channel_id=1, source_target_pairs={{0,16},{1,17},{2,18},{3,19},{16,0},{17,1},{18,2},{19,3},{4,20},{5,... | collective-permute-start | bytes 110600 | tf_op jit(solution)/shard_map/ppermute | solution.py:95
  66.6 4.9 %collective-permute-start.21 = (f32[72,128]{1,0:T(8,128)S(1)}, f32[72,128]{1,0:T(8,128)S(1)}, u32[]{:S(2)}, u32[]{:S(2)}) collective-permute-start(f32[72,128]{1,0:T(8,128)S(1)} %shard_map.122.mine), channel_id=1, source_target_pairs={{0,18},{1,19},{2,16},{3,17},{16,2},{17,3},{18,0},{19,1},{4,22},{5,... | collective-permute-start | bytes 110600 | tf_op jit(solution)/shard_map/ppermute | solution.py:95

commit v6 on v5

--- a/solution.py
+++ b/solution.py
@@ -217,7 +217,8 @@
     gathers, refs = refs[:CHUNKS], refs[CHUNKS:]
     spreads, refs = refs[:CHUNKS], refs[CHUNKS:]
     texts, refs = refs[:CHUNKS], refs[CHUNKS:]
-    held, tokens, mod, weight, rows_out, ends_out, slots_out, video_out, table, sems, small = refs
+    held, kept, tokens, mod, weight, rows_out, ends_out, slots_out, video_out = refs[:9]
+    table, sems, small = refs[9:]
     core = lax.axis_index("narrow") % 2
     sources = (table_in, mod_in, out_weight, hidden)
     copies = [
@@ -226,7 +227,7 @@
     ]
     for copy in copies:
         copy.start()
-    big = load_half(w, 1 - core, held, sems)
+    big = load_half(w, 1 - core, held, sems.at[0]) + load_half(w, core, kept, sems.at[1])
 
     copies[0].wait()
     ranks, counts, others, offset, largest_offset = layout(table)
@@ -273,8 +274,8 @@
         copy.wait()
 
 
-def expand_sent_kernel(k, text, mod, place, *refs):
-    pieces, (w, sums, ends) = refs[: 4 * (k + 1)], refs[4 * (k + 1) : 4 * (k + 1) + 3]
+def expand_sent_kernel(k, count, text, mod, place, *refs):
+    pieces, (w, sums, ends) = refs[:count], refs[count : count + 3]
     z_out, sent_out, side_out = refs[-3:]
     core = lax.axis_index("narrow") % 2
     units = w.shape[1]
@@ -308,20 +309,20 @@
         sent_out[rows:, units:] = ends[...]
 
 
-def first_kept_kernel(z, w, kept_out, sums_out, held, sems):
+def expand_kept_kernel(k, z, w, *refs):
+    kept_out = refs[-1 if k else -2]
     core = lax.axis_index("narrow") % 2
     rows = kept_out.shape[0]
-    for t, copy in enumerate(load_half(w, core, held, sems)):
-        copy.wait()
-        columns = slice(t * TILE, (t + 1) * TILE)
-        product = jnp.dot(z[...], held[:, columns], preferred_element_type=F32)
+    for t in range(0, w.shape[1], TILE):
+        columns = slice(t, t + TILE)
+        product = jnp.dot(z[...], w[:, columns], preferred_element_type=F32)
         kept_out[:, columns] = product[:rows]
-        sums_out[:, columns] = rows_of(product[rows:], core)
-
-
-def kept_kernel(z, w, kept_out):
-    for t in range(0, w.shape[1], TILE):
-        kept_out[:, t : t + TILE] = jnp.dot(z[...], w[:, t : t + TILE], preferred_element_type=F32)
+        if k == 0:
+            refs[-1][:, columns] = rows_of(product[rows:], core)
+
+
+def pair_kernel(first, second, _, out):
+    out[...] = jnp.concatenate([first[...], second[...]], 0)
 
 
 def merge_kernel(k, kept, side, came, sums, ends, total_out, sent_out):
@@ -520,6 +521,7 @@
         + [((2 * size_of(k), 128), F32) for k in chunks]
         + [
             ((features, units), BF16),
+            ((features, units), BF16),
             (hidden.shape, BF16),
             (modulation.shape, F32),
             ((width, features), BF16),
@@ -538,7 +540,7 @@
         "aaaaa",
         [
             pltpu.SMEM(split_table.shape, jnp.int32),
-            pltpu.SemaphoreType.DMA((tiles,)),
+            pltpu.SemaphoreType.DMA((2, tiles)),
             pltpu.SemaphoreType.DMA((4,)),
         ],
     )
@@ -546,53 +548,59 @@
     gathers, made = made[:CHUNKS], made[CHUNKS:]
     spreads, made = made[:CHUNKS], made[CHUNKS:]
     texts, made = made[:CHUNKS], made[CHUNKS:]
-    held_sent, tokens, mod, out_weight, rows_in, ends_mine, slots, video = made
-    for piece in later:
-        arrived.append([piece] + z_swaps(piece))
+    held_sent, held_kept, tokens, mod, out_weight, rows_in, ends_mine, slots, video = made
+    neighbours = [(piece, swap(piece, "wide", 1, 4)) for piece in later]
 
     merged = []
     before = []
     for k in chunks:
         rows = 2 * size_of(k)
         sent_rows = rows + (16 if k == 0 else 0)
-        pieces = [piece for phase in arrived[: k + 1] for piece in phase]
+        pieces = [piece for phase in arrived for piece in phase]
         z, sent, side = call(
-            functools.partial(expand_sent_kernel, k),
+            functools.partial(expand_sent_kernel, k, len(pieces)),
             [((sent_rows, features), BF16), ((sent_rows, payload), BF16), ((rows, 128), BF16)],
             [texts[k], mod, gathers[k], *pieces, held_sent, rows_in, ends_mine, *before],
             "vvv" + "v" * len(pieces) + "vvv" + "a" * len(before),
             weight=LONG,
         )
         came = swap(sent, "narrow", 1, 4)
-        if k == 0:
-            kept, sums, held_kept = call(
-                first_kept_kernel,
-                [((rows, units), F32), ((16, units), BF16), ((features, units), BF16)],
-                [z, in_place(expand_weight)],
-                "va",
-                [pltpu.SemaphoreType.DMA((tiles,))],
-                weight=LONG,
+        pair = []
+        if k + 1 < CHUNKS:
+            pair = call(
+                pair_kernel,
+                [((2 * size_of(k + 1), features), BF16)],
+                [*neighbours[k], z],
+                "vva",
             )
-        else:
-            (kept,) = call(kept_kernel, [((rows, units), F32)], [z, held_kept], "vv", weight=LONG)
+            arrived.append([*pair, swap(*pair, "wide", 2, 4)])
+        kept, *sums_made = call(
+            functools.partial(expand_kept_kernel, k),
+            [((rows, units), F32)] + ([((16, units), BF16)] if k == 0 else []),
+            [z, held_kept, *pair],
+            "vv" + "a" * len(pair),
+            weight=LONG,
+        )
+        sums = sums_made[0] if k == 0 else sums
         total, sent = call(
             functools.partial(merge_kernel, k),
             [((rows, units), F32), ((sent_rows, payload), BF16)],
             [kept, side, came, sums, ends_mine],
             "vvvvv",
         )
-        before = [sent]
+        if k == 0:
+            (held_out,) = call(
+                hold_kernel,
+                [(contract_weight.shape, BF16)],
+                [in_place(contract_weight), sent],
+                "aa",
+                [pltpu.SemaphoreType.DMA((4,))],
+            )
+        before = [sent, held_out]
         merged.append((total, sent, swap(sent, "narrow", 2, 4)))
 
-    (held_out,) = call(
-        hold_kernel,
-        [(contract_weight.shape, BF16)],
-        [in_place(contract_weight), merged[-1][1]],
-        "aa",
-        [pltpu.SemaphoreType.DMA((4,))],
-    )
     returned = []
-    before = [held_out]
+    before = []
     first = merged[0][1:]
     for k in chunks:
         rows = 2 * size_of(k)

time: 72.4 us -> 68.2 us (0.942)
  starting transfers between devices: 31.9 us -> 24.1 us
  waiting for transfers between devices: 23 us -> 27.4 us
  Pallas kernels: 15.8 us -> 14.9 us
    ppermute x22 -> x21, starting transfers between devices: 31.9 us -> 24.1 us  [swap(): return lax.ppermute(array, axis, [(i, i ^ distance) for i in range(size)])]
    ppermute x22 -> x21, waiting for transfers between devices: 23 us -> 27.4 us  [swap(): return lax.ppermute(array, axis, [(i, i ^ distance) for i in range(size)])]
    pallas_call x20 -> x21, Pallas kernels: 15.8 us -> 14.9 us  [call(): pl.pallas_call(kernel, out_shape=[jax.ShapeDtypeStruct(shape, dtype) for...]
  transfers between devices with their start and end apart: 22 -> 21, of which waited for: 11 -> 12; matrix products, arithmetic and copies ran while one was open for 0% -> 0% of each run, Pallas kernels for 19% -> 19%
where the time goes in v6:
time: 68.2 us; the launch traced here: 68 us
  waiting for transfers between devices  27.4 us (40%)
  starting transfers between devices  24.1 us (35%)
  Pallas kernels  14.9 us (22%)
  between operations  1.51 us (2%)
    ppermute x21, waiting for transfers between devices, swap(): return lax.ppermute(array, axis, [(i, i ^ distance) for i in range(size)])  27.4 us
    ppermute x21, starting transfers between devices, swap(): return lax.ppermute(array, axis, [(i, i ^ distance) for i in range(size)])  24.1 us
    pallas_call x21, Pallas kernels, call(): pl.pallas_call(kernel, out_shape=[jax.ShapeDtypeStruct(shape, dtype) for...  14.9 us
  transfers between devices with their start and end apart: 21, of which 12 were waited for; matrix products, arithmetic and copies ran while one was open for 0% of the time, Pallas kernels for 19%

profile of v6, /device:TPU:0, one launch (start us, length us, event | category | flops | bytes accessed | tf_op | source)
XLA Modules:
  0.0 68.0 jit_solution(16706746592163356897)
XLA Ops:
  1.5 3.1 %collective-permute-start = (bf16[64,768]{1,0:T(8,128)(2,1)S(1)}, bf16[64,768]{1,0:T(8,128)(2,1)S(1)}, u32[]{:S(2)}, u32[]{:S(2)}) collective-permute-start(bf16[64,768]{1,0:T(8,128)(2,1)S(1)} %shard_map.105.refs_0_), channel_id=1, source_target_pairs={{0,4},{4,0},{8,12},{12,8},{1,5},{5,1},{9,13},{13,9},{2,6},{6,2},{1... | collective-permute-start | bytes 294920 | tf_op jit(solution)/shard_map/ppermute | solution.py:95
  4.6 2.6 %collective-permute-start.1 = (bf16[64,768]{1,0:T(8,128)(2,1)S(1)}, bf16[64,768]{1,0:T(8,128)(2,1)S(1)}, u32[]{:S(2)}, u32[]{:S(2)}) collective-permute-start(bf16[64,768]{1,0:T(8,128)(2,1)S(1)} %shard_map.105.refs_0_), channel_id=1, source_target_pairs={{0,8},{4,12},{8,0},{12,4},{1,9},{5,13},{9,1},{13,5},{2,10},{6,14},... | collective-permute-start | bytes 294920 | tf_op jit(solution)/shard_map/ppermute | solution.py:95
  7.2 2.6 %shard_map.104 = (bf16[64,768]{1,0:T(8,128)(2,1)S(1)}, bf16[128,256]{1,0:T(8,128)(2,1)S(1)}, bf16[128,512]{1,0:T(8,128)(2,1)S(1)}, bf16[256,128]{1,0:T(8,128)(2,...) custom-call(s32[4]{0:T(128)} %table_in.1, ...), custom_call_target="tpu_custom_call" | custom-call | flops 1 | bytes 1 | tf_op jit(solution)/shard_map/pallas_call | solution.py:484
  10.8 4.3 %collective-permute-done.1.refs_2_ = bf16[64,768]{1,0:T(8,128)(2,1)S(1)} collective-permute-done((bf16[64,768]{1,0:T(8,128)(2,1)S(1)}, bf16[64,768]{1,0:T(8,128)(2,1)S(1)}, u32[]{:S(2)}, u32[]{:S(2)}) %collective-permute-start.1) | collective-permute-done | bytes 98336 | tf_op jit(solution)/shard_map/ppermute | solution.py:95
  16.2 2.5 %collective-permute-start.6 = (bf16[128,768]{1,0:T(8,128)(2,1)S(1)}, bf16[128,768]{1,0:T(8,128)(2,1)S(1)}, u32[]{:S(2)}, u32[]{:S(2)}) collective-permute-start(bf16[128,768]{1,0:T(8,128)(2,1)S(1)} %shard_map.107.refs_0_.refs_4_), channel_id=1, source_target_pairs={{0,8},{4,12},{8,0},{12,4},{1,9},{5,13},{9,1},{13,5},{2,10},{6,14},... | collective-permute-start | bytes 589832 | tf_op jit(solution)/shard_map/ppermute | solution.py:95
  19.4 1.6 %collective-permute-start.5 = (bf16[144,1664]{1,0:T(8,128)(2,1)S(1)}, bf16[144,1664]{1,0:T(8,128)(2,1)S(1)}, u32[]{:S(2)}, u32[]{:S(2)}) collective-permute-start(bf16[144,1664]{1,0:T(8,128)(2,1)S(1)} %get-tuple-element.61._.refs_9_.sent.first_sent), channel_id=1, source_target_pairs={{0,2},{1,3},{2,0},{3,1},{4,6},{5,7},{6,4},{7,5},{8,10},{9,11},{10,... | collective-permute-start | bytes 1437704 | tf_op jit(solution)/shard_map/ppermute | solution.py:95
  21.0 2.4 %shard_map.110.refs_10_.w = bf16[3072,768]{1,0:T(8,128)(2,1)S(1)} custom-call(bf16[3072,768]{1,0:T(8,128)(2,1)} %source.1, bf16[144,1664]{1,0:T(8,128)(2,1)S(1)} %get-tuple-element.61._.refs_9_.sent.first_sent), custom_call_target="tpu_custom_call" | custom-call | flops 1 | bytes 1 | tf_op jit(solution)/shard_map/pallas_call | solution.py:484
  23.4 5.2 %collective-permute-done.6.refs_5_ = bf16[128,768]{1,0:T(8,128)(2,1)S(1)} collective-permute-done((bf16[128,768]{1,0:T(8,128)(2,1)S(1)}, bf16[128,768]{1,0:T(8,128)(2,1)S(1)}, u32[]{:S(2)}, u32[]{:S(2)}) %collective-permute-start.6) | collective-permute-done | bytes 196640 | tf_op jit(solution)/shard_map/ppermute | solution.py:95
  30.0 1.3 %collective-permute-done.7.came = bf16[128,1664]{1,0:T(8,128)(2,1)S(1)} collective-permute-done((bf16[128,1664]{1,0:T(8,128)(2,1)S(1)}, bf16[128,1664]{1,0:T(8,128)(2,1)S(1)}, u32[]{:S(2)}, u32[]{:S(2)}) %collective-permute-start.7) | collective-permute-done | bytes 426016 | tf_op jit(solution)/shard_map/ppermute | solution.py:95
  31.4 1.6 %collective-permute-start.12 = (bf16[128,1664]{1,0:T(8,128)(2,1)S(1)}, bf16[128,1664]{1,0:T(8,128)(2,1)S(1)}, u32[]{:S(2)}, u32[]{:S(2)}) collective-permute-start(bf16[128,1664]{1,0:T(8,128)(2,1)S(1)} %get-tuple-element.67.refs_0_.sent), channel_id=1, source_target_pairs={{0,2},{1,3},{2,0},{3,1},{4,6},{5,7},{6,4},{7,5},{8,10},{9,11},{10,... | collective-permute-start | bytes 1277960 | tf_op jit(solution)/shard_map/ppermute | solution.py:95
  34.3 1.2 %collective-permute-done.8.act = bf16[128,1536]{1,0:T(8,128)(2,1)S(1)} collective-permute-done((bf16[128,1536]{1,0:T(8,128)(2,1)S(1)}, bf16[128,1536]{1,0:T(8,128)(2,1)S(1)}, u32[]{:S(2)}, u32[]{:S(2)}) %collective-permute-start.8) | collective-permute-done | bytes 393248 | tf_op jit(solution)/shard_map/ppermute | solution.py:95
  37.1 1.8 %collective-permute-start.11 = (bf16[64,768]{1,0:T(8,128)(2,1)S(1)}, bf16[64,768]{1,0:T(8,128)(2,1)S(1)}, u32[]{:S(2)}, u32[]{:S(2)}) collective-permute-start(bf16[64,768]{1,0:T(8,128)(2,1)S(1)} %get-tuple-element.74.refs_3_), channel_id=1, source_target_pairs={{0,12},{4,8},{8,4},{12,0},{1,13},{5,9},{9,5},{13,1},{2,14},{6,10},... | collective-permute-start | bytes 294920 | tf_op jit(solution)/shard_map/ppermute | solution.py:95
  38.9 1.0 %collective-permute-start.9 = (bf16[64,768]{1,0:T(8,128)(2,1)S(1)}, bf16[64,768]{1,0:T(8,128)(2,1)S(1)}, u32[]{:S(2)}, u32[]{:S(2)}) collective-permute-start(bf16[64,768]{1,0:T(8,128)(2,1)S(1)} %get-tuple-element.72.refs_1_), channel_id=1, source_target_pairs={{0,4},{4,0},{8,12},{12,8},{1,5},{5,1},{9,13},{13,9},{2,6},{6,2},{1... | collective-permute-start | bytes 294920 | tf_op jit(solution)/shard_map/ppermute | solution.py:95
  39.9 3.5 %collective-permute-done.12.came = bf16[128,1664]{1,0:T(8,128)(2,1)S(1)} collective-permute-done((bf16[128,1664]{1,0:T(8,128)(2,1)S(1)}, bf16[128,1664]{1,0:T(8,128)(2,1)S(1)}, u32[]{:S(2)}, u32[]{:S(2)}) %collective-permute-start.12) | collective-permute-done | bytes 426016 | tf_op jit(solution)/shard_map/ppermute | solution.py:95
  44.7 1.2 %collective-permute-done.13.act = bf16[128,1536]{1,0:T(8,128)(2,1)S(1)} collective-permute-done((bf16[128,1536]{1,0:T(8,128)(2,1)S(1)}, bf16[128,1536]{1,0:T(8,128)(2,1)S(1)}, u32[]{:S(2)}, u32[]{:S(2)}) %collective-permute-start.13) | collective-permute-done | bytes 393248 | tf_op jit(solution)/shard_map/ppermute | solution.py:95
  46.7 3.0 %collective-permute-start.15 = (bf16[64,768]{1,0:T(8,128)(2,1)S(1)}, bf16[64,768]{1,0:T(8,128)(2,1)S(1)}, u32[]{:S(2)}, u32[]{:S(2)}) collective-permute-start(bf16[64,768]{1,0:T(8,128)(2,1)S(1)} %get-tuple-element.79), channel_id=1, source_target_pairs={{0,8},{4,12},{8,0},{12,4},{1,9},{5,13},{9,1},{13,5},{2,10},{6,14},... | collective-permute-start | bytes 294920 | tf_op jit(solution)/shard_map/ppermute | solution.py:95
  49.7 1.4 %collective-permute-start.16 = (bf16[64,768]{1,0:T(8,128)(2,1)S(1)}, bf16[64,768]{1,0:T(8,128)(2,1)S(1)}, u32[]{:S(2)}, u32[]{:S(2)}) collective-permute-start(bf16[64,768]{1,0:T(8,128)(2,1)S(1)} %get-tuple-element.80), channel_id=1, source_target_pairs={{0,12},{4,8},{8,4},{12,0},{1,13},{5,9},{9,5},{13,1},{2,14},{6,10},... | collective-permute-start | bytes 294920 | tf_op jit(solution)/shard_map/ppermute | solution.py:95
  51.8 1.4 %collective-permute-done.14.refs_5_ = bf16[64,768]{1,0:T(8,128)(2,1)S(1)} collective-permute-done((bf16[64,768]{1,0:T(8,128)(2,1)S(1)}, bf16[64,768]{1,0:T(8,128)(2,1)S(1)}, u32[]{:S(2)}, u32[]{:S(2)}) %collective-permute-start.14) | collective-permute-done | bytes 98336 | tf_op jit(solution)/shard_map/ppermute | solution.py:95
  53.1 4.5 %collective-permute-done.15.refs_6_ = bf16[64,768]{1,0:T(8,128)(2,1)S(1)} collective-permute-done((bf16[64,768]{1,0:T(8,128)(2,1)S(1)}, bf16[64,768]{1,0:T(8,128)(2,1)S(1)}, u32[]{:S(2)}, u32[]{:S(2)}) %collective-permute-start.15) | collective-permute-done | bytes 98336 | tf_op jit(solution)/shard_map/ppermute | solution.py:95
  58.4 1.1 %collective-permute-done.17.right = f32[72,128]{1,0:T(8,128)S(1)} collective-permute-done((f32[72,128]{1,0:T(8,128)S(1)}, f32[72,128]{1,0:T(8,128)S(1)}, u32[]{:S(2)}, u32[]{:S(2)}) %collective-permute-start.17) | collective-permute-done | bytes 36896 | tf_op jit(solution)/shard_map/ppermute | solution.py:95
  59.5 1.5 %collective-permute-start.18 = (f32[72,128]{1,0:T(8,128)S(1)}, f32[72,128]{1,0:T(8,128)S(1)}, u32[]{:S(2)}, u32[]{:S(2)}) collective-permute-start(f32[72,128]{1,0:T(8,128)S(1)} %shard_map.123.mine), channel_id=1, source_target_pairs={{0,2},{1,3},{2,0},{3,1},{16,18},{17,19},{18,16},{19,17},{4,6},{5,7... | collective-permute-start | bytes 110600 | tf_op jit(solution)/shard_map/ppermute | solution.py:95
  61.0 1.5 %collective-permute-start.19 = (f32[72,128]{1,0:T(8,128)S(1)}, f32[72,128]{1,0:T(8,128)S(1)}, u32[]{:S(2)}, u32[]{:S(2)}) collective-permute-start(f32[72,128]{1,0:T(8,128)S(1)} %shard_map.123.mine), channel_id=1, source_target_pairs={{0,16},{1,17},{2,18},{3,19},{16,0},{17,1},{18,2},{19,3},{4,20},{5,... | collective-permute-start | bytes 110600 | tf_op jit(solution)/shard_map/ppermute | solution.py:95
  63.6 1.6 %collective-permute-done.19.other = f32[72,128]{1,0:T(8,128)S(1)} collective-permute-done((f32[72,128]{1,0:T(8,128)S(1)}, f32[72,128]{1,0:T(8,128)S(1)}, u32[]{:S(2)}, u32[]{:S(2)}) %collective-permute-start.19) | collective-permute-done | bytes 36896 | tf_op jit(solution)/shard_map/ppermute | solution.py:95
  65.3 2.1 %collective-permute-done.20.other_y = f32[72,128]{1,0:T(8,128)S(1)} collective-permute-done((f32[72,128]{1,0:T(8,128)S(1)}, f32[72,128]{1,0:T(8,128)S(1)}, u32[]{:S(2)}, u32[]{:S(2)}) %collective-permute-start.20) | collective-permute-done | bytes 36896 | tf_op jit(solution)/shard_map/ppermute | solution.py:95
  (43 shorter events, 12.8 us)
Async XLA Ops:
  1.5 9.2 %collective-permute-start = (bf16[64,768]{1,0:T(8,128)(2,1)S(1)}, bf16[64,768]{1,0:T(8,128)(2,1)S(1)}, u32[]{:S(2)}, u32[]{:S(2)}) collective-permute-start(bf16[64,768]{1,0:T(8,128)(2,1)S(1)} %shard_map.105.refs_0_), channel_id=1, source_target_pairs={{0,4},{4,0},{8,12},{12,8},{1,5},{5,1},{9,13},{13,9},{2,6},{6,2},{1... | collective-permute-start | bytes 294920 | tf_op jit(solution)/shard_map/ppermute | solution.py:95
  4.6 10.5 %collective-permute-start.1 = (bf16[64,768]{1,0:T(8,128)(2,1)S(1)}, bf16[64,768]{1,0:T(8,128)(2,1)S(1)}, u32[]{:S(2)}, u32[]{:S(2)}) collective-permute-start(bf16[64,768]{1,0:T(8,128)(2,1)S(1)} %shard_map.105.refs_0_), channel_id=1, source_target_pairs={{0,8},{4,12},{8,0},{12,4},{1,9},{5,13},{9,1},{13,5},{2,10},{6,14},... | collective-permute-start | bytes 294920 | tf_op jit(solution)/shard_map/ppermute | solution.py:95
  7.2 7.9 %collective-permute-start.2 = (bf16[64,768]{1,0:T(8,128)(2,1)S(1)}, bf16[64,768]{1,0:T(8,128)(2,1)S(1)}, u32[]{:S(2)}, u32[]{:S(2)}) collective-permute-start(bf16[64,768]{1,0:T(8,128)(2,1)S(1)} %shard_map.105.refs_0_), channel_id=1, source_target_pairs={{0,12},{4,8},{8,4},{12,0},{1,13},{5,9},{9,5},{13,1},{2,14},{6,10},... | collective-permute-start | bytes 294920 | tf_op jit(solution)/shard_map/ppermute | solution.py:95
  9.8 6.4 %collective-permute-start.3 = (bf16[64,768]{1,0:T(8,128)(2,1)S(1)}, bf16[64,768]{1,0:T(8,128)(2,1)S(1)}, u32[]{:S(2)}, u32[]{:S(2)}) collective-permute-start(bf16[64,768]{1,0:T(8,128)(2,1)S(1)} %get-tuple-element.55.first), channel_id=1, source_target_pairs={{0,4},{4,0},{8,12},{12,8},{1,5},{5,1},{9,13},{13,9},{2,6},{6,2},{1... | collective-permute-start | bytes 294920 | tf_op jit(solution)/shard_map/ppermute | solution.py:95
  16.0 3.3 %collective-permute-start.4 = (bf16[144,1664]{1,0:T(8,128)(2,1)S(1)}, bf16[144,1664]{1,0:T(8,128)(2,1)S(1)}, u32[]{:S(2)}, u32[]{:S(2)}) collective-permute-start(bf16[144,1664]{1,0:T(8,128)(2,1)S(1)} %get-tuple-element.58), channel_id=1, source_target_pairs={{0,1},{1,0},{2,3},{3,2},{4,5},{5,4},{6,7},{7,6},{8,9},{9,8},{10,11... | collective-permute-start | bytes 1437704 | tf_op jit(solution)/shard_map/ppermute | solution.py:95
  16.2 12.3 %collective-permute-start.6 = (bf16[128,768]{1,0:T(8,128)(2,1)S(1)}, bf16[128,768]{1,0:T(8,128)(2,1)S(1)}, u32[]{:S(2)}, u32[]{:S(2)}) collective-permute-start(bf16[128,768]{1,0:T(8,128)(2,1)S(1)} %shard_map.107.refs_0_.refs_4_), channel_id=1, source_target_pairs={{0,8},{4,12},{8,0},{12,4},{1,9},{5,13},{9,1},{13,5},{2,10},{6,14},... | collective-permute-start | bytes 589832 | tf_op jit(solution)/shard_map/ppermute | solution.py:95
  19.4 13.6 %collective-permute-start.5 = (bf16[144,1664]{1,0:T(8,128)(2,1)S(1)}, bf16[144,1664]{1,0:T(8,128)(2,1)S(1)}, u32[]{:S(2)}, u32[]{:S(2)}) collective-permute-start(bf16[144,1664]{1,0:T(8,128)(2,1)S(1)} %get-tuple-element.61._.refs_9_.sent.first_sent), channel_id=1, source_target_pairs={{0,2},{1,3},{2,0},{3,1},{4,6},{5,7},{6,4},{7,5},{8,10},{9,11},{10,... | collective-permute-start | bytes 1437704 | tf_op jit(solution)/shard_map/ppermute | solution.py:95
  29.4 1.8 %collective-permute-start.7 = (bf16[128,1664]{1,0:T(8,128)(2,1)S(1)}, bf16[128,1664]{1,0:T(8,128)(2,1)S(1)}, u32[]{:S(2)}, u32[]{:S(2)}) collective-permute-start(bf16[128,1664]{1,0:T(8,128)(2,1)S(1)} %get-tuple-element.66), channel_id=1, source_target_pairs={{0,1},{1,0},{2,3},{3,2},{4,5},{5,4},{6,7},{7,6},{8,9},{9,8},{10,11... | collective-permute-start | bytes 1277960 | tf_op jit(solution)/shard_map/ppermute | solution.py:95
  31.4 11.9 %collective-permute-start.12 = (bf16[128,1664]{1,0:T(8,128)(2,1)S(1)}, bf16[128,1664]{1,0:T(8,128)(2,1)S(1)}, u32[]{:S(2)}, u32[]{:S(2)}) collective-permute-start(bf16[128,1664]{1,0:T(8,128)(2,1)S(1)} %get-tuple-element.67.refs_0_.sent), channel_id=1, source_target_pairs={{0,2},{1,3},{2,0},{3,1},{4,6},{5,7},{6,4},{7,5},{8,10},{9,11},{10,... | collective-permute-start | bytes 1277960 | tf_op jit(solution)/shard_map/ppermute | solution.py:95
  33.7 1.8 %collective-permute-start.8 = (bf16[128,1536]{1,0:T(8,128)(2,1)S(1)}, bf16[128,1536]{1,0:T(8,128)(2,1)S(1)}, u32[]{:S(2)}, u32[]{:S(2)}) collective-permute-start(bf16[128,1536]{1,0:T(8,128)(2,1)S(1)} %shard_map.114.act), channel_id=1, source_target_pairs={{0,1},{1,0},{2,3},{3,2},{4,5},{5,4},{6,7},{7,6},{8,9},{9,8},{10,11... | collective-permute-start | bytes 1179656 | tf_op jit(solution)/shard_map/ppermute | solution.py:95
  36.3 13.4 %collective-permute-start.10 = (bf16[64,768]{1,0:T(8,128)(2,1)S(1)}, bf16[64,768]{1,0:T(8,128)(2,1)S(1)}, u32[]{:S(2)}, u32[]{:S(2)}) collective-permute-start(bf16[64,768]{1,0:T(8,128)(2,1)S(1)} %get-tuple-element.73.refs_2_), channel_id=1, source_target_pairs={{0,8},{4,12},{8,0},{12,4},{1,9},{5,13},{9,1},{13,5},{2,10},{6,14},... | collective-permute-start | bytes 294920 | tf_op jit(solution)/shard_map/ppermute | solution.py:95
  37.1 14.7 %collective-permute-start.11 = (bf16[64,768]{1,0:T(8,128)(2,1)S(1)}, bf16[64,768]{1,0:T(8,128)(2,1)S(1)}, u32[]{:S(2)}, u32[]{:S(2)}) collective-permute-start(bf16[64,768]{1,0:T(8,128)(2,1)S(1)} %get-tuple-element.74.refs_3_), channel_id=1, source_target_pairs={{0,12},{4,8},{8,4},{12,0},{1,13},{5,9},{9,5},{13,1},{2,14},{6,10},... | collective-permute-start | bytes 294920 | tf_op jit(solution)/shard_map/ppermute | solution.py:95
  38.9 12.9 %collective-permute-start.9 = (bf16[64,768]{1,0:T(8,128)(2,1)S(1)}, bf16[64,768]{1,0:T(8,128)(2,1)S(1)}, u32[]{:S(2)}, u32[]{:S(2)}) collective-permute-start(bf16[64,768]{1,0:T(8,128)(2,1)S(1)} %get-tuple-element.72.refs_1_), channel_id=1, source_target_pairs={{0,4},{4,0},{8,12},{12,8},{1,5},{5,1},{9,13},{13,9},{2,6},{6,2},{1... | collective-permute-start | bytes 294920 | tf_op jit(solution)/shard_map/ppermute | solution.py:95
  44.1 1.8 %collective-permute-start.13 = (bf16[128,1536]{1,0:T(8,128)(2,1)S(1)}, bf16[128,1536]{1,0:T(8,128)(2,1)S(1)}, u32[]{:S(2)}, u32[]{:S(2)}) collective-permute-start(bf16[128,1536]{1,0:T(8,128)(2,1)S(1)} %shard_map.117.act), channel_id=1, source_target_pairs={{0,1},{1,0},{2,3},{3,2},{4,5},{5,4},{6,7},{7,6},{8,9},{9,8},{10,11... | collective-permute-start | bytes 1179656 | tf_op jit(solution)/shard_map/ppermute | solution.py:95
  44.7 13.6 %copy-start = (f32[128,64]{0,1:T(8,128)S(1)}, f32[128,64]{0,1:T(8,128)}, u32[]{:S(2)}) copy-start(f32[128,64]{0,1:T(8,128)} %param.15) | copy-start | bytes 98308
  44.7 13.6 %copy-start.1 = (f32[8,128]{1,0:T(8,128)S(1)}, f32[8,128]{1,0:T(8,128)}, u32[]{:S(2)}) copy-start(f32[8,128]{1,0:T(8,128)} %constant.2.clone.alphas) | copy-start | bytes 12292
  46.7 6.5 %collective-permute-start.14 = (bf16[64,768]{1,0:T(8,128)(2,1)S(1)}, bf16[64,768]{1,0:T(8,128)(2,1)S(1)}, u32[]{:S(2)}, u32[]{:S(2)}) collective-permute-start(bf16[64,768]{1,0:T(8,128)(2,1)S(1)} %get-tuple-element.78), channel_id=1, source_target_pairs={{0,4},{4,0},{8,12},{12,8},{1,5},{5,1},{9,13},{13,9},{2,6},{6,2},{1... | collective-permute-start | bytes 294920 | tf_op jit(solution)/shard_map/ppermute | solution.py:95
  46.7 10.9 %collective-permute-start.15 = (bf16[64,768]{1,0:T(8,128)(2,1)S(1)}, bf16[64,768]{1,0:T(8,128)(2,1)S(1)}, u32[]{:S(2)}, u32[]{:S(2)}) collective-permute-start(bf16[64,768]{1,0:T(8,128)(2,1)S(1)} %get-tuple-element.79), channel_id=1, source_target_pairs={{0,8},{4,12},{8,0},{12,4},{1,9},{5,13},{9,1},{13,5},{2,10},{6,14},... | collective-permute-start | bytes 294920 | tf_op jit(solution)/shard_map/ppermute | solution.py:95
  49.7 7.9 %collective-permute-start.16 = (bf16[64,768]{1,0:T(8,128)(2,1)S(1)}, bf16[64,768]{1,0:T(8,128)(2,1)S(1)}, u32[]{:S(2)}, u32[]{:S(2)}) collective-permute-start(bf16[64,768]{1,0:T(8,128)(2,1)S(1)} %get-tuple-element.80), channel_id=1, source_target_pairs={{0,12},{4,8},{8,4},{12,0},{1,13},{5,9},{9,5},{13,1},{2,14},{6,10},... | collective-permute-start | bytes 294920 | tf_op jit(solution)/shard_map/ppermute | solution.py:95
  58.2 1.3 %collective-permute-start.17 = (f32[72,128]{1,0:T(8,128)S(1)}, f32[72,128]{1,0:T(8,128)S(1)}, u32[]{:S(2)}, u32[]{:S(2)}) collective-permute-start(f32[72,128]{1,0:T(8,128)S(1)} %get-tuple-element.85.left), channel_id=1, source_target_pairs={{0,1},{1,0},{2,3},{3,2},{4,5},{5,4},{6,7},{7,6},{8,9},{9,8},{10,11... | collective-permute-start | bytes 110600 | tf_op jit(solution)/shard_map/ppermute | solution.py:95
  59.5 4.2 %collective-permute-start.18 = (f32[72,128]{1,0:T(8,128)S(1)}, f32[72,128]{1,0:T(8,128)S(1)}, u32[]{:S(2)}, u32[]{:S(2)}) collective-permute-start(f32[72,128]{1,0:T(8,128)S(1)} %shard_map.123.mine), channel_id=1, source_target_pairs={{0,2},{1,3},{2,0},{3,1},{16,18},{17,19},{18,16},{19,17},{4,6},{5,7... | collective-permute-start | bytes 110600 | tf_op jit(solution)/shard_map/ppermute | solution.py:95
  61.0 4.3 %collective-permute-start.19 = (f32[72,128]{1,0:T(8,128)S(1)}, f32[72,128]{1,0:T(8,128)S(1)}, u32[]{:S(2)}, u32[]{:S(2)}) collective-permute-start(f32[72,128]{1,0:T(8,128)S(1)} %shard_map.123.mine), channel_id=1, source_target_pairs={{0,16},{1,17},{2,18},{3,19},{16,0},{17,1},{18,2},{19,3},{4,20},{5,... | collective-permute-start | bytes 110600 | tf_op jit(solution)/shard_map/ppermute | solution.py:95
  62.5 4.9 %collective-permute-start.20 = (f32[72,128]{1,0:T(8,128)S(1)}, f32[72,128]{1,0:T(8,128)S(1)}, u32[]{:S(2)}, u32[]{:S(2)}) collective-permute-start(f32[72,128]{1,0:T(8,128)S(1)} %shard_map.123.mine), channel_id=1, source_target_pairs={{0,18},{1,19},{2,16},{3,17},{16,2},{17,3},{18,0},{19,1},{4,22},{5,... | collective-permute-start | bytes 110600 | tf_op jit(solution)/shard_map/ppermute | solution.py:95

commit v7 on v6

--- a/solution.py
+++ b/solution.py
@@ -206,14 +206,18 @@
     return jnp.concatenate(places, 0)
 
 
-def take_kernel(source, out, sem):
-    copy = pltpu.make_async_copy(source.at[pl.ds(0, out.shape[0]), :], out, sem)
-    copy.start()
-    copy.wait()
+def take_kernel(source, *refs):
+    pieces, sems = refs[:CHUNKS], refs[CHUNKS]
+    copies = []
+    for k in range(CHUNKS):
+        rows = pl.ds(QUOTAS[k], size_of(k))
+        copies.append(pltpu.make_async_copy(source.at[rows, :], pieces[k], sems.at[k]))
+        copies[-1].start()
+    for copy in copies:
+        copy.wait()
 
 
 def prepare_kernel(table_in, hidden, mod_in, out_weight, w, *refs):
-    later, refs = refs[: CHUNKS - 1], refs[CHUNKS - 1 :]
     gathers, refs = refs[:CHUNKS], refs[CHUNKS:]
     spreads, refs = refs[:CHUNKS], refs[CHUNKS:]
     texts, refs = refs[:CHUNKS], refs[CHUNKS:]
@@ -268,8 +272,6 @@
     ends = rows_of(ends, core)
     ends_out[...] = jnp.concatenate([ends, jnp.zeros((16, 128 - ends.shape[1]), BF16)], 1)
     copies[3].wait()
-    for k in range(1, CHUNKS):
-        later[k - 1][...] = tokens[QUOTAS[k] : QUOTAS[k + 1], :]
     for copy in big:
         copy.wait()
 
@@ -321,7 +323,7 @@
             refs[-1][:, columns] = rows_of(product[rows:], core)
 
 
-def pair_kernel(first, second, _, out):
+def pair_kernel(first, second, out):
     out[...] = jnp.concatenate([first[...], second[...]], 0)
 
 
@@ -502,21 +504,29 @@
     payload = units + 128
 
     in_place = lambda array: pltpu.with_memory_space_constraint(array, pltpu.HBM)
-    (piece,) = call(
+    chunks = range(CHUNKS)
+    piece, *later = call(
         take_kernel,
-        [((QUOTAS[1], features), BF16)],
+        [((size_of(k), features), BF16) for k in chunks],
         [in_place(hidden)],
         "a",
-        [pltpu.SemaphoreType.DMA(())],
+        [pltpu.SemaphoreType.DMA((CHUNKS,))],
     )
     arrived = [[piece] + z_swaps(piece)]
+    pairs = [
+        call(
+            pair_kernel,
+            [((2 * piece.shape[0], features), BF16)],
+            [piece, swap(piece, "wide", 1, 4)],
+            "vv",
+        )[0]
+        for piece in later
+    ]
 
     tiles = units // TILE
-    chunks = range(CHUNKS)
     made = call(
         prepare_kernel,
-        [((size_of(k), features), BF16) for k in chunks[1:]]
-        + [((2 * size_of(k), 4 * QUOTAS[k + 1]), BF16) for k in chunks]
+        [((2 * size_of(k), 4 * QUOTAS[k + 1]), BF16) for k in chunks]
         + [((4 * size_of(k), 2 * size_of(k)), BF16) for k in chunks]
         + [((2 * size_of(k), 128), F32) for k in chunks]
         + [
@@ -544,15 +554,12 @@
             pltpu.SemaphoreType.DMA((4,)),
         ],
     )
-    later, made = made[: CHUNKS - 1], made[CHUNKS - 1 :]
     gathers, made = made[:CHUNKS], made[CHUNKS:]
     spreads, made = made[:CHUNKS], made[CHUNKS:]
     texts, made = made[:CHUNKS], made[CHUNKS:]
     held_sent, held_kept, tokens, mod, out_weight, rows_in, ends_mine, slots, video = made
-    neighbours = [(piece, swap(piece, "wide", 1, 4)) for piece in later]
-
     merged = []
-    before = []
+    before = pairs[:1]
     for k in chunks:
         rows = 2 * size_of(k)
         sent_rows = rows + (16 if k == 0 else 0)
@@ -565,20 +572,12 @@
             weight=LONG,
         )
         came = swap(sent, "narrow", 1, 4)
-        pair = []
-        if k + 1 < CHUNKS:
-            pair = call(
-                pair_kernel,
-                [((2 * size_of(k + 1), features), BF16)],
-                [*neighbours[k], z],
-                "vva",
-            )
-            arrived.append([*pair, swap(*pair, "wide", 2, 4)])
+        arrived.extend([pair, swap(pair, "wide", 2, 4)] for pair in pairs[k : k + 1])
         kept, *sums_made = call(
             functools.partial(expand_kept_kernel, k),
             [((rows, units), F32)] + ([((16, units), BF16)] if k == 0 else []),
-            [z, held_kept, *pair],
-            "vv" + "a" * len(pair),
+            [z, held_kept],
+            "vv",
             weight=LONG,
         )
         sums = sums_made[0] if k == 0 else sums

time: 68.2 us -> 72.1 us (1.057)
  starting transfers between devices: 24.1 us -> 30.2 us
  waiting for transfers between devices: 27.4 us -> 25.2 us
    ppermute x21, starting transfers between devices: 24.1 us -> 30.2 us  [swap(): return lax.ppermute(array, axis, [(i, i ^ distance) for i in range(size)])]
    ppermute x21, waiting for transfers between devices: 27.4 us -> 25.2 us  [swap(): return lax.ppermute(array, axis, [(i, i ^ distance) for i in range(size)])]
  transfers between devices with their start and end apart: 21 -> 21, of which waited for: 12 -> 12; matrix products, arithmetic and copies ran while one was open for 0% -> 0% of each run, Pallas kernels for 19% -> 18%
where the time goes in v7:
time: 72.1 us; the launch traced here: 71.9 us
  starting transfers between devices  30.2 us (42%)
  waiting for transfers between devices  25.2 us (35%)
  Pallas kernels  15 us (21%)
  between operations  1.51 us (2%)
    ppermute x21, starting transfers between devices, swap(): return lax.ppermute(array, axis, [(i, i ^ distance) for i in range(size)])  30.2 us
    ppermute x21, waiting for transfers between devices, swap(): return lax.ppermute(array, axis, [(i, i ^ distance) for i in range(size)])  25.2 us
    pallas_call x21, Pallas kernels, call(): pl.pallas_call(kernel, out_shape=[jax.ShapeDtypeStruct(shape, dtype) for...  15 us
  transfers between devices with their start and end apart: 21, of which 12 were waited for; matrix products, arithmetic and copies ran while one was open for 0% of the time, Pallas kernels for 18%

profile of v7, /device:TPU:0, one launch (start us, length us, event | category | flops | bytes accessed | tf_op | source)
XLA Modules:
  0.0 71.9 jit_solution(2480393273920999897)
XLA Ops:
  1.6 3.1 %collective-permute-start.3 = (bf16[64,768]{1,0:T(8,128)(2,1)S(1)}, bf16[64,768]{1,0:T(8,128)(2,1)S(1)}, u32[]{:S(2)}, u32[]{:S(2)}) collective-permute-start(bf16[64,768]{1,0:T(8,128)(2,1)S(1)} %get-tuple-element.55.first), channel_id=1, source_target_pairs={{0,4},{4,0},{8,12},{12,8},{1,5},{5,1},{9,13},{13,9},{2,6},{6,2},{1... | collective-permute-start | bytes 294920 | tf_op jit(solution)/shard_map/ppermute | solution.py:95
  4.8 3.0 %collective-permute-start.1 = (bf16[64,768]{1,0:T(8,128)(2,1)S(1)}, bf16[64,768]{1,0:T(8,128)(2,1)S(1)}, u32[]{:S(2)}, u32[]{:S(2)}) collective-permute-start(bf16[64,768]{1,0:T(8,128)(2,1)S(1)} %get-tuple-element.51.refs_0_), channel_id=1, source_target_pairs={{0,8},{4,12},{8,0},{12,4},{1,9},{5,13},{9,1},{13,5},{2,10},{6,14},... | collective-permute-start | bytes 294920 | tf_op jit(solution)/shard_map/ppermute | solution.py:95
  7.7 1.3 %collective-permute-start.2 = (bf16[64,768]{1,0:T(8,128)(2,1)S(1)}, bf16[64,768]{1,0:T(8,128)(2,1)S(1)}, u32[]{:S(2)}, u32[]{:S(2)}) collective-permute-start(bf16[64,768]{1,0:T(8,128)(2,1)S(1)} %get-tuple-element.51.refs_0_), channel_id=1, source_target_pairs={{0,12},{4,8},{8,4},{12,0},{1,13},{5,9},{9,5},{13,1},{2,14},{6,10},... | collective-permute-start | bytes 294920 | tf_op jit(solution)/shard_map/ppermute | solution.py:95
  9.1 2.6 %shard_map.104 = (bf16[128,256]{1,0:T(8,128)(2,1)S(1)}, bf16[128,512]{1,0:T(8,128)(2,1)S(1)}, bf16[256,128]{1,0:T(8,128)(2,1)S(1)}, bf16[256,128]{1,0:T(8,128)(2...) custom-call(s32[4]{0:T(128)} %table_in.1, ...), custom_call_target="tpu_custom_call" | custom-call | flops 1 | bytes 1 | tf_op jit(solution)/shard_map/pallas_call | solution.py:486
  11.7 1.8 %collective-permute-start.6 = (bf16[128,768]{1,0:T(8,128)(2,1)S(1)}, bf16[128,768]{1,0:T(8,128)(2,1)S(1)}, u32[]{:S(2)}, u32[]{:S(2)}) collective-permute-start(bf16[128,768]{1,0:T(8,128)(2,1)S(1)} %shard_map.106.refs_7_.refs_4_), channel_id=1, source_target_pairs={{0,8},{4,12},{8,0},{12,4},{1,9},{5,13},{9,1},{13,5},{2,10},{6,14},... | collective-permute-start | bytes 589832 | tf_op jit(solution)/shard_map/ppermute | solution.py:95
  13.4 3.6 %collective-permute-done.2.refs_3_ = bf16[64,768]{1,0:T(8,128)(2,1)S(1)} collective-permute-done((bf16[64,768]{1,0:T(8,128)(2,1)S(1)}, bf16[64,768]{1,0:T(8,128)(2,1)S(1)}, u32[]{:S(2)}, u32[]{:S(2)}) %collective-permute-start.2) | collective-permute-done | bytes 98336 | tf_op jit(solution)/shard_map/ppermute | solution.py:95
  18.5 1.3 %collective-permute-done.4.came = bf16[144,1664]{1,0:T(8,128)(2,1)S(1)} collective-permute-done((bf16[144,1664]{1,0:T(8,128)(2,1)S(1)}, bf16[144,1664]{1,0:T(8,128)(2,1)S(1)}, u32[]{:S(2)}, u32[]{:S(2)}) %collective-permute-start.4) | collective-permute-done | bytes 479264 | tf_op jit(solution)/shard_map/ppermute | solution.py:95
  20.0 1.6 %collective-permute-start.5 = (bf16[144,1664]{1,0:T(8,128)(2,1)S(1)}, bf16[144,1664]{1,0:T(8,128)(2,1)S(1)}, u32[]{:S(2)}, u32[]{:S(2)}) collective-permute-start(bf16[144,1664]{1,0:T(8,128)(2,1)S(1)} %get-tuple-element.63._.refs_9_.sent.first_sent), channel_id=1, source_target_pairs={{0,2},{1,3},{2,0},{3,1},{4,6},{5,7},{6,4},{7,5},{8,10},{9,11},{10,... | collective-permute-start | bytes 1437704 | tf_op jit(solution)/shard_map/ppermute | solution.py:95
  21.6 2.4 %shard_map.110.refs_10_.w = bf16[3072,768]{1,0:T(8,128)(2,1)S(1)} custom-call(bf16[3072,768]{1,0:T(8,128)(2,1)} %source.1, bf16[144,1664]{1,0:T(8,128)(2,1)S(1)} %get-tuple-element.63._.refs_9_.sent.first_sent), custom_call_target="tpu_custom_call" | custom-call | flops 1 | bytes 1 | tf_op jit(solution)/shard_map/pallas_call | solution.py:486
  24.0 1.4 %collective-permute-done.6.refs_5_ = bf16[128,768]{1,0:T(8,128)(2,1)S(1)} collective-permute-done((bf16[128,768]{1,0:T(8,128)(2,1)S(1)}, bf16[128,768]{1,0:T(8,128)(2,1)S(1)}, u32[]{:S(2)}, u32[]{:S(2)}) %collective-permute-start.6) | collective-permute-done | bytes 196640 | tf_op jit(solution)/shard_map/ppermute | solution.py:95
  26.7 1.3 %collective-permute-done.7.came = bf16[128,1664]{1,0:T(8,128)(2,1)S(1)} collective-permute-done((bf16[128,1664]{1,0:T(8,128)(2,1)S(1)}, bf16[128,1664]{1,0:T(8,128)(2,1)S(1)}, u32[]{:S(2)}, u32[]{:S(2)}) %collective-permute-start.7) | collective-permute-done | bytes 426016 | tf_op jit(solution)/shard_map/ppermute | solution.py:95
  28.2 1.7 %collective-permute-start.12 = (bf16[128,1664]{1,0:T(8,128)(2,1)S(1)}, bf16[128,1664]{1,0:T(8,128)(2,1)S(1)}, u32[]{:S(2)}, u32[]{:S(2)}) collective-permute-start(bf16[128,1664]{1,0:T(8,128)(2,1)S(1)} %get-tuple-element.69.refs_0_.sent), channel_id=1, source_target_pairs={{0,2},{1,3},{2,0},{3,1},{4,6},{5,7},{6,4},{7,5},{8,10},{9,11},{10,... | collective-permute-start | bytes 1277960 | tf_op jit(solution)/shard_map/ppermute | solution.py:95
  29.8 4.0 %collective-permute-done.5.came.first_came = bf16[144,1664]{1,0:T(8,128)(2,1)S(1)} collective-permute-done((bf16[144,1664]{1,0:T(8,128)(2,1)S(1)}, bf16[144,1664]{1,0:T(8,128)(2,1)S(1)}, u32[]{:S(2)}, u32[]{:S(2)}) %collective-permute-start.5) | collective-permute-done | bytes 479264 | tf_op jit(solution)/shard_map/ppermute | solution.py:95
  35.2 1.2 %collective-permute-done.8.act = bf16[128,1536]{1,0:T(8,128)(2,1)S(1)} collective-permute-done((bf16[128,1536]{1,0:T(8,128)(2,1)S(1)}, bf16[128,1536]{1,0:T(8,128)(2,1)S(1)}, u32[]{:S(2)}, u32[]{:S(2)}) %collective-permute-start.8) | collective-permute-done | bytes 393248 | tf_op jit(solution)/shard_map/ppermute | solution.py:95
  37.2 7.4 %collective-permute-start.10 = (bf16[64,768]{1,0:T(8,128)(2,1)S(1)}, bf16[64,768]{1,0:T(8,128)(2,1)S(1)}, u32[]{:S(2)}, u32[]{:S(2)}) collective-permute-start(bf16[64,768]{1,0:T(8,128)(2,1)S(1)} %get-tuple-element.75.refs_2_), channel_id=1, source_target_pairs={{0,8},{4,12},{8,0},{12,4},{1,9},{5,13},{9,1},{13,5},{2,10},{6,14},... | collective-permute-start | bytes 294920 | tf_op jit(solution)/shard_map/ppermute | solution.py:95
  48.5 2.5 %collective-permute-start.14 = (bf16[64,768]{1,0:T(8,128)(2,1)S(1)}, bf16[64,768]{1,0:T(8,128)(2,1)S(1)}, u32[]{:S(2)}, u32[]{:S(2)}) collective-permute-start(bf16[64,768]{1,0:T(8,128)(2,1)S(1)} %get-tuple-element.80), channel_id=1, source_target_pairs={{0,4},{4,0},{8,12},{12,8},{1,5},{5,1},{9,13},{13,9},{2,6},{6,2},{1... | collective-permute-start | bytes 294920 | tf_op jit(solution)/shard_map/ppermute | solution.py:95
  51.0 2.0 %collective-permute-start.15 = (bf16[64,768]{1,0:T(8,128)(2,1)S(1)}, bf16[64,768]{1,0:T(8,128)(2,1)S(1)}, u32[]{:S(2)}, u32[]{:S(2)}) collective-permute-start(bf16[64,768]{1,0:T(8,128)(2,1)S(1)} %get-tuple-element.81), channel_id=1, source_target_pairs={{0,8},{4,12},{8,0},{12,4},{1,9},{5,13},{9,1},{13,5},{2,10},{6,14},... | collective-permute-start | bytes 294920 | tf_op jit(solution)/shard_map/ppermute | solution.py:95
  53.0 1.4 %collective-permute-start.16 = (bf16[64,768]{1,0:T(8,128)(2,1)S(1)}, bf16[64,768]{1,0:T(8,128)(2,1)S(1)}, u32[]{:S(2)}, u32[]{:S(2)}) collective-permute-start(bf16[64,768]{1,0:T(8,128)(2,1)S(1)} %get-tuple-element.82), channel_id=1, source_target_pairs={{0,12},{4,8},{8,4},{12,0},{1,13},{5,9},{9,5},{13,1},{2,14},{6,10},... | collective-permute-start | bytes 294920 | tf_op jit(solution)/shard_map/ppermute | solution.py:95
  55.0 2.4 %collective-permute-done.14.refs_5_ = bf16[64,768]{1,0:T(8,128)(2,1)S(1)} collective-permute-done((bf16[64,768]{1,0:T(8,128)(2,1)S(1)}, bf16[64,768]{1,0:T(8,128)(2,1)S(1)}, u32[]{:S(2)}, u32[]{:S(2)}) %collective-permute-start.14) | collective-permute-done | bytes 98336 | tf_op jit(solution)/shard_map/ppermute | solution.py:95
  57.5 4.0 %collective-permute-done.16.refs_7_ = bf16[64,768]{1,0:T(8,128)(2,1)S(1)} collective-permute-done((bf16[64,768]{1,0:T(8,128)(2,1)S(1)}, bf16[64,768]{1,0:T(8,128)(2,1)S(1)}, u32[]{:S(2)}, u32[]{:S(2)}) %collective-permute-start.16) | collective-permute-done | bytes 98336 | tf_op jit(solution)/shard_map/ppermute | solution.py:95
  63.4 1.5 %collective-permute-start.18 = (f32[72,128]{1,0:T(8,128)S(1)}, f32[72,128]{1,0:T(8,128)S(1)}, u32[]{:S(2)}, u32[]{:S(2)}) collective-permute-start(f32[72,128]{1,0:T(8,128)S(1)} %shard_map.123.mine), channel_id=1, source_target_pairs={{0,2},{1,3},{2,0},{3,1},{16,18},{17,19},{18,16},{19,17},{4,6},{5,7... | collective-permute-start | bytes 110600 | tf_op jit(solution)/shard_map/ppermute | solution.py:95
  64.9 1.5 %collective-permute-start.19 = (f32[72,128]{1,0:T(8,128)S(1)}, f32[72,128]{1,0:T(8,128)S(1)}, u32[]{:S(2)}, u32[]{:S(2)}) collective-permute-start(f32[72,128]{1,0:T(8,128)S(1)} %shard_map.123.mine), channel_id=1, source_target_pairs={{0,16},{1,17},{2,18},{3,19},{16,0},{17,1},{18,2},{19,3},{4,20},{5,... | collective-permute-start | bytes 110600 | tf_op jit(solution)/shard_map/ppermute | solution.py:95
  67.5 1.6 %collective-permute-done.19.other = f32[72,128]{1,0:T(8,128)S(1)} collective-permute-done((f32[72,128]{1,0:T(8,128)S(1)}, f32[72,128]{1,0:T(8,128)S(1)}, u32[]{:S(2)}, u32[]{:S(2)}) %collective-permute-start.19) | collective-permute-done | bytes 36896 | tf_op jit(solution)/shard_map/ppermute | solution.py:95
  69.2 2.0 %collective-permute-done.20.other_y = f32[72,128]{1,0:T(8,128)S(1)} collective-permute-done((f32[72,128]{1,0:T(8,128)S(1)}, f32[72,128]{1,0:T(8,128)S(1)}, u32[]{:S(2)}, u32[]{:S(2)}) %collective-permute-start.20) | collective-permute-done | bytes 36896 | tf_op jit(solution)/shard_map/ppermute | solution.py:95
  (43 shorter events, 13.9 us)
Async XLA Ops:
  1.6 10.1 %collective-permute-start.3 = (bf16[64,768]{1,0:T(8,128)(2,1)S(1)}, bf16[64,768]{1,0:T(8,128)(2,1)S(1)}, u32[]{:S(2)}, u32[]{:S(2)}) collective-permute-start(bf16[64,768]{1,0:T(8,128)(2,1)S(1)} %get-tuple-element.55.first), channel_id=1, source_target_pairs={{0,4},{4,0},{8,12},{12,8},{1,5},{5,1},{9,13},{13,9},{2,6},{6,2},{1... | collective-permute-start | bytes 294920 | tf_op jit(solution)/shard_map/ppermute | solution.py:95
  4.7 8.8 %collective-permute-start = (bf16[64,768]{1,0:T(8,128)(2,1)S(1)}, bf16[64,768]{1,0:T(8,128)(2,1)S(1)}, u32[]{:S(2)}, u32[]{:S(2)}) collective-permute-start(bf16[64,768]{1,0:T(8,128)(2,1)S(1)} %get-tuple-element.51.refs_0_), channel_id=1, source_target_pairs={{0,4},{4,0},{8,12},{12,8},{1,5},{5,1},{9,13},{13,9},{2,6},{6,2},{1... | collective-permute-start | bytes 294920 | tf_op jit(solution)/shard_map/ppermute | solution.py:95
  4.8 8.7 %collective-permute-start.1 = (bf16[64,768]{1,0:T(8,128)(2,1)S(1)}, bf16[64,768]{1,0:T(8,128)(2,1)S(1)}, u32[]{:S(2)}, u32[]{:S(2)}) collective-permute-start(bf16[64,768]{1,0:T(8,128)(2,1)S(1)} %get-tuple-element.51.refs_0_), channel_id=1, source_target_pairs={{0,8},{4,12},{8,0},{12,4},{1,9},{5,13},{9,1},{13,5},{2,10},{6,14},... | collective-permute-start | bytes 294920 | tf_op jit(solution)/shard_map/ppermute | solution.py:95
  7.7 9.3 %collective-permute-start.2 = (bf16[64,768]{1,0:T(8,128)(2,1)S(1)}, bf16[64,768]{1,0:T(8,128)(2,1)S(1)}, u32[]{:S(2)}, u32[]{:S(2)}) collective-permute-start(bf16[64,768]{1,0:T(8,128)(2,1)S(1)} %get-tuple-element.51.refs_0_), channel_id=1, source_target_pairs={{0,12},{4,8},{8,4},{12,0},{1,13},{5,9},{9,5},{13,1},{2,14},{6,10},... | collective-permute-start | bytes 294920 | tf_op jit(solution)/shard_map/ppermute | solution.py:95
  11.7 13.6 %collective-permute-start.6 = (bf16[128,768]{1,0:T(8,128)(2,1)S(1)}, bf16[128,768]{1,0:T(8,128)(2,1)S(1)}, u32[]{:S(2)}, u32[]{:S(2)}) collective-permute-start(bf16[128,768]{1,0:T(8,128)(2,1)S(1)} %shard_map.106.refs_7_.refs_4_), channel_id=1, source_target_pairs={{0,8},{4,12},{8,0},{12,4},{1,9},{5,13},{9,1},{13,5},{2,10},{6,14},... | collective-permute-start | bytes 589832 | tf_op jit(solution)/shard_map/ppermute | solution.py:95
  17.9 1.9 %collective-permute-start.4 = (bf16[144,1664]{1,0:T(8,128)(2,1)S(1)}, bf16[144,1664]{1,0:T(8,128)(2,1)S(1)}, u32[]{:S(2)}, u32[]{:S(2)}) collective-permute-start(bf16[144,1664]{1,0:T(8,128)(2,1)S(1)} %get-tuple-element.60), channel_id=1, source_target_pairs={{0,1},{1,0},{2,3},{3,2},{4,5},{5,4},{6,7},{7,6},{8,9},{9,8},{10,11... | collective-permute-start | bytes 1437704 | tf_op jit(solution)/shard_map/ppermute | solution.py:95
  20.0 13.9 %collective-permute-start.5 = (bf16[144,1664]{1,0:T(8,128)(2,1)S(1)}, bf16[144,1664]{1,0:T(8,128)(2,1)S(1)}, u32[]{:S(2)}, u32[]{:S(2)}) collective-permute-start(bf16[144,1664]{1,0:T(8,128)(2,1)S(1)} %get-tuple-element.63._.refs_9_.sent.first_sent), channel_id=1, source_target_pairs={{0,2},{1,3},{2,0},{3,1},{4,6},{5,7},{6,4},{7,5},{8,10},{9,11},{10,... | collective-permute-start | bytes 1437704 | tf_op jit(solution)/shard_map/ppermute | solution.py:95
  26.2 1.8 %collective-permute-start.7 = (bf16[128,1664]{1,0:T(8,128)(2,1)S(1)}, bf16[128,1664]{1,0:T(8,128)(2,1)S(1)}, u32[]{:S(2)}, u32[]{:S(2)}) collective-permute-start(bf16[128,1664]{1,0:T(8,128)(2,1)S(1)} %get-tuple-element.68), channel_id=1, source_target_pairs={{0,1},{1,0},{2,3},{3,2},{4,5},{5,4},{6,7},{7,6},{8,9},{9,8},{10,11... | collective-permute-start | bytes 1277960 | tf_op jit(solution)/shard_map/ppermute | solution.py:95
  28.2 17.0 %collective-permute-start.12 = (bf16[128,1664]{1,0:T(8,128)(2,1)S(1)}, bf16[128,1664]{1,0:T(8,128)(2,1)S(1)}, u32[]{:S(2)}, u32[]{:S(2)}) collective-permute-start(bf16[128,1664]{1,0:T(8,128)(2,1)S(1)} %get-tuple-element.69.refs_0_.sent), channel_id=1, source_target_pairs={{0,2},{1,3},{2,0},{3,1},{4,6},{5,7},{6,4},{7,5},{8,10},{9,11},{10,... | collective-permute-start | bytes 1277960 | tf_op jit(solution)/shard_map/ppermute | solution.py:95
  34.6 1.8 %collective-permute-start.8 = (bf16[128,1536]{1,0:T(8,128)(2,1)S(1)}, bf16[128,1536]{1,0:T(8,128)(2,1)S(1)}, u32[]{:S(2)}, u32[]{:S(2)}) collective-permute-start(bf16[128,1536]{1,0:T(8,128)(2,1)S(1)} %shard_map.114.act), channel_id=1, source_target_pairs={{0,1},{1,0},{2,3},{3,2},{4,5},{5,4},{6,7},{7,6},{8,9},{9,8},{10,11... | collective-permute-start | bytes 1179656 | tf_op jit(solution)/shard_map/ppermute | solution.py:95
  37.2 15.8 %collective-permute-start.10 = (bf16[64,768]{1,0:T(8,128)(2,1)S(1)}, bf16[64,768]{1,0:T(8,128)(2,1)S(1)}, u32[]{:S(2)}, u32[]{:S(2)}) collective-permute-start(bf16[64,768]{1,0:T(8,128)(2,1)S(1)} %get-tuple-element.75.refs_2_), channel_id=1, source_target_pairs={{0,8},{4,12},{8,0},{12,4},{1,9},{5,13},{9,1},{13,5},{2,10},{6,14},... | collective-permute-start | bytes 294920 | tf_op jit(solution)/shard_map/ppermute | solution.py:95
  44.6 10.5 %collective-permute-start.11 = (bf16[64,768]{1,0:T(8,128)(2,1)S(1)}, bf16[64,768]{1,0:T(8,128)(2,1)S(1)}, u32[]{:S(2)}, u32[]{:S(2)}) collective-permute-start(bf16[64,768]{1,0:T(8,128)(2,1)S(1)} %get-tuple-element.76.refs_3_), channel_id=1, source_target_pairs={{0,12},{4,8},{8,4},{12,0},{1,13},{5,9},{9,5},{13,1},{2,14},{6,10},... | collective-permute-start | bytes 294920 | tf_op jit(solution)/shard_map/ppermute | solution.py:95
  45.0 10.0 %collective-permute-start.9 = (bf16[64,768]{1,0:T(8,128)(2,1)S(1)}, bf16[64,768]{1,0:T(8,128)(2,1)S(1)}, u32[]{:S(2)}, u32[]{:S(2)}) collective-permute-start(bf16[64,768]{1,0:T(8,128)(2,1)S(1)} %get-tuple-element.74.refs_1_), channel_id=1, source_target_pairs={{0,4},{4,0},{8,12},{12,8},{1,5},{5,1},{9,13},{13,9},{2,6},{6,2},{1... | collective-permute-start | bytes 294920 | tf_op jit(solution)/shard_map/ppermute | solution.py:95
  46.0 1.8 %collective-permute-start.13 = (bf16[128,1536]{1,0:T(8,128)(2,1)S(1)}, bf16[128,1536]{1,0:T(8,128)(2,1)S(1)}, u32[]{:S(2)}, u32[]{:S(2)}) collective-permute-start(bf16[128,1536]{1,0:T(8,128)(2,1)S(1)} %shard_map.117.act), channel_id=1, source_target_pairs={{0,1},{1,0},{2,3},{3,2},{4,5},{5,4},{6,7},{7,6},{8,9},{9,8},{10,11... | collective-permute-start | bytes 1179656 | tf_op jit(solution)/shard_map/ppermute | solution.py:95
  46.5 15.6 %copy-start = (f32[128,64]{0,1:T(8,128)S(1)}, f32[128,64]{0,1:T(8,128)}, u32[]{:S(2)}) copy-start(f32[128,64]{0,1:T(8,128)} %param.15) | copy-start | bytes 98308
  46.6 15.6 %copy-start.1 = (f32[8,128]{1,0:T(8,128)S(1)}, f32[8,128]{1,0:T(8,128)}, u32[]{:S(2)}) copy-start(f32[8,128]{1,0:T(8,128)} %constant.2.clone.alphas) | copy-start | bytes 12292
  48.5 8.9 %collective-permute-start.14 = (bf16[64,768]{1,0:T(8,128)(2,1)S(1)}, bf16[64,768]{1,0:T(8,128)(2,1)S(1)}, u32[]{:S(2)}, u32[]{:S(2)}) collective-permute-start(bf16[64,768]{1,0:T(8,128)(2,1)S(1)} %get-tuple-element.80), channel_id=1, source_target_pairs={{0,4},{4,0},{8,12},{12,8},{1,5},{5,1},{9,13},{13,9},{2,6},{6,2},{1... | collective-permute-start | bytes 294920 | tf_op jit(solution)/shard_map/ppermute | solution.py:95
  51.0 6.5 %collective-permute-start.15 = (bf16[64,768]{1,0:T(8,128)(2,1)S(1)}, bf16[64,768]{1,0:T(8,128)(2,1)S(1)}, u32[]{:S(2)}, u32[]{:S(2)}) collective-permute-start(bf16[64,768]{1,0:T(8,128)(2,1)S(1)} %get-tuple-element.81), channel_id=1, source_target_pairs={{0,8},{4,12},{8,0},{12,4},{1,9},{5,13},{9,1},{13,5},{2,10},{6,14},... | collective-permute-start | bytes 294920 | tf_op jit(solution)/shard_map/ppermute | solution.py:95
  53.0 8.5 %collective-permute-start.16 = (bf16[64,768]{1,0:T(8,128)(2,1)S(1)}, bf16[64,768]{1,0:T(8,128)(2,1)S(1)}, u32[]{:S(2)}, u32[]{:S(2)}) collective-permute-start(bf16[64,768]{1,0:T(8,128)(2,1)S(1)} %get-tuple-element.82), channel_id=1, source_target_pairs={{0,12},{4,8},{8,4},{12,0},{1,13},{5,9},{9,5},{13,1},{2,14},{6,10},... | collective-permute-start | bytes 294920 | tf_op jit(solution)/shard_map/ppermute | solution.py:95
  62.1 1.3 %collective-permute-start.17 = (f32[72,128]{1,0:T(8,128)S(1)}, f32[72,128]{1,0:T(8,128)S(1)}, u32[]{:S(2)}, u32[]{:S(2)}) collective-permute-start(f32[72,128]{1,0:T(8,128)S(1)} %get-tuple-element.87.left), channel_id=1, source_target_pairs={{0,1},{1,0},{2,3},{3,2},{4,5},{5,4},{6,7},{7,6},{8,9},{9,8},{10,11... | collective-permute-start | bytes 110600 | tf_op jit(solution)/shard_map/ppermute | solution.py:95
  63.4 4.2 %collective-permute-start.18 = (f32[72,128]{1,0:T(8,128)S(1)}, f32[72,128]{1,0:T(8,128)S(1)}, u32[]{:S(2)}, u32[]{:S(2)}) collective-permute-start(f32[72,128]{1,0:T(8,128)S(1)} %shard_map.123.mine), channel_id=1, source_target_pairs={{0,2},{1,3},{2,0},{3,1},{16,18},{17,19},{18,16},{19,17},{4,6},{5,7... | collective-permute-start | bytes 110600 | tf_op jit(solution)/shard_map/ppermute | solution.py:95
  64.9 4.3 %collective-permute-start.19 = (f32[72,128]{1,0:T(8,128)S(1)}, f32[72,128]{1,0:T(8,128)S(1)}, u32[]{:S(2)}, u32[]{:S(2)}) collective-permute-start(f32[72,128]{1,0:T(8,128)S(1)} %shard_map.123.mine), channel_id=1, source_target_pairs={{0,16},{1,17},{2,18},{3,19},{16,0},{17,1},{18,2},{19,3},{4,20},{5,... | collective-permute-start | bytes 110600 | tf_op jit(solution)/shard_map/ppermute | solution.py:95
  66.4 4.9 %collective-permute-start.20 = (f32[72,128]{1,0:T(8,128)S(1)}, f32[72,128]{1,0:T(8,128)S(1)}, u32[]{:S(2)}, u32[]{:S(2)}) collective-permute-start(f32[72,128]{1,0:T(8,128)S(1)} %shard_map.123.mine), channel_id=1, source_target_pairs={{0,18},{1,19},{2,16},{3,17},{16,2},{17,3},{18,0},{19,1},{4,22},{5,... | collective-permute-start | bytes 110600 | tf_op jit(solution)/shard_map/ppermute | solution.py:95

commit v8 on v6

--- a/solution.py
+++ b/solution.py
@@ -206,24 +206,29 @@
     return jnp.concatenate(places, 0)
 
 
-def take_kernel(source, out, sem):
-    copy = pltpu.make_async_copy(source.at[pl.ds(0, out.shape[0]), :], out, sem)
-    copy.start()
-    copy.wait()
-
-
-def prepare_kernel(table_in, hidden, mod_in, out_weight, w, *refs):
+def take_kernel(source, whole, piece, sems):
+    copies = [
+        pltpu.make_async_copy(source.at[pl.ds(0, piece.shape[0]), :], piece, sems.at[0]),
+        pltpu.make_async_copy(source, whole, sems.at[1]),
+    ]
+    for copy in copies:
+        copy.start()
+    for copy in copies:
+        copy.wait()
+
+
+def prepare_kernel(table_in, tokens, mod_in, out_weight, w, *refs):
     later, refs = refs[: CHUNKS - 1], refs[CHUNKS - 1 :]
     gathers, refs = refs[:CHUNKS], refs[CHUNKS:]
     spreads, refs = refs[:CHUNKS], refs[CHUNKS:]
     texts, refs = refs[:CHUNKS], refs[CHUNKS:]
-    held, kept, tokens, mod, weight, rows_out, ends_out, slots_out, video_out = refs[:9]
-    table, sems, small = refs[9:]
+    held, kept, mod, weight, rows_out, ends_out, slots_out, video_out = refs[:8]
+    table, sems, small = refs[8:]
     core = lax.axis_index("narrow") % 2
-    sources = (table_in, mod_in, out_weight, hidden)
+    sources = (table_in, mod_in, out_weight)
     copies = [
         pltpu.make_async_copy(source, place, small.at[i])
-        for i, (source, place) in enumerate(zip(sources, (table, mod, weight, tokens)))
+        for i, (source, place) in enumerate(zip(sources, (table, mod, weight)))
     ]
     for copy in copies:
         copy.start()
@@ -267,20 +272,23 @@
     )
     ends = rows_of(ends, core)
     ends_out[...] = jnp.concatenate([ends, jnp.zeros((16, 128 - ends.shape[1]), BF16)], 1)
-    copies[3].wait()
     for k in range(1, CHUNKS):
         later[k - 1][...] = tokens[QUOTAS[k] : QUOTAS[k + 1], :]
     for copy in big:
         copy.wait()
 
 
-def expand_sent_kernel(k, count, text, mod, place, *refs):
-    pieces, (w, sums, ends) = refs[:count], refs[count : count + 3]
+def expand_sent_kernel(k, text, mod, place, own, near, *refs):
+    far, (w, sums, ends) = refs[: 2 * (k + 1)], refs[2 * (k + 1) : 2 * (k + 1) + 3]
     z_out, sent_out, side_out = refs[-3:]
     core = lax.axis_index("narrow") % 2
     units = w.shape[1]
     rows = side_out.shape[0]
-    tokens = jnp.concatenate([piece[...] for piece in pieces], 0)
+    pieces = []
+    for p in range(k + 1):
+        of_chunk = slice(QUOTAS[p], QUOTAS[p + 1])
+        pieces += [own[of_chunk, :], near[of_chunk, :], far[2 * p][...], far[2 * p + 1][...]]
+    tokens = jnp.concatenate(pieces, 0)
     x = jnp.dot(place[...], tokens, preferred_element_type=F32)
     centre = (jnp.sum(x, -1, keepdims=True) / x.shape[1]).astype(BF16).astype(F32)
     x = x - centre
@@ -309,7 +317,7 @@
         sent_out[rows:, units:] = ends[...]
 
 
-def expand_kept_kernel(k, z, w, *refs):
+def expand_kept_kernel(k, z, w, _, *refs):
     kept_out = refs[-1 if k else -2]
     core = lax.axis_index("narrow") % 2
     rows = kept_out.shape[0]
@@ -321,8 +329,8 @@
             refs[-1][:, columns] = rows_of(product[rows:], core)
 
 
-def pair_kernel(first, second, _, out):
-    out[...] = jnp.concatenate([first[...], second[...]], 0)
+def pass_kernel(piece, _, out):
+    out[...] = piece[...]
 
 
 def merge_kernel(k, kept, side, came, sums, ends, total_out, sent_out):
@@ -502,14 +510,15 @@
     payload = units + 128
 
     in_place = lambda array: pltpu.with_memory_space_constraint(array, pltpu.HBM)
-    (piece,) = call(
+    tokens, piece = call(
         take_kernel,
-        [((QUOTAS[1], features), BF16)],
+        [(hidden.shape, BF16), ((QUOTAS[1], features), BF16)],
         [in_place(hidden)],
         "a",
-        [pltpu.SemaphoreType.DMA(())],
-    )
-    arrived = [[piece] + z_swaps(piece)]
+        [pltpu.SemaphoreType.DMA((2,))],
+    )
+    across = swap(piece, "wide", 2, 4)
+    near = swap(tokens, "wide", 1, 4)
 
     tiles = units // TILE
     chunks = range(CHUNKS)
@@ -522,7 +531,6 @@
         + [
             ((features, units), BF16),
             ((features, units), BF16),
-            (hidden.shape, BF16),
             (modulation.shape, F32),
             ((width, features), BF16),
             ((16, features), BF16),
@@ -532,54 +540,46 @@
         ],
         [
             in_place(split_table),
-            in_place(hidden),
+            tokens,
             in_place(modulation),
             in_place(output_weight.T),
             in_place(expand_weight),
         ],
-        "aaaaa",
+        "avaaa",
         [
             pltpu.SMEM(split_table.shape, jnp.int32),
             pltpu.SemaphoreType.DMA((2, tiles)),
-            pltpu.SemaphoreType.DMA((4,)),
+            pltpu.SemaphoreType.DMA((3,)),
         ],
     )
     later, made = made[: CHUNKS - 1], made[CHUNKS - 1 :]
     gathers, made = made[:CHUNKS], made[CHUNKS:]
     spreads, made = made[:CHUNKS], made[CHUNKS:]
     texts, made = made[:CHUNKS], made[CHUNKS:]
-    held_sent, held_kept, tokens, mod, out_weight, rows_in, ends_mine, slots, video = made
-    neighbours = [(piece, swap(piece, "wide", 1, 4)) for piece in later]
+    held_sent, held_kept, mod, out_weight, rows_in, ends_mine, slots, video = made
+    later = [swap(piece, "wide", 2, 4) for piece in later]
+    (across,) = call(pass_kernel, [(across.shape, BF16)], [across, slots], "va")
+    far = [across, swap(across, "wide", 1, 4)]
 
     merged = []
     before = []
     for k in chunks:
         rows = 2 * size_of(k)
         sent_rows = rows + (16 if k == 0 else 0)
-        pieces = [piece for phase in arrived for piece in phase]
         z, sent, side = call(
-            functools.partial(expand_sent_kernel, k, len(pieces)),
+            functools.partial(expand_sent_kernel, k),
             [((sent_rows, features), BF16), ((sent_rows, payload), BF16), ((rows, 128), BF16)],
-            [texts[k], mod, gathers[k], *pieces, held_sent, rows_in, ends_mine, *before],
-            "vvv" + "v" * len(pieces) + "vvv" + "a" * len(before),
+            [texts[k], mod, gathers[k], tokens, near, *far, held_sent, rows_in, ends_mine, *before],
+            "vvvvv" + "v" * len(far) + "vvv" + "a" * len(before),
             weight=LONG,
         )
         came = swap(sent, "narrow", 1, 4)
-        pair = []
-        if k + 1 < CHUNKS:
-            pair = call(
-                pair_kernel,
-                [((2 * size_of(k + 1), features), BF16)],
-                [*neighbours[k], z],
-                "vva",
-            )
-            arrived.append([*pair, swap(*pair, "wide", 2, 4)])
         kept, *sums_made = call(
             functools.partial(expand_kept_kernel, k),
             [((rows, units), F32)] + ([((16, units), BF16)] if k == 0 else []),
-            [z, held_kept, *pair],
-            "vv" + "a" * len(pair),
-            weight=LONG,
+            [z, held_kept, sent],
+            "vva",
+            weight=LONG if k == 0 else 1,
         )
         sums = sums_made[0] if k == 0 else sums
         total, sent = call(
@@ -595,7 +595,13 @@
                 [in_place(contract_weight), sent],
                 "aa",
                 [pltpu.SemaphoreType.DMA((4,))],
+                weight=LONG,
             )
+        if k + 1 < CHUNKS:
+            (across,) = call(
+                pass_kernel, [(later[k].shape, BF16)], [later[k], sent], "va"
+            )
+            far.extend([across, swap(across, "wide", 1, 4)])
         before = [sent, held_out]
         merged.append((total, sent, swap(sent, "narrow", 2, 4)))
 

time: 68.2 us -> 67.7 us (level)
  waiting for transfers between devices: 27.4 us -> 21.8 us
  starting transfers between devices: 24.1 us -> 29.3 us
    ppermute x21, waiting for transfers between devices: 27.4 us -> 21.8 us  [swap(): return lax.ppermute(array, axis, [(i, i ^ distance) for i in range(size)])]
    ppermute x21, starting transfers between devices: 24.1 us -> 29.3 us  [swap(): return lax.ppermute(array, axis, [(i, i ^ distance) for i in range(size)])]
    pallas_call x21 -> x22, Pallas kernels: 14.9 us -> 15 us  [call(): pl.pallas_call(kernel, out_shape=[jax.ShapeDtypeStruct(shape, dtype) for...]
where the time goes in v8:
time: 67.7 us; the launch traced here: 67.6 us
  starting transfers between devices  29.3 us (43%)
  waiting for transfers between devices  21.8 us (32%)
  Pallas kernels  15 us (22%)
  between operations  1.51 us (2%)
    ppermute x21, starting transfers between devices, swap(): return lax.ppermute(array, axis, [(i, i ^ distance) for i in range(size)])  29.3 us
    ppermute x21, waiting for transfers between devices, swap(): return lax.ppermute(array, axis, [(i, i ^ distance) for i in range(size)])  21.8 us
    pallas_call x22, Pallas kernels, call(): pl.pallas_call(kernel, out_shape=[jax.ShapeDtypeStruct(shape, dtype) for...  15 us
  transfers between devices with their start and end apart: 21, of which 12 were waited for; matrix products, arithmetic and copies ran while one was open for 0% of the time, Pallas kernels for 19%

profile of v8, /device:TPU:0, one launch (start us, length us, event | category | flops | bytes accessed | tf_op | source)
XLA Modules:
  0.0 67.6 jit_solution(16329793506351632639)
XLA Ops:
  0.6 1.0 %shard_map.104 = (bf16[128,768]{1,0:T(8,128)(2,1)S(1)}, bf16[64,768]{1,0:T(8,128)(2,1)S(1)}) custom-call(bf16[128,768]{1,0:T(8,128)(2,1)} %bitcast.6), custom_call_target="tpu_custom_call" | custom-call | flops 1 | bytes 1 | tf_op jit(solution)/shard_map/pallas_call | solution.py:492
  1.7 4.1 %collective-permute-start.1 = (bf16[64,768]{1,0:T(8,128)(2,1)S(1)}, bf16[64,768]{1,0:T(8,128)(2,1)S(1)}, u32[]{:S(2)}, u32[]{:S(2)}) collective-permute-start(bf16[64,768]{1,0:T(8,128)(2,1)S(1)} %get-tuple-element.51), channel_id=1, source_target_pairs={{0,8},{4,12},{8,0},{12,4},{1,9},{5,13},{9,1},{13,5},{2,10},{6,14},... | collective-permute-start | bytes 294920 | tf_op jit(solution)/shard_map/ppermute | solution.py:95
  5.8 1.6 %collective-permute-start = (bf16[128,768]{1,0:T(8,128)(2,1)S(1)}, bf16[128,768]{1,0:T(8,128)(2,1)S(1)}, u32[]{:S(2)}, u32[]{:S(2)}) collective-permute-start(bf16[128,768]{1,0:T(8,128)(2,1)S(1)} %get-tuple-element.45.tokens.own.hidden), channel_id=1, source_target_pairs={{0,4},{4,0},{8,12},{12,8},{1,5},{5,1},{9,13},{13,9},{2,6},{6,2},{1... | collective-permute-start | bytes 589832 | tf_op jit(solution)/shard_map/ppermute | solution.py:95
  7.3 2.5 %shard_map.105 = (bf16[64,768]{1,0:T(8,128)(2,1)S(1)}, bf16[128,256]{1,0:T(8,128)(2,1)S(1)}, bf16[128,512]{1,0:T(8,128)(2,1)S(1)}, bf16[256,128]{1,0:T(8,128)(2,...) custom-call(s32[4]{0:T(128)} %table_in.1, ...), custom_call_target="tpu_custom_call" | custom-call | flops 1 | bytes 1 | tf_op jit(solution)/shard_map/pallas_call | solution.py:492
  11.5 3.5 %collective-permute-start.5 = (bf16[64,768]{1,0:T(8,128)(2,1)S(1)}, bf16[64,768]{1,0:T(8,128)(2,1)S(1)}, u32[]{:S(2)}, u32[]{:S(2)}) collective-permute-start(bf16[64,768]{1,0:T(8,128)(2,1)S(1)} %get-tuple-element.65), channel_id=1, source_target_pairs={{0,8},{4,12},{8,0},{12,4},{1,9},{5,13},{9,1},{13,5},{2,10},{6,14},... | collective-permute-start | bytes 294920 | tf_op jit(solution)/shard_map/ppermute | solution.py:95
  16.7 1.3 %collective-permute-done.3.came = bf16[144,1664]{1,0:T(8,128)(2,1)S(1)} collective-permute-done((bf16[144,1664]{1,0:T(8,128)(2,1)S(1)}, bf16[144,1664]{1,0:T(8,128)(2,1)S(1)}, u32[]{:S(2)}, u32[]{:S(2)}) %collective-permute-start.3) | collective-permute-done | bytes 479264 | tf_op jit(solution)/shard_map/ppermute | solution.py:95
  18.2 1.7 %collective-permute-start.4 = (bf16[144,1664]{1,0:T(8,128)(2,1)S(1)}, bf16[144,1664]{1,0:T(8,128)(2,1)S(1)}, u32[]{:S(2)}, u32[]{:S(2)}) collective-permute-start(bf16[144,1664]{1,0:T(8,128)(2,1)S(1)} %get-tuple-element.62._.refs_7_.sent.first_sent), channel_id=1, source_target_pairs={{0,2},{1,3},{2,0},{3,1},{4,6},{5,7},{6,4},{7,5},{8,10},{9,11},{10,... | collective-permute-start | bytes 1437704 | tf_op jit(solution)/shard_map/ppermute | solution.py:95
  19.9 1.4 %collective-permute-start.6 = (bf16[64,768]{1,0:T(8,128)(2,1)S(1)}, bf16[64,768]{1,0:T(8,128)(2,1)S(1)}, u32[]{:S(2)}, u32[]{:S(2)}) collective-permute-start(bf16[64,768]{1,0:T(8,128)(2,1)S(1)} %shard_map.110.refs_2_), channel_id=1, source_target_pairs={{0,4},{4,0},{8,12},{12,8},{1,5},{5,1},{9,13},{13,9},{2,6},{6,2},{1... | collective-permute-start | bytes 294920 | tf_op jit(solution)/shard_map/ppermute | solution.py:95
  21.3 2.4 %shard_map.111.refs_8_.w = bf16[3072,768]{1,0:T(8,128)(2,1)S(1)} custom-call(bf16[3072,768]{1,0:T(8,128)(2,1)} %source.1, bf16[144,1664]{1,0:T(8,128)(2,1)S(1)} %get-tuple-element.62._.refs_7_.sent.first_sent), custom_call_target="tpu_custom_call" | custom-call | flops 10000000000 | bytes 1 | tf_op jit(solution)/shard_map/pallas_call | solution.py:492
  26.0 1.3 %collective-permute-done.7.came = bf16[128,1664]{1,0:T(8,128)(2,1)S(1)} collective-permute-done((bf16[128,1664]{1,0:T(8,128)(2,1)S(1)}, bf16[128,1664]{1,0:T(8,128)(2,1)S(1)}, u32[]{:S(2)}, u32[]{:S(2)}) %collective-permute-start.7) | collective-permute-done | bytes 426016 | tf_op jit(solution)/shard_map/ppermute | solution.py:95
  27.4 1.4 %collective-permute-start.12 = (bf16[128,1664]{1,0:T(8,128)(2,1)S(1)}, bf16[128,1664]{1,0:T(8,128)(2,1)S(1)}, u32[]{:S(2)}, u32[]{:S(2)}) collective-permute-start(bf16[128,1664]{1,0:T(8,128)(2,1)S(1)} %get-tuple-element.69.refs_0_.sent), channel_id=1, source_target_pairs={{0,2},{1,3},{2,0},{3,1},{4,6},{5,7},{6,4},{7,5},{8,10},{9,11},{10,... | collective-permute-start | bytes 1277960 | tf_op jit(solution)/shard_map/ppermute | solution.py:95
  28.8 3.3 %collective-permute-done.4.came.first_came = bf16[144,1664]{1,0:T(8,128)(2,1)S(1)} collective-permute-done((bf16[144,1664]{1,0:T(8,128)(2,1)S(1)}, bf16[144,1664]{1,0:T(8,128)(2,1)S(1)}, u32[]{:S(2)}, u32[]{:S(2)}) %collective-permute-start.4) | collective-permute-done | bytes 479264 | tf_op jit(solution)/shard_map/ppermute | solution.py:95
  33.4 1.2 %collective-permute-done.8.act = bf16[128,1536]{1,0:T(8,128)(2,1)S(1)} collective-permute-done((bf16[128,1536]{1,0:T(8,128)(2,1)S(1)}, bf16[128,1536]{1,0:T(8,128)(2,1)S(1)}, u32[]{:S(2)}, u32[]{:S(2)}) %collective-permute-start.8) | collective-permute-done | bytes 393248 | tf_op jit(solution)/shard_map/ppermute | solution.py:95
  35.4 3.3 %collective-permute-start.10 = (bf16[64,768]{1,0:T(8,128)(2,1)S(1)}, bf16[64,768]{1,0:T(8,128)(2,1)S(1)}, u32[]{:S(2)}, u32[]{:S(2)}) collective-permute-start(bf16[64,768]{1,0:T(8,128)(2,1)S(1)} %get-tuple-element.75.refs_2_), channel_id=1, source_target_pairs={{0,8},{4,12},{8,0},{12,4},{1,9},{5,13},{9,1},{13,5},{2,10},{6,14},... | collective-permute-start | bytes 294920 | tf_op jit(solution)/shard_map/ppermute | solution.py:95
  38.6 1.8 %collective-permute-start.11 = (bf16[64,768]{1,0:T(8,128)(2,1)S(1)}, bf16[64,768]{1,0:T(8,128)(2,1)S(1)}, u32[]{:S(2)}, u32[]{:S(2)}) collective-permute-start(bf16[64,768]{1,0:T(8,128)(2,1)S(1)} %get-tuple-element.76.refs_3_), channel_id=1, source_target_pairs={{0,12},{4,8},{8,4},{12,0},{1,13},{5,9},{9,5},{13,1},{2,14},{6,10},... | collective-permute-start | bytes 294920 | tf_op jit(solution)/shard_map/ppermute | solution.py:95
  42.3 1.2 %collective-permute-done.13.act = bf16[128,1536]{1,0:T(8,128)(2,1)S(1)} collective-permute-done((bf16[128,1536]{1,0:T(8,128)(2,1)S(1)}, bf16[128,1536]{1,0:T(8,128)(2,1)S(1)}, u32[]{:S(2)}, u32[]{:S(2)}) %collective-permute-start.13) | collective-permute-done | bytes 393248 | tf_op jit(solution)/shard_map/ppermute | solution.py:95
  44.3 1.6 %collective-permute-start.14 = (bf16[64,768]{1,0:T(8,128)(2,1)S(1)}, bf16[64,768]{1,0:T(8,128)(2,1)S(1)}, u32[]{:S(2)}, u32[]{:S(2)}) collective-permute-start(bf16[64,768]{1,0:T(8,128)(2,1)S(1)} %get-tuple-element.80), channel_id=1, source_target_pairs={{0,4},{4,0},{8,12},{12,8},{1,5},{5,1},{9,13},{13,9},{2,6},{6,2},{1... | collective-permute-start | bytes 294920 | tf_op jit(solution)/shard_map/ppermute | solution.py:95
  45.9 3.4 %collective-permute-start.15 = (bf16[64,768]{1,0:T(8,128)(2,1)S(1)}, bf16[64,768]{1,0:T(8,128)(2,1)S(1)}, u32[]{:S(2)}, u32[]{:S(2)}) collective-permute-start(bf16[64,768]{1,0:T(8,128)(2,1)S(1)} %get-tuple-element.81), channel_id=1, source_target_pairs={{0,8},{4,12},{8,0},{12,4},{1,9},{5,13},{9,1},{13,5},{2,10},{6,14},... | collective-permute-start | bytes 294920 | tf_op jit(solution)/shard_map/ppermute | solution.py:95
  50.3 6.8 %collective-permute-done.15.refs_6_ = bf16[64,768]{1,0:T(8,128)(2,1)S(1)} collective-permute-done((bf16[64,768]{1,0:T(8,128)(2,1)S(1)}, bf16[64,768]{1,0:T(8,128)(2,1)S(1)}, u32[]{:S(2)}, u32[]{:S(2)}) %collective-permute-start.15) | collective-permute-done | bytes 98336 | tf_op jit(solution)/shard_map/ppermute | solution.py:95
  57.9 1.1 %collective-permute-done.17.right = f32[72,128]{1,0:T(8,128)S(1)} collective-permute-done((f32[72,128]{1,0:T(8,128)S(1)}, f32[72,128]{1,0:T(8,128)S(1)}, u32[]{:S(2)}, u32[]{:S(2)}) %collective-permute-start.17) | collective-permute-done | bytes 36896 | tf_op jit(solution)/shard_map/ppermute | solution.py:95
  59.0 1.5 %collective-permute-start.18 = (f32[72,128]{1,0:T(8,128)S(1)}, f32[72,128]{1,0:T(8,128)S(1)}, u32[]{:S(2)}, u32[]{:S(2)}) collective-permute-start(f32[72,128]{1,0:T(8,128)S(1)} %shard_map.124.mine), channel_id=1, source_target_pairs={{0,2},{1,3},{2,0},{3,1},{16,18},{17,19},{18,16},{19,17},{4,6},{5,7... | collective-permute-start | bytes 110600 | tf_op jit(solution)/shard_map/ppermute | solution.py:95
  60.5 1.5 %collective-permute-start.19 = (f32[72,128]{1,0:T(8,128)S(1)}, f32[72,128]{1,0:T(8,128)S(1)}, u32[]{:S(2)}, u32[]{:S(2)}) collective-permute-start(f32[72,128]{1,0:T(8,128)S(1)} %shard_map.124.mine), channel_id=1, source_target_pairs={{0,16},{1,17},{2,18},{3,19},{16,0},{17,1},{18,2},{19,3},{4,20},{5,... | collective-permute-start | bytes 110600 | tf_op jit(solution)/shard_map/ppermute | solution.py:95
  63.2 1.6 %collective-permute-done.19.other = f32[72,128]{1,0:T(8,128)S(1)} collective-permute-done((f32[72,128]{1,0:T(8,128)S(1)}, f32[72,128]{1,0:T(8,128)S(1)}, u32[]{:S(2)}, u32[]{:S(2)}) %collective-permute-start.19) | collective-permute-done | bytes 36896 | tf_op jit(solution)/shard_map/ppermute | solution.py:95
  64.8 2.1 %collective-permute-done.20.other_y = f32[72,128]{1,0:T(8,128)S(1)} collective-permute-done((f32[72,128]{1,0:T(8,128)S(1)}, f32[72,128]{1,0:T(8,128)S(1)}, u32[]{:S(2)}, u32[]{:S(2)}) %collective-permute-start.20) | collective-permute-done | bytes 36896 | tf_op jit(solution)/shard_map/ppermute | solution.py:95
  (44 shorter events, 13.6 us)
Async XLA Ops:
  1.7 8.9 %collective-permute-start.1 = (bf16[64,768]{1,0:T(8,128)(2,1)S(1)}, bf16[64,768]{1,0:T(8,128)(2,1)S(1)}, u32[]{:S(2)}, u32[]{:S(2)}) collective-permute-start(bf16[64,768]{1,0:T(8,128)(2,1)S(1)} %get-tuple-element.51), channel_id=1, source_target_pairs={{0,8},{4,12},{8,0},{12,4},{1,9},{5,13},{9,1},{13,5},{2,10},{6,14},... | collective-permute-start | bytes 294920 | tf_op jit(solution)/shard_map/ppermute | solution.py:95
  5.8 9.5 %collective-permute-start = (bf16[128,768]{1,0:T(8,128)(2,1)S(1)}, bf16[128,768]{1,0:T(8,128)(2,1)S(1)}, u32[]{:S(2)}, u32[]{:S(2)}) collective-permute-start(bf16[128,768]{1,0:T(8,128)(2,1)S(1)} %get-tuple-element.45.tokens.own.hidden), channel_id=1, source_target_pairs={{0,4},{4,0},{8,12},{12,8},{1,5},{5,1},{9,13},{13,9},{2,6},{6,2},{1... | collective-permute-start | bytes 589832 | tf_op jit(solution)/shard_map/ppermute | solution.py:95
  10.6 4.7 %collective-permute-start.2 = (bf16[64,768]{1,0:T(8,128)(2,1)S(1)}, bf16[64,768]{1,0:T(8,128)(2,1)S(1)}, u32[]{:S(2)}, u32[]{:S(2)}) collective-permute-start(bf16[64,768]{1,0:T(8,128)(2,1)S(1)} %shard_map.106.refs_0_), channel_id=1, source_target_pairs={{0,4},{4,0},{8,12},{12,8},{1,5},{5,1},{9,13},{13,9},{2,6},{6,2},{1... | collective-permute-start | bytes 294920 | tf_op jit(solution)/shard_map/ppermute | solution.py:95
  11.5 8.4 %collective-permute-start.5 = (bf16[64,768]{1,0:T(8,128)(2,1)S(1)}, bf16[64,768]{1,0:T(8,128)(2,1)S(1)}, u32[]{:S(2)}, u32[]{:S(2)}) collective-permute-start(bf16[64,768]{1,0:T(8,128)(2,1)S(1)} %get-tuple-element.65), channel_id=1, source_target_pairs={{0,8},{4,12},{8,0},{12,4},{1,9},{5,13},{9,1},{13,5},{2,10},{6,14},... | collective-permute-start | bytes 294920 | tf_op jit(solution)/shard_map/ppermute | solution.py:95
  16.1 1.9 %collective-permute-start.3 = (bf16[144,1664]{1,0:T(8,128)(2,1)S(1)}, bf16[144,1664]{1,0:T(8,128)(2,1)S(1)}, u32[]{:S(2)}, u32[]{:S(2)}) collective-permute-start(bf16[144,1664]{1,0:T(8,128)(2,1)S(1)} %get-tuple-element.57._), channel_id=1, source_target_pairs={{0,1},{1,0},{2,3},{3,2},{4,5},{5,4},{6,7},{7,6},{8,9},{9,8},{10,11... | collective-permute-start | bytes 1437704 | tf_op jit(solution)/shard_map/ppermute | solution.py:95
  18.2 13.9 %collective-permute-start.4 = (bf16[144,1664]{1,0:T(8,128)(2,1)S(1)}, bf16[144,1664]{1,0:T(8,128)(2,1)S(1)}, u32[]{:S(2)}, u32[]{:S(2)}) collective-permute-start(bf16[144,1664]{1,0:T(8,128)(2,1)S(1)} %get-tuple-element.62._.refs_7_.sent.first_sent), channel_id=1, source_target_pairs={{0,2},{1,3},{2,0},{3,1},{4,6},{5,7},{6,4},{7,5},{8,10},{9,11},{10,... | collective-permute-start | bytes 1437704 | tf_op jit(solution)/shard_map/ppermute | solution.py:95
  19.9 4.7 %collective-permute-start.6 = (bf16[64,768]{1,0:T(8,128)(2,1)S(1)}, bf16[64,768]{1,0:T(8,128)(2,1)S(1)}, u32[]{:S(2)}, u32[]{:S(2)}) collective-permute-start(bf16[64,768]{1,0:T(8,128)(2,1)S(1)} %shard_map.110.refs_2_), channel_id=1, source_target_pairs={{0,4},{4,0},{8,12},{12,8},{1,5},{5,1},{9,13},{13,9},{2,6},{6,2},{1... | collective-permute-start | bytes 294920 | tf_op jit(solution)/shard_map/ppermute | solution.py:95
  25.4 1.8 %collective-permute-start.7 = (bf16[128,1664]{1,0:T(8,128)(2,1)S(1)}, bf16[128,1664]{1,0:T(8,128)(2,1)S(1)}, u32[]{:S(2)}, u32[]{:S(2)}) collective-permute-start(bf16[128,1664]{1,0:T(8,128)(2,1)S(1)} %get-tuple-element.67._), channel_id=1, source_target_pairs={{0,1},{1,0},{2,3},{3,2},{4,5},{5,4},{6,7},{7,6},{8,9},{9,8},{10,11... | collective-permute-start | bytes 1277960 | tf_op jit(solution)/shard_map/ppermute | solution.py:95
  27.4 13.6 %collective-permute-start.12 = (bf16[128,1664]{1,0:T(8,128)(2,1)S(1)}, bf16[128,1664]{1,0:T(8,128)(2,1)S(1)}, u32[]{:S(2)}, u32[]{:S(2)}) collective-permute-start(bf16[128,1664]{1,0:T(8,128)(2,1)S(1)} %get-tuple-element.69.refs_0_.sent), channel_id=1, source_target_pairs={{0,2},{1,3},{2,0},{3,1},{4,6},{5,7},{6,4},{7,5},{8,10},{9,11},{10,... | collective-permute-start | bytes 1277960 | tf_op jit(solution)/shard_map/ppermute | solution.py:95
  32.8 1.8 %collective-permute-start.8 = (bf16[128,1536]{1,0:T(8,128)(2,1)S(1)}, bf16[128,1536]{1,0:T(8,128)(2,1)S(1)}, u32[]{:S(2)}, u32[]{:S(2)}) collective-permute-start(bf16[128,1536]{1,0:T(8,128)(2,1)S(1)} %shard_map.115.act), channel_id=1, source_target_pairs={{0,1},{1,0},{2,3},{3,2},{4,5},{5,4},{6,7},{7,6},{8,9},{9,8},{10,11... | collective-permute-start | bytes 1179656 | tf_op jit(solution)/shard_map/ppermute | solution.py:95
  35.4 13.9 %collective-permute-start.10 = (bf16[64,768]{1,0:T(8,128)(2,1)S(1)}, bf16[64,768]{1,0:T(8,128)(2,1)S(1)}, u32[]{:S(2)}, u32[]{:S(2)}) collective-permute-start(bf16[64,768]{1,0:T(8,128)(2,1)S(1)} %get-tuple-element.75.refs_2_), channel_id=1, source_target_pairs={{0,8},{4,12},{8,0},{12,4},{1,9},{5,13},{9,1},{13,5},{2,10},{6,14},... | collective-permute-start | bytes 294920 | tf_op jit(solution)/shard_map/ppermute | solution.py:95
  38.6 11.6 %collective-permute-start.11 = (bf16[64,768]{1,0:T(8,128)(2,1)S(1)}, bf16[64,768]{1,0:T(8,128)(2,1)S(1)}, u32[]{:S(2)}, u32[]{:S(2)}) collective-permute-start(bf16[64,768]{1,0:T(8,128)(2,1)S(1)} %get-tuple-element.76.refs_3_), channel_id=1, source_target_pairs={{0,12},{4,8},{8,4},{12,0},{1,13},{5,9},{9,5},{13,1},{2,14},{6,10},... | collective-permute-start | bytes 294920 | tf_op jit(solution)/shard_map/ppermute | solution.py:95
  40.5 9.8 %collective-permute-start.9 = (bf16[64,768]{1,0:T(8,128)(2,1)S(1)}, bf16[64,768]{1,0:T(8,128)(2,1)S(1)}, u32[]{:S(2)}, u32[]{:S(2)}) collective-permute-start(bf16[64,768]{1,0:T(8,128)(2,1)S(1)} %get-tuple-element.74.refs_1_), channel_id=1, source_target_pairs={{0,4},{4,0},{8,12},{12,8},{1,5},{5,1},{9,13},{13,9},{2,6},{6,2},{1... | collective-permute-start | bytes 294920 | tf_op jit(solution)/shard_map/ppermute | solution.py:95
  41.7 1.8 %collective-permute-start.13 = (bf16[128,1536]{1,0:T(8,128)(2,1)S(1)}, bf16[128,1536]{1,0:T(8,128)(2,1)S(1)}, u32[]{:S(2)}, u32[]{:S(2)}) collective-permute-start(bf16[128,1536]{1,0:T(8,128)(2,1)S(1)} %shard_map.118.act), channel_id=1, source_target_pairs={{0,1},{1,0},{2,3},{3,2},{4,5},{5,4},{6,7},{7,6},{8,9},{9,8},{10,11... | collective-permute-start | bytes 1179656 | tf_op jit(solution)/shard_map/ppermute | solution.py:95
  42.3 15.5 %copy-start = (f32[128,64]{0,1:T(8,128)S(1)}, f32[128,64]{0,1:T(8,128)}, u32[]{:S(2)}) copy-start(f32[128,64]{0,1:T(8,128)} %param.15) | copy-start | bytes 98308
  42.3 15.5 %copy-start.1 = (f32[8,128]{1,0:T(8,128)S(1)}, f32[8,128]{1,0:T(8,128)}, u32[]{:S(2)}) copy-start(f32[8,128]{1,0:T(8,128)} %constant.2.clone.alphas) | copy-start | bytes 12292
  44.3 6.0 %collective-permute-start.14 = (bf16[64,768]{1,0:T(8,128)(2,1)S(1)}, bf16[64,768]{1,0:T(8,128)(2,1)S(1)}, u32[]{:S(2)}, u32[]{:S(2)}) collective-permute-start(bf16[64,768]{1,0:T(8,128)(2,1)S(1)} %get-tuple-element.80), channel_id=1, source_target_pairs={{0,4},{4,0},{8,12},{12,8},{1,5},{5,1},{9,13},{13,9},{2,6},{6,2},{1... | collective-permute-start | bytes 294920 | tf_op jit(solution)/shard_map/ppermute | solution.py:95
  45.9 11.2 %collective-permute-start.15 = (bf16[64,768]{1,0:T(8,128)(2,1)S(1)}, bf16[64,768]{1,0:T(8,128)(2,1)S(1)}, u32[]{:S(2)}, u32[]{:S(2)}) collective-permute-start(bf16[64,768]{1,0:T(8,128)(2,1)S(1)} %get-tuple-element.81), channel_id=1, source_target_pairs={{0,8},{4,12},{8,0},{12,4},{1,9},{5,13},{9,1},{13,5},{2,10},{6,14},... | collective-permute-start | bytes 294920 | tf_op jit(solution)/shard_map/ppermute | solution.py:95
  49.3 7.8 %collective-permute-start.16 = (bf16[64,768]{1,0:T(8,128)(2,1)S(1)}, bf16[64,768]{1,0:T(8,128)(2,1)S(1)}, u32[]{:S(2)}, u32[]{:S(2)}) collective-permute-start(bf16[64,768]{1,0:T(8,128)(2,1)S(1)} %get-tuple-element.82), channel_id=1, source_target_pairs={{0,12},{4,8},{8,4},{12,0},{1,13},{5,9},{9,5},{13,1},{2,14},{6,10},... | collective-permute-start | bytes 294920 | tf_op jit(solution)/shard_map/ppermute | solution.py:95
  57.7 1.3 %collective-permute-start.17 = (f32[72,128]{1,0:T(8,128)S(1)}, f32[72,128]{1,0:T(8,128)S(1)}, u32[]{:S(2)}, u32[]{:S(2)}) collective-permute-start(f32[72,128]{1,0:T(8,128)S(1)} %get-tuple-element.87.left), channel_id=1, source_target_pairs={{0,1},{1,0},{2,3},{3,2},{4,5},{5,4},{6,7},{7,6},{8,9},{9,8},{10,11... | collective-permute-start | bytes 110600 | tf_op jit(solution)/shard_map/ppermute | solution.py:95
  59.0 4.2 %collective-permute-start.18 = (f32[72,128]{1,0:T(8,128)S(1)}, f32[72,128]{1,0:T(8,128)S(1)}, u32[]{:S(2)}, u32[]{:S(2)}) collective-permute-start(f32[72,128]{1,0:T(8,128)S(1)} %shard_map.124.mine), channel_id=1, source_target_pairs={{0,2},{1,3},{2,0},{3,1},{16,18},{17,19},{18,16},{19,17},{4,6},{5,7... | collective-permute-start | bytes 110600 | tf_op jit(solution)/shard_map/ppermute | solution.py:95
  60.5 4.3 %collective-permute-start.19 = (f32[72,128]{1,0:T(8,128)S(1)}, f32[72,128]{1,0:T(8,128)S(1)}, u32[]{:S(2)}, u32[]{:S(2)}) collective-permute-start(f32[72,128]{1,0:T(8,128)S(1)} %shard_map.124.mine), channel_id=1, source_target_pairs={{0,16},{1,17},{2,18},{3,19},{16,0},{17,1},{18,2},{19,3},{4,20},{5,... | collective-permute-start | bytes 110600 | tf_op jit(solution)/shard_map/ppermute | solution.py:95
  62.0 4.9 %collective-permute-start.20 = (f32[72,128]{1,0:T(8,128)S(1)}, f32[72,128]{1,0:T(8,128)S(1)}, u32[]{:S(2)}, u32[]{:S(2)}) collective-permute-start(f32[72,128]{1,0:T(8,128)S(1)} %shard_map.124.mine), channel_id=1, source_target_pairs={{0,18},{1,19},{2,16},{3,17},{16,2},{17,3},{18,0},{19,1},{4,22},{5,... | collective-permute-start | bytes 110600 | tf_op jit(solution)/shard_map/ppermute | solution.py:95

commit v9 on v8

--- a/solution.py
+++ b/solution.py
@@ -333,7 +333,8 @@
     out[...] = piece[...]
 
 
-def merge_kernel(k, kept, side, came, sums, ends, total_out, sent_out):
+def merge_kernel(k, kept, side, came, sums, ends, *refs):
+    total_out, sent_out = refs[-2:]
     rows, units = kept.shape
     add = lambda left, right: (left[...].astype(F32) + right.astype(F32)).astype(BF16)
     total = kept[...] + came[:rows, :units].astype(F32)
@@ -449,7 +450,7 @@
     out[...] = left[...] + right[...]
 
 
-def noise_kernel(timestep, alphas, video, latent, base_out, factor_out):
+def noise_kernel(timestep, alphas, video, latent, _, out):
     index = lax.broadcasted_iota(jnp.int32, (8, 128), 0) * 128 + lax.broadcasted_iota(
         jnp.int32, (8, 128), 1
     )
@@ -458,12 +459,14 @@
         1,
         keepdims=True,
     )
-    base_out[...] = jnp.where(video[0:1] > 0.5, jnp.sqrt(alpha) * latent[...], 0.0)
-    factor_out[...] = jnp.where(video[...] > 0.5, jnp.sqrt(1.0 - alpha), 0.0)
-
-
-def latent_kernel(base, factor, ends, mine, mine_y, other, other_y, out):
+    width = latent.shape[0]
+    out[:width, :] = jnp.where(video[0:1] > 0.5, jnp.sqrt(alpha) * latent[...], 0.0)
+    out[width:, :] = jnp.where(video[...] > 0.5, jnp.sqrt(1.0 - alpha), 0.0)
+
+
+def latent_kernel(noise, ends, mine, mine_y, other, other_y, out):
     width = out.shape[0]
+    factor = noise[width : width + 1]
 
     def velocity(total):
         average = total[width : width + 1] / D
@@ -477,8 +480,8 @@
     guided = guided + velocity(other[...] + other_y[...]) * jnp.where(
         first, 1.0 - guidance, guidance
     )
-    guided = jnp.where(factor[0:1] > 0.0, guided, 0.0)
-    out[...] = base[...] - factor[0:1] * guided
+    guided = jnp.where(factor > 0.0, guided, 0.0)
+    out[...] = noise[:width] - factor * guided
 
 
 def alpha_constant():
@@ -582,27 +585,35 @@
             weight=LONG if k == 0 else 1,
         )
         sums = sums_made[0] if k == 0 else sums
-        total, sent = call(
-            functools.partial(merge_kernel, k),
-            [((rows, units), F32), ((sent_rows, payload), BF16)],
-            [kept, side, came, sums, ends_mine],
-            "vvvvv",
-        )
-        if k == 0:
+        if k == CHUNKS - 1:
             (held_out,) = call(
                 hold_kernel,
                 [(contract_weight.shape, BF16)],
-                [in_place(contract_weight), sent],
+                [in_place(contract_weight), z],
                 "aa",
                 [pltpu.SemaphoreType.DMA((4,))],
                 weight=LONG,
             )
+        total, sent = call(
+            functools.partial(merge_kernel, k),
+            [((rows, units), F32), ((sent_rows, payload), BF16)],
+            [kept, side, came, sums, ends_mine, *([held_out] if k == CHUNKS - 1 else [])],
+            "vvvvv" + ("a" if k == CHUNKS - 1 else ""),
+        )
         if k + 1 < CHUNKS:
             (across,) = call(
                 pass_kernel, [(later[k].shape, BF16)], [later[k], sent], "va"
             )
             far.extend([across, swap(across, "wide", 1, 4)])
-        before = [sent, held_out]
+        if k == 0:
+            (noise,) = call(
+                noise_kernel,
+                [((width + 8, CAP), F32)],
+                [timestep, alpha_constant(), video, latent.T, sent],
+                "svvva",
+                weight=LONG,
+            )
+        before = [sent, noise]
         merged.append((total, sent, swap(sent, "narrow", 2, 4)))
 
     returned = []
@@ -648,18 +659,11 @@
     (bundle,) = call(
         add_kernel, [((width + 8, CAP), F32)], [bundle, swap(bundle, "narrow", 1, 4)], "vv"
     )
-    base, factor = call(
-        noise_kernel,
-        [((width, CAP), F32), ((8, CAP), F32)],
-        [timestep, alpha_constant(), video, latent.T],
-        "svvv",
-        weight=LONG,
-    )
     (clean_latent,) = call(
         latent_kernel,
         [((width, CAP), F32)],
-        [base, factor, ends, bundle] + [swap(bundle, ("cfg", "narrow"), n, 8) for n in (2, 4, 6)],
-        "vvvvvvv",
+        [noise, ends, bundle] + [swap(bundle, ("cfg", "narrow"), n, 8) for n in (2, 4, 6)],
+        "vvvvvv",
     )
     return (layer_out[None], clean_latent.T)
 

time: 67.7 us -> 66.8 us (0.987)
  starting transfers between devices: 29.3 us -> 28.1 us
    ppermute x21, starting transfers between devices: 29.3 us -> 28.1 us  [swap(): return lax.ppermute(array, axis, [(i, i ^ distance) for i in range(size)])]
  transfers between devices with their start and end apart: 21 -> 21, of which waited for: 12 -> 13; matrix products, arithmetic and copies ran while one was open for 0% -> 0% of each run, Pallas kernels for 19% -> 19%
where the time goes in v9:
time: 66.8 us; the launch traced here: 66.7 us
  starting transfers between devices  28.1 us (42%)
  waiting for transfers between devices  22 us (33%)
  Pallas kernels  15 us (22%)
  between operations  1.51 us (2%)
    ppermute x21, starting transfers between devices, swap(): return lax.ppermute(array, axis, [(i, i ^ distance) for i in range(size)])  28.1 us
    ppermute x21, waiting for transfers between devices, swap(): return lax.ppermute(array, axis, [(i, i ^ distance) for i in range(size)])  22 us
    pallas_call x22, Pallas kernels, call(): pl.pallas_call(kernel, out_shape=[jax.ShapeDtypeStruct(shape, dtype) for...  15 us
  transfers between devices with their start and end apart: 21, of which 13 were waited for; matrix products, arithmetic and copies ran while one was open for 0% of the time, Pallas kernels for 19%

profile of v9, /device:TPU:0, one launch (start us, length us, event | category | flops | bytes accessed | tf_op | source)
XLA Modules:
  0.0 66.7 jit_solution(1317497478215370607)
XLA Ops:
  0.6 1.0 %shard_map.104 = (bf16[128,768]{1,0:T(8,128)(2,1)S(1)}, bf16[64,768]{1,0:T(8,128)(2,1)S(1)}) custom-call(bf16[128,768]{1,0:T(8,128)(2,1)} %bitcast.6), custom_call_target="tpu_custom_call" | custom-call | flops 1 | bytes 1 | tf_op jit(solution)/shard_map/pallas_call | solution.py:495
  1.7 4.1 %collective-permute-start.1 = (bf16[64,768]{1,0:T(8,128)(2,1)S(1)}, bf16[64,768]{1,0:T(8,128)(2,1)S(1)}, u32[]{:S(2)}, u32[]{:S(2)}) collective-permute-start(bf16[64,768]{1,0:T(8,128)(2,1)S(1)} %get-tuple-element.49), channel_id=1, source_target_pairs={{0,8},{4,12},{8,0},{12,4},{1,9},{5,13},{9,1},{13,5},{2,10},{6,14},... | collective-permute-start | bytes 294920 | tf_op jit(solution)/shard_map/ppermute | solution.py:95
  5.8 1.6 %collective-permute-start = (bf16[128,768]{1,0:T(8,128)(2,1)S(1)}, bf16[128,768]{1,0:T(8,128)(2,1)S(1)}, u32[]{:S(2)}, u32[]{:S(2)}) collective-permute-start(bf16[128,768]{1,0:T(8,128)(2,1)S(1)} %get-tuple-element.43.tokens.own.hidden), channel_id=1, source_target_pairs={{0,4},{4,0},{8,12},{12,8},{1,5},{5,1},{9,13},{13,9},{2,6},{6,2},{1... | collective-permute-start | bytes 589832 | tf_op jit(solution)/shard_map/ppermute | solution.py:95
  7.3 2.5 %shard_map.105 = (bf16[64,768]{1,0:T(8,128)(2,1)S(1)}, bf16[128,256]{1,0:T(8,128)(2,1)S(1)}, bf16[128,512]{1,0:T(8,128)(2,1)S(1)}, bf16[256,128]{1,0:T(8,128)(2,...) custom-call(s32[4]{0:T(128)} %table_in.1, ...), custom_call_target="tpu_custom_call" | custom-call | flops 1 | bytes 1 | tf_op jit(solution)/shard_map/pallas_call | solution.py:495
  10.6 0.9 %collective-permute-start.2 = (bf16[64,768]{1,0:T(8,128)(2,1)S(1)}, bf16[64,768]{1,0:T(8,128)(2,1)S(1)}, u32[]{:S(2)}, u32[]{:S(2)}) collective-permute-start(bf16[64,768]{1,0:T(8,128)(2,1)S(1)} %shard_map.106.refs_0_), channel_id=1, source_target_pairs={{0,4},{4,0},{8,12},{12,8},{1,5},{5,1},{9,13},{13,9},{2,6},{6,2},{1... | collective-permute-start | bytes 294920 | tf_op jit(solution)/shard_map/ppermute | solution.py:95
  11.5 3.5 %collective-permute-start.5 = (bf16[64,768]{1,0:T(8,128)(2,1)S(1)}, bf16[64,768]{1,0:T(8,128)(2,1)S(1)}, u32[]{:S(2)}, u32[]{:S(2)}) collective-permute-start(bf16[64,768]{1,0:T(8,128)(2,1)S(1)} %get-tuple-element.63), channel_id=1, source_target_pairs={{0,8},{4,12},{8,0},{12,4},{1,9},{5,13},{9,1},{13,5},{2,10},{6,14},... | collective-permute-start | bytes 294920 | tf_op jit(solution)/shard_map/ppermute | solution.py:95
  17.1 1.3 %collective-permute-done.3.came = bf16[144,1664]{1,0:T(8,128)(2,1)S(1)} collective-permute-done((bf16[144,1664]{1,0:T(8,128)(2,1)S(1)}, bf16[144,1664]{1,0:T(8,128)(2,1)S(1)}, u32[]{:S(2)}, u32[]{:S(2)}) %collective-permute-start.3) | collective-permute-done | bytes 479264 | tf_op jit(solution)/shard_map/ppermute | solution.py:95
  18.6 1.6 %collective-permute-start.4 = (bf16[144,1664]{1,0:T(8,128)(2,1)S(1)}, bf16[144,1664]{1,0:T(8,128)(2,1)S(1)}, u32[]{:S(2)}, u32[]{:S(2)}) collective-permute-start(bf16[144,1664]{1,0:T(8,128)(2,1)S(1)} %get-tuple-element.60._.refs_7_.sent.first_sent), channel_id=1, source_target_pairs={{0,2},{1,3},{2,0},{3,1},{4,6},{5,7},{6,4},{7,5},{8,10},{9,11},{10,... | collective-permute-start | bytes 1437704 | tf_op jit(solution)/shard_map/ppermute | solution.py:95
  20.2 1.1 %collective-permute-start.6 = (bf16[64,768]{1,0:T(8,128)(2,1)S(1)}, bf16[64,768]{1,0:T(8,128)(2,1)S(1)}, u32[]{:S(2)}, u32[]{:S(2)}) collective-permute-start(bf16[64,768]{1,0:T(8,128)(2,1)S(1)} %shard_map.110.refs_2_), channel_id=1, source_target_pairs={{0,4},{4,0},{8,12},{12,8},{1,5},{5,1},{9,13},{13,9},{2,6},{6,2},{1... | collective-permute-start | bytes 294920 | tf_op jit(solution)/shard_map/ppermute | solution.py:95
  21.4 3.4 %collective-permute-done.6.refs_3_ = bf16[64,768]{1,0:T(8,128)(2,1)S(1)} collective-permute-done((bf16[64,768]{1,0:T(8,128)(2,1)S(1)}, bf16[64,768]{1,0:T(8,128)(2,1)S(1)}, u32[]{:S(2)}, u32[]{:S(2)}) %collective-permute-start.6) | collective-permute-done | bytes 98336 | tf_op jit(solution)/shard_map/ppermute | solution.py:95
  25.8 2.4 %shard_map.114.refs_0_.w = bf16[3072,768]{1,0:T(8,128)(2,1)S(1)} custom-call(bf16[3072,768]{1,0:T(8,128)(2,1)} %source.1, bf16[128,768]{1,0:T(8,128)(2,1)S(1)} %get-tuple-element.65.z._), custom_call_target="tpu_custom_call" | custom-call | flops 10000000000 | bytes 1 | tf_op jit(solution)/shard_map/pallas_call | solution.py:495
  28.8 1.1 %collective-permute-start.12 = (bf16[128,1664]{1,0:T(8,128)(2,1)S(1)}, bf16[128,1664]{1,0:T(8,128)(2,1)S(1)}, u32[]{:S(2)}, u32[]{:S(2)}) collective-permute-start(bf16[128,1664]{1,0:T(8,128)(2,1)S(1)} %get-tuple-element.68.refs_0_.sent), channel_id=1, source_target_pairs={{0,2},{1,3},{2,0},{3,1},{4,6},{5,7},{6,4},{7,5},{8,10},{9,11},{10,... | collective-permute-start | bytes 1277960 | tf_op jit(solution)/shard_map/ppermute | solution.py:95
  29.9 1.7 %collective-permute-done.4.came.first_came = bf16[144,1664]{1,0:T(8,128)(2,1)S(1)} collective-permute-done((bf16[144,1664]{1,0:T(8,128)(2,1)S(1)}, bf16[144,1664]{1,0:T(8,128)(2,1)S(1)}, u32[]{:S(2)}, u32[]{:S(2)}) %collective-permute-start.4) | collective-permute-done | bytes 479264 | tf_op jit(solution)/shard_map/ppermute | solution.py:95
  33.0 1.2 %collective-permute-done.8.act = bf16[128,1536]{1,0:T(8,128)(2,1)S(1)} collective-permute-done((bf16[128,1536]{1,0:T(8,128)(2,1)S(1)}, bf16[128,1536]{1,0:T(8,128)(2,1)S(1)}, u32[]{:S(2)}, u32[]{:S(2)}) %collective-permute-start.8) | collective-permute-done | bytes 393248 | tf_op jit(solution)/shard_map/ppermute | solution.py:95
  35.0 1.1 %collective-permute-start.9 = (bf16[64,768]{1,0:T(8,128)(2,1)S(1)}, bf16[64,768]{1,0:T(8,128)(2,1)S(1)}, u32[]{:S(2)}, u32[]{:S(2)}) collective-permute-start(bf16[64,768]{1,0:T(8,128)(2,1)S(1)} %get-tuple-element.73.refs_1_), channel_id=1, source_target_pairs={{0,4},{4,0},{8,12},{12,8},{1,5},{5,1},{9,13},{13,9},{2,6},{6,2},{1... | collective-permute-start | bytes 294920 | tf_op jit(solution)/shard_map/ppermute | solution.py:95
  36.1 4.1 %collective-permute-start.10 = (bf16[64,768]{1,0:T(8,128)(2,1)S(1)}, bf16[64,768]{1,0:T(8,128)(2,1)S(1)}, u32[]{:S(2)}, u32[]{:S(2)}) collective-permute-start(bf16[64,768]{1,0:T(8,128)(2,1)S(1)} %get-tuple-element.74.refs_2_), channel_id=1, source_target_pairs={{0,8},{4,12},{8,0},{12,4},{1,9},{5,13},{9,1},{13,5},{2,10},{6,14},... | collective-permute-start | bytes 294920 | tf_op jit(solution)/shard_map/ppermute | solution.py:95
  40.2 0.9 %collective-permute-done.12.came = bf16[128,1664]{1,0:T(8,128)(2,1)S(1)} collective-permute-done((bf16[128,1664]{1,0:T(8,128)(2,1)S(1)}, bf16[128,1664]{1,0:T(8,128)(2,1)S(1)}, u32[]{:S(2)}, u32[]{:S(2)}) %collective-permute-start.12) | collective-permute-done | bytes 426016 | tf_op jit(solution)/shard_map/ppermute | solution.py:95
  42.4 1.2 %collective-permute-done.13.act = bf16[128,1536]{1,0:T(8,128)(2,1)S(1)} collective-permute-done((bf16[128,1536]{1,0:T(8,128)(2,1)S(1)}, bf16[128,1536]{1,0:T(8,128)(2,1)S(1)}, u32[]{:S(2)}, u32[]{:S(2)}) %collective-permute-start.13) | collective-permute-done | bytes 393248 | tf_op jit(solution)/shard_map/ppermute | solution.py:95
  44.4 1.1 %collective-permute-start.14 = (bf16[64,768]{1,0:T(8,128)(2,1)S(1)}, bf16[64,768]{1,0:T(8,128)(2,1)S(1)}, u32[]{:S(2)}, u32[]{:S(2)}) collective-permute-start(bf16[64,768]{1,0:T(8,128)(2,1)S(1)} %get-tuple-element.79), channel_id=1, source_target_pairs={{0,4},{4,0},{8,12},{12,8},{1,5},{5,1},{9,13},{13,9},{2,6},{6,2},{1... | collective-permute-start | bytes 294920 | tf_op jit(solution)/shard_map/ppermute | solution.py:95
  45.5 4.1 %collective-permute-start.15 = (bf16[64,768]{1,0:T(8,128)(2,1)S(1)}, bf16[64,768]{1,0:T(8,128)(2,1)S(1)}, u32[]{:S(2)}, u32[]{:S(2)}) collective-permute-start(bf16[64,768]{1,0:T(8,128)(2,1)S(1)} %get-tuple-element.80), channel_id=1, source_target_pairs={{0,8},{4,12},{8,0},{12,4},{1,9},{5,13},{9,1},{13,5},{2,10},{6,14},... | collective-permute-start | bytes 294920 | tf_op jit(solution)/shard_map/ppermute | solution.py:95
  49.7 7.7 %collective-permute-done.15.refs_6_ = bf16[64,768]{1,0:T(8,128)(2,1)S(1)} collective-permute-done((bf16[64,768]{1,0:T(8,128)(2,1)S(1)}, bf16[64,768]{1,0:T(8,128)(2,1)S(1)}, u32[]{:S(2)}, u32[]{:S(2)}) %collective-permute-start.15) | collective-permute-done | bytes 98336 | tf_op jit(solution)/shard_map/ppermute | solution.py:95
  58.1 1.2 %collective-permute-done.17.right = f32[72,128]{1,0:T(8,128)S(1)} collective-permute-done((f32[72,128]{1,0:T(8,128)S(1)}, f32[72,128]{1,0:T(8,128)S(1)}, u32[]{:S(2)}, u32[]{:S(2)}) %collective-permute-start.17) | collective-permute-done | bytes 36896 | tf_op jit(solution)/shard_map/ppermute | solution.py:95
  59.3 2.2 %collective-permute-start.20 = (f32[72,128]{1,0:T(8,128)S(1)}, f32[72,128]{1,0:T(8,128)S(1)}, u32[]{:S(2)}, u32[]{:S(2)}) collective-permute-start(f32[72,128]{1,0:T(8,128)S(1)} %shard_map.124.mine), channel_id=1, source_target_pairs={{0,18},{1,19},{2,16},{3,17},{16,2},{17,3},{18,0},{19,1},{4,22},{5,... | collective-permute-start | bytes 110600 | tf_op jit(solution)/shard_map/ppermute | solution.py:95
  64.2 1.3 %collective-permute-done.19.other = f32[72,128]{1,0:T(8,128)S(1)} collective-permute-done((f32[72,128]{1,0:T(8,128)S(1)}, f32[72,128]{1,0:T(8,128)S(1)}, u32[]{:S(2)}, u32[]{:S(2)}) %collective-permute-start.19) | collective-permute-done | bytes 36896 | tf_op jit(solution)/shard_map/ppermute | solution.py:95
  (44 shorter events, 12.8 us)
Async XLA Ops:
  1.7 8.9 %collective-permute-start.1 = (bf16[64,768]{1,0:T(8,128)(2,1)S(1)}, bf16[64,768]{1,0:T(8,128)(2,1)S(1)}, u32[]{:S(2)}, u32[]{:S(2)}) collective-permute-start(bf16[64,768]{1,0:T(8,128)(2,1)S(1)} %get-tuple-element.49), channel_id=1, source_target_pairs={{0,8},{4,12},{8,0},{12,4},{1,9},{5,13},{9,1},{13,5},{2,10},{6,14},... | collective-permute-start | bytes 294920 | tf_op jit(solution)/shard_map/ppermute | solution.py:95
  5.8 9.8 %collective-permute-start = (bf16[128,768]{1,0:T(8,128)(2,1)S(1)}, bf16[128,768]{1,0:T(8,128)(2,1)S(1)}, u32[]{:S(2)}, u32[]{:S(2)}) collective-permute-start(bf16[128,768]{1,0:T(8,128)(2,1)S(1)} %get-tuple-element.43.tokens.own.hidden), channel_id=1, source_target_pairs={{0,4},{4,0},{8,12},{12,8},{1,5},{5,1},{9,13},{13,9},{2,6},{6,2},{1... | collective-permute-start | bytes 589832 | tf_op jit(solution)/shard_map/ppermute | solution.py:95
  10.6 5.0 %collective-permute-start.2 = (bf16[64,768]{1,0:T(8,128)(2,1)S(1)}, bf16[64,768]{1,0:T(8,128)(2,1)S(1)}, u32[]{:S(2)}, u32[]{:S(2)}) collective-permute-start(bf16[64,768]{1,0:T(8,128)(2,1)S(1)} %shard_map.106.refs_0_), channel_id=1, source_target_pairs={{0,4},{4,0},{8,12},{12,8},{1,5},{5,1},{9,13},{13,9},{2,6},{6,2},{1... | collective-permute-start | bytes 294920 | tf_op jit(solution)/shard_map/ppermute | solution.py:95
  11.5 8.7 %collective-permute-start.5 = (bf16[64,768]{1,0:T(8,128)(2,1)S(1)}, bf16[64,768]{1,0:T(8,128)(2,1)S(1)}, u32[]{:S(2)}, u32[]{:S(2)}) collective-permute-start(bf16[64,768]{1,0:T(8,128)(2,1)S(1)} %get-tuple-element.63), channel_id=1, source_target_pairs={{0,8},{4,12},{8,0},{12,4},{1,9},{5,13},{9,1},{13,5},{2,10},{6,14},... | collective-permute-start | bytes 294920 | tf_op jit(solution)/shard_map/ppermute | solution.py:95
  16.5 1.9 %collective-permute-start.3 = (bf16[144,1664]{1,0:T(8,128)(2,1)S(1)}, bf16[144,1664]{1,0:T(8,128)(2,1)S(1)}, u32[]{:S(2)}, u32[]{:S(2)}) collective-permute-start(bf16[144,1664]{1,0:T(8,128)(2,1)S(1)} %get-tuple-element.55._), channel_id=1, source_target_pairs={{0,1},{1,0},{2,3},{3,2},{4,5},{5,4},{6,7},{7,6},{8,9},{9,8},{10,11... | collective-permute-start | bytes 1437704 | tf_op jit(solution)/shard_map/ppermute | solution.py:95
  16.6 4.7 %copy-start = (f32[128,64]{0,1:T(8,128)S(1)}, f32[128,64]{0,1:T(8,128)}, u32[]{:S(2)}) copy-start(f32[128,64]{0,1:T(8,128)} %param.15) | copy-start | bytes 98308
  16.6 4.7 %copy-start.1 = (f32[8,128]{1,0:T(8,128)S(1)}, f32[8,128]{1,0:T(8,128)}, u32[]{:S(2)}) copy-start(f32[8,128]{1,0:T(8,128)} %constant.2.clone.alphas) | copy-start | bytes 12292
  18.6 13.1 %collective-permute-start.4 = (bf16[144,1664]{1,0:T(8,128)(2,1)S(1)}, bf16[144,1664]{1,0:T(8,128)(2,1)S(1)}, u32[]{:S(2)}, u32[]{:S(2)}) collective-permute-start(bf16[144,1664]{1,0:T(8,128)(2,1)S(1)} %get-tuple-element.60._.refs_7_.sent.first_sent), channel_id=1, source_target_pairs={{0,2},{1,3},{2,0},{3,1},{4,6},{5,7},{6,4},{7,5},{8,10},{9,11},{10,... | collective-permute-start | bytes 1437704 | tf_op jit(solution)/shard_map/ppermute | solution.py:95
  20.2 4.7 %collective-permute-start.6 = (bf16[64,768]{1,0:T(8,128)(2,1)S(1)}, bf16[64,768]{1,0:T(8,128)(2,1)S(1)}, u32[]{:S(2)}, u32[]{:S(2)}) collective-permute-start(bf16[64,768]{1,0:T(8,128)(2,1)S(1)} %shard_map.110.refs_2_), channel_id=1, source_target_pairs={{0,4},{4,0},{8,12},{12,8},{1,5},{5,1},{9,13},{13,9},{2,6},{6,2},{1... | collective-permute-start | bytes 294920 | tf_op jit(solution)/shard_map/ppermute | solution.py:95
  25.7 2.9 %collective-permute-start.7 = (bf16[128,1664]{1,0:T(8,128)(2,1)S(1)}, bf16[128,1664]{1,0:T(8,128)(2,1)S(1)}, u32[]{:S(2)}, u32[]{:S(2)}) collective-permute-start(bf16[128,1664]{1,0:T(8,128)(2,1)S(1)} %get-tuple-element.66._), channel_id=1, source_target_pairs={{0,1},{1,0},{2,3},{3,2},{4,5},{5,4},{6,7},{7,6},{8,9},{9,8},{10,11... | collective-permute-start | bytes 1277960 | tf_op jit(solution)/shard_map/ppermute | solution.py:95
  28.8 12.3 %collective-permute-start.12 = (bf16[128,1664]{1,0:T(8,128)(2,1)S(1)}, bf16[128,1664]{1,0:T(8,128)(2,1)S(1)}, u32[]{:S(2)}, u32[]{:S(2)}) collective-permute-start(bf16[128,1664]{1,0:T(8,128)(2,1)S(1)} %get-tuple-element.68.refs_0_.sent), channel_id=1, source_target_pairs={{0,2},{1,3},{2,0},{3,1},{4,6},{5,7},{6,4},{7,5},{8,10},{9,11},{10,... | collective-permute-start | bytes 1277960 | tf_op jit(solution)/shard_map/ppermute | solution.py:95
  32.4 1.8 %collective-permute-start.8 = (bf16[128,1536]{1,0:T(8,128)(2,1)S(1)}, bf16[128,1536]{1,0:T(8,128)(2,1)S(1)}, u32[]{:S(2)}, u32[]{:S(2)}) collective-permute-start(bf16[128,1536]{1,0:T(8,128)(2,1)S(1)} %shard_map.116.act), channel_id=1, source_target_pairs={{0,1},{1,0},{2,3},{3,2},{4,5},{5,4},{6,7},{7,6},{8,9},{9,8},{10,11... | collective-permute-start | bytes 1179656 | tf_op jit(solution)/shard_map/ppermute | solution.py:95
  35.0 14.6 %collective-permute-start.9 = (bf16[64,768]{1,0:T(8,128)(2,1)S(1)}, bf16[64,768]{1,0:T(8,128)(2,1)S(1)}, u32[]{:S(2)}, u32[]{:S(2)}) collective-permute-start(bf16[64,768]{1,0:T(8,128)(2,1)S(1)} %get-tuple-element.73.refs_1_), channel_id=1, source_target_pairs={{0,4},{4,0},{8,12},{12,8},{1,5},{5,1},{9,13},{13,9},{2,6},{6,2},{1... | collective-permute-start | bytes 294920 | tf_op jit(solution)/shard_map/ppermute | solution.py:95
  36.1 13.5 %collective-permute-start.10 = (bf16[64,768]{1,0:T(8,128)(2,1)S(1)}, bf16[64,768]{1,0:T(8,128)(2,1)S(1)}, u32[]{:S(2)}, u32[]{:S(2)}) collective-permute-start(bf16[64,768]{1,0:T(8,128)(2,1)S(1)} %get-tuple-element.74.refs_2_), channel_id=1, source_target_pairs={{0,8},{4,12},{8,0},{12,4},{1,9},{5,13},{9,1},{13,5},{2,10},{6,14},... | collective-permute-start | bytes 294920 | tf_op jit(solution)/shard_map/ppermute | solution.py:95
  40.2 9.5 %collective-permute-start.11 = (bf16[64,768]{1,0:T(8,128)(2,1)S(1)}, bf16[64,768]{1,0:T(8,128)(2,1)S(1)}, u32[]{:S(2)}, u32[]{:S(2)}) collective-permute-start(bf16[64,768]{1,0:T(8,128)(2,1)S(1)} %get-tuple-element.75.refs_3_), channel_id=1, source_target_pairs={{0,12},{4,8},{8,4},{12,0},{1,13},{5,9},{9,5},{13,1},{2,14},{6,10},... | collective-permute-start | bytes 294920 | tf_op jit(solution)/shard_map/ppermute | solution.py:95
  41.8 1.8 %collective-permute-start.13 = (bf16[128,1536]{1,0:T(8,128)(2,1)S(1)}, bf16[128,1536]{1,0:T(8,128)(2,1)S(1)}, u32[]{:S(2)}, u32[]{:S(2)}) collective-permute-start(bf16[128,1536]{1,0:T(8,128)(2,1)S(1)} %shard_map.119.act), channel_id=1, source_target_pairs={{0,1},{1,0},{2,3},{3,2},{4,5},{5,4},{6,7},{7,6},{8,9},{9,8},{10,11... | collective-permute-start | bytes 1179656 | tf_op jit(solution)/shard_map/ppermute | solution.py:95
  44.4 5.3 %collective-permute-start.14 = (bf16[64,768]{1,0:T(8,128)(2,1)S(1)}, bf16[64,768]{1,0:T(8,128)(2,1)S(1)}, u32[]{:S(2)}, u32[]{:S(2)}) collective-permute-start(bf16[64,768]{1,0:T(8,128)(2,1)S(1)} %get-tuple-element.79), channel_id=1, source_target_pairs={{0,4},{4,0},{8,12},{12,8},{1,5},{5,1},{9,13},{13,9},{2,6},{6,2},{1... | collective-permute-start | bytes 294920 | tf_op jit(solution)/shard_map/ppermute | solution.py:95
  45.5 11.9 %collective-permute-start.15 = (bf16[64,768]{1,0:T(8,128)(2,1)S(1)}, bf16[64,768]{1,0:T(8,128)(2,1)S(1)}, u32[]{:S(2)}, u32[]{:S(2)}) collective-permute-start(bf16[64,768]{1,0:T(8,128)(2,1)S(1)} %get-tuple-element.80), channel_id=1, source_target_pairs={{0,8},{4,12},{8,0},{12,4},{1,9},{5,13},{9,1},{13,5},{2,10},{6,14},... | collective-permute-start | bytes 294920 | tf_op jit(solution)/shard_map/ppermute | solution.py:95
  49.6 7.8 %collective-permute-start.16 = (bf16[64,768]{1,0:T(8,128)(2,1)S(1)}, bf16[64,768]{1,0:T(8,128)(2,1)S(1)}, u32[]{:S(2)}, u32[]{:S(2)}) collective-permute-start(bf16[64,768]{1,0:T(8,128)(2,1)S(1)} %get-tuple-element.81), channel_id=1, source_target_pairs={{0,12},{4,8},{8,4},{12,0},{1,13},{5,9},{9,5},{13,1},{2,14},{6,10},... | collective-permute-start | bytes 294920 | tf_op jit(solution)/shard_map/ppermute | solution.py:95
  58.0 1.3 %collective-permute-start.17 = (f32[72,128]{1,0:T(8,128)S(1)}, f32[72,128]{1,0:T(8,128)S(1)}, u32[]{:S(2)}, u32[]{:S(2)}) collective-permute-start(f32[72,128]{1,0:T(8,128)S(1)} %get-tuple-element.83.left), channel_id=1, source_target_pairs={{0,1},{1,0},{2,3},{3,2},{4,5},{5,4},{6,7},{7,6},{8,9},{9,8},{10,11... | collective-permute-start | bytes 110600 | tf_op jit(solution)/shard_map/ppermute | solution.py:95
  59.3 4.9 %collective-permute-start.20 = (f32[72,128]{1,0:T(8,128)S(1)}, f32[72,128]{1,0:T(8,128)S(1)}, u32[]{:S(2)}, u32[]{:S(2)}) collective-permute-start(f32[72,128]{1,0:T(8,128)S(1)} %shard_map.124.mine), channel_id=1, source_target_pairs={{0,18},{1,19},{2,16},{3,17},{16,2},{17,3},{18,0},{19,1},{4,22},{5,... | collective-permute-start | bytes 110600 | tf_op jit(solution)/shard_map/ppermute | solution.py:95
  61.5 4.0 %collective-permute-start.19 = (f32[72,128]{1,0:T(8,128)S(1)}, f32[72,128]{1,0:T(8,128)S(1)}, u32[]{:S(2)}, u32[]{:S(2)}) collective-permute-start(f32[72,128]{1,0:T(8,128)S(1)} %shard_map.124.mine), channel_id=1, source_target_pairs={{0,16},{1,17},{2,18},{3,19},{16,0},{17,1},{18,2},{19,3},{4,20},{5,... | collective-permute-start | bytes 110600 | tf_op jit(solution)/shard_map/ppermute | solution.py:95
  62.0 4.0 %collective-permute-start.18 = (f32[72,128]{1,0:T(8,128)S(1)}, f32[72,128]{1,0:T(8,128)S(1)}, u32[]{:S(2)}, u32[]{:S(2)}) collective-permute-start(f32[72,128]{1,0:T(8,128)S(1)} %shard_map.124.mine), channel_id=1, source_target_pairs={{0,2},{1,3},{2,0},{3,1},{16,18},{17,19},{18,16},{19,17},{4,6},{5,7... | collective-permute-start | bytes 110600 | tf_op jit(solution)/shard_map/ppermute | solution.py:95

commit v10 on v9

--- a/solution.py
+++ b/solution.py
@@ -162,7 +162,8 @@
     return jnp.concatenate([high.astype(F32), low.astype(F32)], 0).astype(BF16)
 
 
-def hold_kernel(source, _, place, sems):
+def hold_kernel(source, *refs):
+    place, sems = refs[-2:]
     for copy in load(source, place, sems):
         copy.wait()
 
@@ -333,23 +334,32 @@
     out[...] = piece[...]
 
 
+def across_rows(side):
+    height = side.shape[0]
+    if height < 128:
+        side = jnp.concatenate([side, jnp.zeros((128 - height, 128), F32)], 0)
+    return side.T
+
+
 def merge_kernel(k, kept, side, came, sums, ends, *refs):
-    total_out, sent_out = refs[-2:]
+    total_out, sent_out, side_out, stats_out = refs[-4:]
     rows, units = kept.shape
-    add = lambda left, right: (left[...].astype(F32) + right.astype(F32)).astype(BF16)
+    add = lambda left, right: left[...].astype(F32) + right.astype(F32)
     total = kept[...] + came[:rows, :units].astype(F32)
     total_out[...] = total
-    sent_out[:rows, :units] = total.astype(BF16)
-    sent_out[:rows, units:] = add(side, came[:rows, units:])
+    sent_out[:rows, :] = total.astype(BF16)
+    both = add(side, came[:rows, units:])
+    side_out[...] = both
+    stats_out[:32, :] = across_rows(both)[:32].astype(BF16)
     if k == 0:
-        sent_out[rows:, :units] = add(sums, came[rows:, :units])
-        sent_out[rows:, units:] = add(ends, came[rows:, units:])
-
-
-def activate_kernel(features, text, total, sent, came, first_sent, first_came, *refs):
+        sent_out[rows:, :] = add(sums, came[rows:, :units]).astype(BF16)
+        stats_out[32:, :] = add(ends, came[rows:, units:]).astype(BF16)
+
+
+def activate_kernel(features, text, total, came, side, stats, first_sent, first_came, *refs):
     act_out = refs[-1]
     rows, units = total.shape
-    sides = [sent[:rows, units:].astype(F32), came[:rows, units:].astype(F32)]
+    sides = [side[...], across_rows(stats[:32, :].astype(F32))[:rows]]
     lane = lax.broadcasted_iota(jnp.int32, (rows, 128), 1)
     field = lane % 4
     summed = sides[0] + sides[1]
@@ -388,13 +398,13 @@
         act_out[:, columns] = jax.nn.gelu(pre * scale + extra, approximate=True).astype(BF16)
 
 
-def contract_own_kernel(k, act, w, mine, first_sent, first_came, out, *ends_out):
+def contract_own_kernel(k, act, w, mine, chip, other, out, *ends_out):
     core = lax.axis_index("narrow") % 2
     units = w.shape[0] // 2
     rows = pl.ds(pl.multiple_of(core * units, 128), units)
     out[...] = jnp.dot(act[...], w[rows, :], preferred_element_type=F32)
     if k == 0:
-        total = first_sent[-16:, units:].astype(F32) + first_came[-16:, units:].astype(F32)
+        total = chip[-16:, :].astype(F32) + other[-16:, :].astype(F32)
         total = total[:8] + total[8:]
         total = total + pltpu.roll(total, 4, 0)
         own = mine[...].astype(F32)
@@ -464,7 +474,7 @@
     out[width:, :] = jnp.where(video[...] > 0.5, jnp.sqrt(1.0 - alpha), 0.0)
 
 
-def latent_kernel(noise, ends, mine, mine_y, other, other_y, out):
+def latent_kernel(noise, ends, mine, other_y, other, mine_y, out):
     width = out.shape[0]
     factor = noise[width : width + 1]
 
@@ -585,26 +595,31 @@
             weight=LONG if k == 0 else 1,
         )
         sums = sums_made[0] if k == 0 else sums
-        if k == CHUNKS - 1:
-            (held_out,) = call(
-                hold_kernel,
-                [(contract_weight.shape, BF16)],
-                [in_place(contract_weight), z],
-                "aa",
-                [pltpu.SemaphoreType.DMA((4,))],
-                weight=LONG,
-            )
-        total, sent = call(
+        total, sent, side, stats = call(
             functools.partial(merge_kernel, k),
-            [((rows, units), F32), ((sent_rows, payload), BF16)],
-            [kept, side, came, sums, ends_mine, *([held_out] if k == CHUNKS - 1 else [])],
-            "vvvvv" + ("a" if k == CHUNKS - 1 else ""),
+            [
+                ((rows, units), F32),
+                ((sent_rows, units), BF16),
+                ((rows, 128), F32),
+                ((sent_rows - rows + 32, 128), BF16),
+            ],
+            [kept, side, came, sums, ends_mine],
+            "vvvvv",
         )
         if k + 1 < CHUNKS:
             (across,) = call(
                 pass_kernel, [(later[k].shape, BF16)], [later[k], sent], "va"
             )
             far.extend([across, swap(across, "wide", 1, 4)])
+        if k == 0:
+            (held_out,) = call(
+                hold_kernel,
+                [(contract_weight.shape, BF16)],
+                [in_place(contract_weight), across, stats],
+                "aaa",
+                [pltpu.SemaphoreType.DMA((4,))],
+                weight=LONG,
+            )
         if k == 0:
             (noise,) = call(
                 noise_kernel,
@@ -613,28 +628,29 @@
                 "svvva",
                 weight=LONG,
             )
-        before = [sent, noise]
-        merged.append((total, sent, swap(sent, "narrow", 2, 4)))
+        before = [sent, noise, held_out]
+        came, stats_came = [swap(array, "narrow", 2, 4) for array in (sent, stats)]
+        merged.append((sent, stats, [total, came, side, stats_came]))
 
     returned = []
     before = []
-    first = merged[0][1:]
+    first = [merged[0][0], merged[0][2][1]]
+    first_stats = [merged[0][1], merged[0][2][3]]
     for k in chunks:
         rows = 2 * size_of(k)
-        total, sent, came = merged[k]
         if k + 1 < CHUNKS:
-            before = before + [merged[k + 1][1]]
+            before = before + [merged[k + 1][0], merged[k + 1][1]]
         (act,) = call(
             functools.partial(activate_kernel, features),
             [((rows, units), BF16)],
-            [texts[k], total, sent, came, *first, *before],
-            "vvvvvv" + "a" * len(before),
+            [texts[k], *merged[k][2], *first, *before],
+            "vvvvvvv" + "a" * len(before),
         )
         act_came = swap(act, "narrow", 1, 4)
         out, *ends_made = call(
             functools.partial(contract_own_kernel, k),
             [((rows, features), F32)] + ([((128, 128), F32)] if k == 0 else []),
-            [act, held_out, ends_mine, *first],
+            [act, held_out, ends_mine, *first_stats],
             "vvvvv",
             weight=LONG,
         )
@@ -646,8 +662,8 @@
             "vvvv",
         )
         before = pieces
-        returned.append(pieces[0])
-        returned.extend(swap(pieces[s], "wide", s, 4) for s in (1, 2, 3))
+        distances = (3, 2, 1) if k + 1 < CHUNKS else (3, 2, 1)
+        returned += [pieces[0], *(swap(pieces[s], "wide", s, 4) for s in distances)]
 
     layer, bundle = call(
         finish_kernel,
@@ -662,7 +678,7 @@
     (clean_latent,) = call(
         latent_kernel,
         [((width, CAP), F32)],
-        [noise, ends, bundle] + [swap(bundle, ("cfg", "narrow"), n, 8) for n in (2, 4, 6)],
+        [noise, ends, bundle] + [swap(bundle, ("cfg", "narrow"), n, 8) for n in (6, 4, 2)],
         "vvvvvv",
     )
     return (layer_out[None], clean_latent.T)

time: 66.8 us -> 65.8 us (0.985)
  waiting for transfers between devices: 22 us -> 19.2 us
  starting transfers between devices: 28.1 us -> 29.7 us
    ppermute x21 -> x23, waiting for transfers between devices: 22 us -> 19.2 us  [swap(): return lax.ppermute(array, axis, [(i, i ^ distance) for i in range(size)])]
    ppermute x21 -> x23, starting transfers between devices: 28.1 us -> 29.7 us  [swap(): return lax.ppermute(array, axis, [(i, i ^ distance) for i in range(size)])]
  transfers between devices with their start and end apart: 21 -> 23, of which waited for: 13 -> 13; matrix products, arithmetic and copies ran while one was open for 0% -> 0% of each run, Pallas kernels for 19% -> 20%
where the time goes in v10:
time: 65.8 us; the launch traced here: 65.7 us
  starting transfers between devices  29.7 us (45%)
  waiting for transfers between devices  19.2 us (29%)
  Pallas kernels  15.2 us (23%)
  between operations  1.48 us (2%)
    ppermute x23, starting transfers between devices, swap(): return lax.ppermute(array, axis, [(i, i ^ distance) for i in range(size)])  29.7 us
    ppermute x23, waiting for transfers between devices, swap(): return lax.ppermute(array, axis, [(i, i ^ distance) for i in range(size)])  19.2 us
    pallas_call x22, Pallas kernels, call(): pl.pallas_call(kernel, out_shape=[jax.ShapeDtypeStruct(shape, dtype) for...  15.2 us
  transfers between devices with their start and end apart: 23, of which 13 were waited for; matrix products, arithmetic and copies ran while one was open for 0% of the time, Pallas kernels for 20%

profile of v10, /device:TPU:0, one launch (start us, length us, event | category | flops | bytes accessed | tf_op | source)
XLA Modules:
  0.0 65.7 jit_solution(8403407918547981104)
XLA Ops:
  0.6 1.0 %shard_map.104 = (bf16[128,768]{1,0:T(8,128)(2,1)S(1)}, bf16[64,768]{1,0:T(8,128)(2,1)S(1)}) custom-call(bf16[128,768]{1,0:T(8,128)(2,1)} %bitcast.6), custom_call_target="tpu_custom_call" | custom-call | flops 1 | bytes 1 | tf_op jit(solution)/shard_map/pallas_call | solution.py:505
  1.7 4.1 %collective-permute-start.1 = (bf16[64,768]{1,0:T(8,128)(2,1)S(1)}, bf16[64,768]{1,0:T(8,128)(2,1)S(1)}, u32[]{:S(2)}, u32[]{:S(2)}) collective-permute-start(bf16[64,768]{1,0:T(8,128)(2,1)S(1)} %get-tuple-element.53), channel_id=1, source_target_pairs={{0,8},{4,12},{8,0},{12,4},{1,9},{5,13},{9,1},{13,5},{2,10},{6,14},... | collective-permute-start | bytes 294920 | tf_op jit(solution)/shard_map/ppermute | solution.py:95
  5.8 1.6 %collective-permute-start = (bf16[128,768]{1,0:T(8,128)(2,1)S(1)}, bf16[128,768]{1,0:T(8,128)(2,1)S(1)}, u32[]{:S(2)}, u32[]{:S(2)}) collective-permute-start(bf16[128,768]{1,0:T(8,128)(2,1)S(1)} %get-tuple-element.47.tokens.own.hidden), channel_id=1, source_target_pairs={{0,4},{4,0},{8,12},{12,8},{1,5},{5,1},{9,13},{13,9},{2,6},{6,2},{1... | collective-permute-start | bytes 589832 | tf_op jit(solution)/shard_map/ppermute | solution.py:95
  7.3 2.5 %shard_map.105 = (bf16[64,768]{1,0:T(8,128)(2,1)S(1)}, bf16[128,256]{1,0:T(8,128)(2,1)S(1)}, bf16[128,512]{1,0:T(8,128)(2,1)S(1)}, bf16[256,128]{1,0:T(8,128)(2,...) custom-call(s32[4]{0:T(128)} %table_in.1, ...), custom_call_target="tpu_custom_call" | custom-call | flops 1 | bytes 1 | tf_op jit(solution)/shard_map/pallas_call | solution.py:505
  10.6 0.9 %collective-permute-start.2 = (bf16[64,768]{1,0:T(8,128)(2,1)S(1)}, bf16[64,768]{1,0:T(8,128)(2,1)S(1)}, u32[]{:S(2)}, u32[]{:S(2)}) collective-permute-start(bf16[64,768]{1,0:T(8,128)(2,1)S(1)} %shard_map.106.refs_0_), channel_id=1, source_target_pairs={{0,4},{4,0},{8,12},{12,8},{1,5},{5,1},{9,13},{13,9},{2,6},{6,2},{1... | collective-permute-start | bytes 294920 | tf_op jit(solution)/shard_map/ppermute | solution.py:95
  11.5 3.5 %collective-permute-start.6 = (bf16[64,768]{1,0:T(8,128)(2,1)S(1)}, bf16[64,768]{1,0:T(8,128)(2,1)S(1)}, u32[]{:S(2)}, u32[]{:S(2)}) collective-permute-start(bf16[64,768]{1,0:T(8,128)(2,1)S(1)} %get-tuple-element.69), channel_id=1, source_target_pairs={{0,8},{4,12},{8,0},{12,4},{1,9},{5,13},{9,1},{13,5},{2,10},{6,14},... | collective-permute-start | bytes 294920 | tf_op jit(solution)/shard_map/ppermute | solution.py:95
  17.1 1.3 %collective-permute-done.3.came = bf16[144,1664]{1,0:T(8,128)(2,1)S(1)} collective-permute-done((bf16[144,1664]{1,0:T(8,128)(2,1)S(1)}, bf16[144,1664]{1,0:T(8,128)(2,1)S(1)}, u32[]{:S(2)}, u32[]{:S(2)}) %collective-permute-start.3) | collective-permute-done | bytes 479264 | tf_op jit(solution)/shard_map/ppermute | solution.py:95
  18.6 1.5 %collective-permute-start.4 = (bf16[144,1536]{1,0:T(8,128)(2,1)S(1)}, bf16[144,1536]{1,0:T(8,128)(2,1)S(1)}, u32[]{:S(2)}, u32[]{:S(2)}) collective-permute-start(bf16[144,1536]{1,0:T(8,128)(2,1)S(1)} %get-tuple-element.64._.refs_7_.first_sent), channel_id=1, source_target_pairs={{0,2},{1,3},{2,0},{3,1},{4,6},{5,7},{6,4},{7,5},{8,10},{9,11},{10,... | collective-permute-start | bytes 1327112 | tf_op jit(solution)/shard_map/ppermute | solution.py:95
  20.2 1.1 %collective-permute-start.7 = (bf16[64,768]{1,0:T(8,128)(2,1)S(1)}, bf16[64,768]{1,0:T(8,128)(2,1)S(1)}, u32[]{:S(2)}, u32[]{:S(2)}) collective-permute-start(bf16[64,768]{1,0:T(8,128)(2,1)S(1)} %shard_map.110.refs_0_.refs_2_), channel_id=1, source_target_pairs={{0,4},{4,0},{8,12},{12,8},{1,5},{5,1},{9,13},{13,9},{2,6},{6,2},{1... | collective-permute-start | bytes 294920 | tf_op jit(solution)/shard_map/ppermute | solution.py:95
  21.3 2.4 %shard_map.112.refs_9_.w = bf16[3072,768]{1,0:T(8,128)(2,1)S(1)} custom-call(bf16[3072,768]{1,0:T(8,128)(2,1)} %source.1, bf16[64,768]{1,0:T(8,128)(2,1)S(1)} %shard_map.110.refs_0_.refs_2_, bf16[48,128]{1,0:T(8,128)(2,1)S(1)} %get-tuple-element.66.refs_1_.chip), custom_call_target="tpu_custom_call" | custom-call | flops 10000000000 | bytes 1 | tf_op jit(solution)/shard_map/pallas_call | solution.py:505
  23.8 1.0 %collective-permute-done.7.refs_3_ = bf16[64,768]{1,0:T(8,128)(2,1)S(1)} collective-permute-done((bf16[64,768]{1,0:T(8,128)(2,1)S(1)}, bf16[64,768]{1,0:T(8,128)(2,1)S(1)}, u32[]{:S(2)}, u32[]{:S(2)}) %collective-permute-start.7) | collective-permute-done | bytes 98336 | tf_op jit(solution)/shard_map/ppermute | solution.py:95
  25.8 1.1 %collective-permute-start.5 = (bf16[48,128]{1,0:T(8,128)(2,1)S(1)}, bf16[48,128]{1,0:T(8,128)(2,1)S(1)}, u32[]{:S(2)}, u32[]{:S(2)}) collective-permute-start(bf16[48,128]{1,0:T(8,128)(2,1)S(1)} %get-tuple-element.66.refs_1_.chip), channel_id=1, source_target_pairs={{0,2},{1,3},{2,0},{3,1},{4,6},{5,7},{6,4},{7,5},{8,10},{9,11},{10,... | collective-permute-start | bytes 36872 | tf_op jit(solution)/shard_map/ppermute | solution.py:95
  27.7 1.1 %collective-permute-start.13 = (bf16[128,1536]{1,0:T(8,128)(2,1)S(1)}, bf16[128,1536]{1,0:T(8,128)(2,1)S(1)}, u32[]{:S(2)}, u32[]{:S(2)}) collective-permute-start(bf16[128,1536]{1,0:T(8,128)(2,1)S(1)} %get-tuple-element.74.refs_0_), channel_id=1, source_target_pairs={{0,2},{1,3},{2,0},{3,1},{4,6},{5,7},{6,4},{7,5},{8,10},{9,11},{10,... | collective-permute-start | bytes 1179656 | tf_op jit(solution)/shard_map/ppermute | solution.py:95
  28.8 1.0 %collective-permute-start.14 = (bf16[32,128]{1,0:T(8,128)(2,1)S(1)}, bf16[32,128]{1,0:T(8,128)(2,1)S(1)}, u32[]{:S(2)}, u32[]{:S(2)}) collective-permute-start(bf16[32,128]{1,0:T(8,128)(2,1)S(1)} %get-tuple-element.75.refs_1_), channel_id=1, source_target_pairs={{0,2},{1,3},{2,0},{3,1},{4,6},{5,7},{6,4},{7,5},{8,10},{9,11},{10,... | collective-permute-start | bytes 24584 | tf_op jit(solution)/shard_map/ppermute | solution.py:95
  29.8 1.8 %collective-permute-done.5.stats.other = bf16[48,128]{1,0:T(8,128)(2,1)S(1)} collective-permute-done((bf16[48,128]{1,0:T(8,128)(2,1)S(1)}, bf16[48,128]{1,0:T(8,128)(2,1)S(1)}, u32[]{:S(2)}, u32[]{:S(2)}) %collective-permute-start.5) | collective-permute-done | bytes 12320 | tf_op jit(solution)/shard_map/ppermute | solution.py:95
  33.0 1.2 %collective-permute-done.9.act = bf16[128,1536]{1,0:T(8,128)(2,1)S(1)} collective-permute-done((bf16[128,1536]{1,0:T(8,128)(2,1)S(1)}, bf16[128,1536]{1,0:T(8,128)(2,1)S(1)}, u32[]{:S(2)}, u32[]{:S(2)}) %collective-permute-start.9) | collective-permute-done | bytes 393248 | tf_op jit(solution)/shard_map/ppermute | solution.py:95
  35.0 4.7 %collective-permute-start.10 = (bf16[64,768]{1,0:T(8,128)(2,1)S(1)}, bf16[64,768]{1,0:T(8,128)(2,1)S(1)}, u32[]{:S(2)}, u32[]{:S(2)}) collective-permute-start(bf16[64,768]{1,0:T(8,128)(2,1)S(1)} %get-tuple-element.80.refs_3_), channel_id=1, source_target_pairs={{0,12},{4,8},{8,4},{12,0},{1,13},{5,9},{9,5},{13,1},{2,14},{6,10},... | collective-permute-start | bytes 294920 | tf_op jit(solution)/shard_map/ppermute | solution.py:95
  41.8 1.2 %collective-permute-done.15.act = bf16[128,1536]{1,0:T(8,128)(2,1)S(1)} collective-permute-done((bf16[128,1536]{1,0:T(8,128)(2,1)S(1)}, bf16[128,1536]{1,0:T(8,128)(2,1)S(1)}, u32[]{:S(2)}, u32[]{:S(2)}) %collective-permute-start.15) | collective-permute-done | bytes 393248 | tf_op jit(solution)/shard_map/ppermute | solution.py:95
  43.7 4.0 %collective-permute-start.16 = (bf16[64,768]{1,0:T(8,128)(2,1)S(1)}, bf16[64,768]{1,0:T(8,128)(2,1)S(1)}, u32[]{:S(2)}, u32[]{:S(2)}) collective-permute-start(bf16[64,768]{1,0:T(8,128)(2,1)S(1)} %get-tuple-element.87), channel_id=1, source_target_pairs={{0,12},{4,8},{8,4},{12,0},{1,13},{5,9},{9,5},{13,1},{2,14},{6,10},... | collective-permute-start | bytes 294920 | tf_op jit(solution)/shard_map/ppermute | solution.py:95
  48.4 3.0 %collective-permute-done.16.refs_5_ = bf16[64,768]{1,0:T(8,128)(2,1)S(1)} collective-permute-done((bf16[64,768]{1,0:T(8,128)(2,1)S(1)}, bf16[64,768]{1,0:T(8,128)(2,1)S(1)}, u32[]{:S(2)}, u32[]{:S(2)}) %collective-permute-start.16) | collective-permute-done | bytes 98336 | tf_op jit(solution)/shard_map/ppermute | solution.py:95
  51.5 4.3 %collective-permute-done.17.refs_6_ = bf16[64,768]{1,0:T(8,128)(2,1)S(1)} collective-permute-done((bf16[64,768]{1,0:T(8,128)(2,1)S(1)}, bf16[64,768]{1,0:T(8,128)(2,1)S(1)}, u32[]{:S(2)}, u32[]{:S(2)}) %collective-permute-start.17) | collective-permute-done | bytes 98336 | tf_op jit(solution)/shard_map/ppermute | solution.py:95
  56.4 1.2 %collective-permute-done.19.right = f32[72,128]{1,0:T(8,128)S(1)} collective-permute-done((f32[72,128]{1,0:T(8,128)S(1)}, f32[72,128]{1,0:T(8,128)S(1)}, u32[]{:S(2)}, u32[]{:S(2)}) %collective-permute-start.19) | collective-permute-done | bytes 36896 | tf_op jit(solution)/shard_map/ppermute | solution.py:95
  57.7 2.8 %collective-permute-start.20 = (f32[72,128]{1,0:T(8,128)S(1)}, f32[72,128]{1,0:T(8,128)S(1)}, u32[]{:S(2)}, u32[]{:S(2)}) collective-permute-start(f32[72,128]{1,0:T(8,128)S(1)} %shard_map.124.mine), channel_id=1, source_target_pairs={{0,18},{1,19},{2,16},{3,17},{16,2},{17,3},{18,0},{19,1},{4,22},{5,... | collective-permute-start | bytes 110600 | tf_op jit(solution)/shard_map/ppermute | solution.py:95
  62.6 1.8 %collective-permute-done.21.other = f32[72,128]{1,0:T(8,128)S(1)} collective-permute-done((f32[72,128]{1,0:T(8,128)S(1)}, f32[72,128]{1,0:T(8,128)S(1)}, u32[]{:S(2)}, u32[]{:S(2)}) %collective-permute-start.21) | collective-permute-done | bytes 36896 | tf_op jit(solution)/shard_map/ppermute | solution.py:95
  (48 shorter events, 13.9 us)
Async XLA Ops:
  1.7 8.9 %collective-permute-start.1 = (bf16[64,768]{1,0:T(8,128)(2,1)S(1)}, bf16[64,768]{1,0:T(8,128)(2,1)S(1)}, u32[]{:S(2)}, u32[]{:S(2)}) collective-permute-start(bf16[64,768]{1,0:T(8,128)(2,1)S(1)} %get-tuple-element.53), channel_id=1, source_target_pairs={{0,8},{4,12},{8,0},{12,4},{1,9},{5,13},{9,1},{13,5},{2,10},{6,14},... | collective-permute-start | bytes 294920 | tf_op jit(solution)/shard_map/ppermute | solution.py:95
  5.8 9.8 %collective-permute-start = (bf16[128,768]{1,0:T(8,128)(2,1)S(1)}, bf16[128,768]{1,0:T(8,128)(2,1)S(1)}, u32[]{:S(2)}, u32[]{:S(2)}) collective-permute-start(bf16[128,768]{1,0:T(8,128)(2,1)S(1)} %get-tuple-element.47.tokens.own.hidden), channel_id=1, source_target_pairs={{0,4},{4,0},{8,12},{12,8},{1,5},{5,1},{9,13},{13,9},{2,6},{6,2},{1... | collective-permute-start | bytes 589832 | tf_op jit(solution)/shard_map/ppermute | solution.py:95
  10.6 5.0 %collective-permute-start.2 = (bf16[64,768]{1,0:T(8,128)(2,1)S(1)}, bf16[64,768]{1,0:T(8,128)(2,1)S(1)}, u32[]{:S(2)}, u32[]{:S(2)}) collective-permute-start(bf16[64,768]{1,0:T(8,128)(2,1)S(1)} %shard_map.106.refs_0_), channel_id=1, source_target_pairs={{0,4},{4,0},{8,12},{12,8},{1,5},{5,1},{9,13},{13,9},{2,6},{6,2},{1... | collective-permute-start | bytes 294920 | tf_op jit(solution)/shard_map/ppermute | solution.py:95
  11.5 8.7 %collective-permute-start.6 = (bf16[64,768]{1,0:T(8,128)(2,1)S(1)}, bf16[64,768]{1,0:T(8,128)(2,1)S(1)}, u32[]{:S(2)}, u32[]{:S(2)}) collective-permute-start(bf16[64,768]{1,0:T(8,128)(2,1)S(1)} %get-tuple-element.69), channel_id=1, source_target_pairs={{0,8},{4,12},{8,0},{12,4},{1,9},{5,13},{9,1},{13,5},{2,10},{6,14},... | collective-permute-start | bytes 294920 | tf_op jit(solution)/shard_map/ppermute | solution.py:95
  16.5 1.9 %collective-permute-start.3 = (bf16[144,1664]{1,0:T(8,128)(2,1)S(1)}, bf16[144,1664]{1,0:T(8,128)(2,1)S(1)}, u32[]{:S(2)}, u32[]{:S(2)}) collective-permute-start(bf16[144,1664]{1,0:T(8,128)(2,1)S(1)} %get-tuple-element.59._), channel_id=1, source_target_pairs={{0,1},{1,0},{2,3},{3,2},{4,5},{5,4},{6,7},{7,6},{8,9},{9,8},{10,11... | collective-permute-start | bytes 1437704 | tf_op jit(solution)/shard_map/ppermute | solution.py:95
  18.6 13.0 %collective-permute-start.4 = (bf16[144,1536]{1,0:T(8,128)(2,1)S(1)}, bf16[144,1536]{1,0:T(8,128)(2,1)S(1)}, u32[]{:S(2)}, u32[]{:S(2)}) collective-permute-start(bf16[144,1536]{1,0:T(8,128)(2,1)S(1)} %get-tuple-element.64._.refs_7_.first_sent), channel_id=1, source_target_pairs={{0,2},{1,3},{2,0},{3,1},{4,6},{5,7},{6,4},{7,5},{8,10},{9,11},{10,... | collective-permute-start | bytes 1327112 | tf_op jit(solution)/shard_map/ppermute | solution.py:95
  20.2 4.7 %collective-permute-start.7 = (bf16[64,768]{1,0:T(8,128)(2,1)S(1)}, bf16[64,768]{1,0:T(8,128)(2,1)S(1)}, u32[]{:S(2)}, u32[]{:S(2)}) collective-permute-start(bf16[64,768]{1,0:T(8,128)(2,1)S(1)} %shard_map.110.refs_0_.refs_2_), channel_id=1, source_target_pairs={{0,4},{4,0},{8,12},{12,8},{1,5},{5,1},{9,13},{13,9},{2,6},{6,2},{1... | collective-permute-start | bytes 294920 | tf_op jit(solution)/shard_map/ppermute | solution.py:95
  21.3 2.4 %copy-start.1 = (f32[8,128]{1,0:T(8,128)S(1)}, f32[8,128]{1,0:T(8,128)}, u32[]{:S(2)}) copy-start(f32[8,128]{1,0:T(8,128)} %constant.2.clone.alphas) | copy-start | bytes 12292
  25.7 1.8 %collective-permute-start.8 = (bf16[128,1664]{1,0:T(8,128)(2,1)S(1)}, bf16[128,1664]{1,0:T(8,128)(2,1)S(1)}, u32[]{:S(2)}, u32[]{:S(2)}) collective-permute-start(bf16[128,1664]{1,0:T(8,128)(2,1)S(1)} %get-tuple-element.72._), channel_id=1, source_target_pairs={{0,1},{1,0},{2,3},{3,2},{4,5},{5,4},{6,7},{7,6},{8,9},{9,8},{10,11... | collective-permute-start | bytes 1277960 | tf_op jit(solution)/shard_map/ppermute | solution.py:95
  25.8 5.9 %collective-permute-start.5 = (bf16[48,128]{1,0:T(8,128)(2,1)S(1)}, bf16[48,128]{1,0:T(8,128)(2,1)S(1)}, u32[]{:S(2)}, u32[]{:S(2)}) collective-permute-start(bf16[48,128]{1,0:T(8,128)(2,1)S(1)} %get-tuple-element.66.refs_1_.chip), channel_id=1, source_target_pairs={{0,2},{1,3},{2,0},{3,1},{4,6},{5,7},{6,4},{7,5},{8,10},{9,11},{10,... | collective-permute-start | bytes 36872 | tf_op jit(solution)/shard_map/ppermute | solution.py:95
  27.7 12.6 %collective-permute-start.13 = (bf16[128,1536]{1,0:T(8,128)(2,1)S(1)}, bf16[128,1536]{1,0:T(8,128)(2,1)S(1)}, u32[]{:S(2)}, u32[]{:S(2)}) collective-permute-start(bf16[128,1536]{1,0:T(8,128)(2,1)S(1)} %get-tuple-element.74.refs_0_), channel_id=1, source_target_pairs={{0,2},{1,3},{2,0},{3,1},{4,6},{5,7},{6,4},{7,5},{8,10},{9,11},{10,... | collective-permute-start | bytes 1179656 | tf_op jit(solution)/shard_map/ppermute | solution.py:95
  28.8 11.5 %collective-permute-start.14 = (bf16[32,128]{1,0:T(8,128)(2,1)S(1)}, bf16[32,128]{1,0:T(8,128)(2,1)S(1)}, u32[]{:S(2)}, u32[]{:S(2)}) collective-permute-start(bf16[32,128]{1,0:T(8,128)(2,1)S(1)} %get-tuple-element.75.refs_1_), channel_id=1, source_target_pairs={{0,2},{1,3},{2,0},{3,1},{4,6},{5,7},{6,4},{7,5},{8,10},{9,11},{10,... | collective-permute-start | bytes 24584 | tf_op jit(solution)/shard_map/ppermute | solution.py:95
  32.5 1.8 %collective-permute-start.9 = (bf16[128,1536]{1,0:T(8,128)(2,1)S(1)}, bf16[128,1536]{1,0:T(8,128)(2,1)S(1)}, u32[]{:S(2)}, u32[]{:S(2)}) collective-permute-start(bf16[128,1536]{1,0:T(8,128)(2,1)S(1)} %shard_map.116.act), channel_id=1, source_target_pairs={{0,1},{1,0},{2,3},{3,2},{4,5},{5,4},{6,7},{7,6},{8,9},{9,8},{10,11... | collective-permute-start | bytes 1179656 | tf_op jit(solution)/shard_map/ppermute | solution.py:95
  35.0 12.7 %collective-permute-start.10 = (bf16[64,768]{1,0:T(8,128)(2,1)S(1)}, bf16[64,768]{1,0:T(8,128)(2,1)S(1)}, u32[]{:S(2)}, u32[]{:S(2)}) collective-permute-start(bf16[64,768]{1,0:T(8,128)(2,1)S(1)} %get-tuple-element.80.refs_3_), channel_id=1, source_target_pairs={{0,12},{4,8},{8,4},{12,0},{1,13},{5,9},{9,5},{13,1},{2,14},{6,10},... | collective-permute-start | bytes 294920 | tf_op jit(solution)/shard_map/ppermute | solution.py:95
  39.7 8.7 %collective-permute-start.11 = (bf16[64,768]{1,0:T(8,128)(2,1)S(1)}, bf16[64,768]{1,0:T(8,128)(2,1)S(1)}, u32[]{:S(2)}, u32[]{:S(2)}) collective-permute-start(bf16[64,768]{1,0:T(8,128)(2,1)S(1)} %get-tuple-element.81.refs_2_), channel_id=1, source_target_pairs={{0,8},{4,12},{8,0},{12,4},{1,9},{5,13},{9,1},{13,5},{2,10},{6,14},... | collective-permute-start | bytes 294920 | tf_op jit(solution)/shard_map/ppermute | solution.py:95
  39.7 8.7 %collective-permute-start.12 = (bf16[64,768]{1,0:T(8,128)(2,1)S(1)}, bf16[64,768]{1,0:T(8,128)(2,1)S(1)}, u32[]{:S(2)}, u32[]{:S(2)}) collective-permute-start(bf16[64,768]{1,0:T(8,128)(2,1)S(1)} %get-tuple-element.82.refs_1_), channel_id=1, source_target_pairs={{0,4},{4,0},{8,12},{12,8},{1,5},{5,1},{9,13},{13,9},{2,6},{6,2},{1... | collective-permute-start | bytes 294920 | tf_op jit(solution)/shard_map/ppermute | solution.py:95
  41.2 1.8 %collective-permute-start.15 = (bf16[128,1536]{1,0:T(8,128)(2,1)S(1)}, bf16[128,1536]{1,0:T(8,128)(2,1)S(1)}, u32[]{:S(2)}, u32[]{:S(2)}) collective-permute-start(bf16[128,1536]{1,0:T(8,128)(2,1)S(1)} %shard_map.119.act), channel_id=1, source_target_pairs={{0,1},{1,0},{2,3},{3,2},{4,5},{5,4},{6,7},{7,6},{8,9},{9,8},{10,11... | collective-permute-start | bytes 1179656 | tf_op jit(solution)/shard_map/ppermute | solution.py:95
  43.7 7.7 %collective-permute-start.16 = (bf16[64,768]{1,0:T(8,128)(2,1)S(1)}, bf16[64,768]{1,0:T(8,128)(2,1)S(1)}, u32[]{:S(2)}, u32[]{:S(2)}) collective-permute-start(bf16[64,768]{1,0:T(8,128)(2,1)S(1)} %get-tuple-element.87), channel_id=1, source_target_pairs={{0,12},{4,8},{8,4},{12,0},{1,13},{5,9},{9,5},{13,1},{2,14},{6,10},... | collective-permute-start | bytes 294920 | tf_op jit(solution)/shard_map/ppermute | solution.py:95
  47.8 8.0 %collective-permute-start.17 = (bf16[64,768]{1,0:T(8,128)(2,1)S(1)}, bf16[64,768]{1,0:T(8,128)(2,1)S(1)}, u32[]{:S(2)}, u32[]{:S(2)}) collective-permute-start(bf16[64,768]{1,0:T(8,128)(2,1)S(1)} %get-tuple-element.88), channel_id=1, source_target_pairs={{0,8},{4,12},{8,0},{12,4},{1,9},{5,13},{9,1},{13,5},{2,10},{6,14},... | collective-permute-start | bytes 294920 | tf_op jit(solution)/shard_map/ppermute | solution.py:95
  47.8 8.0 %collective-permute-start.18 = (bf16[64,768]{1,0:T(8,128)(2,1)S(1)}, bf16[64,768]{1,0:T(8,128)(2,1)S(1)}, u32[]{:S(2)}, u32[]{:S(2)}) collective-permute-start(bf16[64,768]{1,0:T(8,128)(2,1)S(1)} %get-tuple-element.89), channel_id=1, source_target_pairs={{0,4},{4,0},{8,12},{12,8},{1,5},{5,1},{9,13},{13,9},{2,6},{6,2},{1... | collective-permute-start | bytes 294920 | tf_op jit(solution)/shard_map/ppermute | solution.py:95
  56.4 1.3 %collective-permute-start.19 = (f32[72,128]{1,0:T(8,128)S(1)}, f32[72,128]{1,0:T(8,128)S(1)}, u32[]{:S(2)}, u32[]{:S(2)}) collective-permute-start(f32[72,128]{1,0:T(8,128)S(1)} %get-tuple-element.91.left), channel_id=1, source_target_pairs={{0,1},{1,0},{2,3},{3,2},{4,5},{5,4},{6,7},{7,6},{8,9},{9,8},{10,11... | collective-permute-start | bytes 110600 | tf_op jit(solution)/shard_map/ppermute | solution.py:95
  57.7 5.0 %collective-permute-start.20 = (f32[72,128]{1,0:T(8,128)S(1)}, f32[72,128]{1,0:T(8,128)S(1)}, u32[]{:S(2)}, u32[]{:S(2)}) collective-permute-start(f32[72,128]{1,0:T(8,128)S(1)} %shard_map.124.mine), channel_id=1, source_target_pairs={{0,18},{1,19},{2,16},{3,17},{16,2},{17,3},{18,0},{19,1},{4,22},{5,... | collective-permute-start | bytes 110600 | tf_op jit(solution)/shard_map/ppermute | solution.py:95
  60.5 4.0 %collective-permute-start.21 = (f32[72,128]{1,0:T(8,128)S(1)}, f32[72,128]{1,0:T(8,128)S(1)}, u32[]{:S(2)}, u32[]{:S(2)}) collective-permute-start(f32[72,128]{1,0:T(8,128)S(1)} %shard_map.124.mine), channel_id=1, source_target_pairs={{0,16},{1,17},{2,18},{3,19},{16,0},{17,1},{18,2},{19,3},{4,20},{5,... | collective-permute-start | bytes 110600 | tf_op jit(solution)/shard_map/ppermute | solution.py:95
  61.0 4.0 %collective-permute-start.22 = (f32[72,128]{1,0:T(8,128)S(1)}, f32[72,128]{1,0:T(8,128)S(1)}, u32[]{:S(2)}, u32[]{:S(2)}) collective-permute-start(f32[72,128]{1,0:T(8,128)S(1)} %shard_map.124.mine), channel_id=1, source_target_pairs={{0,2},{1,3},{2,0},{3,1},{16,18},{17,19},{18,16},{19,17},{4,6},{5,7... | collective-permute-start | bytes 110600 | tf_op jit(solution)/shard_map/ppermute | solution.py:95
  (1 other events, 2.4 us)

commit v11 on v10

--- a/solution.py
+++ b/solution.py
@@ -218,13 +218,14 @@
         copy.wait()
 
 
-def prepare_kernel(table_in, tokens, mod_in, out_weight, w, *refs):
+def prepare_kernel(table_in, timestep, tokens, mod_in, out_weight, w, *refs):
     later, refs = refs[: CHUNKS - 1], refs[CHUNKS - 1 :]
     gathers, refs = refs[:CHUNKS], refs[CHUNKS:]
     spreads, refs = refs[:CHUNKS], refs[CHUNKS:]
     texts, refs = refs[:CHUNKS], refs[CHUNKS:]
-    held, kept, mod, weight, rows_out, ends_out, slots_out, video_out = refs[:8]
-    table, sems, small = refs[8:]
+    held, kept, mod, weight, rows_out, ends_out, slots_out, video_out, step_out = refs[:9]
+    table, sems, small = refs[9:]
+    step_out[...] = jnp.full(step_out.shape, timestep[0], jnp.int32)
     core = lax.axis_index("narrow") % 2
     sources = (table_in, mod_in, out_weight)
     copies = [
@@ -284,7 +285,7 @@
     z_out, sent_out, side_out = refs[-3:]
     core = lax.axis_index("narrow") % 2
     units = w.shape[1]
-    rows = side_out.shape[0]
+    rows = place.shape[0]
     pieces = []
     for p in range(k + 1):
         of_chunk = slice(QUOTAS[p], QUOTAS[p + 1])
@@ -297,11 +298,15 @@
     if k == 0:
         z = jnp.concatenate([z, sums[...]], 0)
     z_out[...] = z
+    if k == 0:
+        lead = side_out.shape[1] - 8 * 128
+        side_out[:, units:lead] = ends[...]
     for t in range(0, units, TILE):
-        product = jnp.dot(z, w[:, t : t + TILE], preferred_element_type=F32)
-        sent_out[:rows, t : t + TILE] = product[:rows].astype(BF16)
+        columns = slice(t, t + TILE)
+        product = jnp.dot(z, w[:, columns], preferred_element_type=F32)
+        sent_out[:, columns] = product[:rows].astype(BF16)
         if k == 0:
-            sent_out[rows:, t : t + TILE] = rows_of(product[rows:], core)
+            side_out[:, columns] = rows_of(product[rows:], core)
     total = jnp.sum(x, -1, keepdims=True)
     square = jnp.sum(x * x, -1, keepdims=True)
     total_high = total.astype(BF16).astype(F32)
@@ -312,13 +317,14 @@
     side = jnp.where(lane == 17, total - total_high, side)
     side = jnp.where(lane == 18, square_high, side)
     side = jnp.where(lane == 19, square - square_high, side).astype(BF16)
-    side_out[...] = side
-    sent_out[:rows, units:] = side
     if k == 0:
-        sent_out[rows:, units:] = ends[...]
-
-
-def expand_kept_kernel(k, z, w, _, *refs):
+        for i in range(rows // 16):
+            side_out[:, lead + 128 * i : lead + 128 * (i + 1)] = side[16 * i : 16 * (i + 1)]
+    else:
+        side_out[...] = side
+
+
+def expand_kept_kernel(k, z, w, _, __, *refs):
     kept_out = refs[-1 if k else -2]
     core = lax.axis_index("narrow") % 2
     rows = kept_out.shape[0]
@@ -341,25 +347,35 @@
     return side.T
 
 
-def merge_kernel(k, kept, side, came, sums, ends, *refs):
-    total_out, sent_out, side_out, stats_out = refs[-4:]
-    rows, units = kept.shape
-    add = lambda left, right: left[...].astype(F32) + right.astype(F32)
-    total = kept[...] + came[:rows, :units].astype(F32)
-    total_out[...] = total
-    sent_out[:rows, :] = total.astype(BF16)
-    both = add(side, came[:rows, units:])
+def stats_kernel(k, rows, side, came, *refs):
+    side_out, stats_out = refs[-2:]
+    lead = stats_out.shape[1] - 256
+    if k == 0:
+        kept_sums = refs[0]
+        units = kept_sums.shape[1]
+        stats_out[:, :units] = (kept_sums[...].astype(F32) + came[:, :units].astype(F32)).astype(BF16)
+        both = side[:, units:].astype(F32) + came[:, units:].astype(F32)
+        stats_out[:, units:lead] = both[:, : lead - units].astype(BF16)
+        both = both[:, lead - units :]
+        both = jnp.concatenate([both[:, 128 * i : 128 * (i + 1)] for i in range(rows // 16)], 0)
+    else:
+        both = side[...].astype(F32) + came[...].astype(F32)
     side_out[...] = both
-    stats_out[:32, :] = across_rows(both)[:32].astype(BF16)
-    if k == 0:
-        sent_out[rows:, :] = add(sums, came[rows:, :units]).astype(BF16)
-        stats_out[32:, :] = add(ends, came[rows:, units:]).astype(BF16)
+    stats = across_rows(both)[:32].astype(BF16)
+    stats_out[:, lead : lead + 128] = stats[:16]
+    stats_out[:, lead + 128 :] = stats[16:]
+
+
+def merge_kernel(kept, came, _, sent_out):
+    sent_out[...] = (kept[...] + came[...].astype(F32)).astype(BF16)
 
 
 def activate_kernel(features, text, total, came, side, stats, first_sent, first_came, *refs):
     act_out = refs[-1]
-    rows, units = total.shape
-    sides = [side[...], across_rows(stats[:32, :].astype(F32))[:rows]]
+    rows, units = act_out.shape
+    lead = stats.shape[1] - 256
+    stats = jnp.concatenate([stats[:, lead : lead + 128], stats[:, lead + 128 :]], 0)
+    sides = [side[...], across_rows(stats.astype(F32))[:rows]]
     lane = lax.broadcasted_iota(jnp.int32, (rows, 128), 1)
     field = lane % 4
     summed = sides[0] + sides[1]
@@ -389,11 +405,11 @@
             packed = part if packed is None else packed + part
             shift += 8
     packed = packed[:, :64].astype(BF16)
-    own, other = first_sent[-16:, :units], first_came[-16:, :units]
+    own, other = first_sent[:, :units], first_came[:, :units]
     factors = jnp.concatenate([own, own, other, other], 0)
     for t in range(0, units, TILE):
         columns = slice(t, t + TILE)
-        pre = total[:, columns] + came[:rows, columns].astype(F32)
+        pre = total[:rows, columns].astype(F32) + came[:rows, columns].astype(F32)
         extra = jnp.dot(packed, factors[:, columns], preferred_element_type=F32)
         act_out[:, columns] = jax.nn.gelu(pre * scale + extra, approximate=True).astype(BF16)
 
@@ -404,7 +420,9 @@
     rows = pl.ds(pl.multiple_of(core * units, 128), units)
     out[...] = jnp.dot(act[...], w[rows, :], preferred_element_type=F32)
     if k == 0:
-        total = chip[-16:, :].astype(F32) + other[-16:, :].astype(F32)
+        units = w.shape[0] // 2
+        ends = slice(units, units + 128)
+        total = chip[:, ends].astype(F32) + other[:, ends].astype(F32)
         total = total[:8] + total[8:]
         total = total + pltpu.roll(total, 4, 0)
         own = mine[...].astype(F32)
@@ -460,12 +478,12 @@
     out[...] = left[...] + right[...]
 
 
-def noise_kernel(timestep, alphas, video, latent, _, out):
+def noise_kernel(step, alphas, video, latent, _, out):
     index = lax.broadcasted_iota(jnp.int32, (8, 128), 0) * 128 + lax.broadcasted_iota(
         jnp.int32, (8, 128), 1
     )
     alpha = jnp.sum(
-        jnp.sum(jnp.where(index == timestep[0], alphas[...], 0.0), 0, keepdims=True),
+        jnp.sum(jnp.where(index == step[...], alphas[...], 0.0), 0, keepdims=True),
         1,
         keepdims=True,
     )
@@ -550,15 +568,17 @@
             ((16, 128), BF16),
             ((CAP, 128), F32),
             ((8, CAP), F32),
+            ((8, 128), jnp.int32),
         ],
         [
             in_place(split_table),
+            timestep,
             tokens,
             in_place(modulation),
             in_place(output_weight.T),
             in_place(expand_weight),
         ],
-        "avaaa",
+        "asvaaa",
         [
             pltpu.SMEM(split_table.shape, jnp.int32),
             pltpu.SemaphoreType.DMA((2, tiles)),
@@ -569,7 +589,7 @@
     gathers, made = made[:CHUNKS], made[CHUNKS:]
     spreads, made = made[:CHUNKS], made[CHUNKS:]
     texts, made = made[:CHUNKS], made[CHUNKS:]
-    held_sent, held_kept, mod, out_weight, rows_in, ends_mine, slots, video = made
+    held_sent, held_kept, mod, out_weight, rows_in, ends_mine, slots, video, step = made
     later = [swap(piece, "wide", 2, 4) for piece in later]
     (across,) = call(pass_kernel, [(across.shape, BF16)], [across, slots], "va")
     far = [across, swap(across, "wide", 1, 4)]
@@ -578,34 +598,34 @@
     before = []
     for k in chunks:
         rows = 2 * size_of(k)
-        sent_rows = rows + (16 if k == 0 else 0)
+        extra = 16 if k == 0 else 0
         z, sent, side = call(
             functools.partial(expand_sent_kernel, k),
-            [((sent_rows, features), BF16), ((sent_rows, payload), BF16), ((rows, 128), BF16)],
+            [
+                ((rows + extra, features), BF16),
+                ((rows, units), BF16),
+                ((16, payload + 8 * rows) if k == 0 else (rows, 128), BF16),
+            ],
             [texts[k], mod, gathers[k], tokens, near, *far, held_sent, rows_in, ends_mine, *before],
             "vvvvv" + "v" * len(far) + "vvv" + "a" * len(before),
             weight=LONG,
         )
-        came = swap(sent, "narrow", 1, 4)
+        side_came, came = [swap(array, "narrow", 1, 4) for array in (side, sent)]
         kept, *sums_made = call(
             functools.partial(expand_kept_kernel, k),
             [((rows, units), F32)] + ([((16, units), BF16)] if k == 0 else []),
-            [z, held_kept, sent],
-            "vva",
-            weight=LONG if k == 0 else 1,
+            [z, held_kept, sent, side],
+            "vvaa",
+            weight=LONG,
         )
-        sums = sums_made[0] if k == 0 else sums
-        total, sent, side, stats = call(
-            functools.partial(merge_kernel, k),
-            [
-                ((rows, units), F32),
-                ((sent_rows, units), BF16),
-                ((rows, 128), F32),
-                ((sent_rows - rows + 32, 128), BF16),
-            ],
-            [kept, side, came, sums, ends_mine],
-            "vvvvv",
+        side, stats = call(
+            functools.partial(stats_kernel, k, rows),
+            [((rows, 128), F32), ((16, 256 + (payload if k == 0 else 0)), BF16)],
+            [side, side_came, *sums_made],
+            "vv" + "v" * len(sums_made),
         )
+        stats_came = swap(stats, "narrow", 2, 4)
+        (sent,) = call(merge_kernel, [((rows, units), BF16)], [kept, came, stats], "vva")
         if k + 1 < CHUNKS:
             (across,) = call(
                 pass_kernel, [(later[k].shape, BF16)], [later[k], sent], "va"
@@ -624,18 +644,17 @@
             (noise,) = call(
                 noise_kernel,
                 [((width + 8, CAP), F32)],
-                [timestep, alpha_constant(), video, latent.T, sent],
-                "svvva",
+                [step, alpha_constant(), video, latent.T, sent],
+                "vvvva",
                 weight=LONG,
             )
         before = [sent, noise, held_out]
-        came, stats_came = [swap(array, "narrow", 2, 4) for array in (sent, stats)]
-        merged.append((sent, stats, [total, came, side, stats_came]))
+        came = swap(sent, "narrow", 2, 4)
+        merged.append((sent, stats, [sent, came, side, stats_came]))
 
     returned = []
     before = []
-    first = [merged[0][0], merged[0][2][1]]
-    first_stats = [merged[0][1], merged[0][2][3]]
+    first = [merged[0][1], merged[0][2][3]]
     for k in chunks:
         rows = 2 * size_of(k)
         if k + 1 < CHUNKS:
@@ -650,7 +669,7 @@
         out, *ends_made = call(
             functools.partial(contract_own_kernel, k),
             [((rows, features), F32)] + ([((128, 128), F32)] if k == 0 else []),
-            [act, held_out, ends_mine, *first_stats],
+            [act, held_out, ends_mine, *first],
             "vvvvv",
             weight=LONG,
         )

time: 65.8 us -> 64.9 us (0.986)
  waiting for transfers between devices: 19.2 us -> 16.2 us
  starting transfers between devices: 29.7 us -> 31.9 us
    ppermute x23 -> x25, waiting for transfers between devices: 19.2 us -> 16.2 us  [swap(): return lax.ppermute(array, axis, [(i, i ^ distance) for i in range(size)])]
    ppermute x23 -> x25, starting transfers between devices: 29.7 us -> 31.9 us  [swap(): return lax.ppermute(array, axis, [(i, i ^ distance) for i in range(size)])]
    pallas_call x22 -> x24, Pallas kernels: 15.2 us -> 15.1 us  [call(): pl.pallas_call(kernel, out_shape=[jax.ShapeDtypeStruct(shape, dtype) for...]
  transfers between devices with their start and end apart: 23 -> 25, of which waited for: 13 -> 14; matrix products, arithmetic and copies ran while one was open for 0% -> 0% of each run, Pallas kernels for 20% -> 20%
where the time goes in v11:
time: 64.9 us; the launch traced here: 64.7 us
  starting transfers between devices  31.9 us (49%)
  waiting for transfers between devices  16.2 us (25%)
  Pallas kernels  15.1 us (23%)
  between operations  1.49 us (2%)
    ppermute x25, starting transfers between devices, swap(): return lax.ppermute(array, axis, [(i, i ^ distance) for i in range(size)])  31.9 us
    ppermute x25, waiting for transfers between devices, swap(): return lax.ppermute(array, axis, [(i, i ^ distance) for i in range(size)])  16.2 us
    pallas_call x24, Pallas kernels, call(): pl.pallas_call(kernel, out_shape=[jax.ShapeDtypeStruct(shape, dtype) for...  15.1 us
  transfers between devices with their start and end apart: 25, of which 14 were waited for; matrix products, arithmetic and copies ran while one was open for 0% of the time, Pallas kernels for 20%

profile of v11, /device:TPU:0, one launch (start us, length us, event | category | flops | bytes accessed | tf_op | source)
XLA Modules:
  0.0 64.7 jit_solution(6254759798702358480)
XLA Ops:
  0.6 1.0 %shard_map.104 = (bf16[128,768]{1,0:T(8,128)(2,1)S(1)}, bf16[64,768]{1,0:T(8,128)(2,1)S(1)}) custom-call(bf16[128,768]{1,0:T(8,128)(2,1)} %bitcast.6), custom_call_target="tpu_custom_call" | custom-call | flops 1 | bytes 1 | tf_op jit(solution)/shard_map/pallas_call | solution.py:523
  1.7 4.1 %collective-permute-start.1 = (bf16[64,768]{1,0:T(8,128)(2,1)S(1)}, bf16[64,768]{1,0:T(8,128)(2,1)S(1)}, u32[]{:S(2)}, u32[]{:S(2)}) collective-permute-start(bf16[64,768]{1,0:T(8,128)(2,1)S(1)} %get-tuple-element.50), channel_id=1, source_target_pairs={{0,8},{4,12},{8,0},{12,4},{1,9},{5,13},{9,1},{13,5},{2,10},{6,14},... | collective-permute-start | bytes 294920 | tf_op jit(solution)/shard_map/ppermute | solution.py:95
  5.8 1.6 %collective-permute-start = (bf16[128,768]{1,0:T(8,128)(2,1)S(1)}, bf16[128,768]{1,0:T(8,128)(2,1)S(1)}, u32[]{:S(2)}, u32[]{:S(2)}) collective-permute-start(bf16[128,768]{1,0:T(8,128)(2,1)S(1)} %get-tuple-element.44.tokens.own.hidden), channel_id=1, source_target_pairs={{0,4},{4,0},{8,12},{12,8},{1,5},{5,1},{9,13},{13,9},{2,6},{6,2},{1... | collective-permute-start | bytes 589832 | tf_op jit(solution)/shard_map/ppermute | solution.py:95
  8.0 2.5 %shard_map.105 = (bf16[64,768]{1,0:T(8,128)(2,1)S(1)}, bf16[128,256]{1,0:T(8,128)(2,1)S(1)}, bf16[128,512]{1,0:T(8,128)(2,1)S(1)}, bf16[256,128]{1,0:T(8,128)(2,...) custom-call(s32[4]{0:T(128)} %table_in.1, ...), custom_call_target="tpu_custom_call" | custom-call | flops 1 | bytes 1 | tf_op jit(solution)/shard_map/pallas_call | solution.py:523
  10.6 0.9 %collective-permute-start.2 = (bf16[64,768]{1,0:T(8,128)(2,1)S(1)}, bf16[64,768]{1,0:T(8,128)(2,1)S(1)}, u32[]{:S(2)}, u32[]{:S(2)}) collective-permute-start(bf16[64,768]{1,0:T(8,128)(2,1)S(1)} %shard_map.106.refs_0_), channel_id=1, source_target_pairs={{0,4},{4,0},{8,12},{12,8},{1,5},{5,1},{9,13},{13,9},{2,6},{6,2},{1... | collective-permute-start | bytes 294920 | tf_op jit(solution)/shard_map/ppermute | solution.py:95
  11.5 3.5 %collective-permute-start.7 = (bf16[64,768]{1,0:T(8,128)(2,1)S(1)}, bf16[64,768]{1,0:T(8,128)(2,1)S(1)}, u32[]{:S(2)}, u32[]{:S(2)}) collective-permute-start(bf16[64,768]{1,0:T(8,128)(2,1)S(1)} %get-tuple-element.64), channel_id=1, source_target_pairs={{0,8},{4,12},{8,0},{12,4},{1,9},{5,13},{9,1},{13,5},{2,10},{6,14},... | collective-permute-start | bytes 294920 | tf_op jit(solution)/shard_map/ppermute | solution.py:95
  15.2 0.9 %shard_map.107 = (bf16[144,768]{1,0:T(8,128)(2,1)S(1)}, bf16[128,1536]{1,0:T(8,128)(2,1)S(1)}, bf16[16,2688]{1,0:T(8,128)(2,1)S(1)}) custom-call(f32[128,128]{1,0:T(8,128)S(1)} %get-tuple-element.48.text, f32[8,768]{1,0:T(8,128)S(1)} %get-tuple-element.46.mod, bf16[128,256]{1,0:T(8,128)(2,1)S(1)} %get-tuple-element.49.place, ...), custom_call_target="tpu_custom_call" | custom-call | flops 10000000000 | bytes 1 | tf_op jit(solution)/shard_map/pallas_call | solution.py:523
  17.5 1.6 %collective-permute-start.6 = (bf16[16,1920]{1,0:T(8,128)(2,1)S(1)}, bf16[16,1920]{1,0:T(8,128)(2,1)S(1)}, u32[]{:S(2)}, u32[]{:S(2)}) collective-permute-start(bf16[16,1920]{1,0:T(8,128)(2,1)S(1)} %get-tuple-element.60._.refs_1_.first_sent.chip), channel_id=1, source_target_pairs={{0,2},{1,3},{2,0},{3,1},{4,6},{5,7},{6,4},{7,5},{8,10},{9,11},{10,... | collective-permute-start | bytes 184328 | tf_op jit(solution)/shard_map/ppermute | solution.py:95
  19.9 1.5 %collective-permute-start.8 = (bf16[64,768]{1,0:T(8,128)(2,1)S(1)}, bf16[64,768]{1,0:T(8,128)(2,1)S(1)}, u32[]{:S(2)}, u32[]{:S(2)}) collective-permute-start(bf16[64,768]{1,0:T(8,128)(2,1)S(1)} %shard_map.111.refs_0_.refs_2_), channel_id=1, source_target_pairs={{0,4},{4,0},{8,12},{12,8},{1,5},{5,1},{9,13},{13,9},{2,6},{6,2},{1... | collective-permute-start | bytes 294920 | tf_op jit(solution)/shard_map/ppermute | solution.py:95
  21.3 2.4 %shard_map.113.refs_9_.w = bf16[3072,768]{1,0:T(8,128)(2,1)S(1)} custom-call(bf16[3072,768]{1,0:T(8,128)(2,1)} %source.1, bf16[64,768]{1,0:T(8,128)(2,1)S(1)} %shard_map.111.refs_0_.refs_2_, bf16[16,1920]{1,0:T(8,128)(2,1)S(1)} %get-tuple-element.60._.refs_1_.first_sent.chip), custom_call_target="tpu_custom_call" | custom-call | flops 10000000000 | bytes 1 | tf_op jit(solution)/shard_map/pallas_call | solution.py:523
  23.8 0.9 %collective-permute-done.8.refs_3_ = bf16[64,768]{1,0:T(8,128)(2,1)S(1)} collective-permute-done((bf16[64,768]{1,0:T(8,128)(2,1)S(1)}, bf16[64,768]{1,0:T(8,128)(2,1)S(1)}, u32[]{:S(2)}, u32[]{:S(2)}) %collective-permute-start.8) | collective-permute-done | bytes 98336 | tf_op jit(solution)/shard_map/ppermute | solution.py:95
  24.7 0.9 %shard_map.114 = (bf16[128,768]{1,0:T(8,128)(2,1)S(1)}, bf16[128,1536]{1,0:T(8,128)(2,1)S(1)}, bf16[128,128]{1,0:T(8,128)(2,1)S(1)}) custom-call(f32[128,128]{1,0:T(8,128)S(1)} %get-tuple-element.62.text, f32[8,768]{1,0:T(8,128)S(1)} %get-tuple-element.46.mod, bf16[128,512]{1,0:T(8,128)(2,1)S(1)} %get-tuple-element.63.place, ...), custom_call_target="tpu_custom_call" | custom-call | flops 10000000000 | bytes 1 | tf_op jit(solution)/shard_map/pallas_call | solution.py:523
  26.9 1.4 %collective-permute-start.16 = (bf16[16,256]{1,0:T(8,128)(2,1)S(1)}, bf16[16,256]{1,0:T(8,128)(2,1)S(1)}, u32[]{:S(2)}, u32[]{:S(2)}) collective-permute-start(bf16[16,256]{1,0:T(8,128)(2,1)S(1)} %get-tuple-element.70._.refs_1_), channel_id=1, source_target_pairs={{0,2},{1,3},{2,0},{3,1},{4,6},{5,7},{6,4},{7,5},{8,10},{9,11},{10,... | collective-permute-start | bytes 24584 | tf_op jit(solution)/shard_map/ppermute | solution.py:95
  29.1 1.2 %collective-permute-done.5.came = bf16[128,1536]{1,0:T(8,128)(2,1)S(1)} collective-permute-done((bf16[128,1536]{1,0:T(8,128)(2,1)S(1)}, bf16[128,1536]{1,0:T(8,128)(2,1)S(1)}, u32[]{:S(2)}, u32[]{:S(2)}) %collective-permute-start.5) | collective-permute-done | bytes 393248 | tf_op jit(solution)/shard_map/ppermute | solution.py:95
  31.7 1.2 %collective-permute-done.11.act = bf16[128,1536]{1,0:T(8,128)(2,1)S(1)} collective-permute-done((bf16[128,1536]{1,0:T(8,128)(2,1)S(1)}, bf16[128,1536]{1,0:T(8,128)(2,1)S(1)}, u32[]{:S(2)}, u32[]{:S(2)}) %collective-permute-start.11) | collective-permute-done | bytes 393248 | tf_op jit(solution)/shard_map/ppermute | solution.py:95
  33.7 5.0 %collective-permute-start.12 = (bf16[64,768]{1,0:T(8,128)(2,1)S(1)}, bf16[64,768]{1,0:T(8,128)(2,1)S(1)}, u32[]{:S(2)}, u32[]{:S(2)}) collective-permute-start(bf16[64,768]{1,0:T(8,128)(2,1)S(1)} %get-tuple-element.75.refs_3_), channel_id=1, source_target_pairs={{0,12},{4,8},{8,4},{12,0},{1,13},{5,9},{9,5},{13,1},{2,14},{6,10},... | collective-permute-start | bytes 294920 | tf_op jit(solution)/shard_map/ppermute | solution.py:95
  40.8 1.2 %collective-permute-done.17.act = bf16[128,1536]{1,0:T(8,128)(2,1)S(1)} collective-permute-done((bf16[128,1536]{1,0:T(8,128)(2,1)S(1)}, bf16[128,1536]{1,0:T(8,128)(2,1)S(1)}, u32[]{:S(2)}, u32[]{:S(2)}) %collective-permute-start.17) | collective-permute-done | bytes 393248 | tf_op jit(solution)/shard_map/ppermute | solution.py:95
  42.8 4.9 %collective-permute-start.18 = (bf16[64,768]{1,0:T(8,128)(2,1)S(1)}, bf16[64,768]{1,0:T(8,128)(2,1)S(1)}, u32[]{:S(2)}, u32[]{:S(2)}) collective-permute-start(bf16[64,768]{1,0:T(8,128)(2,1)S(1)} %get-tuple-element.81), channel_id=1, source_target_pairs={{0,12},{4,8},{8,4},{12,0},{1,13},{5,9},{9,5},{13,1},{2,14},{6,10},... | collective-permute-start | bytes 294920 | tf_op jit(solution)/shard_map/ppermute | solution.py:95
  48.3 3.0 %collective-permute-done.18.refs_5_ = bf16[64,768]{1,0:T(8,128)(2,1)S(1)} collective-permute-done((bf16[64,768]{1,0:T(8,128)(2,1)S(1)}, bf16[64,768]{1,0:T(8,128)(2,1)S(1)}, u32[]{:S(2)}, u32[]{:S(2)}) %collective-permute-start.18) | collective-permute-done | bytes 98336 | tf_op jit(solution)/shard_map/ppermute | solution.py:95
  51.4 4.3 %collective-permute-done.19.refs_6_ = bf16[64,768]{1,0:T(8,128)(2,1)S(1)} collective-permute-done((bf16[64,768]{1,0:T(8,128)(2,1)S(1)}, bf16[64,768]{1,0:T(8,128)(2,1)S(1)}, u32[]{:S(2)}, u32[]{:S(2)}) %collective-permute-start.19) | collective-permute-done | bytes 98336 | tf_op jit(solution)/shard_map/ppermute | solution.py:95
  56.3 1.2 %collective-permute-done.21.right = f32[72,128]{1,0:T(8,128)S(1)} collective-permute-done((f32[72,128]{1,0:T(8,128)S(1)}, f32[72,128]{1,0:T(8,128)S(1)}, u32[]{:S(2)}, u32[]{:S(2)}) %collective-permute-start.21) | collective-permute-done | bytes 36896 | tf_op jit(solution)/shard_map/ppermute | solution.py:95
  57.5 2.0 %collective-permute-start.22 = (f32[72,128]{1,0:T(8,128)S(1)}, f32[72,128]{1,0:T(8,128)S(1)}, u32[]{:S(2)}, u32[]{:S(2)}) collective-permute-start(f32[72,128]{1,0:T(8,128)S(1)} %shard_map.126.mine), channel_id=1, source_target_pairs={{0,18},{1,19},{2,16},{3,17},{16,2},{17,3},{18,0},{19,1},{4,22},{5,... | collective-permute-start | bytes 110600 | tf_op jit(solution)/shard_map/ppermute | solution.py:95
  60.0 1.0 %collective-permute-start.24 = (f32[72,128]{1,0:T(8,128)S(1)}, f32[72,128]{1,0:T(8,128)S(1)}, u32[]{:S(2)}, u32[]{:S(2)}) collective-permute-start(f32[72,128]{1,0:T(8,128)S(1)} %shard_map.126.mine), channel_id=1, source_target_pairs={{0,2},{1,3},{2,0},{3,1},{16,18},{17,19},{18,16},{19,17},{4,6},{5,7... | collective-permute-start | bytes 110600 | tf_op jit(solution)/shard_map/ppermute | solution.py:95
  62.4 1.0 %collective-permute-done.23.other = f32[72,128]{1,0:T(8,128)S(1)} collective-permute-done((f32[72,128]{1,0:T(8,128)S(1)}, f32[72,128]{1,0:T(8,128)S(1)}, u32[]{:S(2)}, u32[]{:S(2)}) %collective-permute-start.23) | collective-permute-done | bytes 36896 | tf_op jit(solution)/shard_map/ppermute | solution.py:95
  (54 shorter events, 14.0 us)
Async XLA Ops:
  1.7 8.9 %collective-permute-start.1 = (bf16[64,768]{1,0:T(8,128)(2,1)S(1)}, bf16[64,768]{1,0:T(8,128)(2,1)S(1)}, u32[]{:S(2)}, u32[]{:S(2)}) collective-permute-start(bf16[64,768]{1,0:T(8,128)(2,1)S(1)} %get-tuple-element.50), channel_id=1, source_target_pairs={{0,8},{4,12},{8,0},{12,4},{1,9},{5,13},{9,1},{13,5},{2,10},{6,14},... | collective-permute-start | bytes 294920 | tf_op jit(solution)/shard_map/ppermute | solution.py:95
  5.8 9.5 %collective-permute-start = (bf16[128,768]{1,0:T(8,128)(2,1)S(1)}, bf16[128,768]{1,0:T(8,128)(2,1)S(1)}, u32[]{:S(2)}, u32[]{:S(2)}) collective-permute-start(bf16[128,768]{1,0:T(8,128)(2,1)S(1)} %get-tuple-element.44.tokens.own.hidden), channel_id=1, source_target_pairs={{0,4},{4,0},{8,12},{12,8},{1,5},{5,1},{9,13},{13,9},{2,6},{6,2},{1... | collective-permute-start | bytes 589832 | tf_op jit(solution)/shard_map/ppermute | solution.py:95
  10.6 4.7 %collective-permute-start.2 = (bf16[64,768]{1,0:T(8,128)(2,1)S(1)}, bf16[64,768]{1,0:T(8,128)(2,1)S(1)}, u32[]{:S(2)}, u32[]{:S(2)}) collective-permute-start(bf16[64,768]{1,0:T(8,128)(2,1)S(1)} %shard_map.106.refs_0_), channel_id=1, source_target_pairs={{0,4},{4,0},{8,12},{12,8},{1,5},{5,1},{9,13},{13,9},{2,6},{6,2},{1... | collective-permute-start | bytes 294920 | tf_op jit(solution)/shard_map/ppermute | solution.py:95
  11.5 8.4 %collective-permute-start.7 = (bf16[64,768]{1,0:T(8,128)(2,1)S(1)}, bf16[64,768]{1,0:T(8,128)(2,1)S(1)}, u32[]{:S(2)}, u32[]{:S(2)}) collective-permute-start(bf16[64,768]{1,0:T(8,128)(2,1)S(1)} %get-tuple-element.64), channel_id=1, source_target_pairs={{0,8},{4,12},{8,0},{12,4},{1,9},{5,13},{9,1},{13,5},{2,10},{6,14},... | collective-permute-start | bytes 294920 | tf_op jit(solution)/shard_map/ppermute | solution.py:95
  16.1 1.3 %collective-permute-start.4 = (bf16[16,2688]{1,0:T(8,128)(2,1)S(1)}, bf16[16,2688]{1,0:T(8,128)(2,1)S(1)}, u32[]{:S(2)}, u32[]{:S(2)}) collective-permute-start(bf16[16,2688]{1,0:T(8,128)(2,1)S(1)} %get-tuple-element.57.__.side), channel_id=1, source_target_pairs={{0,1},{1,0},{2,3},{3,2},{4,5},{5,4},{6,7},{7,6},{8,9},{9,8},{10,11... | collective-permute-start | bytes 258056 | tf_op jit(solution)/shard_map/ppermute | solution.py:95
  16.2 3.0 %collective-permute-start.3 = (bf16[128,1536]{1,0:T(8,128)(2,1)S(1)}, bf16[128,1536]{1,0:T(8,128)(2,1)S(1)}, u32[]{:S(2)}, u32[]{:S(2)}) collective-permute-start(bf16[128,1536]{1,0:T(8,128)(2,1)S(1)} %get-tuple-element.56._), channel_id=1, source_target_pairs={{0,1},{1,0},{2,3},{3,2},{4,5},{5,4},{6,7},{7,6},{8,9},{9,8},{10,11... | collective-permute-start | bytes 1179656 | tf_op jit(solution)/shard_map/ppermute | solution.py:95
  17.5 11.6 %collective-permute-start.6 = (bf16[16,1920]{1,0:T(8,128)(2,1)S(1)}, bf16[16,1920]{1,0:T(8,128)(2,1)S(1)}, u32[]{:S(2)}, u32[]{:S(2)}) collective-permute-start(bf16[16,1920]{1,0:T(8,128)(2,1)S(1)} %get-tuple-element.60._.refs_1_.first_sent.chip), channel_id=1, source_target_pairs={{0,2},{1,3},{2,0},{3,1},{4,6},{5,7},{6,4},{7,5},{8,10},{9,11},{10,... | collective-permute-start | bytes 184328 | tf_op jit(solution)/shard_map/ppermute | solution.py:95
  19.3 11.0 %collective-permute-start.5 = (bf16[128,1536]{1,0:T(8,128)(2,1)S(1)}, bf16[128,1536]{1,0:T(8,128)(2,1)S(1)}, u32[]{:S(2)}, u32[]{:S(2)}) collective-permute-start(bf16[128,1536]{1,0:T(8,128)(2,1)S(1)} %shard_map.110._.refs_7_.total), channel_id=1, source_target_pairs={{0,2},{1,3},{2,0},{3,1},{4,6},{5,7},{6,4},{7,5},{8,10},{9,11},{10,... | collective-permute-start | bytes 1179656 | tf_op jit(solution)/shard_map/ppermute | solution.py:95
  19.9 4.8 %collective-permute-start.8 = (bf16[64,768]{1,0:T(8,128)(2,1)S(1)}, bf16[64,768]{1,0:T(8,128)(2,1)S(1)}, u32[]{:S(2)}, u32[]{:S(2)}) collective-permute-start(bf16[64,768]{1,0:T(8,128)(2,1)S(1)} %shard_map.111.refs_0_.refs_2_), channel_id=1, source_target_pairs={{0,4},{4,0},{8,12},{12,8},{1,5},{5,1},{9,13},{13,9},{2,6},{6,2},{1... | collective-permute-start | bytes 294920 | tf_op jit(solution)/shard_map/ppermute | solution.py:95
  25.7 2.7 %collective-permute-start.9 = (bf16[128,1536]{1,0:T(8,128)(2,1)S(1)}, bf16[128,1536]{1,0:T(8,128)(2,1)S(1)}, u32[]{:S(2)}, u32[]{:S(2)}) collective-permute-start(bf16[128,1536]{1,0:T(8,128)(2,1)S(1)} %get-tuple-element.68._), channel_id=1, source_target_pairs={{0,1},{1,0},{2,3},{3,2},{4,5},{5,4},{6,7},{7,6},{8,9},{9,8},{10,11... | collective-permute-start | bytes 1179656 | tf_op jit(solution)/shard_map/ppermute | solution.py:95
  26.9 12.5 %collective-permute-start.16 = (bf16[16,256]{1,0:T(8,128)(2,1)S(1)}, bf16[16,256]{1,0:T(8,128)(2,1)S(1)}, u32[]{:S(2)}, u32[]{:S(2)}) collective-permute-start(bf16[16,256]{1,0:T(8,128)(2,1)S(1)} %get-tuple-element.70._.refs_1_), channel_id=1, source_target_pairs={{0,2},{1,3},{2,0},{3,1},{4,6},{5,7},{6,4},{7,5},{8,10},{9,11},{10,... | collective-permute-start | bytes 24584 | tf_op jit(solution)/shard_map/ppermute | solution.py:95
  28.4 11.0 %collective-permute-start.15 = (bf16[128,1536]{1,0:T(8,128)(2,1)S(1)}, bf16[128,1536]{1,0:T(8,128)(2,1)S(1)}, u32[]{:S(2)}, u32[]{:S(2)}) collective-permute-start(bf16[128,1536]{1,0:T(8,128)(2,1)S(1)} %shard_map.117.refs_0_.total), channel_id=1, source_target_pairs={{0,2},{1,3},{2,0},{3,1},{4,6},{5,7},{6,4},{7,5},{8,10},{9,11},{10,... | collective-permute-start | bytes 1179656 | tf_op jit(solution)/shard_map/ppermute | solution.py:95
  31.1 1.8 %collective-permute-start.11 = (bf16[128,1536]{1,0:T(8,128)(2,1)S(1)}, bf16[128,1536]{1,0:T(8,128)(2,1)S(1)}, u32[]{:S(2)}, u32[]{:S(2)}) collective-permute-start(bf16[128,1536]{1,0:T(8,128)(2,1)S(1)} %shard_map.118.act), channel_id=1, source_target_pairs={{0,1},{1,0},{2,3},{3,2},{4,5},{5,4},{6,7},{7,6},{8,9},{9,8},{10,11... | collective-permute-start | bytes 1179656 | tf_op jit(solution)/shard_map/ppermute | solution.py:95
  33.7 14.0 %collective-permute-start.12 = (bf16[64,768]{1,0:T(8,128)(2,1)S(1)}, bf16[64,768]{1,0:T(8,128)(2,1)S(1)}, u32[]{:S(2)}, u32[]{:S(2)}) collective-permute-start(bf16[64,768]{1,0:T(8,128)(2,1)S(1)} %get-tuple-element.75.refs_3_), channel_id=1, source_target_pairs={{0,12},{4,8},{8,4},{12,0},{1,13},{5,9},{9,5},{13,1},{2,14},{6,10},... | collective-permute-start | bytes 294920 | tf_op jit(solution)/shard_map/ppermute | solution.py:95
  38.7 9.6 %collective-permute-start.13 = (bf16[64,768]{1,0:T(8,128)(2,1)S(1)}, bf16[64,768]{1,0:T(8,128)(2,1)S(1)}, u32[]{:S(2)}, u32[]{:S(2)}) collective-permute-start(bf16[64,768]{1,0:T(8,128)(2,1)S(1)} %get-tuple-element.76.refs_2_), channel_id=1, source_target_pairs={{0,8},{4,12},{8,0},{12,4},{1,9},{5,13},{9,1},{13,5},{2,10},{6,14},... | collective-permute-start | bytes 294920 | tf_op jit(solution)/shard_map/ppermute | solution.py:95
  38.7 9.6 %collective-permute-start.14 = (bf16[64,768]{1,0:T(8,128)(2,1)S(1)}, bf16[64,768]{1,0:T(8,128)(2,1)S(1)}, u32[]{:S(2)}, u32[]{:S(2)}) collective-permute-start(bf16[64,768]{1,0:T(8,128)(2,1)S(1)} %get-tuple-element.77.refs_1_), channel_id=1, source_target_pairs={{0,4},{4,0},{8,12},{12,8},{1,5},{5,1},{9,13},{13,9},{2,6},{6,2},{1... | collective-permute-start | bytes 294920 | tf_op jit(solution)/shard_map/ppermute | solution.py:95
  40.2 1.8 %collective-permute-start.17 = (bf16[128,1536]{1,0:T(8,128)(2,1)S(1)}, bf16[128,1536]{1,0:T(8,128)(2,1)S(1)}, u32[]{:S(2)}, u32[]{:S(2)}) collective-permute-start(bf16[128,1536]{1,0:T(8,128)(2,1)S(1)} %shard_map.121.act), channel_id=1, source_target_pairs={{0,1},{1,0},{2,3},{3,2},{4,5},{5,4},{6,7},{7,6},{8,9},{9,8},{10,11... | collective-permute-start | bytes 1179656 | tf_op jit(solution)/shard_map/ppermute | solution.py:95
  42.8 8.6 %collective-permute-start.18 = (bf16[64,768]{1,0:T(8,128)(2,1)S(1)}, bf16[64,768]{1,0:T(8,128)(2,1)S(1)}, u32[]{:S(2)}, u32[]{:S(2)}) collective-permute-start(bf16[64,768]{1,0:T(8,128)(2,1)S(1)} %get-tuple-element.81), channel_id=1, source_target_pairs={{0,12},{4,8},{8,4},{12,0},{1,13},{5,9},{9,5},{13,1},{2,14},{6,10},... | collective-permute-start | bytes 294920 | tf_op jit(solution)/shard_map/ppermute | solution.py:95
  47.7 8.0 %collective-permute-start.19 = (bf16[64,768]{1,0:T(8,128)(2,1)S(1)}, bf16[64,768]{1,0:T(8,128)(2,1)S(1)}, u32[]{:S(2)}, u32[]{:S(2)}) collective-permute-start(bf16[64,768]{1,0:T(8,128)(2,1)S(1)} %get-tuple-element.82), channel_id=1, source_target_pairs={{0,8},{4,12},{8,0},{12,4},{1,9},{5,13},{9,1},{13,5},{2,10},{6,14},... | collective-permute-start | bytes 294920 | tf_op jit(solution)/shard_map/ppermute | solution.py:95
  47.7 8.0 %collective-permute-start.20 = (bf16[64,768]{1,0:T(8,128)(2,1)S(1)}, bf16[64,768]{1,0:T(8,128)(2,1)S(1)}, u32[]{:S(2)}, u32[]{:S(2)}) collective-permute-start(bf16[64,768]{1,0:T(8,128)(2,1)S(1)} %get-tuple-element.83), channel_id=1, source_target_pairs={{0,4},{4,0},{8,12},{12,8},{1,5},{5,1},{9,13},{13,9},{2,6},{6,2},{1... | collective-permute-start | bytes 294920 | tf_op jit(solution)/shard_map/ppermute | solution.py:95
  56.2 1.3 %collective-permute-start.21 = (f32[72,128]{1,0:T(8,128)S(1)}, f32[72,128]{1,0:T(8,128)S(1)}, u32[]{:S(2)}, u32[]{:S(2)}) collective-permute-start(f32[72,128]{1,0:T(8,128)S(1)} %get-tuple-element.85.left), channel_id=1, source_target_pairs={{0,1},{1,0},{2,3},{3,2},{4,5},{5,4},{6,7},{7,6},{8,9},{9,8},{10,11... | collective-permute-start | bytes 110600 | tf_op jit(solution)/shard_map/ppermute | solution.py:95
  57.5 4.9 %collective-permute-start.22 = (f32[72,128]{1,0:T(8,128)S(1)}, f32[72,128]{1,0:T(8,128)S(1)}, u32[]{:S(2)}, u32[]{:S(2)}) collective-permute-start(f32[72,128]{1,0:T(8,128)S(1)} %shard_map.126.mine), channel_id=1, source_target_pairs={{0,18},{1,19},{2,16},{3,17},{16,2},{17,3},{18,0},{19,1},{4,22},{5,... | collective-permute-start | bytes 110600 | tf_op jit(solution)/shard_map/ppermute | solution.py:95
  59.5 4.0 %collective-permute-start.23 = (f32[72,128]{1,0:T(8,128)S(1)}, f32[72,128]{1,0:T(8,128)S(1)}, u32[]{:S(2)}, u32[]{:S(2)}) collective-permute-start(f32[72,128]{1,0:T(8,128)S(1)} %shard_map.126.mine), channel_id=1, source_target_pairs={{0,16},{1,17},{2,18},{3,19},{16,0},{17,1},{18,2},{19,3},{4,20},{5,... | collective-permute-start | bytes 110600 | tf_op jit(solution)/shard_map/ppermute | solution.py:95
  60.0 4.0 %collective-permute-start.24 = (f32[72,128]{1,0:T(8,128)S(1)}, f32[72,128]{1,0:T(8,128)S(1)}, u32[]{:S(2)}, u32[]{:S(2)}) collective-permute-start(f32[72,128]{1,0:T(8,128)S(1)} %shard_map.126.mine), channel_id=1, source_target_pairs={{0,2},{1,3},{2,0},{3,1},{16,18},{17,19},{18,16},{19,17},{4,6},{5,7... | collective-permute-start | bytes 110600 | tf_op jit(solution)/shard_map/ppermute | solution.py:95
  (3 other events, 9.0 us)

commit v12 on v11

--- a/solution.py
+++ b/solution.py
@@ -207,30 +207,25 @@
     return jnp.concatenate(places, 0)
 
 
-def take_kernel(source, whole, piece, sems):
-    copies = [
-        pltpu.make_async_copy(source.at[pl.ds(0, piece.shape[0]), :], piece, sems.at[0]),
-        pltpu.make_async_copy(source, whole, sems.at[1]),
-    ]
-    for copy in copies:
-        copy.start()
-    for copy in copies:
-        copy.wait()
-
-
-def prepare_kernel(table_in, timestep, tokens, mod_in, out_weight, w, *refs):
+def take_kernel(source, piece, sem):
+    copy = pltpu.make_async_copy(source.at[pl.ds(0, piece.shape[0]), :], piece, sem)
+    copy.start()
+    copy.wait()
+
+
+def prepare_kernel(table_in, timestep, tokens_in, mod_in, out_weight, w, *refs):
     later, refs = refs[: CHUNKS - 1], refs[CHUNKS - 1 :]
     gathers, refs = refs[:CHUNKS], refs[CHUNKS:]
     spreads, refs = refs[:CHUNKS], refs[CHUNKS:]
     texts, refs = refs[:CHUNKS], refs[CHUNKS:]
-    held, kept, mod, weight, rows_out, ends_out, slots_out, video_out, step_out = refs[:9]
-    table, sems, small = refs[9:]
+    held, kept, tokens, mod, weight, rows_out, ends_out, slots_out, video_out, step_out = refs[:10]
+    table, sems, small = refs[10:]
     step_out[...] = jnp.full(step_out.shape, timestep[0], jnp.int32)
     core = lax.axis_index("narrow") % 2
-    sources = (table_in, mod_in, out_weight)
+    sources = (table_in, mod_in, out_weight, tokens_in)
     copies = [
         pltpu.make_async_copy(source, place, small.at[i])
-        for i, (source, place) in enumerate(zip(sources, (table, mod, weight)))
+        for i, (source, place) in enumerate(zip(sources, (table, mod, weight, tokens)))
     ]
     for copy in copies:
         copy.start()
@@ -274,6 +269,7 @@
     )
     ends = rows_of(ends, core)
     ends_out[...] = jnp.concatenate([ends, jnp.zeros((16, 128 - ends.shape[1]), BF16)], 1)
+    copies[3].wait()
     for k in range(1, CHUNKS):
         later[k - 1][...] = tokens[QUOTAS[k] : QUOTAS[k + 1], :]
     for copy in big:
@@ -541,15 +537,15 @@
     payload = units + 128
 
     in_place = lambda array: pltpu.with_memory_space_constraint(array, pltpu.HBM)
-    tokens, piece = call(
+    (piece,) = call(
         take_kernel,
-        [(hidden.shape, BF16), ((QUOTAS[1], features), BF16)],
+        [((QUOTAS[1], features), BF16)],
         [in_place(hidden)],
         "a",
-        [pltpu.SemaphoreType.DMA((2,))],
+        [pltpu.SemaphoreType.DMA(())],
     )
     across = swap(piece, "wide", 2, 4)
-    near = swap(tokens, "wide", 1, 4)
+    near = swap(hidden, "wide", 1, 4)
 
     tiles = units // TILE
     chunks = range(CHUNKS)
@@ -562,6 +558,7 @@
         + [
             ((features, units), BF16),
             ((features, units), BF16),
+            (hidden.shape, BF16),
             (modulation.shape, F32),
             ((width, features), BF16),
             ((16, features), BF16),
@@ -573,23 +570,23 @@
         [
             in_place(split_table),
             timestep,
-            tokens,
+            in_place(hidden),
             in_place(modulation),
             in_place(output_weight.T),
             in_place(expand_weight),
         ],
-        "asvaaa",
+        "asaaaa",
         [
             pltpu.SMEM(split_table.shape, jnp.int32),
             pltpu.SemaphoreType.DMA((2, tiles)),
-            pltpu.SemaphoreType.DMA((3,)),
+            pltpu.SemaphoreType.DMA((4,)),
         ],
     )
     later, made = made[: CHUNKS - 1], made[CHUNKS - 1 :]
     gathers, made = made[:CHUNKS], made[CHUNKS:]
     spreads, made = made[:CHUNKS], made[CHUNKS:]
     texts, made = made[:CHUNKS], made[CHUNKS:]
-    held_sent, held_kept, mod, out_weight, rows_in, ends_mine, slots, video, step = made
+    held_sent, held_kept, tokens, mod, out_weight, rows_in, ends_mine, slots, video, step = made
     later = [swap(piece, "wide", 2, 4) for piece in later]
     (across,) = call(pass_kernel, [(across.shape, BF16)], [across, slots], "va")
     far = [across, swap(across, "wide", 1, 4)]
@@ -681,7 +678,7 @@
             "vvvv",
         )
         before = pieces
-        distances = (3, 2, 1) if k + 1 < CHUNKS else (3, 2, 1)
+        distances = (3, 2, 1) if k + 1 < CHUNKS else (2, 3, 1)
         returned += [pieces[0], *(swap(pieces[s], "wide", s, 4) for s in distances)]
 
     layer, bundle = call(

time: 64.9 us -> 64 us (0.986)
  no operation moved by 1% of the time
where the time goes in v12:
time: 64 us; the launch traced here: 63.8 us
  starting transfers between devices  31.3 us (49%)
  waiting for transfers between devices  16 us (25%)
  Pallas kernels  15.1 us (24%)
  between operations  1.51 us (2%)
    ppermute x25, starting transfers between devices, swap(): return lax.ppermute(array, axis, [(i, i ^ distance) for i in range(size)])  31.3 us
    ppermute x25, waiting for transfers between devices, swap(): return lax.ppermute(array, axis, [(i, i ^ distance) for i in range(size)])  16 us
    pallas_call x24, Pallas kernels, call(): pl.pallas_call(kernel, out_shape=[jax.ShapeDtypeStruct(shape, dtype) for...  15.1 us
  transfers between devices with their start and end apart: 25, of which 14 were waited for; matrix products, arithmetic and copies ran while one was open for 0% of the time, Pallas kernels for 20%

profile of v12, /device:TPU:0, one launch (start us, length us, event | category | flops | bytes accessed | tf_op | source)
XLA Modules:
  0.0 63.8 jit_solution(12238758643457853574)
XLA Ops:
  0.6 0.9 %shard_map.105 = bf16[64,768]{1,0:T(8,128)(2,1)S(1)} custom-call(bf16[128,768]{1,0:T(8,128)(2,1)} %bitcast.6), custom_call_target="tpu_custom_call" | custom-call | flops 1 | bytes 1 | tf_op jit(solution)/shard_map/pallas_call | solution.py:519
  1.5 4.1 %collective-permute-start.1 = (bf16[64,768]{1,0:T(8,128)(2,1)S(1)}, bf16[64,768]{1,0:T(8,128)(2,1)S(1)}, u32[]{:S(2)}, u32[]{:S(2)}) collective-permute-start(bf16[64,768]{1,0:T(8,128)(2,1)S(1)} %shard_map.105), channel_id=1, source_target_pairs={{0,8},{4,12},{8,0},{12,4},{1,9},{5,13},{9,1},{13,5},{2,10},{6,14},... | collective-permute-start | bytes 294920 | tf_op jit(solution)/shard_map/ppermute | solution.py:95
  5.6 1.6 %collective-permute-start = (bf16[128,768]{1,0:T(8,128)(2,1)}, bf16[128,768]{1,0:T(8,128)(2,1)S(1)}, u32[]{:S(2)}, u32[]{:S(2)}) collective-permute-start(bf16[128,768]{1,0:T(8,128)(2,1)} %bitcast.7), channel_id=1, source_target_pairs={{0,4},{4,0},{8,12},{12,8},{1,5},{5,1},{9,13},{13,9},{2,6},{6,2},{1... | collective-permute-start | bytes 589832 | tf_op jit(solution)/shard_map/ppermute | solution.py:95
  7.9 2.6 %shard_map.104 = (bf16[64,768]{1,0:T(8,128)(2,1)S(1)}, bf16[128,256]{1,0:T(8,128)(2,1)S(1)}, bf16[128,512]{1,0:T(8,128)(2,1)S(1)}, bf16[256,128]{1,0:T(8,128)(2,...) custom-call(s32[4]{0:T(128)} %table_in.1, ...), custom_call_target="tpu_custom_call" | custom-call | flops 1 | bytes 1 | tf_op jit(solution)/shard_map/pallas_call | solution.py:519
  11.3 3.5 %collective-permute-start.7 = (bf16[64,768]{1,0:T(8,128)(2,1)S(1)}, bf16[64,768]{1,0:T(8,128)(2,1)S(1)}, u32[]{:S(2)}, u32[]{:S(2)}) collective-permute-start(bf16[64,768]{1,0:T(8,128)(2,1)S(1)} %get-tuple-element.62), channel_id=1, source_target_pairs={{0,8},{4,12},{8,0},{12,4},{1,9},{5,13},{9,1},{13,5},{2,10},{6,14},... | collective-permute-start | bytes 294920 | tf_op jit(solution)/shard_map/ppermute | solution.py:95
  15.3 0.9 %shard_map.107 = (bf16[144,768]{1,0:T(8,128)(2,1)S(1)}, bf16[128,1536]{1,0:T(8,128)(2,1)S(1)}, bf16[16,2688]{1,0:T(8,128)(2,1)S(1)}) custom-call(f32[128,128]{1,0:T(8,128)S(1)} %get-tuple-element.47.text, f32[8,768]{1,0:T(8,128)S(1)} %get-tuple-element.45.mod, bf16[128,256]{1,0:T(8,128)(2,1)S(1)} %get-tuple-element.48.place, ...), custom_call_target="tpu_custom_call" | custom-call | flops 10000000000 | bytes 1 | tf_op jit(solution)/shard_map/pallas_call | solution.py:519
  17.6 1.6 %collective-permute-start.6 = (bf16[16,1920]{1,0:T(8,128)(2,1)S(1)}, bf16[16,1920]{1,0:T(8,128)(2,1)S(1)}, u32[]{:S(2)}, u32[]{:S(2)}) collective-permute-start(bf16[16,1920]{1,0:T(8,128)(2,1)S(1)} %get-tuple-element.58._.refs_1_.first_sent.chip), channel_id=1, source_target_pairs={{0,2},{1,3},{2,0},{3,1},{4,6},{5,7},{6,4},{7,5},{8,10},{9,11},{10,... | collective-permute-start | bytes 184328 | tf_op jit(solution)/shard_map/ppermute | solution.py:95
  19.9 1.3 %collective-permute-start.8 = (bf16[64,768]{1,0:T(8,128)(2,1)S(1)}, bf16[64,768]{1,0:T(8,128)(2,1)S(1)}, u32[]{:S(2)}, u32[]{:S(2)}) collective-permute-start(bf16[64,768]{1,0:T(8,128)(2,1)S(1)} %shard_map.111.refs_0_.refs_2_), channel_id=1, source_target_pairs={{0,4},{4,0},{8,12},{12,8},{1,5},{5,1},{9,13},{13,9},{2,6},{6,2},{1... | collective-permute-start | bytes 294920 | tf_op jit(solution)/shard_map/ppermute | solution.py:95
  21.2 2.4 %shard_map.113.refs_9_.w = bf16[3072,768]{1,0:T(8,128)(2,1)S(1)} custom-call(bf16[3072,768]{1,0:T(8,128)(2,1)} %source.1, bf16[64,768]{1,0:T(8,128)(2,1)S(1)} %shard_map.111.refs_0_.refs_2_, bf16[16,1920]{1,0:T(8,128)(2,1)S(1)} %get-tuple-element.58._.refs_1_.first_sent.chip), custom_call_target="tpu_custom_call" | custom-call | flops 10000000000 | bytes 1 | tf_op jit(solution)/shard_map/pallas_call | solution.py:519
  23.7 1.0 %collective-permute-done.8.refs_3_ = bf16[64,768]{1,0:T(8,128)(2,1)S(1)} collective-permute-done((bf16[64,768]{1,0:T(8,128)(2,1)S(1)}, bf16[64,768]{1,0:T(8,128)(2,1)S(1)}, u32[]{:S(2)}, u32[]{:S(2)}) %collective-permute-start.8) | collective-permute-done | bytes 98336 | tf_op jit(solution)/shard_map/ppermute | solution.py:95
  24.7 0.8 %shard_map.114 = (bf16[128,768]{1,0:T(8,128)(2,1)S(1)}, bf16[128,1536]{1,0:T(8,128)(2,1)S(1)}, bf16[128,128]{1,0:T(8,128)(2,1)S(1)}) custom-call(f32[128,128]{1,0:T(8,128)S(1)} %get-tuple-element.60.text, f32[8,768]{1,0:T(8,128)S(1)} %get-tuple-element.45.mod, bf16[128,512]{1,0:T(8,128)(2,1)S(1)} %get-tuple-element.61.place, ...), custom_call_target="tpu_custom_call" | custom-call | flops 10000000000 | bytes 1 | tf_op jit(solution)/shard_map/pallas_call | solution.py:519
  26.9 1.4 %collective-permute-start.16 = (bf16[16,256]{1,0:T(8,128)(2,1)S(1)}, bf16[16,256]{1,0:T(8,128)(2,1)S(1)}, u32[]{:S(2)}, u32[]{:S(2)}) collective-permute-start(bf16[16,256]{1,0:T(8,128)(2,1)S(1)} %get-tuple-element.68._.refs_1_), channel_id=1, source_target_pairs={{0,2},{1,3},{2,0},{3,1},{4,6},{5,7},{6,4},{7,5},{8,10},{9,11},{10,... | collective-permute-start | bytes 24584 | tf_op jit(solution)/shard_map/ppermute | solution.py:95
  29.1 1.2 %collective-permute-done.5.came = bf16[128,1536]{1,0:T(8,128)(2,1)S(1)} collective-permute-done((bf16[128,1536]{1,0:T(8,128)(2,1)S(1)}, bf16[128,1536]{1,0:T(8,128)(2,1)S(1)}, u32[]{:S(2)}, u32[]{:S(2)}) %collective-permute-start.5) | collective-permute-done | bytes 393248 | tf_op jit(solution)/shard_map/ppermute | solution.py:95
  31.7 1.2 %collective-permute-done.11.act = bf16[128,1536]{1,0:T(8,128)(2,1)S(1)} collective-permute-done((bf16[128,1536]{1,0:T(8,128)(2,1)S(1)}, bf16[128,1536]{1,0:T(8,128)(2,1)S(1)}, u32[]{:S(2)}, u32[]{:S(2)}) %collective-permute-start.11) | collective-permute-done | bytes 393248 | tf_op jit(solution)/shard_map/ppermute | solution.py:95
  33.7 4.8 %collective-permute-start.12 = (bf16[64,768]{1,0:T(8,128)(2,1)S(1)}, bf16[64,768]{1,0:T(8,128)(2,1)S(1)}, u32[]{:S(2)}, u32[]{:S(2)}) collective-permute-start(bf16[64,768]{1,0:T(8,128)(2,1)S(1)} %get-tuple-element.73.refs_3_), channel_id=1, source_target_pairs={{0,12},{4,8},{8,4},{12,0},{1,13},{5,9},{9,5},{13,1},{2,14},{6,10},... | collective-permute-start | bytes 294920 | tf_op jit(solution)/shard_map/ppermute | solution.py:95
  40.8 1.2 %collective-permute-done.17.act = bf16[128,1536]{1,0:T(8,128)(2,1)S(1)} collective-permute-done((bf16[128,1536]{1,0:T(8,128)(2,1)S(1)}, bf16[128,1536]{1,0:T(8,128)(2,1)S(1)}, u32[]{:S(2)}, u32[]{:S(2)}) %collective-permute-start.17) | collective-permute-done | bytes 393248 | tf_op jit(solution)/shard_map/ppermute | solution.py:95
  42.7 3.3 %collective-permute-start.18 = (bf16[64,768]{1,0:T(8,128)(2,1)S(1)}, bf16[64,768]{1,0:T(8,128)(2,1)S(1)}, u32[]{:S(2)}, u32[]{:S(2)}) collective-permute-start(bf16[64,768]{1,0:T(8,128)(2,1)S(1)} %get-tuple-element.79), channel_id=1, source_target_pairs={{0,8},{4,12},{8,0},{12,4},{1,9},{5,13},{9,1},{13,5},{2,10},{6,14},... | collective-permute-start | bytes 294920 | tf_op jit(solution)/shard_map/ppermute | solution.py:95
  46.1 1.5 %collective-permute-start.19 = (bf16[64,768]{1,0:T(8,128)(2,1)S(1)}, bf16[64,768]{1,0:T(8,128)(2,1)S(1)}, u32[]{:S(2)}, u32[]{:S(2)}) collective-permute-start(bf16[64,768]{1,0:T(8,128)(2,1)S(1)} %get-tuple-element.80), channel_id=1, source_target_pairs={{0,12},{4,8},{8,4},{12,0},{1,13},{5,9},{9,5},{13,1},{2,14},{6,10},... | collective-permute-start | bytes 294920 | tf_op jit(solution)/shard_map/ppermute | solution.py:95
  48.1 5.8 %collective-permute-done.18.refs_5_ = bf16[64,768]{1,0:T(8,128)(2,1)S(1)} collective-permute-done((bf16[64,768]{1,0:T(8,128)(2,1)S(1)}, bf16[64,768]{1,0:T(8,128)(2,1)S(1)}, u32[]{:S(2)}, u32[]{:S(2)}) %collective-permute-start.18) | collective-permute-done | bytes 98336 | tf_op jit(solution)/shard_map/ppermute | solution.py:95
  53.9 0.9 %collective-permute-done.20.refs_7_ = bf16[64,768]{1,0:T(8,128)(2,1)S(1)} collective-permute-done((bf16[64,768]{1,0:T(8,128)(2,1)S(1)}, bf16[64,768]{1,0:T(8,128)(2,1)S(1)}, u32[]{:S(2)}, u32[]{:S(2)}) %collective-permute-start.20) | collective-permute-done | bytes 98336 | tf_op jit(solution)/shard_map/ppermute | solution.py:95
  55.5 1.2 %collective-permute-done.21.right = f32[72,128]{1,0:T(8,128)S(1)} collective-permute-done((f32[72,128]{1,0:T(8,128)S(1)}, f32[72,128]{1,0:T(8,128)S(1)}, u32[]{:S(2)}, u32[]{:S(2)}) %collective-permute-start.21) | collective-permute-done | bytes 36896 | tf_op jit(solution)/shard_map/ppermute | solution.py:95
  56.7 2.0 %collective-permute-start.22 = (f32[72,128]{1,0:T(8,128)S(1)}, f32[72,128]{1,0:T(8,128)S(1)}, u32[]{:S(2)}, u32[]{:S(2)}) collective-permute-start(f32[72,128]{1,0:T(8,128)S(1)} %shard_map.126.mine), channel_id=1, source_target_pairs={{0,18},{1,19},{2,16},{3,17},{16,2},{17,3},{18,0},{19,1},{4,22},{5,... | collective-permute-start | bytes 110600 | tf_op jit(solution)/shard_map/ppermute | solution.py:95
  59.2 1.0 %collective-permute-start.24 = (f32[72,128]{1,0:T(8,128)S(1)}, f32[72,128]{1,0:T(8,128)S(1)}, u32[]{:S(2)}, u32[]{:S(2)}) collective-permute-start(f32[72,128]{1,0:T(8,128)S(1)} %shard_map.126.mine), channel_id=1, source_target_pairs={{0,2},{1,3},{2,0},{3,1},{16,18},{17,19},{18,16},{19,17},{4,6},{5,7... | collective-permute-start | bytes 110600 | tf_op jit(solution)/shard_map/ppermute | solution.py:95
  61.5 1.1 %collective-permute-done.23.other = f32[72,128]{1,0:T(8,128)S(1)} collective-permute-done((f32[72,128]{1,0:T(8,128)S(1)}, f32[72,128]{1,0:T(8,128)S(1)}, u32[]{:S(2)}, u32[]{:S(2)}) %collective-permute-start.23) | collective-permute-done | bytes 36896 | tf_op jit(solution)/shard_map/ppermute | solution.py:95
  (54 shorter events, 15.0 us)
Async XLA Ops:
  1.5 8.9 %collective-permute-start.1 = (bf16[64,768]{1,0:T(8,128)(2,1)S(1)}, bf16[64,768]{1,0:T(8,128)(2,1)S(1)}, u32[]{:S(2)}, u32[]{:S(2)}) collective-permute-start(bf16[64,768]{1,0:T(8,128)(2,1)S(1)} %shard_map.105), channel_id=1, source_target_pairs={{0,8},{4,12},{8,0},{12,4},{1,9},{5,13},{9,1},{13,5},{2,10},{6,14},... | collective-permute-start | bytes 294920 | tf_op jit(solution)/shard_map/ppermute | solution.py:95
  5.6 9.6 %collective-permute-start = (bf16[128,768]{1,0:T(8,128)(2,1)}, bf16[128,768]{1,0:T(8,128)(2,1)S(1)}, u32[]{:S(2)}, u32[]{:S(2)}) collective-permute-start(bf16[128,768]{1,0:T(8,128)(2,1)} %bitcast.7), channel_id=1, source_target_pairs={{0,4},{4,0},{8,12},{12,8},{1,5},{5,1},{9,13},{13,9},{2,6},{6,2},{1... | collective-permute-start | bytes 589832 | tf_op jit(solution)/shard_map/ppermute | solution.py:95
  10.5 4.8 %collective-permute-start.2 = (bf16[64,768]{1,0:T(8,128)(2,1)S(1)}, bf16[64,768]{1,0:T(8,128)(2,1)S(1)}, u32[]{:S(2)}, u32[]{:S(2)}) collective-permute-start(bf16[64,768]{1,0:T(8,128)(2,1)S(1)} %shard_map.106.refs_0_), channel_id=1, source_target_pairs={{0,4},{4,0},{8,12},{12,8},{1,5},{5,1},{9,13},{13,9},{2,6},{6,2},{1... | collective-permute-start | bytes 294920 | tf_op jit(solution)/shard_map/ppermute | solution.py:95
  11.3 8.5 %collective-permute-start.7 = (bf16[64,768]{1,0:T(8,128)(2,1)S(1)}, bf16[64,768]{1,0:T(8,128)(2,1)S(1)}, u32[]{:S(2)}, u32[]{:S(2)}) collective-permute-start(bf16[64,768]{1,0:T(8,128)(2,1)S(1)} %get-tuple-element.62), channel_id=1, source_target_pairs={{0,8},{4,12},{8,0},{12,4},{1,9},{5,13},{9,1},{13,5},{2,10},{6,14},... | collective-permute-start | bytes 294920 | tf_op jit(solution)/shard_map/ppermute | solution.py:95
  16.1 1.3 %collective-permute-start.4 = (bf16[16,2688]{1,0:T(8,128)(2,1)S(1)}, bf16[16,2688]{1,0:T(8,128)(2,1)S(1)}, u32[]{:S(2)}, u32[]{:S(2)}) collective-permute-start(bf16[16,2688]{1,0:T(8,128)(2,1)S(1)} %get-tuple-element.55.__.side), channel_id=1, source_target_pairs={{0,1},{1,0},{2,3},{3,2},{4,5},{5,4},{6,7},{7,6},{8,9},{9,8},{10,11... | collective-permute-start | bytes 258056 | tf_op jit(solution)/shard_map/ppermute | solution.py:95
  16.2 3.0 %collective-permute-start.3 = (bf16[128,1536]{1,0:T(8,128)(2,1)S(1)}, bf16[128,1536]{1,0:T(8,128)(2,1)S(1)}, u32[]{:S(2)}, u32[]{:S(2)}) collective-permute-start(bf16[128,1536]{1,0:T(8,128)(2,1)S(1)} %get-tuple-element.54._), channel_id=1, source_target_pairs={{0,1},{1,0},{2,3},{3,2},{4,5},{5,4},{6,7},{7,6},{8,9},{9,8},{10,11... | collective-permute-start | bytes 1179656 | tf_op jit(solution)/shard_map/ppermute | solution.py:95
  17.6 11.5 %collective-permute-start.6 = (bf16[16,1920]{1,0:T(8,128)(2,1)S(1)}, bf16[16,1920]{1,0:T(8,128)(2,1)S(1)}, u32[]{:S(2)}, u32[]{:S(2)}) collective-permute-start(bf16[16,1920]{1,0:T(8,128)(2,1)S(1)} %get-tuple-element.58._.refs_1_.first_sent.chip), channel_id=1, source_target_pairs={{0,2},{1,3},{2,0},{3,1},{4,6},{5,7},{6,4},{7,5},{8,10},{9,11},{10,... | collective-permute-start | bytes 184328 | tf_op jit(solution)/shard_map/ppermute | solution.py:95
  19.3 11.1 %collective-permute-start.5 = (bf16[128,1536]{1,0:T(8,128)(2,1)S(1)}, bf16[128,1536]{1,0:T(8,128)(2,1)S(1)}, u32[]{:S(2)}, u32[]{:S(2)}) collective-permute-start(bf16[128,1536]{1,0:T(8,128)(2,1)S(1)} %shard_map.110._.refs_7_.total), channel_id=1, source_target_pairs={{0,2},{1,3},{2,0},{3,1},{4,6},{5,7},{6,4},{7,5},{8,10},{9,11},{10,... | collective-permute-start | bytes 1179656 | tf_op jit(solution)/shard_map/ppermute | solution.py:95
  19.9 4.8 %collective-permute-start.8 = (bf16[64,768]{1,0:T(8,128)(2,1)S(1)}, bf16[64,768]{1,0:T(8,128)(2,1)S(1)}, u32[]{:S(2)}, u32[]{:S(2)}) collective-permute-start(bf16[64,768]{1,0:T(8,128)(2,1)S(1)} %shard_map.111.refs_0_.refs_2_), channel_id=1, source_target_pairs={{0,4},{4,0},{8,12},{12,8},{1,5},{5,1},{9,13},{13,9},{2,6},{6,2},{1... | collective-permute-start | bytes 294920 | tf_op jit(solution)/shard_map/ppermute | solution.py:95
  25.6 2.7 %collective-permute-start.9 = (bf16[128,1536]{1,0:T(8,128)(2,1)S(1)}, bf16[128,1536]{1,0:T(8,128)(2,1)S(1)}, u32[]{:S(2)}, u32[]{:S(2)}) collective-permute-start(bf16[128,1536]{1,0:T(8,128)(2,1)S(1)} %get-tuple-element.66._), channel_id=1, source_target_pairs={{0,1},{1,0},{2,3},{3,2},{4,5},{5,4},{6,7},{7,6},{8,9},{9,8},{10,11... | collective-permute-start | bytes 1179656 | tf_op jit(solution)/shard_map/ppermute | solution.py:95
  26.9 12.3 %collective-permute-start.16 = (bf16[16,256]{1,0:T(8,128)(2,1)S(1)}, bf16[16,256]{1,0:T(8,128)(2,1)S(1)}, u32[]{:S(2)}, u32[]{:S(2)}) collective-permute-start(bf16[16,256]{1,0:T(8,128)(2,1)S(1)} %get-tuple-element.68._.refs_1_), channel_id=1, source_target_pairs={{0,2},{1,3},{2,0},{3,1},{4,6},{5,7},{6,4},{7,5},{8,10},{9,11},{10,... | collective-permute-start | bytes 24584 | tf_op jit(solution)/shard_map/ppermute | solution.py:95
  28.4 11.0 %collective-permute-start.15 = (bf16[128,1536]{1,0:T(8,128)(2,1)S(1)}, bf16[128,1536]{1,0:T(8,128)(2,1)S(1)}, u32[]{:S(2)}, u32[]{:S(2)}) collective-permute-start(bf16[128,1536]{1,0:T(8,128)(2,1)S(1)} %shard_map.117.refs_0_.total), channel_id=1, source_target_pairs={{0,2},{1,3},{2,0},{3,1},{4,6},{5,7},{6,4},{7,5},{8,10},{9,11},{10,... | collective-permute-start | bytes 1179656 | tf_op jit(solution)/shard_map/ppermute | solution.py:95
  31.1 1.8 %collective-permute-start.11 = (bf16[128,1536]{1,0:T(8,128)(2,1)S(1)}, bf16[128,1536]{1,0:T(8,128)(2,1)S(1)}, u32[]{:S(2)}, u32[]{:S(2)}) collective-permute-start(bf16[128,1536]{1,0:T(8,128)(2,1)S(1)} %shard_map.118.act), channel_id=1, source_target_pairs={{0,1},{1,0},{2,3},{3,2},{4,5},{5,4},{6,7},{7,6},{8,9},{9,8},{10,11... | collective-permute-start | bytes 1179656 | tf_op jit(solution)/shard_map/ppermute | solution.py:95
  33.7 13.9 %collective-permute-start.12 = (bf16[64,768]{1,0:T(8,128)(2,1)S(1)}, bf16[64,768]{1,0:T(8,128)(2,1)S(1)}, u32[]{:S(2)}, u32[]{:S(2)}) collective-permute-start(bf16[64,768]{1,0:T(8,128)(2,1)S(1)} %get-tuple-element.73.refs_3_), channel_id=1, source_target_pairs={{0,12},{4,8},{8,4},{12,0},{1,13},{5,9},{9,5},{13,1},{2,14},{6,10},... | collective-permute-start | bytes 294920 | tf_op jit(solution)/shard_map/ppermute | solution.py:95
  38.6 9.5 %collective-permute-start.13 = (bf16[64,768]{1,0:T(8,128)(2,1)S(1)}, bf16[64,768]{1,0:T(8,128)(2,1)S(1)}, u32[]{:S(2)}, u32[]{:S(2)}) collective-permute-start(bf16[64,768]{1,0:T(8,128)(2,1)S(1)} %get-tuple-element.74.refs_2_), channel_id=1, source_target_pairs={{0,8},{4,12},{8,0},{12,4},{1,9},{5,13},{9,1},{13,5},{2,10},{6,14},... | collective-permute-start | bytes 294920 | tf_op jit(solution)/shard_map/ppermute | solution.py:95
  38.6 9.5 %collective-permute-start.14 = (bf16[64,768]{1,0:T(8,128)(2,1)S(1)}, bf16[64,768]{1,0:T(8,128)(2,1)S(1)}, u32[]{:S(2)}, u32[]{:S(2)}) collective-permute-start(bf16[64,768]{1,0:T(8,128)(2,1)S(1)} %get-tuple-element.75.refs_1_), channel_id=1, source_target_pairs={{0,4},{4,0},{8,12},{12,8},{1,5},{5,1},{9,13},{13,9},{2,6},{6,2},{1... | collective-permute-start | bytes 294920 | tf_op jit(solution)/shard_map/ppermute | solution.py:95
  40.2 1.8 %collective-permute-start.17 = (bf16[128,1536]{1,0:T(8,128)(2,1)S(1)}, bf16[128,1536]{1,0:T(8,128)(2,1)S(1)}, u32[]{:S(2)}, u32[]{:S(2)}) collective-permute-start(bf16[128,1536]{1,0:T(8,128)(2,1)S(1)} %shard_map.121.act), channel_id=1, source_target_pairs={{0,1},{1,0},{2,3},{3,2},{4,5},{5,4},{6,7},{7,6},{8,9},{9,8},{10,11... | collective-permute-start | bytes 1179656 | tf_op jit(solution)/shard_map/ppermute | solution.py:95
  42.7 11.2 %collective-permute-start.18 = (bf16[64,768]{1,0:T(8,128)(2,1)S(1)}, bf16[64,768]{1,0:T(8,128)(2,1)S(1)}, u32[]{:S(2)}, u32[]{:S(2)}) collective-permute-start(bf16[64,768]{1,0:T(8,128)(2,1)S(1)} %get-tuple-element.79), channel_id=1, source_target_pairs={{0,8},{4,12},{8,0},{12,4},{1,9},{5,13},{9,1},{13,5},{2,10},{6,14},... | collective-permute-start | bytes 294920 | tf_op jit(solution)/shard_map/ppermute | solution.py:95
  46.1 7.8 %collective-permute-start.19 = (bf16[64,768]{1,0:T(8,128)(2,1)S(1)}, bf16[64,768]{1,0:T(8,128)(2,1)S(1)}, u32[]{:S(2)}, u32[]{:S(2)}) collective-permute-start(bf16[64,768]{1,0:T(8,128)(2,1)S(1)} %get-tuple-element.80), channel_id=1, source_target_pairs={{0,12},{4,8},{8,4},{12,0},{1,13},{5,9},{9,5},{13,1},{2,14},{6,10},... | collective-permute-start | bytes 294920 | tf_op jit(solution)/shard_map/ppermute | solution.py:95
  47.6 7.2 %collective-permute-start.20 = (bf16[64,768]{1,0:T(8,128)(2,1)S(1)}, bf16[64,768]{1,0:T(8,128)(2,1)S(1)}, u32[]{:S(2)}, u32[]{:S(2)}) collective-permute-start(bf16[64,768]{1,0:T(8,128)(2,1)S(1)} %get-tuple-element.81), channel_id=1, source_target_pairs={{0,4},{4,0},{8,12},{12,8},{1,5},{5,1},{9,13},{13,9},{2,6},{6,2},{1... | collective-permute-start | bytes 294920 | tf_op jit(solution)/shard_map/ppermute | solution.py:95
  55.4 1.3 %collective-permute-start.21 = (f32[72,128]{1,0:T(8,128)S(1)}, f32[72,128]{1,0:T(8,128)S(1)}, u32[]{:S(2)}, u32[]{:S(2)}) collective-permute-start(f32[72,128]{1,0:T(8,128)S(1)} %get-tuple-element.83.left), channel_id=1, source_target_pairs={{0,1},{1,0},{2,3},{3,2},{4,5},{5,4},{6,7},{7,6},{8,9},{9,8},{10,11... | collective-permute-start | bytes 110600 | tf_op jit(solution)/shard_map/ppermute | solution.py:95
  56.7 4.9 %collective-permute-start.22 = (f32[72,128]{1,0:T(8,128)S(1)}, f32[72,128]{1,0:T(8,128)S(1)}, u32[]{:S(2)}, u32[]{:S(2)}) collective-permute-start(f32[72,128]{1,0:T(8,128)S(1)} %shard_map.126.mine), channel_id=1, source_target_pairs={{0,18},{1,19},{2,16},{3,17},{16,2},{17,3},{18,0},{19,1},{4,22},{5,... | collective-permute-start | bytes 110600 | tf_op jit(solution)/shard_map/ppermute | solution.py:95
  58.6 4.0 %collective-permute-start.23 = (f32[72,128]{1,0:T(8,128)S(1)}, f32[72,128]{1,0:T(8,128)S(1)}, u32[]{:S(2)}, u32[]{:S(2)}) collective-permute-start(f32[72,128]{1,0:T(8,128)S(1)} %shard_map.126.mine), channel_id=1, source_target_pairs={{0,16},{1,17},{2,18},{3,19},{16,0},{17,1},{18,2},{19,3},{4,20},{5,... | collective-permute-start | bytes 110600 | tf_op jit(solution)/shard_map/ppermute | solution.py:95
  59.2 4.0 %collective-permute-start.24 = (f32[72,128]{1,0:T(8,128)S(1)}, f32[72,128]{1,0:T(8,128)S(1)}, u32[]{:S(2)}, u32[]{:S(2)}) collective-permute-start(f32[72,128]{1,0:T(8,128)S(1)} %shard_map.126.mine), channel_id=1, source_target_pairs={{0,2},{1,3},{2,0},{3,1},{16,18},{17,19},{18,16},{19,17},{4,6},{5,7... | collective-permute-start | bytes 110600 | tf_op jit(solution)/shard_map/ppermute | solution.py:95
  (3 other events, 8.7 us)

commit v13 on v12

--- a/solution.py
+++ b/solution.py
@@ -83,7 +83,7 @@
 CAP = 128
 CHUNKS = len(QUOTAS) - 1
 F32, BF16 = jnp.float32, jnp.bfloat16
-TILE = 512
+TILE = 768
 LONG = 10**10
 
 
@@ -366,9 +366,9 @@
     sent_out[...] = (kept[...] + came[...].astype(F32)).astype(BF16)
 
 
-def activate_kernel(features, text, total, came, side, stats, first_sent, first_came, *refs):
-    act_out = refs[-1]
-    rows, units = act_out.shape
+def rows_kernel(features, text, side, stats, *refs):
+    out = refs[-1]
+    rows = side.shape[0]
     lead = stats.shape[1] - 256
     stats = jnp.concatenate([stats[:, lead : lead + 128], stats[:, lead + 128 :]], 0)
     sides = [side[...], across_rows(stats.astype(F32))[:rows]]
@@ -400,7 +400,13 @@
             part = pltpu.roll(part, shift, 1) if shift else part
             packed = part if packed is None else packed + part
             shift += 8
-    packed = packed[:, :64].astype(BF16)
+    out[...] = jnp.where(lane < 64, packed, scale)
+
+
+def activate_kernel(total, came, rows_in, first_sent, first_came, *refs):
+    act_out = refs[-1]
+    rows, units = act_out.shape
+    packed, scale = rows_in[:, :64].astype(BF16), rows_in[:, 64:65]
     own, other = first_sent[:, :units], first_came[:, :units]
     factors = jnp.concatenate([own, own, other, other], 0)
     for t in range(0, units, TILE):
@@ -427,7 +433,8 @@
         ends_out[0][...] = jnp.concatenate([total, own, jnp.zeros((112, 128), F32)], 0).T
 
 
-def contract_other_kernel(k, place, act, so_far, w, *outs):
+def contract_other_kernel(k, place, act, so_far, w, *refs):
+    outs = refs[-4:]
     core = lax.axis_index("narrow") % 2
     units = w.shape[0] // 2
     rows = pl.ds(pl.multiple_of((1 - core) * units, 128), units)
@@ -652,17 +659,28 @@
     returned = []
     before = []
     first = [merged[0][1], merged[0][2][3]]
+    def rows_call(k, *after):
+        return call(
+            functools.partial(rows_kernel, features),
+            [((2 * size_of(k), 128), F32)],
+            [texts[k], *merged[k][2][2:], *after],
+            "vvv" + "a" * len(after),
+        )[0]
+
+    of_rows = [rows_call(0, merged[-1][0])]
     for k in chunks:
         rows = 2 * size_of(k)
         if k + 1 < CHUNKS:
             before = before + [merged[k + 1][0], merged[k + 1][1]]
         (act,) = call(
-            functools.partial(activate_kernel, features),
+            activate_kernel,
             [((rows, units), BF16)],
-            [texts[k], *merged[k][2], *first, *before],
-            "vvvvvvv" + "a" * len(before),
+            [*merged[k][2][:2], of_rows[k], *first, *before],
+            "vvvvv" + "a" * len(before),
         )
         act_came = swap(act, "narrow", 1, 4)
+        if k + 1 < CHUNKS:
+            of_rows.append(rows_call(k + 1, act))
         out, *ends_made = call(
             functools.partial(contract_own_kernel, k),
             [((rows, features), F32)] + ([((128, 128), F32)] if k == 0 else []),
@@ -674,8 +692,8 @@
         pieces = call(
             functools.partial(contract_other_kernel, k),
             [((size_of(k), features), BF16)] * 4,
-            [spreads[k], act_came, out, held_out],
-            "vvvv",
+            [spreads[k], act_came, out, held_out, *of_rows[k + 1 : k + 2]],
+            "vvvv" + "a" * len(of_rows[k + 1 : k + 2]),
         )
         before = pieces
         distances = (3, 2, 1) if k + 1 < CHUNKS else (2, 3, 1)

time: 64 us -> 63.7 us (level)
  waiting for transfers between devices: 16 us -> 15.3 us
    ppermute x25, waiting for transfers between devices: 16 us -> 15.3 us  [swap(): return lax.ppermute(array, axis, [(i, i ^ distance) for i in range(size)])]
    pallas_call x24 -> x26, Pallas kernels: 15.1 us -> 15.5 us  [call(): pl.pallas_call(kernel, out_shape=[jax.ShapeDtypeStruct(shape, dtype) for...]
  transfers between devices with their start and end apart: 25 -> 25, of which waited for: 14 -> 14; matrix products, arithmetic and copies ran while one was open for 0% -> 0% of each run, Pallas kernels for 20% -> 21%
where the time goes in v13:
time: 63.7 us; the launch traced here: 63.5 us
  starting transfers between devices  31.2 us (49%)
  Pallas kernels  15.5 us (24%)
  waiting for transfers between devices  15.3 us (24%)
  between operations  1.52 us (2%)
    ppermute x25, starting transfers between devices, swap(): return lax.ppermute(array, axis, [(i, i ^ distance) for i in range(size)])  31.2 us
    pallas_call x26, Pallas kernels, call(): pl.pallas_call(kernel, out_shape=[jax.ShapeDtypeStruct(shape, dtype) for...  15.5 us
    ppermute x25, waiting for transfers between devices, swap(): return lax.ppermute(array, axis, [(i, i ^ distance) for i in range(size)])  15.3 us
  transfers between devices with their start and end apart: 25, of which 14 were waited for; matrix products, arithmetic and copies ran while one was open for 0% of the time, Pallas kernels for 21%

profile of v13, /device:TPU:0, one launch (start us, length us, event | category | flops | bytes accessed | tf_op | source)
XLA Modules:
  0.0 63.5 jit_solution(6987954527647982597)
XLA Ops:
  0.6 0.9 %shard_map.105 = bf16[64,768]{1,0:T(8,128)(2,1)S(1)} custom-call(bf16[128,768]{1,0:T(8,128)(2,1)} %bitcast.6), custom_call_target="tpu_custom_call" | custom-call | flops 1 | bytes 1 | tf_op jit(solution)/shard_map/pallas_call | solution.py:526
  1.5 4.1 %collective-permute-start.1 = (bf16[64,768]{1,0:T(8,128)(2,1)S(1)}, bf16[64,768]{1,0:T(8,128)(2,1)S(1)}, u32[]{:S(2)}, u32[]{:S(2)}) collective-permute-start(bf16[64,768]{1,0:T(8,128)(2,1)S(1)} %shard_map.105), channel_id=1, source_target_pairs={{0,8},{4,12},{8,0},{12,4},{1,9},{5,13},{9,1},{13,5},{2,10},{6,14},... | collective-permute-start | bytes 294920 | tf_op jit(solution)/shard_map/ppermute | solution.py:95
  5.6 1.6 %collective-permute-start = (bf16[128,768]{1,0:T(8,128)(2,1)}, bf16[128,768]{1,0:T(8,128)(2,1)S(1)}, u32[]{:S(2)}, u32[]{:S(2)}) collective-permute-start(bf16[128,768]{1,0:T(8,128)(2,1)} %bitcast.7), channel_id=1, source_target_pairs={{0,4},{4,0},{8,12},{12,8},{1,5},{5,1},{9,13},{13,9},{2,6},{6,2},{1... | collective-permute-start | bytes 589832 | tf_op jit(solution)/shard_map/ppermute | solution.py:95
  7.9 2.6 %shard_map.104 = (bf16[64,768]{1,0:T(8,128)(2,1)S(1)}, bf16[128,256]{1,0:T(8,128)(2,1)S(1)}, bf16[128,512]{1,0:T(8,128)(2,1)S(1)}, bf16[256,128]{1,0:T(8,128)(2,...) custom-call(s32[4]{0:T(128)} %table_in.1, ...), custom_call_target="tpu_custom_call" | custom-call | flops 1 | bytes 1 | tf_op jit(solution)/shard_map/pallas_call | solution.py:526
  10.5 0.8 %collective-permute-start.2 = (bf16[64,768]{1,0:T(8,128)(2,1)S(1)}, bf16[64,768]{1,0:T(8,128)(2,1)S(1)}, u32[]{:S(2)}, u32[]{:S(2)}) collective-permute-start(bf16[64,768]{1,0:T(8,128)(2,1)S(1)} %shard_map.106.refs_0_), channel_id=1, source_target_pairs={{0,4},{4,0},{8,12},{12,8},{1,5},{5,1},{9,13},{13,9},{2,6},{6,2},{1... | collective-permute-start | bytes 294920 | tf_op jit(solution)/shard_map/ppermute | solution.py:95
  11.3 3.5 %collective-permute-start.7 = (bf16[64,768]{1,0:T(8,128)(2,1)S(1)}, bf16[64,768]{1,0:T(8,128)(2,1)S(1)}, u32[]{:S(2)}, u32[]{:S(2)}) collective-permute-start(bf16[64,768]{1,0:T(8,128)(2,1)S(1)} %get-tuple-element.62), channel_id=1, source_target_pairs={{0,8},{4,12},{8,0},{12,4},{1,9},{5,13},{9,1},{13,5},{2,10},{6,14},... | collective-permute-start | bytes 294920 | tf_op jit(solution)/shard_map/ppermute | solution.py:95
  15.3 0.9 %shard_map.107 = (bf16[144,768]{1,0:T(8,128)(2,1)S(1)}, bf16[128,1536]{1,0:T(8,128)(2,1)S(1)}, bf16[16,2688]{1,0:T(8,128)(2,1)S(1)}) custom-call(f32[128,128]{1,0:T(8,128)S(1)} %get-tuple-element.47.text, f32[8,768]{1,0:T(8,128)S(1)} %get-tuple-element.45.mod, bf16[128,256]{1,0:T(8,128)(2,1)S(1)} %get-tuple-element.48.place, ...), custom_call_target="tpu_custom_call" | custom-call | flops 10000000000 | bytes 1 | tf_op jit(solution)/shard_map/pallas_call | solution.py:526
  17.6 1.6 %collective-permute-start.6 = (bf16[16,1920]{1,0:T(8,128)(2,1)S(1)}, bf16[16,1920]{1,0:T(8,128)(2,1)S(1)}, u32[]{:S(2)}, u32[]{:S(2)}) collective-permute-start(bf16[16,1920]{1,0:T(8,128)(2,1)S(1)} %get-tuple-element.58._.refs_1_.first_sent.chip), channel_id=1, source_target_pairs={{0,2},{1,3},{2,0},{3,1},{4,6},{5,7},{6,4},{7,5},{8,10},{9,11},{10,... | collective-permute-start | bytes 184328 | tf_op jit(solution)/shard_map/ppermute | solution.py:95
  19.9 1.3 %collective-permute-start.8 = (bf16[64,768]{1,0:T(8,128)(2,1)S(1)}, bf16[64,768]{1,0:T(8,128)(2,1)S(1)}, u32[]{:S(2)}, u32[]{:S(2)}) collective-permute-start(bf16[64,768]{1,0:T(8,128)(2,1)S(1)} %shard_map.111.refs_0_.refs_2_), channel_id=1, source_target_pairs={{0,4},{4,0},{8,12},{12,8},{1,5},{5,1},{9,13},{13,9},{2,6},{6,2},{1... | collective-permute-start | bytes 294920 | tf_op jit(solution)/shard_map/ppermute | solution.py:95
  21.2 2.4 %shard_map.113.refs_9_.w = bf16[3072,768]{1,0:T(8,128)(2,1)S(1)} custom-call(bf16[3072,768]{1,0:T(8,128)(2,1)} %source.1, bf16[64,768]{1,0:T(8,128)(2,1)S(1)} %shard_map.111.refs_0_.refs_2_, bf16[16,1920]{1,0:T(8,128)(2,1)S(1)} %get-tuple-element.58._.refs_1_.first_sent.chip), custom_call_target="tpu_custom_call" | custom-call | flops 10000000000 | bytes 1 | tf_op jit(solution)/shard_map/pallas_call | solution.py:526
  23.7 1.0 %collective-permute-done.8.refs_3_ = bf16[64,768]{1,0:T(8,128)(2,1)S(1)} collective-permute-done((bf16[64,768]{1,0:T(8,128)(2,1)S(1)}, bf16[64,768]{1,0:T(8,128)(2,1)S(1)}, u32[]{:S(2)}, u32[]{:S(2)}) %collective-permute-start.8) | collective-permute-done | bytes 98336 | tf_op jit(solution)/shard_map/ppermute | solution.py:95
  24.7 0.9 %shard_map.114 = (bf16[128,768]{1,0:T(8,128)(2,1)S(1)}, bf16[128,1536]{1,0:T(8,128)(2,1)S(1)}, bf16[128,128]{1,0:T(8,128)(2,1)S(1)}) custom-call(f32[128,128]{1,0:T(8,128)S(1)} %get-tuple-element.60.text, f32[8,768]{1,0:T(8,128)S(1)} %get-tuple-element.45.mod, bf16[128,512]{1,0:T(8,128)(2,1)S(1)} %get-tuple-element.61.place, ...), custom_call_target="tpu_custom_call" | custom-call | flops 10000000000 | bytes 1 | tf_op jit(solution)/shard_map/pallas_call | solution.py:526
  26.9 1.4 %collective-permute-start.12 = (bf16[16,256]{1,0:T(8,128)(2,1)S(1)}, bf16[16,256]{1,0:T(8,128)(2,1)S(1)}, u32[]{:S(2)}, u32[]{:S(2)}) collective-permute-start(bf16[16,256]{1,0:T(8,128)(2,1)S(1)} %get-tuple-element.68._.refs_1_), channel_id=1, source_target_pairs={{0,2},{1,3},{2,0},{3,1},{4,6},{5,7},{6,4},{7,5},{8,10},{9,11},{10,... | collective-permute-start | bytes 24584 | tf_op jit(solution)/shard_map/ppermute | solution.py:95
  33.4 4.9 %collective-permute-start.13 = (bf16[64,768]{1,0:T(8,128)(2,1)S(1)}, bf16[64,768]{1,0:T(8,128)(2,1)S(1)}, u32[]{:S(2)}, u32[]{:S(2)}) collective-permute-start(bf16[64,768]{1,0:T(8,128)(2,1)S(1)} %get-tuple-element.74.refs_3_), channel_id=1, source_target_pairs={{0,12},{4,8},{8,4},{12,0},{1,13},{5,9},{9,5},{13,1},{2,14},{6,10},... | collective-permute-start | bytes 294920 | tf_op jit(solution)/shard_map/ppermute | solution.py:95
  40.4 1.2 %collective-permute-done.17.act = bf16[128,1536]{1,0:T(8,128)(2,1)S(1)} collective-permute-done((bf16[128,1536]{1,0:T(8,128)(2,1)S(1)}, bf16[128,1536]{1,0:T(8,128)(2,1)S(1)}, u32[]{:S(2)}, u32[]{:S(2)}) %collective-permute-start.17) | collective-permute-done | bytes 393248 | tf_op jit(solution)/shard_map/ppermute | solution.py:95
  41.6 0.8 %shard_map.125 = (bf16[64,768]{1,0:T(8,128)(2,1)S(1)}, bf16[64,768]{1,0:T(8,128)(2,1)S(1)}, bf16[64,768]{1,0:T(8,128)(2,1)S(1)}, bf16[64,768]{1,0:T(8,128)(2,1)S(1)}) custom-call(bf16[256,128]{1,0:T(8,128)(2,1)S(1)} %get-tuple-element.77.place, bf16[128,1536]{1,0:T(8,128)(2,1)S(1)} %collective-permute-done.17.act, f32[128,768]{1,0:T(8,128)S(1)} %shard_map.124.so_far, ...), custom_call_target="tpu_custom_call" | custom-call | flops 1 | bytes 1 | tf_op jit(solution)/shard_map/pallas_call | solution.py:526
  42.4 3.3 %collective-permute-start.18 = (bf16[64,768]{1,0:T(8,128)(2,1)S(1)}, bf16[64,768]{1,0:T(8,128)(2,1)S(1)}, u32[]{:S(2)}, u32[]{:S(2)}) collective-permute-start(bf16[64,768]{1,0:T(8,128)(2,1)S(1)} %get-tuple-element.79), channel_id=1, source_target_pairs={{0,8},{4,12},{8,0},{12,4},{1,9},{5,13},{9,1},{13,5},{2,10},{6,14},... | collective-permute-start | bytes 294920 | tf_op jit(solution)/shard_map/ppermute | solution.py:95
  45.7 1.5 %collective-permute-start.19 = (bf16[64,768]{1,0:T(8,128)(2,1)S(1)}, bf16[64,768]{1,0:T(8,128)(2,1)S(1)}, u32[]{:S(2)}, u32[]{:S(2)}) collective-permute-start(bf16[64,768]{1,0:T(8,128)(2,1)S(1)} %get-tuple-element.80), channel_id=1, source_target_pairs={{0,12},{4,8},{8,4},{12,0},{1,13},{5,9},{9,5},{13,1},{2,14},{6,10},... | collective-permute-start | bytes 294920 | tf_op jit(solution)/shard_map/ppermute | solution.py:95
  47.8 5.8 %collective-permute-done.18.refs_5_ = bf16[64,768]{1,0:T(8,128)(2,1)S(1)} collective-permute-done((bf16[64,768]{1,0:T(8,128)(2,1)S(1)}, bf16[64,768]{1,0:T(8,128)(2,1)S(1)}, u32[]{:S(2)}, u32[]{:S(2)}) %collective-permute-start.18) | collective-permute-done | bytes 98336 | tf_op jit(solution)/shard_map/ppermute | solution.py:95
  53.6 0.9 %collective-permute-done.20.refs_7_ = bf16[64,768]{1,0:T(8,128)(2,1)S(1)} collective-permute-done((bf16[64,768]{1,0:T(8,128)(2,1)S(1)}, bf16[64,768]{1,0:T(8,128)(2,1)S(1)}, u32[]{:S(2)}, u32[]{:S(2)}) %collective-permute-start.20) | collective-permute-done | bytes 98336 | tf_op jit(solution)/shard_map/ppermute | solution.py:95
  55.1 1.2 %collective-permute-done.21.right = f32[72,128]{1,0:T(8,128)S(1)} collective-permute-done((f32[72,128]{1,0:T(8,128)S(1)}, f32[72,128]{1,0:T(8,128)S(1)}, u32[]{:S(2)}, u32[]{:S(2)}) %collective-permute-start.21) | collective-permute-done | bytes 36896 | tf_op jit(solution)/shard_map/ppermute | solution.py:95
  56.3 2.0 %collective-permute-start.22 = (f32[72,128]{1,0:T(8,128)S(1)}, f32[72,128]{1,0:T(8,128)S(1)}, u32[]{:S(2)}, u32[]{:S(2)}) collective-permute-start(f32[72,128]{1,0:T(8,128)S(1)} %shard_map.128.mine), channel_id=1, source_target_pairs={{0,18},{1,19},{2,16},{3,17},{16,2},{17,3},{18,0},{19,1},{4,22},{5,... | collective-permute-start | bytes 110600 | tf_op jit(solution)/shard_map/ppermute | solution.py:95
  58.9 1.0 %collective-permute-start.24 = (f32[72,128]{1,0:T(8,128)S(1)}, f32[72,128]{1,0:T(8,128)S(1)}, u32[]{:S(2)}, u32[]{:S(2)}) collective-permute-start(f32[72,128]{1,0:T(8,128)S(1)} %shard_map.128.mine), channel_id=1, source_target_pairs={{0,2},{1,3},{2,0},{3,1},{16,18},{17,19},{18,16},{19,17},{4,6},{5,7... | collective-permute-start | bytes 110600 | tf_op jit(solution)/shard_map/ppermute | solution.py:95
  61.2 1.1 %collective-permute-done.23.other = f32[72,128]{1,0:T(8,128)S(1)} collective-permute-done((f32[72,128]{1,0:T(8,128)S(1)}, f32[72,128]{1,0:T(8,128)S(1)}, u32[]{:S(2)}, u32[]{:S(2)}) %collective-permute-start.23) | collective-permute-done | bytes 36896 | tf_op jit(solution)/shard_map/ppermute | solution.py:95
  (56 shorter events, 15.4 us)
Async XLA Ops:
  1.5 9.0 %collective-permute-start.1 = (bf16[64,768]{1,0:T(8,128)(2,1)S(1)}, bf16[64,768]{1,0:T(8,128)(2,1)S(1)}, u32[]{:S(2)}, u32[]{:S(2)}) collective-permute-start(bf16[64,768]{1,0:T(8,128)(2,1)S(1)} %shard_map.105), channel_id=1, source_target_pairs={{0,8},{4,12},{8,0},{12,4},{1,9},{5,13},{9,1},{13,5},{2,10},{6,14},... | collective-permute-start | bytes 294920 | tf_op jit(solution)/shard_map/ppermute | solution.py:95
  5.6 9.6 %collective-permute-start = (bf16[128,768]{1,0:T(8,128)(2,1)}, bf16[128,768]{1,0:T(8,128)(2,1)S(1)}, u32[]{:S(2)}, u32[]{:S(2)}) collective-permute-start(bf16[128,768]{1,0:T(8,128)(2,1)} %bitcast.7), channel_id=1, source_target_pairs={{0,4},{4,0},{8,12},{12,8},{1,5},{5,1},{9,13},{13,9},{2,6},{6,2},{1... | collective-permute-start | bytes 589832 | tf_op jit(solution)/shard_map/ppermute | solution.py:95
  10.5 4.7 %collective-permute-start.2 = (bf16[64,768]{1,0:T(8,128)(2,1)S(1)}, bf16[64,768]{1,0:T(8,128)(2,1)S(1)}, u32[]{:S(2)}, u32[]{:S(2)}) collective-permute-start(bf16[64,768]{1,0:T(8,128)(2,1)S(1)} %shard_map.106.refs_0_), channel_id=1, source_target_pairs={{0,4},{4,0},{8,12},{12,8},{1,5},{5,1},{9,13},{13,9},{2,6},{6,2},{1... | collective-permute-start | bytes 294920 | tf_op jit(solution)/shard_map/ppermute | solution.py:95
  11.3 8.5 %collective-permute-start.7 = (bf16[64,768]{1,0:T(8,128)(2,1)S(1)}, bf16[64,768]{1,0:T(8,128)(2,1)S(1)}, u32[]{:S(2)}, u32[]{:S(2)}) collective-permute-start(bf16[64,768]{1,0:T(8,128)(2,1)S(1)} %get-tuple-element.62), channel_id=1, source_target_pairs={{0,8},{4,12},{8,0},{12,4},{1,9},{5,13},{9,1},{13,5},{2,10},{6,14},... | collective-permute-start | bytes 294920 | tf_op jit(solution)/shard_map/ppermute | solution.py:95
  16.1 1.3 %collective-permute-start.4 = (bf16[16,2688]{1,0:T(8,128)(2,1)S(1)}, bf16[16,2688]{1,0:T(8,128)(2,1)S(1)}, u32[]{:S(2)}, u32[]{:S(2)}) collective-permute-start(bf16[16,2688]{1,0:T(8,128)(2,1)S(1)} %get-tuple-element.55.__.side), channel_id=1, source_target_pairs={{0,1},{1,0},{2,3},{3,2},{4,5},{5,4},{6,7},{7,6},{8,9},{9,8},{10,11... | collective-permute-start | bytes 258056 | tf_op jit(solution)/shard_map/ppermute | solution.py:95
  16.2 3.0 %collective-permute-start.3 = (bf16[128,1536]{1,0:T(8,128)(2,1)S(1)}, bf16[128,1536]{1,0:T(8,128)(2,1)S(1)}, u32[]{:S(2)}, u32[]{:S(2)}) collective-permute-start(bf16[128,1536]{1,0:T(8,128)(2,1)S(1)} %get-tuple-element.54._), channel_id=1, source_target_pairs={{0,1},{1,0},{2,3},{3,2},{4,5},{5,4},{6,7},{7,6},{8,9},{9,8},{10,11... | collective-permute-start | bytes 1179656 | tf_op jit(solution)/shard_map/ppermute | solution.py:95
  17.6 11.5 %collective-permute-start.6 = (bf16[16,1920]{1,0:T(8,128)(2,1)S(1)}, bf16[16,1920]{1,0:T(8,128)(2,1)S(1)}, u32[]{:S(2)}, u32[]{:S(2)}) collective-permute-start(bf16[16,1920]{1,0:T(8,128)(2,1)S(1)} %get-tuple-element.58._.refs_1_.first_sent.chip), channel_id=1, source_target_pairs={{0,2},{1,3},{2,0},{3,1},{4,6},{5,7},{6,4},{7,5},{8,10},{9,11},{10,... | collective-permute-start | bytes 184328 | tf_op jit(solution)/shard_map/ppermute | solution.py:95
  19.3 11.1 %collective-permute-start.5 = (bf16[128,1536]{1,0:T(8,128)(2,1)S(1)}, bf16[128,1536]{1,0:T(8,128)(2,1)S(1)}, u32[]{:S(2)}, u32[]{:S(2)}) collective-permute-start(bf16[128,1536]{1,0:T(8,128)(2,1)S(1)} %shard_map.110._.refs_7_.total), channel_id=1, source_target_pairs={{0,2},{1,3},{2,0},{3,1},{4,6},{5,7},{6,4},{7,5},{8,10},{9,11},{10,... | collective-permute-start | bytes 1179656 | tf_op jit(solution)/shard_map/ppermute | solution.py:95
  19.9 4.8 %collective-permute-start.8 = (bf16[64,768]{1,0:T(8,128)(2,1)S(1)}, bf16[64,768]{1,0:T(8,128)(2,1)S(1)}, u32[]{:S(2)}, u32[]{:S(2)}) collective-permute-start(bf16[64,768]{1,0:T(8,128)(2,1)S(1)} %shard_map.111.refs_0_.refs_2_), channel_id=1, source_target_pairs={{0,4},{4,0},{8,12},{12,8},{1,5},{5,1},{9,13},{13,9},{2,6},{6,2},{1... | collective-permute-start | bytes 294920 | tf_op jit(solution)/shard_map/ppermute | solution.py:95
  25.6 2.7 %collective-permute-start.9 = (bf16[128,1536]{1,0:T(8,128)(2,1)S(1)}, bf16[128,1536]{1,0:T(8,128)(2,1)S(1)}, u32[]{:S(2)}, u32[]{:S(2)}) collective-permute-start(bf16[128,1536]{1,0:T(8,128)(2,1)S(1)} %get-tuple-element.66._), channel_id=1, source_target_pairs={{0,1},{1,0},{2,3},{3,2},{4,5},{5,4},{6,7},{7,6},{8,9},{9,8},{10,11... | collective-permute-start | bytes 1179656 | tf_op jit(solution)/shard_map/ppermute | solution.py:95
  26.9 4.5 %collective-permute-start.12 = (bf16[16,256]{1,0:T(8,128)(2,1)S(1)}, bf16[16,256]{1,0:T(8,128)(2,1)S(1)}, u32[]{:S(2)}, u32[]{:S(2)}) collective-permute-start(bf16[16,256]{1,0:T(8,128)(2,1)S(1)} %get-tuple-element.68._.refs_1_), channel_id=1, source_target_pairs={{0,2},{1,3},{2,0},{3,1},{4,6},{5,7},{6,4},{7,5},{8,10},{9,11},{10,... | collective-permute-start | bytes 24584 | tf_op jit(solution)/shard_map/ppermute | solution.py:95
  28.4 11.0 %collective-permute-start.16 = (bf16[128,1536]{1,0:T(8,128)(2,1)S(1)}, bf16[128,1536]{1,0:T(8,128)(2,1)S(1)}, u32[]{:S(2)}, u32[]{:S(2)}) collective-permute-start(bf16[128,1536]{1,0:T(8,128)(2,1)S(1)} %shard_map.117.refs_0_.total), channel_id=1, source_target_pairs={{0,2},{1,3},{2,0},{3,1},{4,6},{5,7},{6,4},{7,5},{8,10},{9,11},{10,... | collective-permute-start | bytes 1179656 | tf_op jit(solution)/shard_map/ppermute | solution.py:95
  30.8 1.8 %collective-permute-start.11 = (bf16[128,1536]{1,0:T(8,128)(2,1)S(1)}, bf16[128,1536]{1,0:T(8,128)(2,1)S(1)}, u32[]{:S(2)}, u32[]{:S(2)}) collective-permute-start(bf16[128,1536]{1,0:T(8,128)(2,1)S(1)} %shard_map.119.act.refs_0_), channel_id=1, source_target_pairs={{0,1},{1,0},{2,3},{3,2},{4,5},{5,4},{6,7},{7,6},{8,9},{9,8},{10,11... | collective-permute-start | bytes 1179656 | tf_op jit(solution)/shard_map/ppermute | solution.py:95
  33.4 13.9 %collective-permute-start.13 = (bf16[64,768]{1,0:T(8,128)(2,1)S(1)}, bf16[64,768]{1,0:T(8,128)(2,1)S(1)}, u32[]{:S(2)}, u32[]{:S(2)}) collective-permute-start(bf16[64,768]{1,0:T(8,128)(2,1)S(1)} %get-tuple-element.74.refs_3_), channel_id=1, source_target_pairs={{0,12},{4,8},{8,4},{12,0},{1,13},{5,9},{9,5},{13,1},{2,14},{6,10},... | collective-permute-start | bytes 294920 | tf_op jit(solution)/shard_map/ppermute | solution.py:95
  38.2 9.5 %collective-permute-start.14 = (bf16[64,768]{1,0:T(8,128)(2,1)S(1)}, bf16[64,768]{1,0:T(8,128)(2,1)S(1)}, u32[]{:S(2)}, u32[]{:S(2)}) collective-permute-start(bf16[64,768]{1,0:T(8,128)(2,1)S(1)} %get-tuple-element.75.refs_2_), channel_id=1, source_target_pairs={{0,8},{4,12},{8,0},{12,4},{1,9},{5,13},{9,1},{13,5},{2,10},{6,14},... | collective-permute-start | bytes 294920 | tf_op jit(solution)/shard_map/ppermute | solution.py:95
  38.2 9.5 %collective-permute-start.15 = (bf16[64,768]{1,0:T(8,128)(2,1)S(1)}, bf16[64,768]{1,0:T(8,128)(2,1)S(1)}, u32[]{:S(2)}, u32[]{:S(2)}) collective-permute-start(bf16[64,768]{1,0:T(8,128)(2,1)S(1)} %get-tuple-element.76.refs_1_), channel_id=1, source_target_pairs={{0,4},{4,0},{8,12},{12,8},{1,5},{5,1},{9,13},{13,9},{2,6},{6,2},{1... | collective-permute-start | bytes 294920 | tf_op jit(solution)/shard_map/ppermute | solution.py:95
  39.9 1.8 %collective-permute-start.17 = (bf16[128,1536]{1,0:T(8,128)(2,1)S(1)}, bf16[128,1536]{1,0:T(8,128)(2,1)S(1)}, u32[]{:S(2)}, u32[]{:S(2)}) collective-permute-start(bf16[128,1536]{1,0:T(8,128)(2,1)S(1)} %shard_map.123.act), channel_id=1, source_target_pairs={{0,1},{1,0},{2,3},{3,2},{4,5},{5,4},{6,7},{7,6},{8,9},{9,8},{10,11... | collective-permute-start | bytes 1179656 | tf_op jit(solution)/shard_map/ppermute | solution.py:95
  42.4 11.2 %collective-permute-start.18 = (bf16[64,768]{1,0:T(8,128)(2,1)S(1)}, bf16[64,768]{1,0:T(8,128)(2,1)S(1)}, u32[]{:S(2)}, u32[]{:S(2)}) collective-permute-start(bf16[64,768]{1,0:T(8,128)(2,1)S(1)} %get-tuple-element.79), channel_id=1, source_target_pairs={{0,8},{4,12},{8,0},{12,4},{1,9},{5,13},{9,1},{13,5},{2,10},{6,14},... | collective-permute-start | bytes 294920 | tf_op jit(solution)/shard_map/ppermute | solution.py:95
  45.7 7.8 %collective-permute-start.19 = (bf16[64,768]{1,0:T(8,128)(2,1)S(1)}, bf16[64,768]{1,0:T(8,128)(2,1)S(1)}, u32[]{:S(2)}, u32[]{:S(2)}) collective-permute-start(bf16[64,768]{1,0:T(8,128)(2,1)S(1)} %get-tuple-element.80), channel_id=1, source_target_pairs={{0,12},{4,8},{8,4},{12,0},{1,13},{5,9},{9,5},{13,1},{2,14},{6,10},... | collective-permute-start | bytes 294920 | tf_op jit(solution)/shard_map/ppermute | solution.py:95
  47.3 7.2 %collective-permute-start.20 = (bf16[64,768]{1,0:T(8,128)(2,1)S(1)}, bf16[64,768]{1,0:T(8,128)(2,1)S(1)}, u32[]{:S(2)}, u32[]{:S(2)}) collective-permute-start(bf16[64,768]{1,0:T(8,128)(2,1)S(1)} %get-tuple-element.81), channel_id=1, source_target_pairs={{0,4},{4,0},{8,12},{12,8},{1,5},{5,1},{9,13},{13,9},{2,6},{6,2},{1... | collective-permute-start | bytes 294920 | tf_op jit(solution)/shard_map/ppermute | solution.py:95
  55.1 1.3 %collective-permute-start.21 = (f32[72,128]{1,0:T(8,128)S(1)}, f32[72,128]{1,0:T(8,128)S(1)}, u32[]{:S(2)}, u32[]{:S(2)}) collective-permute-start(f32[72,128]{1,0:T(8,128)S(1)} %get-tuple-element.83.left), channel_id=1, source_target_pairs={{0,1},{1,0},{2,3},{3,2},{4,5},{5,4},{6,7},{7,6},{8,9},{9,8},{10,11... | collective-permute-start | bytes 110600 | tf_op jit(solution)/shard_map/ppermute | solution.py:95
  56.3 4.9 %collective-permute-start.22 = (f32[72,128]{1,0:T(8,128)S(1)}, f32[72,128]{1,0:T(8,128)S(1)}, u32[]{:S(2)}, u32[]{:S(2)}) collective-permute-start(f32[72,128]{1,0:T(8,128)S(1)} %shard_map.128.mine), channel_id=1, source_target_pairs={{0,18},{1,19},{2,16},{3,17},{16,2},{17,3},{18,0},{19,1},{4,22},{5,... | collective-permute-start | bytes 110600 | tf_op jit(solution)/shard_map/ppermute | solution.py:95
  58.3 4.0 %collective-permute-start.23 = (f32[72,128]{1,0:T(8,128)S(1)}, f32[72,128]{1,0:T(8,128)S(1)}, u32[]{:S(2)}, u32[]{:S(2)}) collective-permute-start(f32[72,128]{1,0:T(8,128)S(1)} %shard_map.128.mine), channel_id=1, source_target_pairs={{0,16},{1,17},{2,18},{3,19},{16,0},{17,1},{18,2},{19,3},{4,20},{5,... | collective-permute-start | bytes 110600 | tf_op jit(solution)/shard_map/ppermute | solution.py:95
  58.9 4.0 %collective-permute-start.24 = (f32[72,128]{1,0:T(8,128)S(1)}, f32[72,128]{1,0:T(8,128)S(1)}, u32[]{:S(2)}, u32[]{:S(2)}) collective-permute-start(f32[72,128]{1,0:T(8,128)S(1)} %shard_map.128.mine), channel_id=1, source_target_pairs={{0,2},{1,3},{2,0},{3,1},{16,18},{17,19},{18,16},{19,17},{4,6},{5,7... | collective-permute-start | bytes 110600 | tf_op jit(solution)/shard_map/ppermute | solution.py:95
  (3 other events, 8.7 us)

commit v14 on v13

--- a/solution.py
+++ b/solution.py
@@ -81,6 +81,7 @@
 
 QUOTAS = (0, 64, 128)
 CAP = 128
+VIDEO = 32
 CHUNKS = len(QUOTAS) - 1
 F32, BF16 = jnp.float32, jnp.bfloat16
 TILE = 768
@@ -430,7 +431,7 @@
         own = mine[...].astype(F32)
         own = own[:8] + own[8:]
         own = own + pltpu.roll(own, 4, 0)
-        ends_out[0][...] = jnp.concatenate([total, own, jnp.zeros((112, 128), F32)], 0).T
+        ends_out[0][...] = jnp.concatenate([total, own, jnp.zeros((112, 128), F32)], 0)
 
 
 def contract_other_kernel(k, place, act, so_far, w, *refs):
@@ -459,18 +460,25 @@
     layer = jnp.where(slots[:, 0:1] > 0.5, layer, 0.0).astype(BF16)
     layer_out[...] = layer
     x = layer.astype(F32)
-    centre = jnp.sum(x, -1, keepdims=True) / x.shape[1]
-    ones = jnp.ones((8, x.shape[1]), BF16)
-    across = lambda left, right: lax.dot_general(
-        left, right, (((1,), (1,)), ((), ())), preferred_element_type=F32
-    )
-    high, low = high_low(x * x)
-    total, square = across(ones, layer), across(ones, high) + across(ones, low)
+    total = jnp.sum(x, -1, keepdims=True)
+    square = jnp.sum(x * x, -1, keepdims=True)
+    centre = total / x.shape[1]
     width = out_weight.shape[0]
-    product = across(out_weight[...], ((x - centre) * (1.0 + mod[7:8, :])).astype(BF16))
-    bundle_out[:width, :] = product + total[0:1] / x.shape[1] * ends[:width, 8:9]
-    row = lax.broadcasted_iota(jnp.int32, (8, CAP), 0)
-    bundle_out[width:, :] = jnp.where(row == 0, total, square)
+    product = lax.dot_general(
+        ((x - centre) * (1.0 + mod[7:8, :])).astype(BF16),
+        out_weight[...],
+        (((1,), (1,)), ((), ())),
+        preferred_element_type=F32,
+    )
+    product = product + centre * ends[8:9, :width]
+    lane = lax.broadcasted_iota(jnp.int32, (CAP, width), 1)
+    side = jnp.where(lane == 0, total, jnp.where(lane == 1, square, 0.0))
+    video = (slots[:, 0:1] > 0.5) & (slots[:, 1:2] < 0.5)
+    bundle = jnp.where(video, jnp.concatenate([product, side], 1), 0.0)
+    kept = bundle[:VIDEO]
+    for first in range(VIDEO, CAP, VIDEO):
+        kept = kept + bundle[first : first + VIDEO]
+    bundle_out[...] = kept
 
 
 def write_kernel(layer, out):
@@ -500,17 +508,19 @@
     factor = noise[width : width + 1]
 
     def velocity(total):
-        average = total[width : width + 1] / D
-        variance = total[width + 1 : width + 2] / D - average * average
-        return (total[:width] - average * ends[:width, 0:1]) * lax.rsqrt(
+        average = total[:, width : width + 1] / D
+        variance = total[:, width + 1 : width + 2] / D - average * average
+        return (total[:, :width] - average * ends[0:1, :width]) * lax.rsqrt(
             variance + norm_eps
-        ) + ends[:width, 1:2]
+        ) + ends[1:2, :width]
 
     first = lax.axis_index("cfg") == 0
     guided = velocity(mine[...] + mine_y[...]) * jnp.where(first, guidance, 1.0 - guidance)
     guided = guided + velocity(other[...] + other_y[...]) * jnp.where(
         first, 1.0 - guidance, guidance
     )
+    guided = jnp.concatenate([guided] * (CAP // VIDEO), 0)
+    guided = jnp.concatenate([guided, jnp.zeros((CAP, 128 - width), F32)], 1).T[:width]
     guided = jnp.where(factor > 0.0, guided, 0.0)
     out[...] = noise[:width] - factor * guided
 
@@ -701,13 +711,13 @@
 
     layer, bundle = call(
         finish_kernel,
-        [((CAP, features), BF16), ((width + 8, CAP), F32)],
+        [((CAP, features), BF16), ((VIDEO, 2 * width), F32)],
         [slots, tokens, mod, out_weight, ends, *returned],
         "v" * (5 + len(returned)),
     )
     (layer_out,) = call(write_kernel, [((CAP, features), BF16)], [layer], "v", weight=LONG)
     (bundle,) = call(
-        add_kernel, [((width + 8, CAP), F32)], [bundle, swap(bundle, "narrow", 1, 4)], "vv"
+        add_kernel, [((VIDEO, 2 * width), F32)], [bundle, swap(bundle, "narrow", 1, 4)], "vv"
     )
     (clean_latent,) = call(
         latent_kernel,

time: 63.7 us -> 63.5 us (level)
  no operation moved by 1% of the time
where the time goes in v14:
time: 63.5 us; the launch traced here: 63.3 us
  starting transfers between devices  31.2 us (49%)
  Pallas kernels  15.6 us (25%)
  waiting for transfers between devices  15 us (24%)
  between operations  1.52 us (2%)
    ppermute x25, starting transfers between devices, swap(): return lax.ppermute(array, axis, [(i, i ^ distance) for i in range(size)])  31.2 us
    pallas_call x26, Pallas kernels, call(): pl.pallas_call(kernel, out_shape=[jax.ShapeDtypeStruct(shape, dtype) for...  15.6 us
    ppermute x25, waiting for transfers between devices, swap(): return lax.ppermute(array, axis, [(i, i ^ distance) for i in range(size)])  15 us
  transfers between devices with their start and end apart: 25, of which 14 were waited for; matrix products, arithmetic and copies ran while one was open for 0% of the time, Pallas kernels for 21%

profile of v14, /device:TPU:0, one launch (start us, length us, event | category | flops | bytes accessed | tf_op | source)
XLA Modules:
  0.0 63.3 jit_solution(15988425639488567232)
XLA Ops:
  0.6 0.9 %shard_map.105 = bf16[64,768]{1,0:T(8,128)(2,1)S(1)} custom-call(bf16[128,768]{1,0:T(8,128)(2,1)} %bitcast.6), custom_call_target="tpu_custom_call" | custom-call | flops 1 | bytes 1 | tf_op jit(solution)/shard_map/pallas_call | solution.py:536
  1.5 4.1 %collective-permute-start.1 = (bf16[64,768]{1,0:T(8,128)(2,1)S(1)}, bf16[64,768]{1,0:T(8,128)(2,1)S(1)}, u32[]{:S(2)}, u32[]{:S(2)}) collective-permute-start(bf16[64,768]{1,0:T(8,128)(2,1)S(1)} %shard_map.105), channel_id=1, source_target_pairs={{0,8},{4,12},{8,0},{12,4},{1,9},{5,13},{9,1},{13,5},{2,10},{6,14},... | collective-permute-start | bytes 294920 | tf_op jit(solution)/shard_map/ppermute | solution.py:96
  5.6 1.6 %collective-permute-start = (bf16[128,768]{1,0:T(8,128)(2,1)}, bf16[128,768]{1,0:T(8,128)(2,1)S(1)}, u32[]{:S(2)}, u32[]{:S(2)}) collective-permute-start(bf16[128,768]{1,0:T(8,128)(2,1)} %bitcast.7), channel_id=1, source_target_pairs={{0,4},{4,0},{8,12},{12,8},{1,5},{5,1},{9,13},{13,9},{2,6},{6,2},{1... | collective-permute-start | bytes 589832 | tf_op jit(solution)/shard_map/ppermute | solution.py:96
  7.9 2.6 %shard_map.104 = (bf16[64,768]{1,0:T(8,128)(2,1)S(1)}, bf16[128,256]{1,0:T(8,128)(2,1)S(1)}, bf16[128,512]{1,0:T(8,128)(2,1)S(1)}, bf16[256,128]{1,0:T(8,128)(2,...) custom-call(s32[4]{0:T(128)} %table_in.1, ...), custom_call_target="tpu_custom_call" | custom-call | flops 1 | bytes 1 | tf_op jit(solution)/shard_map/pallas_call | solution.py:536
  10.5 0.8 %collective-permute-start.2 = (bf16[64,768]{1,0:T(8,128)(2,1)S(1)}, bf16[64,768]{1,0:T(8,128)(2,1)S(1)}, u32[]{:S(2)}, u32[]{:S(2)}) collective-permute-start(bf16[64,768]{1,0:T(8,128)(2,1)S(1)} %shard_map.106.refs_0_), channel_id=1, source_target_pairs={{0,4},{4,0},{8,12},{12,8},{1,5},{5,1},{9,13},{13,9},{2,6},{6,2},{1... | collective-permute-start | bytes 294920 | tf_op jit(solution)/shard_map/ppermute | solution.py:96
  11.3 3.5 %collective-permute-start.7 = (bf16[64,768]{1,0:T(8,128)(2,1)S(1)}, bf16[64,768]{1,0:T(8,128)(2,1)S(1)}, u32[]{:S(2)}, u32[]{:S(2)}) collective-permute-start(bf16[64,768]{1,0:T(8,128)(2,1)S(1)} %get-tuple-element.62), channel_id=1, source_target_pairs={{0,8},{4,12},{8,0},{12,4},{1,9},{5,13},{9,1},{13,5},{2,10},{6,14},... | collective-permute-start | bytes 294920 | tf_op jit(solution)/shard_map/ppermute | solution.py:96
  15.3 0.9 %shard_map.107 = (bf16[144,768]{1,0:T(8,128)(2,1)S(1)}, bf16[128,1536]{1,0:T(8,128)(2,1)S(1)}, bf16[16,2688]{1,0:T(8,128)(2,1)S(1)}) custom-call(f32[128,128]{1,0:T(8,128)S(1)} %get-tuple-element.47.text, f32[8,768]{1,0:T(8,128)S(1)} %get-tuple-element.45.mod, bf16[128,256]{1,0:T(8,128)(2,1)S(1)} %get-tuple-element.48.place, ...), custom_call_target="tpu_custom_call" | custom-call | flops 10000000000 | bytes 1 | tf_op jit(solution)/shard_map/pallas_call | solution.py:536
  17.6 1.6 %collective-permute-start.6 = (bf16[16,1920]{1,0:T(8,128)(2,1)S(1)}, bf16[16,1920]{1,0:T(8,128)(2,1)S(1)}, u32[]{:S(2)}, u32[]{:S(2)}) collective-permute-start(bf16[16,1920]{1,0:T(8,128)(2,1)S(1)} %get-tuple-element.58._.refs_1_.first_sent.chip), channel_id=1, source_target_pairs={{0,2},{1,3},{2,0},{3,1},{4,6},{5,7},{6,4},{7,5},{8,10},{9,11},{10,... | collective-permute-start | bytes 184328 | tf_op jit(solution)/shard_map/ppermute | solution.py:96
  19.9 1.3 %collective-permute-start.8 = (bf16[64,768]{1,0:T(8,128)(2,1)S(1)}, bf16[64,768]{1,0:T(8,128)(2,1)S(1)}, u32[]{:S(2)}, u32[]{:S(2)}) collective-permute-start(bf16[64,768]{1,0:T(8,128)(2,1)S(1)} %shard_map.111.refs_0_.refs_2_), channel_id=1, source_target_pairs={{0,4},{4,0},{8,12},{12,8},{1,5},{5,1},{9,13},{13,9},{2,6},{6,2},{1... | collective-permute-start | bytes 294920 | tf_op jit(solution)/shard_map/ppermute | solution.py:96
  21.2 2.4 %shard_map.113.refs_9_.w = bf16[3072,768]{1,0:T(8,128)(2,1)S(1)} custom-call(bf16[3072,768]{1,0:T(8,128)(2,1)} %source.1, bf16[64,768]{1,0:T(8,128)(2,1)S(1)} %shard_map.111.refs_0_.refs_2_, bf16[16,1920]{1,0:T(8,128)(2,1)S(1)} %get-tuple-element.58._.refs_1_.first_sent.chip), custom_call_target="tpu_custom_call" | custom-call | flops 10000000000 | bytes 1 | tf_op jit(solution)/shard_map/pallas_call | solution.py:536
  23.7 1.0 %collective-permute-done.8.refs_3_ = bf16[64,768]{1,0:T(8,128)(2,1)S(1)} collective-permute-done((bf16[64,768]{1,0:T(8,128)(2,1)S(1)}, bf16[64,768]{1,0:T(8,128)(2,1)S(1)}, u32[]{:S(2)}, u32[]{:S(2)}) %collective-permute-start.8) | collective-permute-done | bytes 98336 | tf_op jit(solution)/shard_map/ppermute | solution.py:96
  24.7 0.9 %shard_map.114 = (bf16[128,768]{1,0:T(8,128)(2,1)S(1)}, bf16[128,1536]{1,0:T(8,128)(2,1)S(1)}, bf16[128,128]{1,0:T(8,128)(2,1)S(1)}) custom-call(f32[128,128]{1,0:T(8,128)S(1)} %get-tuple-element.60.text, f32[8,768]{1,0:T(8,128)S(1)} %get-tuple-element.45.mod, bf16[128,512]{1,0:T(8,128)(2,1)S(1)} %get-tuple-element.61.place, ...), custom_call_target="tpu_custom_call" | custom-call | flops 10000000000 | bytes 1 | tf_op jit(solution)/shard_map/pallas_call | solution.py:536
  26.9 1.4 %collective-permute-start.12 = (bf16[16,256]{1,0:T(8,128)(2,1)S(1)}, bf16[16,256]{1,0:T(8,128)(2,1)S(1)}, u32[]{:S(2)}, u32[]{:S(2)}) collective-permute-start(bf16[16,256]{1,0:T(8,128)(2,1)S(1)} %get-tuple-element.68._.refs_1_), channel_id=1, source_target_pairs={{0,2},{1,3},{2,0},{3,1},{4,6},{5,7},{6,4},{7,5},{8,10},{9,11},{10,... | collective-permute-start | bytes 24584 | tf_op jit(solution)/shard_map/ppermute | solution.py:96
  33.4 4.9 %collective-permute-start.13 = (bf16[64,768]{1,0:T(8,128)(2,1)S(1)}, bf16[64,768]{1,0:T(8,128)(2,1)S(1)}, u32[]{:S(2)}, u32[]{:S(2)}) collective-permute-start(bf16[64,768]{1,0:T(8,128)(2,1)S(1)} %get-tuple-element.74.refs_3_), channel_id=1, source_target_pairs={{0,12},{4,8},{8,4},{12,0},{1,13},{5,9},{9,5},{13,1},{2,14},{6,10},... | collective-permute-start | bytes 294920 | tf_op jit(solution)/shard_map/ppermute | solution.py:96
  40.4 1.2 %collective-permute-done.17.act = bf16[128,1536]{1,0:T(8,128)(2,1)S(1)} collective-permute-done((bf16[128,1536]{1,0:T(8,128)(2,1)S(1)}, bf16[128,1536]{1,0:T(8,128)(2,1)S(1)}, u32[]{:S(2)}, u32[]{:S(2)}) %collective-permute-start.17) | collective-permute-done | bytes 393248 | tf_op jit(solution)/shard_map/ppermute | solution.py:96
  42.4 3.3 %collective-permute-start.18 = (bf16[64,768]{1,0:T(8,128)(2,1)S(1)}, bf16[64,768]{1,0:T(8,128)(2,1)S(1)}, u32[]{:S(2)}, u32[]{:S(2)}) collective-permute-start(bf16[64,768]{1,0:T(8,128)(2,1)S(1)} %get-tuple-element.79), channel_id=1, source_target_pairs={{0,8},{4,12},{8,0},{12,4},{1,9},{5,13},{9,1},{13,5},{2,10},{6,14},... | collective-permute-start | bytes 294920 | tf_op jit(solution)/shard_map/ppermute | solution.py:96
  45.7 1.5 %collective-permute-start.19 = (bf16[64,768]{1,0:T(8,128)(2,1)S(1)}, bf16[64,768]{1,0:T(8,128)(2,1)S(1)}, u32[]{:S(2)}, u32[]{:S(2)}) collective-permute-start(bf16[64,768]{1,0:T(8,128)(2,1)S(1)} %get-tuple-element.80), channel_id=1, source_target_pairs={{0,12},{4,8},{8,4},{12,0},{1,13},{5,9},{9,5},{13,1},{2,14},{6,10},... | collective-permute-start | bytes 294920 | tf_op jit(solution)/shard_map/ppermute | solution.py:96
  47.8 5.8 %collective-permute-done.18.refs_5_ = bf16[64,768]{1,0:T(8,128)(2,1)S(1)} collective-permute-done((bf16[64,768]{1,0:T(8,128)(2,1)S(1)}, bf16[64,768]{1,0:T(8,128)(2,1)S(1)}, u32[]{:S(2)}, u32[]{:S(2)}) %collective-permute-start.18) | collective-permute-done | bytes 98336 | tf_op jit(solution)/shard_map/ppermute | solution.py:96
  53.6 0.9 %collective-permute-done.20.refs_7_ = bf16[64,768]{1,0:T(8,128)(2,1)S(1)} collective-permute-done((bf16[64,768]{1,0:T(8,128)(2,1)S(1)}, bf16[64,768]{1,0:T(8,128)(2,1)S(1)}, u32[]{:S(2)}, u32[]{:S(2)}) %collective-permute-start.20) | collective-permute-done | bytes 98336 | tf_op jit(solution)/shard_map/ppermute | solution.py:96
  55.0 1.2 %collective-permute-done.21.right = f32[32,128]{1,0:T(8,128)S(1)} collective-permute-done((f32[32,128]{1,0:T(8,128)S(1)}, f32[32,128]{1,0:T(8,128)S(1)}, u32[]{:S(2)}, u32[]{:S(2)}) %collective-permute-start.21) | collective-permute-done | bytes 16416 | tf_op jit(solution)/shard_map/ppermute | solution.py:96
  56.2 2.0 %collective-permute-start.22 = (f32[32,128]{1,0:T(8,128)S(1)}, f32[32,128]{1,0:T(8,128)S(1)}, u32[]{:S(2)}, u32[]{:S(2)}) collective-permute-start(f32[32,128]{1,0:T(8,128)S(1)} %shard_map.128.mine), channel_id=1, source_target_pairs={{0,18},{1,19},{2,16},{3,17},{16,2},{17,3},{18,0},{19,1},{4,22},{5,... | collective-permute-start | bytes 49160 | tf_op jit(solution)/shard_map/ppermute | solution.py:96
  58.7 1.0 %collective-permute-start.24 = (f32[32,128]{1,0:T(8,128)S(1)}, f32[32,128]{1,0:T(8,128)S(1)}, u32[]{:S(2)}, u32[]{:S(2)}) collective-permute-start(f32[32,128]{1,0:T(8,128)S(1)} %shard_map.128.mine), channel_id=1, source_target_pairs={{0,2},{1,3},{2,0},{3,1},{16,18},{17,19},{18,16},{19,17},{4,6},{5,7... | collective-permute-start | bytes 49160 | tf_op jit(solution)/shard_map/ppermute | solution.py:96
  60.9 1.1 %collective-permute-done.23.other = f32[32,128]{1,0:T(8,128)S(1)} collective-permute-done((f32[32,128]{1,0:T(8,128)S(1)}, f32[32,128]{1,0:T(8,128)S(1)}, u32[]{:S(2)}, u32[]{:S(2)}) %collective-permute-start.23) | collective-permute-done | bytes 16416 | tf_op jit(solution)/shard_map/ppermute | solution.py:96
  62.5 0.9 %shard_map.129 = f32[64,128]{1,0:T(8,128)} custom-call(f32[72,128]{1,0:T(8,128)S(1)} %shard_map.112.refs_8_.noise, f32[128,128]{1,0:T(8,128)S(1)} %get-tuple-element.69.ends, f32[32,128]{1,0:T(8,128)S(1)} %shard_map.128.mine, f32[32,128]{1,0:T(8,128)S(1)} %collective-permute-done.22.other_y, f32[32,128]{1,0:T(8,128)S(1)} %collective-permute-done.23.other, ...), custom_call_target="tpu_custom_call" | custom-call | flops 1 | bytes 1 | tf_op jit(solution)/shard_map/pallas_call | solution.py:536
  (56 shorter events, 15.2 us)
Async XLA Ops:
  1.5 9.0 %collective-permute-start.1 = (bf16[64,768]{1,0:T(8,128)(2,1)S(1)}, bf16[64,768]{1,0:T(8,128)(2,1)S(1)}, u32[]{:S(2)}, u32[]{:S(2)}) collective-permute-start(bf16[64,768]{1,0:T(8,128)(2,1)S(1)} %shard_map.105), channel_id=1, source_target_pairs={{0,8},{4,12},{8,0},{12,4},{1,9},{5,13},{9,1},{13,5},{2,10},{6,14},... | collective-permute-start | bytes 294920 | tf_op jit(solution)/shard_map/ppermute | solution.py:96
  5.6 9.6 %collective-permute-start = (bf16[128,768]{1,0:T(8,128)(2,1)}, bf16[128,768]{1,0:T(8,128)(2,1)S(1)}, u32[]{:S(2)}, u32[]{:S(2)}) collective-permute-start(bf16[128,768]{1,0:T(8,128)(2,1)} %bitcast.7), channel_id=1, source_target_pairs={{0,4},{4,0},{8,12},{12,8},{1,5},{5,1},{9,13},{13,9},{2,6},{6,2},{1... | collective-permute-start | bytes 589832 | tf_op jit(solution)/shard_map/ppermute | solution.py:96
  10.5 4.7 %collective-permute-start.2 = (bf16[64,768]{1,0:T(8,128)(2,1)S(1)}, bf16[64,768]{1,0:T(8,128)(2,1)S(1)}, u32[]{:S(2)}, u32[]{:S(2)}) collective-permute-start(bf16[64,768]{1,0:T(8,128)(2,1)S(1)} %shard_map.106.refs_0_), channel_id=1, source_target_pairs={{0,4},{4,0},{8,12},{12,8},{1,5},{5,1},{9,13},{13,9},{2,6},{6,2},{1... | collective-permute-start | bytes 294920 | tf_op jit(solution)/shard_map/ppermute | solution.py:96
  11.3 8.5 %collective-permute-start.7 = (bf16[64,768]{1,0:T(8,128)(2,1)S(1)}, bf16[64,768]{1,0:T(8,128)(2,1)S(1)}, u32[]{:S(2)}, u32[]{:S(2)}) collective-permute-start(bf16[64,768]{1,0:T(8,128)(2,1)S(1)} %get-tuple-element.62), channel_id=1, source_target_pairs={{0,8},{4,12},{8,0},{12,4},{1,9},{5,13},{9,1},{13,5},{2,10},{6,14},... | collective-permute-start | bytes 294920 | tf_op jit(solution)/shard_map/ppermute | solution.py:96
  16.1 1.3 %collective-permute-start.4 = (bf16[16,2688]{1,0:T(8,128)(2,1)S(1)}, bf16[16,2688]{1,0:T(8,128)(2,1)S(1)}, u32[]{:S(2)}, u32[]{:S(2)}) collective-permute-start(bf16[16,2688]{1,0:T(8,128)(2,1)S(1)} %get-tuple-element.55.__.side), channel_id=1, source_target_pairs={{0,1},{1,0},{2,3},{3,2},{4,5},{5,4},{6,7},{7,6},{8,9},{9,8},{10,11... | collective-permute-start | bytes 258056 | tf_op jit(solution)/shard_map/ppermute | solution.py:96
  16.2 3.0 %collective-permute-start.3 = (bf16[128,1536]{1,0:T(8,128)(2,1)S(1)}, bf16[128,1536]{1,0:T(8,128)(2,1)S(1)}, u32[]{:S(2)}, u32[]{:S(2)}) collective-permute-start(bf16[128,1536]{1,0:T(8,128)(2,1)S(1)} %get-tuple-element.54._), channel_id=1, source_target_pairs={{0,1},{1,0},{2,3},{3,2},{4,5},{5,4},{6,7},{7,6},{8,9},{9,8},{10,11... | collective-permute-start | bytes 1179656 | tf_op jit(solution)/shard_map/ppermute | solution.py:96
  17.6 11.5 %collective-permute-start.6 = (bf16[16,1920]{1,0:T(8,128)(2,1)S(1)}, bf16[16,1920]{1,0:T(8,128)(2,1)S(1)}, u32[]{:S(2)}, u32[]{:S(2)}) collective-permute-start(bf16[16,1920]{1,0:T(8,128)(2,1)S(1)} %get-tuple-element.58._.refs_1_.first_sent.chip), channel_id=1, source_target_pairs={{0,2},{1,3},{2,0},{3,1},{4,6},{5,7},{6,4},{7,5},{8,10},{9,11},{10,... | collective-permute-start | bytes 184328 | tf_op jit(solution)/shard_map/ppermute | solution.py:96
  19.3 11.1 %collective-permute-start.5 = (bf16[128,1536]{1,0:T(8,128)(2,1)S(1)}, bf16[128,1536]{1,0:T(8,128)(2,1)S(1)}, u32[]{:S(2)}, u32[]{:S(2)}) collective-permute-start(bf16[128,1536]{1,0:T(8,128)(2,1)S(1)} %shard_map.110._.refs_7_.total), channel_id=1, source_target_pairs={{0,2},{1,3},{2,0},{3,1},{4,6},{5,7},{6,4},{7,5},{8,10},{9,11},{10,... | collective-permute-start | bytes 1179656 | tf_op jit(solution)/shard_map/ppermute | solution.py:96
  19.9 4.8 %collective-permute-start.8 = (bf16[64,768]{1,0:T(8,128)(2,1)S(1)}, bf16[64,768]{1,0:T(8,128)(2,1)S(1)}, u32[]{:S(2)}, u32[]{:S(2)}) collective-permute-start(bf16[64,768]{1,0:T(8,128)(2,1)S(1)} %shard_map.111.refs_0_.refs_2_), channel_id=1, source_target_pairs={{0,4},{4,0},{8,12},{12,8},{1,5},{5,1},{9,13},{13,9},{2,6},{6,2},{1... | collective-permute-start | bytes 294920 | tf_op jit(solution)/shard_map/ppermute | solution.py:96
  25.6 1.3 %collective-permute-start.10 = (bf16[128,128]{1,0:T(8,128)(2,1)S(1)}, bf16[128,128]{1,0:T(8,128)(2,1)S(1)}, u32[]{:S(2)}, u32[]{:S(2)}) collective-permute-start(bf16[128,128]{1,0:T(8,128)(2,1)S(1)} %get-tuple-element.67.__.side), channel_id=1, source_target_pairs={{0,1},{1,0},{2,3},{3,2},{4,5},{5,4},{6,7},{7,6},{8,9},{9,8},{10,11... | collective-permute-start | bytes 98312 | tf_op jit(solution)/shard_map/ppermute | solution.py:96
  25.6 2.7 %collective-permute-start.9 = (bf16[128,1536]{1,0:T(8,128)(2,1)S(1)}, bf16[128,1536]{1,0:T(8,128)(2,1)S(1)}, u32[]{:S(2)}, u32[]{:S(2)}) collective-permute-start(bf16[128,1536]{1,0:T(8,128)(2,1)S(1)} %get-tuple-element.66._), channel_id=1, source_target_pairs={{0,1},{1,0},{2,3},{3,2},{4,5},{5,4},{6,7},{7,6},{8,9},{9,8},{10,11... | collective-permute-start | bytes 1179656 | tf_op jit(solution)/shard_map/ppermute | solution.py:96
  26.9 4.5 %collective-permute-start.12 = (bf16[16,256]{1,0:T(8,128)(2,1)S(1)}, bf16[16,256]{1,0:T(8,128)(2,1)S(1)}, u32[]{:S(2)}, u32[]{:S(2)}) collective-permute-start(bf16[16,256]{1,0:T(8,128)(2,1)S(1)} %get-tuple-element.68._.refs_1_), channel_id=1, source_target_pairs={{0,2},{1,3},{2,0},{3,1},{4,6},{5,7},{6,4},{7,5},{8,10},{9,11},{10,... | collective-permute-start | bytes 24584 | tf_op jit(solution)/shard_map/ppermute | solution.py:96
  28.4 11.0 %collective-permute-start.16 = (bf16[128,1536]{1,0:T(8,128)(2,1)S(1)}, bf16[128,1536]{1,0:T(8,128)(2,1)S(1)}, u32[]{:S(2)}, u32[]{:S(2)}) collective-permute-start(bf16[128,1536]{1,0:T(8,128)(2,1)S(1)} %shard_map.117.refs_0_.total), channel_id=1, source_target_pairs={{0,2},{1,3},{2,0},{3,1},{4,6},{5,7},{6,4},{7,5},{8,10},{9,11},{10,... | collective-permute-start | bytes 1179656 | tf_op jit(solution)/shard_map/ppermute | solution.py:96
  30.8 1.8 %collective-permute-start.11 = (bf16[128,1536]{1,0:T(8,128)(2,1)S(1)}, bf16[128,1536]{1,0:T(8,128)(2,1)S(1)}, u32[]{:S(2)}, u32[]{:S(2)}) collective-permute-start(bf16[128,1536]{1,0:T(8,128)(2,1)S(1)} %shard_map.119.act.refs_0_), channel_id=1, source_target_pairs={{0,1},{1,0},{2,3},{3,2},{4,5},{5,4},{6,7},{7,6},{8,9},{9,8},{10,11... | collective-permute-start | bytes 1179656 | tf_op jit(solution)/shard_map/ppermute | solution.py:96
  33.4 13.9 %collective-permute-start.13 = (bf16[64,768]{1,0:T(8,128)(2,1)S(1)}, bf16[64,768]{1,0:T(8,128)(2,1)S(1)}, u32[]{:S(2)}, u32[]{:S(2)}) collective-permute-start(bf16[64,768]{1,0:T(8,128)(2,1)S(1)} %get-tuple-element.74.refs_3_), channel_id=1, source_target_pairs={{0,12},{4,8},{8,4},{12,0},{1,13},{5,9},{9,5},{13,1},{2,14},{6,10},... | collective-permute-start | bytes 294920 | tf_op jit(solution)/shard_map/ppermute | solution.py:96
  38.2 9.5 %collective-permute-start.14 = (bf16[64,768]{1,0:T(8,128)(2,1)S(1)}, bf16[64,768]{1,0:T(8,128)(2,1)S(1)}, u32[]{:S(2)}, u32[]{:S(2)}) collective-permute-start(bf16[64,768]{1,0:T(8,128)(2,1)S(1)} %get-tuple-element.75.refs_2_), channel_id=1, source_target_pairs={{0,8},{4,12},{8,0},{12,4},{1,9},{5,13},{9,1},{13,5},{2,10},{6,14},... | collective-permute-start | bytes 294920 | tf_op jit(solution)/shard_map/ppermute | solution.py:96
  38.2 9.5 %collective-permute-start.15 = (bf16[64,768]{1,0:T(8,128)(2,1)S(1)}, bf16[64,768]{1,0:T(8,128)(2,1)S(1)}, u32[]{:S(2)}, u32[]{:S(2)}) collective-permute-start(bf16[64,768]{1,0:T(8,128)(2,1)S(1)} %get-tuple-element.76.refs_1_), channel_id=1, source_target_pairs={{0,4},{4,0},{8,12},{12,8},{1,5},{5,1},{9,13},{13,9},{2,6},{6,2},{1... | collective-permute-start | bytes 294920 | tf_op jit(solution)/shard_map/ppermute | solution.py:96
  39.9 1.8 %collective-permute-start.17 = (bf16[128,1536]{1,0:T(8,128)(2,1)S(1)}, bf16[128,1536]{1,0:T(8,128)(2,1)S(1)}, u32[]{:S(2)}, u32[]{:S(2)}) collective-permute-start(bf16[128,1536]{1,0:T(8,128)(2,1)S(1)} %shard_map.123.act), channel_id=1, source_target_pairs={{0,1},{1,0},{2,3},{3,2},{4,5},{5,4},{6,7},{7,6},{8,9},{9,8},{10,11... | collective-permute-start | bytes 1179656 | tf_op jit(solution)/shard_map/ppermute | solution.py:96
  42.4 11.2 %collective-permute-start.18 = (bf16[64,768]{1,0:T(8,128)(2,1)S(1)}, bf16[64,768]{1,0:T(8,128)(2,1)S(1)}, u32[]{:S(2)}, u32[]{:S(2)}) collective-permute-start(bf16[64,768]{1,0:T(8,128)(2,1)S(1)} %get-tuple-element.79), channel_id=1, source_target_pairs={{0,8},{4,12},{8,0},{12,4},{1,9},{5,13},{9,1},{13,5},{2,10},{6,14},... | collective-permute-start | bytes 294920 | tf_op jit(solution)/shard_map/ppermute | solution.py:96
  45.7 7.8 %collective-permute-start.19 = (bf16[64,768]{1,0:T(8,128)(2,1)S(1)}, bf16[64,768]{1,0:T(8,128)(2,1)S(1)}, u32[]{:S(2)}, u32[]{:S(2)}) collective-permute-start(bf16[64,768]{1,0:T(8,128)(2,1)S(1)} %get-tuple-element.80), channel_id=1, source_target_pairs={{0,12},{4,8},{8,4},{12,0},{1,13},{5,9},{9,5},{13,1},{2,14},{6,10},... | collective-permute-start | bytes 294920 | tf_op jit(solution)/shard_map/ppermute | solution.py:96
  47.3 7.2 %collective-permute-start.20 = (bf16[64,768]{1,0:T(8,128)(2,1)S(1)}, bf16[64,768]{1,0:T(8,128)(2,1)S(1)}, u32[]{:S(2)}, u32[]{:S(2)}) collective-permute-start(bf16[64,768]{1,0:T(8,128)(2,1)S(1)} %get-tuple-element.81), channel_id=1, source_target_pairs={{0,4},{4,0},{8,12},{12,8},{1,5},{5,1},{9,13},{13,9},{2,6},{6,2},{1... | collective-permute-start | bytes 294920 | tf_op jit(solution)/shard_map/ppermute | solution.py:96
  56.2 4.6 %collective-permute-start.22 = (f32[32,128]{1,0:T(8,128)S(1)}, f32[32,128]{1,0:T(8,128)S(1)}, u32[]{:S(2)}, u32[]{:S(2)}) collective-permute-start(f32[32,128]{1,0:T(8,128)S(1)} %shard_map.128.mine), channel_id=1, source_target_pairs={{0,18},{1,19},{2,16},{3,17},{16,2},{17,3},{18,0},{19,1},{4,22},{5,... | collective-permute-start | bytes 49160 | tf_op jit(solution)/shard_map/ppermute | solution.py:96
  58.2 3.7 %collective-permute-start.23 = (f32[32,128]{1,0:T(8,128)S(1)}, f32[32,128]{1,0:T(8,128)S(1)}, u32[]{:S(2)}, u32[]{:S(2)}) collective-permute-start(f32[32,128]{1,0:T(8,128)S(1)} %shard_map.128.mine), channel_id=1, source_target_pairs={{0,16},{1,17},{2,18},{3,19},{16,0},{17,1},{18,2},{19,3},{4,20},{5,... | collective-permute-start | bytes 49160 | tf_op jit(solution)/shard_map/ppermute | solution.py:96
  58.7 3.7 %collective-permute-start.24 = (f32[32,128]{1,0:T(8,128)S(1)}, f32[32,128]{1,0:T(8,128)S(1)}, u32[]{:S(2)}, u32[]{:S(2)}) collective-permute-start(f32[32,128]{1,0:T(8,128)S(1)} %shard_map.128.mine), channel_id=1, source_target_pairs={{0,2},{1,3},{2,0},{3,1},{16,18},{17,19},{18,16},{19,17},{4,6},{5,7... | collective-permute-start | bytes 49160 | tf_op jit(solution)/shard_map/ppermute | solution.py:96
  (3 other events, 8.7 us)

commit v15 on v14

--- a/solution.py
+++ b/solution.py
@@ -446,14 +446,21 @@
         outs[s][...] = spread[s * size : (s + 1) * size]
 
 
+def total_kernel(first, second, third, fourth, *refs):
+    total = first[...].astype(F32) + second[...].astype(F32)
+    refs[-1][...] = total + (third[...].astype(F32) + fourth[...].astype(F32))
+
+
 def finish_kernel(slots, hidden, mod, out_weight, ends, *refs):
-    pieces, (layer_out, bundle_out) = refs[: 4 * CHUNKS], refs[4 * CHUNKS :]
+    totals, pieces = refs[: CHUNKS - 1], refs[CHUNKS - 1 : -2]
+    layer_out, bundle_out = refs[-2:]
+    total = pieces[0][...].astype(F32)
+    for piece in pieces[1:]:
+        total = total + piece[...].astype(F32)
+    totals = [*(earlier[...] for earlier in totals), total]
     result = jnp.zeros(hidden.shape, F32)
     for k in range(CHUNKS):
-        total = pieces[4 * k][...].astype(F32)
-        for s in (1, 2, 3):
-            total = total + pieces[4 * k + s][...].astype(F32)
-        total = jnp.concatenate([total] * (CAP // size_of(k)), 0)
+        total = jnp.concatenate([totals[k]] * (CAP // size_of(k)), 0)
         result = jnp.where(slots[:, 2 + k : 3 + k] > 0.5, total, result)
     gate = jnp.where(slots[:, 1:2] > 0.5, mod[5:6, :], mod[2:3, :])
     layer = hidden[...].astype(F32) + gate * result
@@ -707,7 +714,12 @@
         )
         before = pieces
         distances = (3, 2, 1) if k + 1 < CHUNKS else (2, 3, 1)
-        returned += [pieces[0], *(swap(pieces[s], "wide", s, 4) for s in distances)]
+        arrived = [pieces[0], *(swap(pieces[s], "wide", s, 4) for s in distances)]
+        if k + 1 < CHUNKS:
+            arrived = call(
+                total_kernel, [((size_of(k), features), F32)], arrived, "vvvv", weight=LONG
+            )
+        returned += arrived
 
     layer, bundle = call(
         finish_kernel,

time: 63.5 us -> 63.5 us (level)
    pallas_call x26 -> x27, Pallas kernels: 15.6 us -> 15.6 us  [call(): pl.pallas_call(kernel, out_shape=[jax.ShapeDtypeStruct(shape, dtype) for...]
where the time goes in v15:
time: 63.5 us; the launch traced here: 63.3 us
  starting transfers between devices  31.2 us (49%)
  Pallas kernels  15.6 us (25%)
  waiting for transfers between devices  14.9 us (23%)
  between operations  1.52 us (2%)
    ppermute x25, starting transfers between devices, swap(): return lax.ppermute(array, axis, [(i, i ^ distance) for i in range(size)])  31.2 us
    pallas_call x27, Pallas kernels, call(): pl.pallas_call(kernel, out_shape=[jax.ShapeDtypeStruct(shape, dtype) for...  15.6 us
    ppermute x25, waiting for transfers between devices, swap(): return lax.ppermute(array, axis, [(i, i ^ distance) for i in range(size)])  14.9 us
  transfers between devices with their start and end apart: 25, of which 14 were waited for; matrix products, arithmetic and copies ran while one was open for 0% of the time, Pallas kernels for 21%

profile of v15, /device:TPU:0, one launch (start us, length us, event | category | flops | bytes accessed | tf_op | source)
XLA Modules:
  0.0 63.3 jit_solution(11849148930149697883)
XLA Ops:
  0.6 0.9 %shard_map.105 = bf16[64,768]{1,0:T(8,128)(2,1)S(1)} custom-call(bf16[128,768]{1,0:T(8,128)(2,1)} %bitcast.6), custom_call_target="tpu_custom_call" | custom-call | flops 1 | bytes 1 | tf_op jit(solution)/shard_map/pallas_call | solution.py:543
  1.5 4.1 %collective-permute-start.1 = (bf16[64,768]{1,0:T(8,128)(2,1)S(1)}, bf16[64,768]{1,0:T(8,128)(2,1)S(1)}, u32[]{:S(2)}, u32[]{:S(2)}) collective-permute-start(bf16[64,768]{1,0:T(8,128)(2,1)S(1)} %shard_map.105), channel_id=1, source_target_pairs={{0,8},{4,12},{8,0},{12,4},{1,9},{5,13},{9,1},{13,5},{2,10},{6,14},... | collective-permute-start | bytes 294920 | tf_op jit(solution)/shard_map/ppermute | solution.py:96
  5.6 1.6 %collective-permute-start = (bf16[128,768]{1,0:T(8,128)(2,1)}, bf16[128,768]{1,0:T(8,128)(2,1)S(1)}, u32[]{:S(2)}, u32[]{:S(2)}) collective-permute-start(bf16[128,768]{1,0:T(8,128)(2,1)} %bitcast.7), channel_id=1, source_target_pairs={{0,4},{4,0},{8,12},{12,8},{1,5},{5,1},{9,13},{13,9},{2,6},{6,2},{1... | collective-permute-start | bytes 589832 | tf_op jit(solution)/shard_map/ppermute | solution.py:96
  7.9 2.6 %shard_map.104 = (bf16[64,768]{1,0:T(8,128)(2,1)S(1)}, bf16[128,256]{1,0:T(8,128)(2,1)S(1)}, bf16[128,512]{1,0:T(8,128)(2,1)S(1)}, bf16[256,128]{1,0:T(8,128)(2,...) custom-call(s32[4]{0:T(128)} %table_in.1, ...), custom_call_target="tpu_custom_call" | custom-call | flops 1 | bytes 1 | tf_op jit(solution)/shard_map/pallas_call | solution.py:543
  10.5 0.8 %collective-permute-start.2 = (bf16[64,768]{1,0:T(8,128)(2,1)S(1)}, bf16[64,768]{1,0:T(8,128)(2,1)S(1)}, u32[]{:S(2)}, u32[]{:S(2)}) collective-permute-start(bf16[64,768]{1,0:T(8,128)(2,1)S(1)} %shard_map.106.refs_0_), channel_id=1, source_target_pairs={{0,4},{4,0},{8,12},{12,8},{1,5},{5,1},{9,13},{13,9},{2,6},{6,2},{1... | collective-permute-start | bytes 294920 | tf_op jit(solution)/shard_map/ppermute | solution.py:96
  11.3 3.5 %collective-permute-start.7 = (bf16[64,768]{1,0:T(8,128)(2,1)S(1)}, bf16[64,768]{1,0:T(8,128)(2,1)S(1)}, u32[]{:S(2)}, u32[]{:S(2)}) collective-permute-start(bf16[64,768]{1,0:T(8,128)(2,1)S(1)} %get-tuple-element.62), channel_id=1, source_target_pairs={{0,8},{4,12},{8,0},{12,4},{1,9},{5,13},{9,1},{13,5},{2,10},{6,14},... | collective-permute-start | bytes 294920 | tf_op jit(solution)/shard_map/ppermute | solution.py:96
  15.3 0.9 %shard_map.107 = (bf16[144,768]{1,0:T(8,128)(2,1)S(1)}, bf16[128,1536]{1,0:T(8,128)(2,1)S(1)}, bf16[16,2688]{1,0:T(8,128)(2,1)S(1)}) custom-call(f32[128,128]{1,0:T(8,128)S(1)} %get-tuple-element.47.text, f32[8,768]{1,0:T(8,128)S(1)} %get-tuple-element.45.mod, bf16[128,256]{1,0:T(8,128)(2,1)S(1)} %get-tuple-element.48.place, ...), custom_call_target="tpu_custom_call" | custom-call | flops 10000000000 | bytes 1 | tf_op jit(solution)/shard_map/pallas_call | solution.py:543
  17.6 1.6 %collective-permute-start.6 = (bf16[16,1920]{1,0:T(8,128)(2,1)S(1)}, bf16[16,1920]{1,0:T(8,128)(2,1)S(1)}, u32[]{:S(2)}, u32[]{:S(2)}) collective-permute-start(bf16[16,1920]{1,0:T(8,128)(2,1)S(1)} %get-tuple-element.58._.refs_1_.first_sent.chip), channel_id=1, source_target_pairs={{0,2},{1,3},{2,0},{3,1},{4,6},{5,7},{6,4},{7,5},{8,10},{9,11},{10,... | collective-permute-start | bytes 184328 | tf_op jit(solution)/shard_map/ppermute | solution.py:96
  19.9 1.3 %collective-permute-start.8 = (bf16[64,768]{1,0:T(8,128)(2,1)S(1)}, bf16[64,768]{1,0:T(8,128)(2,1)S(1)}, u32[]{:S(2)}, u32[]{:S(2)}) collective-permute-start(bf16[64,768]{1,0:T(8,128)(2,1)S(1)} %shard_map.111.refs_0_.refs_2_), channel_id=1, source_target_pairs={{0,4},{4,0},{8,12},{12,8},{1,5},{5,1},{9,13},{13,9},{2,6},{6,2},{1... | collective-permute-start | bytes 294920 | tf_op jit(solution)/shard_map/ppermute | solution.py:96
  21.2 2.4 %shard_map.113.refs_9_.w = bf16[3072,768]{1,0:T(8,128)(2,1)S(1)} custom-call(bf16[3072,768]{1,0:T(8,128)(2,1)} %source.1, bf16[64,768]{1,0:T(8,128)(2,1)S(1)} %shard_map.111.refs_0_.refs_2_, bf16[16,1920]{1,0:T(8,128)(2,1)S(1)} %get-tuple-element.58._.refs_1_.first_sent.chip), custom_call_target="tpu_custom_call" | custom-call | flops 10000000000 | bytes 1 | tf_op jit(solution)/shard_map/pallas_call | solution.py:543
  23.7 1.0 %collective-permute-done.8.refs_3_ = bf16[64,768]{1,0:T(8,128)(2,1)S(1)} collective-permute-done((bf16[64,768]{1,0:T(8,128)(2,1)S(1)}, bf16[64,768]{1,0:T(8,128)(2,1)S(1)}, u32[]{:S(2)}, u32[]{:S(2)}) %collective-permute-start.8) | collective-permute-done | bytes 98336 | tf_op jit(solution)/shard_map/ppermute | solution.py:96
  24.7 0.9 %shard_map.114 = (bf16[128,768]{1,0:T(8,128)(2,1)S(1)}, bf16[128,1536]{1,0:T(8,128)(2,1)S(1)}, bf16[128,128]{1,0:T(8,128)(2,1)S(1)}) custom-call(f32[128,128]{1,0:T(8,128)S(1)} %get-tuple-element.60.text, f32[8,768]{1,0:T(8,128)S(1)} %get-tuple-element.45.mod, bf16[128,512]{1,0:T(8,128)(2,1)S(1)} %get-tuple-element.61.place, ...), custom_call_target="tpu_custom_call" | custom-call | flops 10000000000 | bytes 1 | tf_op jit(solution)/shard_map/pallas_call | solution.py:543
  26.9 1.4 %collective-permute-start.12 = (bf16[16,256]{1,0:T(8,128)(2,1)S(1)}, bf16[16,256]{1,0:T(8,128)(2,1)S(1)}, u32[]{:S(2)}, u32[]{:S(2)}) collective-permute-start(bf16[16,256]{1,0:T(8,128)(2,1)S(1)} %get-tuple-element.68._.refs_1_), channel_id=1, source_target_pairs={{0,2},{1,3},{2,0},{3,1},{4,6},{5,7},{6,4},{7,5},{8,10},{9,11},{10,... | collective-permute-start | bytes 24584 | tf_op jit(solution)/shard_map/ppermute | solution.py:96
  33.4 4.8 %collective-permute-start.13 = (bf16[64,768]{1,0:T(8,128)(2,1)S(1)}, bf16[64,768]{1,0:T(8,128)(2,1)S(1)}, u32[]{:S(2)}, u32[]{:S(2)}) collective-permute-start(bf16[64,768]{1,0:T(8,128)(2,1)S(1)} %get-tuple-element.74.refs_3_), channel_id=1, source_target_pairs={{0,12},{4,8},{8,4},{12,0},{1,13},{5,9},{9,5},{13,1},{2,14},{6,10},... | collective-permute-start | bytes 294920 | tf_op jit(solution)/shard_map/ppermute | solution.py:96
  40.4 1.2 %collective-permute-done.17.act = bf16[128,1536]{1,0:T(8,128)(2,1)S(1)} collective-permute-done((bf16[128,1536]{1,0:T(8,128)(2,1)S(1)}, bf16[128,1536]{1,0:T(8,128)(2,1)S(1)}, u32[]{:S(2)}, u32[]{:S(2)}) %collective-permute-start.17) | collective-permute-done | bytes 393248 | tf_op jit(solution)/shard_map/ppermute | solution.py:96
  42.4 3.3 %collective-permute-start.18 = (bf16[64,768]{1,0:T(8,128)(2,1)S(1)}, bf16[64,768]{1,0:T(8,128)(2,1)S(1)}, u32[]{:S(2)}, u32[]{:S(2)}) collective-permute-start(bf16[64,768]{1,0:T(8,128)(2,1)S(1)} %get-tuple-element.79), channel_id=1, source_target_pairs={{0,8},{4,12},{8,0},{12,4},{1,9},{5,13},{9,1},{13,5},{2,10},{6,14},... | collective-permute-start | bytes 294920 | tf_op jit(solution)/shard_map/ppermute | solution.py:96
  45.7 1.5 %collective-permute-start.19 = (bf16[64,768]{1,0:T(8,128)(2,1)S(1)}, bf16[64,768]{1,0:T(8,128)(2,1)S(1)}, u32[]{:S(2)}, u32[]{:S(2)}) collective-permute-start(bf16[64,768]{1,0:T(8,128)(2,1)S(1)} %get-tuple-element.80), channel_id=1, source_target_pairs={{0,12},{4,8},{8,4},{12,0},{1,13},{5,9},{9,5},{13,1},{2,14},{6,10},... | collective-permute-start | bytes 294920 | tf_op jit(solution)/shard_map/ppermute | solution.py:96
  47.8 5.8 %collective-permute-done.18.refs_2_ = bf16[64,768]{1,0:T(8,128)(2,1)S(1)} collective-permute-done((bf16[64,768]{1,0:T(8,128)(2,1)S(1)}, bf16[64,768]{1,0:T(8,128)(2,1)S(1)}, u32[]{:S(2)}, u32[]{:S(2)}) %collective-permute-start.18) | collective-permute-done | bytes 98336 | tf_op jit(solution)/shard_map/ppermute | solution.py:96
  53.6 0.9 %collective-permute-done.20.refs_4_ = bf16[64,768]{1,0:T(8,128)(2,1)S(1)} collective-permute-done((bf16[64,768]{1,0:T(8,128)(2,1)S(1)}, bf16[64,768]{1,0:T(8,128)(2,1)S(1)}, u32[]{:S(2)}, u32[]{:S(2)}) %collective-permute-start.20) | collective-permute-done | bytes 98336 | tf_op jit(solution)/shard_map/ppermute | solution.py:96
  55.0 1.2 %collective-permute-done.21.right = f32[32,128]{1,0:T(8,128)S(1)} collective-permute-done((f32[32,128]{1,0:T(8,128)S(1)}, f32[32,128]{1,0:T(8,128)S(1)}, u32[]{:S(2)}, u32[]{:S(2)}) %collective-permute-start.21) | collective-permute-done | bytes 16416 | tf_op jit(solution)/shard_map/ppermute | solution.py:96
  56.2 2.0 %collective-permute-start.22 = (f32[32,128]{1,0:T(8,128)S(1)}, f32[32,128]{1,0:T(8,128)S(1)}, u32[]{:S(2)}, u32[]{:S(2)}) collective-permute-start(f32[32,128]{1,0:T(8,128)S(1)} %shard_map.129.mine), channel_id=1, source_target_pairs={{0,18},{1,19},{2,16},{3,17},{16,2},{17,3},{18,0},{19,1},{4,22},{5,... | collective-permute-start | bytes 49160 | tf_op jit(solution)/shard_map/ppermute | solution.py:96
  58.7 1.0 %collective-permute-start.24 = (f32[32,128]{1,0:T(8,128)S(1)}, f32[32,128]{1,0:T(8,128)S(1)}, u32[]{:S(2)}, u32[]{:S(2)}) collective-permute-start(f32[32,128]{1,0:T(8,128)S(1)} %shard_map.129.mine), channel_id=1, source_target_pairs={{0,2},{1,3},{2,0},{3,1},{16,18},{17,19},{18,16},{19,17},{4,6},{5,7... | collective-permute-start | bytes 49160 | tf_op jit(solution)/shard_map/ppermute | solution.py:96
  60.8 1.1 %collective-permute-done.23.other = f32[32,128]{1,0:T(8,128)S(1)} collective-permute-done((f32[32,128]{1,0:T(8,128)S(1)}, f32[32,128]{1,0:T(8,128)S(1)}, u32[]{:S(2)}, u32[]{:S(2)}) %collective-permute-start.23) | collective-permute-done | bytes 16416 | tf_op jit(solution)/shard_map/ppermute | solution.py:96
  62.4 0.9 %shard_map.130 = f32[64,128]{1,0:T(8,128)} custom-call(f32[72,128]{1,0:T(8,128)S(1)} %shard_map.112.refs_8_.noise, f32[128,128]{1,0:T(8,128)S(1)} %get-tuple-element.69.ends, f32[32,128]{1,0:T(8,128)S(1)} %shard_map.129.mine, f32[32,128]{1,0:T(8,128)S(1)} %collective-permute-done.22.other_y, f32[32,128]{1,0:T(8,128)S(1)} %collective-permute-done.23.other, ...), custom_call_target="tpu_custom_call" | custom-call | flops 1 | bytes 1 | tf_op jit(solution)/shard_map/pallas_call | solution.py:543
  (57 shorter events, 15.2 us)
Async XLA Ops:
  1.5 9.0 %collective-permute-start.1 = (bf16[64,768]{1,0:T(8,128)(2,1)S(1)}, bf16[64,768]{1,0:T(8,128)(2,1)S(1)}, u32[]{:S(2)}, u32[]{:S(2)}) collective-permute-start(bf16[64,768]{1,0:T(8,128)(2,1)S(1)} %shard_map.105), channel_id=1, source_target_pairs={{0,8},{4,12},{8,0},{12,4},{1,9},{5,13},{9,1},{13,5},{2,10},{6,14},... | collective-permute-start | bytes 294920 | tf_op jit(solution)/shard_map/ppermute | solution.py:96
  5.6 9.6 %collective-permute-start = (bf16[128,768]{1,0:T(8,128)(2,1)}, bf16[128,768]{1,0:T(8,128)(2,1)S(1)}, u32[]{:S(2)}, u32[]{:S(2)}) collective-permute-start(bf16[128,768]{1,0:T(8,128)(2,1)} %bitcast.7), channel_id=1, source_target_pairs={{0,4},{4,0},{8,12},{12,8},{1,5},{5,1},{9,13},{13,9},{2,6},{6,2},{1... | collective-permute-start | bytes 589832 | tf_op jit(solution)/shard_map/ppermute | solution.py:96
  10.5 4.7 %collective-permute-start.2 = (bf16[64,768]{1,0:T(8,128)(2,1)S(1)}, bf16[64,768]{1,0:T(8,128)(2,1)S(1)}, u32[]{:S(2)}, u32[]{:S(2)}) collective-permute-start(bf16[64,768]{1,0:T(8,128)(2,1)S(1)} %shard_map.106.refs_0_), channel_id=1, source_target_pairs={{0,4},{4,0},{8,12},{12,8},{1,5},{5,1},{9,13},{13,9},{2,6},{6,2},{1... | collective-permute-start | bytes 294920 | tf_op jit(solution)/shard_map/ppermute | solution.py:96
  11.3 8.5 %collective-permute-start.7 = (bf16[64,768]{1,0:T(8,128)(2,1)S(1)}, bf16[64,768]{1,0:T(8,128)(2,1)S(1)}, u32[]{:S(2)}, u32[]{:S(2)}) collective-permute-start(bf16[64,768]{1,0:T(8,128)(2,1)S(1)} %get-tuple-element.62), channel_id=1, source_target_pairs={{0,8},{4,12},{8,0},{12,4},{1,9},{5,13},{9,1},{13,5},{2,10},{6,14},... | collective-permute-start | bytes 294920 | tf_op jit(solution)/shard_map/ppermute | solution.py:96
  16.1 1.3 %collective-permute-start.4 = (bf16[16,2688]{1,0:T(8,128)(2,1)S(1)}, bf16[16,2688]{1,0:T(8,128)(2,1)S(1)}, u32[]{:S(2)}, u32[]{:S(2)}) collective-permute-start(bf16[16,2688]{1,0:T(8,128)(2,1)S(1)} %get-tuple-element.55.__.side), channel_id=1, source_target_pairs={{0,1},{1,0},{2,3},{3,2},{4,5},{5,4},{6,7},{7,6},{8,9},{9,8},{10,11... | collective-permute-start | bytes 258056 | tf_op jit(solution)/shard_map/ppermute | solution.py:96
  16.2 3.0 %collective-permute-start.3 = (bf16[128,1536]{1,0:T(8,128)(2,1)S(1)}, bf16[128,1536]{1,0:T(8,128)(2,1)S(1)}, u32[]{:S(2)}, u32[]{:S(2)}) collective-permute-start(bf16[128,1536]{1,0:T(8,128)(2,1)S(1)} %get-tuple-element.54._), channel_id=1, source_target_pairs={{0,1},{1,0},{2,3},{3,2},{4,5},{5,4},{6,7},{7,6},{8,9},{9,8},{10,11... | collective-permute-start | bytes 1179656 | tf_op jit(solution)/shard_map/ppermute | solution.py:96
  17.6 11.5 %collective-permute-start.6 = (bf16[16,1920]{1,0:T(8,128)(2,1)S(1)}, bf16[16,1920]{1,0:T(8,128)(2,1)S(1)}, u32[]{:S(2)}, u32[]{:S(2)}) collective-permute-start(bf16[16,1920]{1,0:T(8,128)(2,1)S(1)} %get-tuple-element.58._.refs_1_.first_sent.chip), channel_id=1, source_target_pairs={{0,2},{1,3},{2,0},{3,1},{4,6},{5,7},{6,4},{7,5},{8,10},{9,11},{10,... | collective-permute-start | bytes 184328 | tf_op jit(solution)/shard_map/ppermute | solution.py:96
  19.3 11.1 %collective-permute-start.5 = (bf16[128,1536]{1,0:T(8,128)(2,1)S(1)}, bf16[128,1536]{1,0:T(8,128)(2,1)S(1)}, u32[]{:S(2)}, u32[]{:S(2)}) collective-permute-start(bf16[128,1536]{1,0:T(8,128)(2,1)S(1)} %shard_map.110._.refs_7_.total), channel_id=1, source_target_pairs={{0,2},{1,3},{2,0},{3,1},{4,6},{5,7},{6,4},{7,5},{8,10},{9,11},{10,... | collective-permute-start | bytes 1179656 | tf_op jit(solution)/shard_map/ppermute | solution.py:96
  19.9 4.8 %collective-permute-start.8 = (bf16[64,768]{1,0:T(8,128)(2,1)S(1)}, bf16[64,768]{1,0:T(8,128)(2,1)S(1)}, u32[]{:S(2)}, u32[]{:S(2)}) collective-permute-start(bf16[64,768]{1,0:T(8,128)(2,1)S(1)} %shard_map.111.refs_0_.refs_2_), channel_id=1, source_target_pairs={{0,4},{4,0},{8,12},{12,8},{1,5},{5,1},{9,13},{13,9},{2,6},{6,2},{1... | collective-permute-start | bytes 294920 | tf_op jit(solution)/shard_map/ppermute | solution.py:96
  25.6 1.3 %collective-permute-start.10 = (bf16[128,128]{1,0:T(8,128)(2,1)S(1)}, bf16[128,128]{1,0:T(8,128)(2,1)S(1)}, u32[]{:S(2)}, u32[]{:S(2)}) collective-permute-start(bf16[128,128]{1,0:T(8,128)(2,1)S(1)} %get-tuple-element.67.__.side), channel_id=1, source_target_pairs={{0,1},{1,0},{2,3},{3,2},{4,5},{5,4},{6,7},{7,6},{8,9},{9,8},{10,11... | collective-permute-start | bytes 98312 | tf_op jit(solution)/shard_map/ppermute | solution.py:96
  25.6 2.7 %collective-permute-start.9 = (bf16[128,1536]{1,0:T(8,128)(2,1)S(1)}, bf16[128,1536]{1,0:T(8,128)(2,1)S(1)}, u32[]{:S(2)}, u32[]{:S(2)}) collective-permute-start(bf16[128,1536]{1,0:T(8,128)(2,1)S(1)} %get-tuple-element.66._), channel_id=1, source_target_pairs={{0,1},{1,0},{2,3},{3,2},{4,5},{5,4},{6,7},{7,6},{8,9},{9,8},{10,11... | collective-permute-start | bytes 1179656 | tf_op jit(solution)/shard_map/ppermute | solution.py:96
  26.9 4.5 %collective-permute-start.12 = (bf16[16,256]{1,0:T(8,128)(2,1)S(1)}, bf16[16,256]{1,0:T(8,128)(2,1)S(1)}, u32[]{:S(2)}, u32[]{:S(2)}) collective-permute-start(bf16[16,256]{1,0:T(8,128)(2,1)S(1)} %get-tuple-element.68._.refs_1_), channel_id=1, source_target_pairs={{0,2},{1,3},{2,0},{3,1},{4,6},{5,7},{6,4},{7,5},{8,10},{9,11},{10,... | collective-permute-start | bytes 24584 | tf_op jit(solution)/shard_map/ppermute | solution.py:96
  28.4 11.0 %collective-permute-start.16 = (bf16[128,1536]{1,0:T(8,128)(2,1)S(1)}, bf16[128,1536]{1,0:T(8,128)(2,1)S(1)}, u32[]{:S(2)}, u32[]{:S(2)}) collective-permute-start(bf16[128,1536]{1,0:T(8,128)(2,1)S(1)} %shard_map.117.refs_0_.total), channel_id=1, source_target_pairs={{0,2},{1,3},{2,0},{3,1},{4,6},{5,7},{6,4},{7,5},{8,10},{9,11},{10,... | collective-permute-start | bytes 1179656 | tf_op jit(solution)/shard_map/ppermute | solution.py:96
  30.8 1.8 %collective-permute-start.11 = (bf16[128,1536]{1,0:T(8,128)(2,1)S(1)}, bf16[128,1536]{1,0:T(8,128)(2,1)S(1)}, u32[]{:S(2)}, u32[]{:S(2)}) collective-permute-start(bf16[128,1536]{1,0:T(8,128)(2,1)S(1)} %shard_map.119.act.refs_0_), channel_id=1, source_target_pairs={{0,1},{1,0},{2,3},{3,2},{4,5},{5,4},{6,7},{7,6},{8,9},{9,8},{10,11... | collective-permute-start | bytes 1179656 | tf_op jit(solution)/shard_map/ppermute | solution.py:96
  33.4 13.9 %collective-permute-start.13 = (bf16[64,768]{1,0:T(8,128)(2,1)S(1)}, bf16[64,768]{1,0:T(8,128)(2,1)S(1)}, u32[]{:S(2)}, u32[]{:S(2)}) collective-permute-start(bf16[64,768]{1,0:T(8,128)(2,1)S(1)} %get-tuple-element.74.refs_3_), channel_id=1, source_target_pairs={{0,12},{4,8},{8,4},{12,0},{1,13},{5,9},{9,5},{13,1},{2,14},{6,10},... | collective-permute-start | bytes 294920 | tf_op jit(solution)/shard_map/ppermute | solution.py:96
  38.2 9.5 %collective-permute-start.14 = (bf16[64,768]{1,0:T(8,128)(2,1)S(1)}, bf16[64,768]{1,0:T(8,128)(2,1)S(1)}, u32[]{:S(2)}, u32[]{:S(2)}) collective-permute-start(bf16[64,768]{1,0:T(8,128)(2,1)S(1)} %get-tuple-element.75.refs_2_), channel_id=1, source_target_pairs={{0,8},{4,12},{8,0},{12,4},{1,9},{5,13},{9,1},{13,5},{2,10},{6,14},... | collective-permute-start | bytes 294920 | tf_op jit(solution)/shard_map/ppermute | solution.py:96
  38.2 9.5 %collective-permute-start.15 = (bf16[64,768]{1,0:T(8,128)(2,1)S(1)}, bf16[64,768]{1,0:T(8,128)(2,1)S(1)}, u32[]{:S(2)}, u32[]{:S(2)}) collective-permute-start(bf16[64,768]{1,0:T(8,128)(2,1)S(1)} %get-tuple-element.76.refs_1_), channel_id=1, source_target_pairs={{0,4},{4,0},{8,12},{12,8},{1,5},{5,1},{9,13},{13,9},{2,6},{6,2},{1... | collective-permute-start | bytes 294920 | tf_op jit(solution)/shard_map/ppermute | solution.py:96
  39.9 1.8 %collective-permute-start.17 = (bf16[128,1536]{1,0:T(8,128)(2,1)S(1)}, bf16[128,1536]{1,0:T(8,128)(2,1)S(1)}, u32[]{:S(2)}, u32[]{:S(2)}) collective-permute-start(bf16[128,1536]{1,0:T(8,128)(2,1)S(1)} %shard_map.124.act), channel_id=1, source_target_pairs={{0,1},{1,0},{2,3},{3,2},{4,5},{5,4},{6,7},{7,6},{8,9},{9,8},{10,11... | collective-permute-start | bytes 1179656 | tf_op jit(solution)/shard_map/ppermute | solution.py:96
  42.4 11.2 %collective-permute-start.18 = (bf16[64,768]{1,0:T(8,128)(2,1)S(1)}, bf16[64,768]{1,0:T(8,128)(2,1)S(1)}, u32[]{:S(2)}, u32[]{:S(2)}) collective-permute-start(bf16[64,768]{1,0:T(8,128)(2,1)S(1)} %get-tuple-element.79), channel_id=1, source_target_pairs={{0,8},{4,12},{8,0},{12,4},{1,9},{5,13},{9,1},{13,5},{2,10},{6,14},... | collective-permute-start | bytes 294920 | tf_op jit(solution)/shard_map/ppermute | solution.py:96
  45.7 7.8 %collective-permute-start.19 = (bf16[64,768]{1,0:T(8,128)(2,1)S(1)}, bf16[64,768]{1,0:T(8,128)(2,1)S(1)}, u32[]{:S(2)}, u32[]{:S(2)}) collective-permute-start(bf16[64,768]{1,0:T(8,128)(2,1)S(1)} %get-tuple-element.80), channel_id=1, source_target_pairs={{0,12},{4,8},{8,4},{12,0},{1,13},{5,9},{9,5},{13,1},{2,14},{6,10},... | collective-permute-start | bytes 294920 | tf_op jit(solution)/shard_map/ppermute | solution.py:96
  47.3 7.2 %collective-permute-start.20 = (bf16[64,768]{1,0:T(8,128)(2,1)S(1)}, bf16[64,768]{1,0:T(8,128)(2,1)S(1)}, u32[]{:S(2)}, u32[]{:S(2)}) collective-permute-start(bf16[64,768]{1,0:T(8,128)(2,1)S(1)} %get-tuple-element.81), channel_id=1, source_target_pairs={{0,4},{4,0},{8,12},{12,8},{1,5},{5,1},{9,13},{13,9},{2,6},{6,2},{1... | collective-permute-start | bytes 294920 | tf_op jit(solution)/shard_map/ppermute | solution.py:96
  56.2 4.6 %collective-permute-start.22 = (f32[32,128]{1,0:T(8,128)S(1)}, f32[32,128]{1,0:T(8,128)S(1)}, u32[]{:S(2)}, u32[]{:S(2)}) collective-permute-start(f32[32,128]{1,0:T(8,128)S(1)} %shard_map.129.mine), channel_id=1, source_target_pairs={{0,18},{1,19},{2,16},{3,17},{16,2},{17,3},{18,0},{19,1},{4,22},{5,... | collective-permute-start | bytes 49160 | tf_op jit(solution)/shard_map/ppermute | solution.py:96
  58.2 3.7 %collective-permute-start.23 = (f32[32,128]{1,0:T(8,128)S(1)}, f32[32,128]{1,0:T(8,128)S(1)}, u32[]{:S(2)}, u32[]{:S(2)}) collective-permute-start(f32[32,128]{1,0:T(8,128)S(1)} %shard_map.129.mine), channel_id=1, source_target_pairs={{0,16},{1,17},{2,18},{3,19},{16,0},{17,1},{18,2},{19,3},{4,20},{5,... | collective-permute-start | bytes 49160 | tf_op jit(solution)/shard_map/ppermute | solution.py:96
  58.7 3.7 %collective-permute-start.24 = (f32[32,128]{1,0:T(8,128)S(1)}, f32[32,128]{1,0:T(8,128)S(1)}, u32[]{:S(2)}, u32[]{:S(2)}) collective-permute-start(f32[32,128]{1,0:T(8,128)S(1)} %shard_map.129.mine), channel_id=1, source_target_pairs={{0,2},{1,3},{2,0},{3,1},{16,18},{17,19},{18,16},{19,17},{4,6},{5,7... | collective-permute-start | bytes 49160 | tf_op jit(solution)/shard_map/ppermute | solution.py:96
  (3 other events, 8.8 us)
